TPU v7x, 32 devices: a whole 2x2x4 slice. The times are simulated.
32 devices in a mesh: dom: 8 (over z, y), chan: 4 (over x, core).
Axes of the slice: x: 2, y: 2, z: 4, core: 2. Of those that a mesh axis runs over, the one named last changes fastest.
Arguments:
- features: bfloat16 [256, 8192], P('chan', 'dom'), may hold values from -6 to 6
- cotangent: bfloat16 [256, 8192], P('chan', 'dom'), may hold values from -6 to 6
- weights: bfloat16 [9, 256, 256], P(None, 'chan'), may hold values from -0.375 to 0.375
- tile_values: float32 [512, 128, 128], P('dom'), may hold values from -0.046875 to 0.046875
- tile_cols: int32 [8, 8, 8], P('dom'), may hold values from 0 to 11, as said below
- send_list: int32 [8, 4, 128], P('dom'), may hold values from 0 to 1023
Outputs:
- input_grad: float32 [256, 8192], P('chan', 'dom')
- weight_grad: float32 [9, 256, 256], P(None, None, 'chan')
Inputs may be any that keep to these rules, and one draw needn't show every extreme that they name: `tile_cols`: values below 8 are blocks of the partition's own nodes; 8 + s is the block received from neighbour slot s. Tile 0 of row block r has column block r.
All inputs are finite; a program needn't handle non-finite values.
Results may differ from a plain program's by a relative error of at most 0.0003.
Values may be sent and summed in bfloat16 or wider, within the bound.
No kernel may reach another device: no remote copies, remote signals or barrier semaphores. Data moves between devices by JAX's collectives and lax.ppermute only.
A program may use at most 128 MiB of HBM per device.

v0:
```python
import types

import jax
import jax.numpy as jnp
from jax import lax
from jax.experimental import pallas as pl
from jax.experimental.pallas import tpu as pltpu
from jax.sharding import PartitionSpec as P

F32, BF16 = jnp.float32, jnp.bfloat16
SLOTS = 4
WIDE = 256
MIB = 1 << 20
RING = 8
KINDS = (2, 0, 3, 1)


def dot(a, b, contract=(1, 0)):
    return lax.dot_general(
        a, b, (((contract[0],), (contract[1],)), ((), ())), preferred_element_type=F32
    )


def halves(x):
    high = x.astype(BF16)
    return high, (x - high.astype(F32)).astype(BF16)


def call(body, ins, outs, scratch=(), flops=0):
    specs, operands = [], []
    for value in ins.values():
        x, place = value if isinstance(value, tuple) else (value, "vmem")
        if place == "vmem":
            x = pltpu.with_memory_space_constraint(x, pltpu.VMEM)
        specs.append(pl.BlockSpec(memory_space={"smem": pltpu.SMEM, "any": pl.ANY}.get(place, pltpu.VMEM)))
        operands.append(x)
    shapes = [
        pltpu.VMEM(shape, dtype) if kept else jax.ShapeDtypeStruct(shape, dtype)
        for shape, dtype, kept in outs.values()
    ]

    def kernel(*refs):
        n, m = len(ins), len(outs)
        i = types.SimpleNamespace(**dict(zip(ins, refs[:n])))
        o = types.SimpleNamespace(**dict(zip(outs, refs[n : n + m])))
        body(i, o, *refs[n + m :])

    got = pl.pallas_call(
        kernel,
        out_shape=shapes,
        in_specs=specs,
        out_specs=[pl.BlockSpec(memory_space=pltpu.VMEM)] * len(outs),
        scratch_shapes=list(scratch),
        compiler_params=pltpu.CompilerParams(vmem_limit_bytes=32 * MIB),
        cost_estimate=pl.CostEstimate(flops=flops, bytes_accessed=MIB, transcendentals=0),
    )(*operands)
    return dict(zip(outs, got))


def exchange(blocks):
    size = lax.axis_size("dom")
    pairs = [[], [], [], []]
    for p in range(size):
        odd, far = p % 2, (p // 2) % 2
        pairs[0].append((p, (p + 1) % size if odd else (p - 1) % size))
        pairs[1].append((p, (p - 1) % size if odd else (p + 1) % size))
        pairs[2].append((p, (p - 2) % size if far else (p + 2) % size))
        pairs[3].append((p, (p + 2) % size if far else (p - 2) % size))
    return [lax.ppermute(block, "dom", pairs[kind]) for block, kind in zip(blocks, KINDS)]


def dealt(side, forth1, back1, forth2, back2):
    odd, far = side[0] == 1, side[1] == 1
    kinds = [
        lambda: jnp.where(odd, forth1, back1),
        lambda: jnp.where(odd, back1, forth1),
        lambda: jnp.where(far, back2, forth2),
        lambda: jnp.where(far, forth2, back2),
    ]
    return [None if kind < 2 and forth1 is None else kinds[kind]() for kind in KINDS]


def undealt(side, got):
    odd, far = side[0] == 1, side[1] == 1
    k = [got[KINDS.index(kind)] for kind in range(SLOTS)]
    near = (None, None)
    if k[0] is not None:
        near = (jnp.where(odd, k[1], k[0]), jnp.where(odd, k[0], k[1]))
    return *near, jnp.where(far, k[2], k[3]), jnp.where(far, k[3], k[2])


def gather(x):
    size = lax.axis_size("chan")
    bit, blocks = size // 2, [x]
    while bit:
        blocks = blocks + [
            lax.ppermute(block, "chan", [(c, c ^ bit) for c in range(size)]) for block in blocks
        ]
        bit //= 2
    return blocks


def collect(place, blocks, out, base=0):
    masks, bit = [0], len(blocks) // 2
    while bit:
        masks = masks + [m ^ bit for m in masks]
        bit //= 2
    for mask, block in zip(masks, blocks):
        rows = block.shape[0]
        out[pl.ds(pl.multiple_of((place ^ mask) * rows, rows), rows), :] = block


def prepare(i, o, total, held, sems):
    count, tile, _ = held.shape
    nodes = o.pick.shape[0]
    blocks = nodes // tile
    odd, far = i.side[0], i.side[1]
    per_row = count // blocks
    copies = [
        pltpu.make_async_copy(
            i.tiles.at[pl.ds(r * per_row, per_row)], held.at[pl.ds(r * per_row, per_row)], sems.at[r]
        )
        for r in range(blocks)
    ]
    for copy in copies:
        copy.start()
    total[...] = jnp.zeros_like(total)
    rows = lax.broadcasted_iota(jnp.int32, (nodes, tile), 0)
    lists = i.lists[...]
    order = dealt(i.side, lists[0:1], lists[1:2], lists[2:3], lists[3:4])
    for k, wanted in enumerate(order):
        hit = rows == jnp.broadcast_to(wanted, rows.shape)
        o.pick[:, k * tile : (k + 1) * tile] = hit.astype(F32).astype(BF16)
    for r, copy in enumerate(copies):
        copy.wait()
        here = slice(r * tile, (r + 1) * tile)
        for j in range(per_row):
            col = i.cols[r * per_row + j]
            slot = col - blocks
            kind = jnp.where(slot < 2, slot ^ odd, slot ^ (1 - far))
            place = sum(jnp.where(kind == k, KINDS.index(k), 0) for k in range(SLOTS))
            col = jnp.where(slot >= 0, blocks + place, col)
            at = pl.ds(pl.multiple_of(col * tile, tile), tile)
            total[at, here] += held[r * per_row + j]
        high, low = halves(total[:, here])
        o.high[:, here] = high
        o.low[:, here] = low


def summed(both):
    rows = both.shape[0] // 2
    return both[:rows] + both[rows:]


def write_sends(sends, parts, extra=()):
    for k, ref in enumerate(sends):
        at, width = 0, ref.shape[1]
        for part in parts:
            ref[at : at + part.shape[0], :] = part[:, k * width : (k + 1) * width]
            at += part.shape[0]
        for blocks in extra:
            if blocks[k] is not None:
                ref[at : at + blocks[k].shape[0], :] = blocks[k]
                at += blocks[k].shape[0]


def back_halo(both, i, nodes):
    rows = both.shape[0] // 2
    return summed(dot(both, i.high[nodes:, :], (1, 1))) + dot(both[:rows], i.low[nodes:, :], (1, 1))


def correlate(u_high, u_low, g_high, g_low=None):
    total = dot(u_high, g_high, (1, 1))
    if u_low is not None:
        total += dot(u_low, g_high, (1, 1))
    if g_low is not None:
        total += dot(u_high, g_low, (1, 1))
    half = total.shape[1] // 2
    return jnp.concatenate([total[:, :half], total[:, half:]], axis=0)


def sends_of(o):
    return [getattr(o, f"send{k}") for k in range(SLOTS)]


def begin(i, o):
    local, nodes = i.own.shape
    blocks = [getattr(i, f"block{k}")[...] for k in range(len(vars(i)) - 7)]
    collect(i.side[3], [i.own[...]] + blocks, o.gathered)
    first = dot(i.weight[...], o.gathered[...])
    own = i.own[...].astype(F32)
    o.state[:local] = first
    o.state[local:] = own
    high, low = halves(first)
    o.both[:local] = high
    o.both[local : 2 * local] = i.own[...]
    o.both[2 * local : 3 * local] = low
    o.both[3 * local :] = jnp.zeros_like(low)
    feat = i.feat[...]
    back = dot(feat, i.high[nodes:, :], (1, 1)) + dot(feat, i.low[nodes:, :], (1, 1))
    write_sends(sends_of(o), [summed(dot(o.both[...], i.pick[...])), back])


def make_inner(step, top, chains):
    def inner(i, o):
        rows, nodes = o.part.shape
        local = rows // chains
        scale = 1.0 if step == top else 2.0
        width = i.both.shape[0] // 2
        lhs = jnp.concatenate([i.both[:rows], i.both[width : width + rows]], axis=0)
        for start in range(0, nodes, WIDE):
            here = slice(start, start + WIDE)
            total = summed(dot(lhs, i.high[:nodes, here])) + dot(lhs[:rows], i.low[:nodes, here])
            mixed = dot(i.weight[...], i.gathered[:, here])
            value = scale * total[:local] + mixed
            if step > 1:
                value -= i.before[:local, here]
            o.part[:local, here] = value
            if chains > 1:
                value = (1.0 if step == 1 else 2.0) * total[local:]
                if step > 1:
                    value -= i.before[local:, here]
                o.part[local:, here] = value
        if step == 1:
            feat = i.feat[...]
            for start in range(0, nodes, WIDE):
                here = slice(start, start + WIDE)
                o.fpart[:, here] = dot(feat, i.high[here, :], (1, 1)) + dot(feat, i.low[here, :], (1, 1))
        if step == 2:
            for start in range(0, nodes, WIDE):
                here = slice(start, start + WIDE)
                total = summed(dot(i.fboth[...], i.high[here, :], (1, 1)))
                total += dot(i.fboth[:local], i.low[here, :], (1, 1))
                o.fpart[:, here] = 2.0 * total - i.feat[:, here].astype(F32)

    return inner


def halo_product(i, lhs, rows, here, nodes):
    return summed(dot(lhs, i.high[nodes:, here])) + dot(lhs[:rows], i.low[nodes:, here])


def split_halos(i, rows):
    got = [getattr(i, f"halo{k}") for k in range(SLOTS)]
    high, low = halves(jnp.concatenate([ref[:rows, :] for ref in got], axis=1))
    return jnp.concatenate([high, low], axis=0)


def payload(i, at, rows, near=True):
    return undealt(
        i.side,
        [
            getattr(i, f"halo{k}")[at : at + rows, :] if near or kind >= 2 else None
            for k, kind in enumerate(KINDS)
        ],
    )


def make_outer(step, chains, following, ring):
    def outer(i, o):
        rows, nodes = i.part.shape
        local = rows // chains
        lhs = split_halos(i, rows)
        for start in range(0, nodes, WIDE):
            here = slice(start, start + WIDE)
            total = halo_product(i, lhs, rows, here, nodes)
            for chain in range(chains):
                mine = slice(chain * local, (chain + 1) * local)
                state = i.part[mine, here] + (1.0 if chain == 1 and step == 1 else 2.0) * total[mine]
                o.state[mine, here] = state
                high, low = halves(state)
                o.both[mine, here] = high
                o.both[rows + chain * local : rows + (chain + 1) * local, here] = low
        live = following * local
        moving = o.both[...]
        if following < chains:
            moving = jnp.concatenate([o.both[:live], o.both[rows : rows + live]], axis=0)
        parts, extra = [summed(dot(moving, i.pick[...]))], []
        if step <= 2:
            got = [getattr(i, f"halo{k}")[rows : rows + local, :] for k in range(SLOTS)]
            high, low = halves(jnp.concatenate(got, axis=1))
            lhs = jnp.concatenate([high, low], axis=0)
            for start in range(0, nodes, WIDE):
                here = slice(start, start + WIDE)
                total = summed(dot(lhs, i.pick[here, :], (1, 1)))
                high, low = halves(i.fpart[:, here] + (1.0 if step == 1 else 2.0) * total)
                o.fboth[:local, here] = high
                o.fboth[local:, here] = low
            if step == 1:
                parts.append(back_halo(o.fboth[...], i, nodes))
        if ring:
            unit = i.side[2]
            size = o.send0.shape[1]
            half = size // 2

            def at(offset):
                return (unit + offset + RING) % RING

            def newest(old):
                return 2.0 * correlate(
                    o.both[local : 2 * local], o.both[rows + local :], i.g_high[...], i.g_low[...]
                ) - old

            if step == 4:
                o.stack[0:4] = i.early[0:4]
                o.stack[4] = correlate(o.both[local : 2 * local], o.both[rows + local :], i.feat_all[...])
                o.stack[5] = i.early[4]
                o.stack[6] = newest(i.early[2])
                o.stack[7] = jnp.zeros_like(o.stack[7])
                forth = jnp.concatenate([o.stack[at(3)], o.stack[at(4), :half]], axis=0)
                back = jnp.concatenate([o.stack[at(-3)], o.stack[at(4), half:]], axis=0)
                extra.append(dealt(i.side, None, None, forth, back))
            if step == 5:
                _, _, m2, p2 = payload(i, rows, size + half, near=False)
                o.seven[...] = newest(i.stack[3])
                to_forth = i.stack[at(2)]
                to_back = i.stack[at(-2)]
                extra.append(
                    dealt(
                        i.side,
                        i.stack[at(1)] + m2[:size],
                        i.stack[at(-1)] + p2[:size],
                        jnp.concatenate([to_forth[:half] + m2[size:], to_forth[half:]], axis=0),
                        jnp.concatenate([to_back[:half], to_back[half:] + p2[size:]], axis=0),
                    )
                )
                extra.append([o.seven[...]] * SLOTS)
            if step == 6:
                m1, p1, m2, p2 = payload(i, rows, size)
                o.done[...] = i.stack[at(0)] + m1 + p1 + m2 + p2
                extra.append([o.done[...]] * SLOTS)
                m1, p1, m2, p2 = payload(i, rows + size, size)
                o.seven[...] = i.seven[...] + m1 + p1 + m2 + p2
                o.eight[...] = newest(i.stack[4])
                extra.append([o.eight[...]] * SLOTS)
                extra.append(dealt(i.side, None, None, m1, p1 + p2))
            if step == 7:
                m1, p1, m2, p2 = payload(i, rows, size)
                o.found[0] = i.done[...]
                for slot, value in enumerate((m1, p1, m2, p2)):
                    o.found[1 + slot] = value
                extra.append(dealt(i.side, m2, p2, m2[:half], p2[half:]))
                m1, p1, m2, p2 = payload(i, rows + size, size)
                o.eight[...] = i.eight[...] + m1 + p1 + m2 + p2
                extra.append(dealt(i.side, None, None, m1, p1 + p2))
                _, _, m2, p2 = payload(i, rows + 2 * size, size, near=False)
                o.seven[...] = i.seven[...] + m2 + p2
        write_sends(sends_of(o), parts, extra)

    return outer


def early(i, o):
    local = i.both1.shape[0] // 4
    o.early[0] = correlate(i.own[...], None, i.feat_all[...])
    for k in range(1, 4):
        ref = getattr(i, f"both{k}")
        o.early[k] = correlate(ref[local : 2 * local], ref[3 * local :], i.feat_all[...])
    o.early[4] = 2.0 * correlate(
        i.both3[local : 2 * local], i.both3[3 * local :], i.g_high[...], i.g_low[...]
    ) - o.early[1]


def make_last(scale):
    def last(i, o):
        rows, nodes = i.part.shape
        lhs = split_halos(i, rows)
        for start in range(0, nodes, WIDE):
            here = slice(start, start + WIDE)
            o.result[:, here] = i.part[:, here] + halo_product(i, lhs, rows, here, nodes)
        if not hasattr(i, "found"):
            return
        size = i.halo0.shape[1]
        half = size // 2

        def put(k, chunk):
            for h in range(2):
                o.grads[k, h * size : (h + 1) * size, :] = scale * chunk[h * half : (h + 1) * half].T

        unit = i.side[2]
        for slot, offset in enumerate((0, -1, 1, -2, 2)):
            where = (unit + offset + RING) % RING

            @pl.when(where < 7)
            def _():
                put(where, i.found[slot])

        m1, p1, _, _ = payload(i, rows, size)
        from_two = []
        for k, kind in enumerate(KINDS):
            ref = getattr(i, f"halo{k}")
            start = rows + (size if kind < 2 else 0)
            from_two.append(None if kind < 2 else ref[rows : rows + half, :])
        _, _, m2, p2 = undealt(i.side, from_two)
        for offset, chunk in ((-3, m1), (3, p1), (4, jnp.concatenate([m2, p2], axis=0))):
            where = (unit + offset + RING) % RING

            @pl.when(where < 7)
            def _():
                put(where, chunk)

        _, _, m2, p2 = payload(i, rows + half, size, near=False)
        put(7, i.seven[...])
        put(8, i.eight[...] + m2 + p2)

    return last


def after(x, marker):
    return lax.optimization_barrier((x, marker))


def local(features, cotangent, weights, tile_values, tile_cols, send_list):
    top = weights.shape[0] - 1
    channels, nodes = features.shape
    count, tile = tile_values.shape[0], tile_values.shape[-1]
    every = weights.shape[2]
    wide = nodes + SLOTS * tile
    parts = lax.axis_size("dom")
    ring = parts == RING and top == RING and channels * every == tile * tile
    place = lax.axis_index("dom")
    side = jnp.stack([place % 2, (place // 2) % 2, place, lax.axis_index("chan")]).astype(jnp.int32)
    side = (side, "smem")
    scale = float(parts * nodes) ** (-0.5)

    blocks = gather(cotangent)
    ready = call(
        prepare,
        dict(
            cols=(tile_cols.reshape(-1), "smem"), side=side, lists=(send_list[0], ""), tiles=(tile_values, "any")
        ),
        dict(
            high=((wide, nodes), BF16, True),
            low=((wide, nodes), BF16, True),
            pick=((nodes, SLOTS * tile), BF16, True),
        ),
        [
            pltpu.VMEM((wide, nodes), F32),
            pltpu.VMEM((count, tile, tile), F32),
            pltpu.SemaphoreType.DMA((nodes // tile,)),
        ],
    )
    matrix = dict(high=ready["high"], low=ready["low"])
    pick = dict(pick=ready["pick"])

    def messages(rows, extra=(0, 0)):
        return {
            f"send{k}": ((rows + extra[0 if kind < 2 else 1], tile), F32, False)
            for k, kind in enumerate(KINDS)
        }

    def state_outs(chains):
        rows = chains * channels
        return dict(state=((rows, nodes), F32, True), both=((2 * rows, nodes), BF16, True))

    got = call(
        begin,
        dict(
            side=side,
            own=(cotangent, ""),
            feat=(features, ""),
            weight=(weights[top], ""),
            **matrix,
            **pick,
            **{f"block{k}": (block, "") for k, block in enumerate(blocks[1:])},
        ),
        dict(gathered=((every, nodes), BF16, True), **state_outs(2), **messages(3 * channels)),
    )
    gathered = got["gathered"]
    chunk = ((tile, tile), F32, True)
    extras = {4: (0, tile + tile // 2), 5: (2 * tile, 2 * tile), 6: (2 * tile, 3 * tile), 7: (tile, tile // 2 + tile)}
    kept, before, boths = {}, None, {}
    result = None
    for step in range(1, top + 1):
        chains = 2 if step <= top - 2 else 1
        following = 2 if step + 1 <= top - 2 else 1
        halos = {f"halo{k}": (x, "") for k, x in enumerate(exchange([got[f"send{k}"] for k in range(SLOTS)]))}
        ins = dict(both=got["both"], weight=(weights[top - step], ""), gathered=gathered, **matrix)
        outs = dict(part=((chains * channels, nodes), F32, True))
        if step > 1:
            ins["before"] = before
        if step <= 2:
            ins["feat"] = (features, "")
            outs["fpart"] = ((channels, nodes), F32, True)
        if step == 2:
            ins["fboth"] = got["fboth"]
        inside = call(
            make_inner(step, top, chains), ins, outs, flops=2 * chains * channels * nodes * nodes * 3
        )
        part = inside["part"]
        if step == 1:
            feat, part = after(features, part)
            feat_blocks = gather(feat)
        if step == 3:
            back, part = after(got["fboth"], part)
            back_blocks = gather(back)
        if step == 4:

            def settle(i, o):
                n = len(feat_blocks)
                collect(i.side[3], [getattr(i, f"f{k}")[...] for k in range(n)], o.feat_all)
                rows = channels
                back = [getattr(i, f"b{k}") for k in range(n)]
                collect(i.side[3], [ref[:rows] for ref in back], o.g_high)
                collect(i.side[3], [ref[rows:] for ref in back], o.g_low)

            whole = ((every, nodes), BF16, True)
            kept = call(
                settle,
                dict(
                    side=side,
                    **{f"f{k}": (x, "") for k, x in enumerate(feat_blocks)},
                    **{f"b{k}": (x, "") for k, x in enumerate(back_blocks)},
                ),
                dict(feat_all=whole, g_high=whole, g_low=whole),
            )
            first = call(
                early,
                dict(own=(cotangent, ""), **kept, **{f"both{k}": boths[k] for k in (1, 2, 3)}),
                dict(early=((5, tile, tile), F32, True)),
            )
        if step == top:
            ins = dict(part=part, side=side, **matrix, **halos)
            outs = dict(result=((channels, nodes), F32, False))
            if ring:
                ins.update(found=got["found"], seven=got["seven"], eight=got["eight"])
                outs["grads"] = ((top + 1, every, channels), F32, False)
            final = call(make_last(scale), ins, outs)
            result = final["result"]
            break
        ins = dict(part=part, side=side, **matrix, **pick, **halos)
        outs = state_outs(chains)
        if step <= 2:
            ins["fpart"] = inside["fpart"]
            outs["fboth"] = ((2 * channels, nodes), BF16, True)
        extra = (0, 0)
        if ring and step >= 4:
            extra = extras[step]
            if step <= 6:
                ins.update(g_high=kept["g_high"], g_low=kept["g_low"])
            if step == 4:
                ins.update(feat_all=kept["feat_all"], early=first["early"])
                outs["stack"] = ((RING, tile, tile), F32, True)
            if step in (5, 6):
                ins["stack"] = stack
            if step >= 5:
                outs["seven"] = chunk
            if step >= 6:
                ins["seven"] = got["seven"]
                outs["eight"] = chunk
            if step == 6:
                outs["done"] = chunk
            if step == 7:
                ins.update(done=got["done"], eight=got["eight"])
                outs["found"] = ((5, tile, tile), F32, True)
        sent = following + (1 if step == 1 else 0)
        outs.update(messages(sent * channels, extra))
        before = got["state"]
        got = call(make_outer(step, chains, following, ring and step >= 4), ins, outs)
        boths[step] = got["both"]
        if step == 4 and ring:
            stack = got["stack"]
    if ring:
        return result, final["grads"]

    def rest(i, o):
        o.out[0:4] = i.early[0:4]
        o.out[5] = i.early[4]
        for k in (4, 5, 6):
            ref = getattr(i, f"both{k}")
            high, low = ref[channels : 2 * channels], ref[3 * channels :]
            if k == 4:
                o.out[4] = correlate(high, low, i.feat_all[...])
            o.out[k + 2] = 2.0 * correlate(high, low, i.g_high[...], i.g_low[...]) - o.out[k - 2]

    grads = call(
        rest,
        dict(early=first["early"], **kept, **{f"both{k}": boths[k] for k in (4, 5, 6)}),
        dict(out=((top + 1, 2 * channels, every // 2), F32, True)),
    )["out"]
    grads = lax.psum(grads, "dom").reshape(top + 1, 2, channels, every // 2)
    return result, grads.transpose(0, 1, 3, 2).reshape(top + 1, every, channels) * scale


def solution(mesh):
    placed = (
        P("chan", "dom"),
        P("chan", "dom"),
        P(None, "chan", None),
        P("dom", None, None),
        P("dom", None, None),
        P("dom", None, None),
    )
    return jax.shard_map(
        local,
        mesh=mesh,
        in_specs=placed,
        out_specs=(P("chan", "dom"), P(None, None, "chan")),
        check_vma=False,
    )
```

profile of v0, /device:TPU:0, one launch (start us, length us, event | category | flops | bytes accessed | tf_op | source)
XLA Modules:
  0.0 139.8 jit_solution(10294789268049777292)
XLA Ops:
  0.6 3.0 %collective-permute-start = (bf16[64,1024]{1,0:T(8,128)(2,1)}, bf16[64,1024]{1,0:T(8,128)(2,1)S(1)}, u32[]{:S(2)}, u32[]{:S(2)}) collective-permute-start(bf16[64,1024]{1,0:T(8,128)(2,1)} %refs_0_.1), channel_id=1, source_target_pairs={{0,2},{1,3},{2,0},{3,1},{4,6},{5,7},{6,4},{7,5},{8,10},{9,11},{10,... | collective-permute-start | bytes 393224 | tf_op jit(solution)/shard_map/ppermute | solution.py:97
  4.5 2.2 %copy-done = f32[64,128,128]{2,1,0:T(8,128)S(1)} copy-done((f32[64,128,128]{2,1,0:T(8,128)S(1)}, f32[64,128,128]{2,1,0:T(8,128)}, u32[]{:S(2)}) %copy-start) | copy-done | bytes 4194328
  7.4 6.2 %shard_map.77 = (bf16[1536,1024]{1,0:T(8,128)(2,1)S(1)}, bf16[1536,1024]{1,0:T(8,128)(2,1)S(1)}, bf16[1024,512]{1,0:T(8,128)(2,1)S(1)}) custom-call(s32[64]{0:T(128)S(1)} %reshape.7.refs_0_, s32[4]{0:T(128)S(1)} %pad_add_fusion.refs_1_.refs_0_, s32[4,128]{1,0:T(4,128)S(1)} %bitcast.23, f32[64,128,128]{2,1,0:T(8,128)S(1)} %copy-done), custom_call_target="tpu_custom_call" | custom-call | bytes 1048576 | tf_op jit(solution)/shard_map/pallas_call | solution.py:48
  15.1 1.8 %shard_map.78 = (bf16[256,1024]{1,0:T(8,128)(2,1)S(1)}, f32[128,1024]{1,0:T(8,128)S(1)}, bf16[256,1024]{1,0:T(8,128)(2,1)S(1)}, f32[192,128]{1,0:T(8,128)S(1)}, ...) custom-call(s32[4]{0:T(128)S(1)} %pad_add_fusion.refs_1_.refs_0_, ...), custom_call_target="tpu_custom_call" | custom-call | bytes 1048576 | tf_op jit(solution)/shard_map/pallas_call | solution.py:48
  16.9 1.7 %collective-permute-start.3 = (f32[192,128]{1,0:T(8,128)S(1)}, f32[192,128]{1,0:T(8,128)S(1)}, u32[]{:S(2)}, u32[]{:S(2)}) collective-permute-start(f32[192,128]{1,0:T(8,128)S(1)} %get-tuple-element.81), channel_id=1, source_target_pairs={{0,8},{4,12},{8,0},{12,4},{16,24},{20,28},{24,16},{28,20},{1,9},{5... | collective-permute-start | bytes 294920 | tf_op jit(solution)/shard_map/ppermute | solution.py:69
  18.6 3.4 %collective-permute-start.4 = (f32[192,128]{1,0:T(8,128)S(1)}, f32[192,128]{1,0:T(8,128)S(1)}, u32[]{:S(2)}, u32[]{:S(2)}) collective-permute-start(f32[192,128]{1,0:T(8,128)S(1)} %get-tuple-element.82), channel_id=1, source_target_pairs={{0,28},{4,8},{8,4},{12,16},{16,12},{20,24},{24,20},{28,0},{1,29},{... | collective-permute-start | bytes 294920 | tf_op jit(solution)/shard_map/ppermute | solution.py:69
  22.0 1.6 %collective-permute-start.5 = (f32[192,128]{1,0:T(8,128)S(1)}, f32[192,128]{1,0:T(8,128)S(1)}, u32[]{:S(2)}, u32[]{:S(2)}) collective-permute-start(f32[192,128]{1,0:T(8,128)S(1)} %get-tuple-element.83), channel_id=1, source_target_pairs={{0,24},{4,28},{8,16},{12,20},{16,8},{20,12},{24,0},{28,4},{1,25},{... | collective-permute-start | bytes 294920 | tf_op jit(solution)/shard_map/ppermute | solution.py:69
  23.8 2.3 %shard_map.79 = (f32[128,1024]{1,0:T(8,128)S(1)}, f32[64,1024]{1,0:T(8,128)S(1)}) custom-call(bf16[256,1024]{1,0:T(8,128)(2,1)S(1)} %get-tuple-element.77.refs_0_, bf16[64,256]{1,0:T(8,128)(2,1)S(1)} %get-tuple-element.154.refs_1_, bf16[256,1024]{1,0:T(8,128)(2,1)S(1)} %get-tuple-element.78.refs_2_, ...), custom_call_target="tpu_custom_call" | custom-call | flops 805306368 | bytes 1048576 | tf_op jit(solution)/shard_map/pallas_call | solution.py:48
  26.2 1.7 %collective-permute-done.4.refs_6_ = f32[192,128]{1,0:T(8,128)S(1)} collective-permute-done((f32[192,128]{1,0:T(8,128)S(1)}, f32[192,128]{1,0:T(8,128)S(1)}, u32[]{:S(2)}, u32[]{:S(2)}) %collective-permute-start.4) | collective-permute-done | bytes 98336 | tf_op jit(solution)/shard_map/ppermute | solution.py:69
  29.3 2.3 %shard_map.80 = (f32[128,1024]{1,0:T(8,128)S(1)}, bf16[256,1024]{1,0:T(8,128)(2,1)S(1)}, bf16[128,1024]{1,0:T(8,128)(2,1)S(1)}, f32[192,128]{1,0:T(8,128)S(1)}, ...) custom-call(f32[128,1024]{1,0:T(8,128)S(1)} %get-tuple-element.80.refs_0_, ...), custom_call_target="tpu_custom_call" | custom-call | bytes 1048576 | tf_op jit(solution)/shard_map/pallas_call | solution.py:48
  31.7 3.2 %collective-permute-start.8 = (f32[192,128]{1,0:T(8,128)S(1)}, f32[192,128]{1,0:T(8,128)S(1)}, u32[]{:S(2)}, u32[]{:S(2)}) collective-permute-start(f32[192,128]{1,0:T(8,128)S(1)} %get-tuple-element.91), channel_id=1, source_target_pairs={{0,28},{4,8},{8,4},{12,16},{16,12},{20,24},{24,20},{28,0},{1,29},{... | collective-permute-start | bytes 294920 | tf_op jit(solution)/shard_map/ppermute | solution.py:69
  34.9 1.2 collective-permute-start.9
  37.1 2.4 %shard_map.81 = (f32[128,1024]{1,0:T(8,128)S(1)}, f32[64,1024]{1,0:T(8,128)S(1)}) custom-call(bf16[256,1024]{1,0:T(8,128)(2,1)S(1)} %get-tuple-element.86.refs_0_.refs_4_, bf16[64,256]{1,0:T(8,128)(2,1)S(1)} %get-tuple-element.153.refs_1_, bf16[256,1024]{1,0:T(8,128)(2,1)S(1)} %get-tuple-element.78.refs_2_, ...), custom_call_target="tpu_custom_call" | custom-call | flops 805306368 | bytes 1048576 | tf_op jit(solution)/shard_map/pallas_call | solution.py:48
  41.6 1.7 %shard_map.82 = (f32[128,1024]{1,0:T(8,128)S(1)}, bf16[256,1024]{1,0:T(8,128)(2,1)S(1)}, bf16[128,1024]{1,0:T(8,128)(2,1)S(1)}, f32[128,128]{1,0:T(8,128)S(1)}, ...) custom-call(f32[128,1024]{1,0:T(8,128)S(1)} %get-tuple-element.89.refs_0_, ...), custom_call_target="tpu_custom_call" | custom-call | bytes 1048576 | tf_op jit(solution)/shard_map/pallas_call | solution.py:48
  43.3 1.3 shard_map.83.refs_0_
  45.2 1.5 %collective-permute-start.19 = (bf16[64,1024]{1,0:T(8,128)(2,1)S(1)}, bf16[64,1024]{1,0:T(8,128)(2,1)S(1)}, u32[]{:S(2)}, u32[]{:S(2)}) collective-permute-start(bf16[64,1024]{1,0:T(8,128)(2,1)S(1)} %copy-done.1), channel_id=1, source_target_pairs={{0,2},{1,3},{2,0},{3,1},{4,6},{5,7},{6,4},{7,5},{8,10},{9,11},{10,... | collective-permute-start | bytes 393224 | tf_op jit(solution)/shard_map/ppermute | solution.py:97
  47.6 1.4 collective-permute-start.12
  49.0 4.7 %collective-permute-done.22.refs_6_ = bf16[128,1024]{1,0:T(8,128)(2,1)S(1)} collective-permute-done((bf16[128,1024]{1,0:T(8,128)(2,1)S(1)}, bf16[128,1024]{1,0:T(8,128)(2,1)S(1)}, u32[]{:S(2)}, u32[]{:S(2)}) %collective-permute-start.22) | collective-permute-done | bytes 262176 | tf_op jit(solution)/shard_map/ppermute | solution.py:97
  53.8 1.4 %collective-permute-done.19.refs_2_ = bf16[64,1024]{1,0:T(8,128)(2,1)S(1)} collective-permute-done((bf16[64,1024]{1,0:T(8,128)(2,1)S(1)}, bf16[64,1024]{1,0:T(8,128)(2,1)S(1)}, u32[]{:S(2)}, u32[]{:S(2)}) %collective-permute-start.19) | collective-permute-done | bytes 131104 | tf_op jit(solution)/shard_map/ppermute | solution.py:97
  56.4 4.9 %collective-permute-done.13.refs_7_ = f32[128,128]{1,0:T(8,128)S(1)} collective-permute-done((f32[128,128]{1,0:T(8,128)S(1)}, f32[128,128]{1,0:T(8,128)S(1)}, u32[]{:S(2)}, u32[]{:S(2)}) %collective-permute-start.13) | collective-permute-done | bytes 65568 | tf_op jit(solution)/shard_map/ppermute | solution.py:69
  61.9 3.6 %collective-permute-done.14.refs_8_ = f32[128,128]{1,0:T(8,128)S(1)} collective-permute-done((f32[128,128]{1,0:T(8,128)S(1)}, f32[128,128]{1,0:T(8,128)S(1)}, u32[]{:S(2)}, u32[]{:S(2)}) %collective-permute-start.14) | collective-permute-done | bytes 65568 | tf_op jit(solution)/shard_map/ppermute | solution.py:69
  65.5 1.4 %shard_map.84 = (f32[128,1024]{1,0:T(8,128)S(1)}, bf16[256,1024]{1,0:T(8,128)(2,1)S(1)}, f32[128,128]{1,0:T(8,128)S(1)}, f32[128,128]{1,0:T(8,128)S(1)}, f32[128,128]{1,0:T(8,128)S(1)}, /*index=5*/f32[128,128]{1,0:T(8,128)S(1)}) custom-call(f32[128,1024]{1,0:T(8,128)S(1)} %shard_map.83.refs_0_, s32[4]{0:T(128)S(1)} %pad_add_fusion.refs_1_.refs_0_, ...), custom_call_target="tpu_custom_call" | custom-call | bytes 1048576 | tf_op jit(solution)/shard_map/pallas_call | solution.py:48
  67.0 1.7 %collective-permute-start.16 = (f32[128,128]{1,0:T(8,128)S(1)}, f32[128,128]{1,0:T(8,128)S(1)}, u32[]{:S(2)}, u32[]{:S(2)}) collective-permute-start(f32[128,128]{1,0:T(8,128)S(1)} %get-tuple-element.106), channel_id=1, source_target_pairs={{0,28},{4,8},{8,4},{12,16},{16,12},{20,24},{24,20},{28,0},{1,29},{... | collective-permute-start | bytes 196616 | tf_op jit(solution)/shard_map/ppermute | solution.py:69
  68.7 1.9 %collective-permute-start.17 = (f32[128,128]{1,0:T(8,128)S(1)}, f32[128,128]{1,0:T(8,128)S(1)}, u32[]{:S(2)}, u32[]{:S(2)}) collective-permute-start(f32[128,128]{1,0:T(8,128)S(1)} %get-tuple-element.107), channel_id=1, source_target_pairs={{0,24},{4,28},{8,16},{12,20},{16,8},{20,12},{24,0},{28,4},{1,25},{... | collective-permute-start | bytes 196616 | tf_op jit(solution)/shard_map/ppermute | solution.py:69
  70.7 1.7 %collective-permute-start.18 = (f32[128,128]{1,0:T(8,128)S(1)}, f32[128,128]{1,0:T(8,128)S(1)}, u32[]{:S(2)}, u32[]{:S(2)}) collective-permute-start(f32[128,128]{1,0:T(8,128)S(1)} %get-tuple-element.108), channel_id=1, source_target_pairs={{0,4},{4,0},{8,12},{12,8},{16,20},{20,16},{24,28},{28,24},{1,5},{5... | collective-permute-start | bytes 196616 | tf_op jit(solution)/shard_map/ppermute | solution.py:69
  74.1 1.7 %shard_map.87.refs_12_ = f32[5,128,128]{2,1,0:T(8,128)S(1)} custom-call(bf16[64,1024]{1,0:T(8,128)(2,1)S(1)} %copy-done.2, bf16[256,1024]{1,0:T(8,128)(2,1)S(1)} %get-tuple-element.113.refs_1_.refs_11_, bf16[256,1024]{1,0:T(8,128)(2,1)S(1)} %get-tuple-element.111.refs_2_.refs_9_, bf16[256,1024]{1,0:T(8,128)(2,1)S(1)} %get-tuple-element.112.refs_3_.refs_10_, ...), custom_call_target="tpu_custom_call" | custom-call | bytes 1048576 | tf_op jit(solution)/shard_map/pallas_call | solution.py:48
  75.9 2.3 %shard_map.88 = (f32[128,1024]{1,0:T(8,128)S(1)}, bf16[256,1024]{1,0:T(8,128)(2,1)S(1)}, f32[8,128,128]{2,1,0:T(8,128)S(1)}, f32[320,128]{1,0:T(8,128)S(1)}, f32...) custom-call(f32[128,1024]{1,0:T(8,128)S(1)} %shard_map.85.refs_0_, ...), custom_call_target="tpu_custom_call" | custom-call | bytes 1048576 | tf_op jit(solution)/shard_map/pallas_call | solution.py:48
  78.3 2.0 %collective-permute-start.27 = (f32[320,128]{1,0:T(8,128)S(1)}, f32[320,128]{1,0:T(8,128)S(1)}, u32[]{:S(2)}, u32[]{:S(2)}) collective-permute-start(f32[320,128]{1,0:T(8,128)S(1)} %get-tuple-element.118), channel_id=1, source_target_pairs={{0,24},{4,28},{8,16},{12,20},{16,8},{20,12},{24,0},{28,4},{1,25},{... | collective-permute-start | bytes 491528 | tf_op jit(solution)/shard_map/ppermute | solution.py:69
  80.3 2.1 %collective-permute-start.26 = (f32[128,128]{1,0:T(8,128)S(1)}, f32[128,128]{1,0:T(8,128)S(1)}, u32[]{:S(2)}, u32[]{:S(2)}) collective-permute-start(f32[128,128]{1,0:T(8,128)S(1)} %get-tuple-element.117), channel_id=1, source_target_pairs={{0,28},{4,8},{8,4},{12,16},{16,12},{20,24},{24,20},{28,0},{1,29},{... | collective-permute-start | bytes 196616 | tf_op jit(solution)/shard_map/ppermute | solution.py:69
  82.8 1.1 shard_map.89.refs_0_
  83.9 3.5 %collective-permute-done.26.refs_6_ = f32[128,128]{1,0:T(8,128)S(1)} collective-permute-done((f32[128,128]{1,0:T(8,128)S(1)}, f32[128,128]{1,0:T(8,128)S(1)}, u32[]{:S(2)}, u32[]{:S(2)}) %collective-permute-start.26) | collective-permute-done | bytes 65568 | tf_op jit(solution)/shard_map/ppermute | solution.py:69
  87.4 2.3 %shard_map.90 = (f32[128,1024]{1,0:T(8,128)S(1)}, bf16[256,1024]{1,0:T(8,128)(2,1)S(1)}, f32[128,128]{1,0:T(8,128)S(1)}, f32[384,128]{1,0:T(8,128)S(1)}, f32[384...) custom-call(f32[128,1024]{1,0:T(8,128)S(1)} %shard_map.89.refs_0_, ...), custom_call_target="tpu_custom_call" | custom-call | bytes 1048576 | tf_op jit(solution)/shard_map/pallas_call | solution.py:48
  89.8 2.6 %collective-permute-start.30 = (f32[384,128]{1,0:T(8,128)S(1)}, f32[384,128]{1,0:T(8,128)S(1)}, u32[]{:S(2)}, u32[]{:S(2)}) collective-permute-start(f32[384,128]{1,0:T(8,128)S(1)} %get-tuple-element.124), channel_id=1, source_target_pairs={{0,28},{4,8},{8,4},{12,16},{16,12},{20,24},{24,20},{28,0},{1,29},{... | collective-permute-start | bytes 589832 | tf_op jit(solution)/shard_map/ppermute | solution.py:69
  92.4 1.9 %collective-permute-start.31 = (f32[384,128]{1,0:T(8,128)S(1)}, f32[384,128]{1,0:T(8,128)S(1)}, u32[]{:S(2)}, u32[]{:S(2)}) collective-permute-start(f32[384,128]{1,0:T(8,128)S(1)} %get-tuple-element.125), channel_id=1, source_target_pairs={{0,24},{4,28},{8,16},{12,20},{16,8},{20,12},{24,0},{28,4},{1,25},{... | collective-permute-start | bytes 589832 | tf_op jit(solution)/shard_map/ppermute | solution.py:69
  95.2 1.1 shard_map.91.refs_0_
  96.2 2.1 %collective-permute-done.30.refs_6_ = f32[384,128]{1,0:T(8,128)S(1)} collective-permute-done((f32[384,128]{1,0:T(8,128)S(1)}, f32[384,128]{1,0:T(8,128)S(1)}, u32[]{:S(2)}, u32[]{:S(2)}) %collective-permute-start.30) | collective-permute-done | bytes 196640 | tf_op jit(solution)/shard_map/ppermute | solution.py:69
  98.4 2.3 %collective-permute-done.31.refs_7_ = f32[384,128]{1,0:T(8,128)S(1)} collective-permute-done((f32[384,128]{1,0:T(8,128)S(1)}, f32[384,128]{1,0:T(8,128)S(1)}, u32[]{:S(2)}, u32[]{:S(2)}) %collective-permute-start.31) | collective-permute-done | bytes 196640 | tf_op jit(solution)/shard_map/ppermute | solution.py:69
  100.7 2.3 %shard_map.92 = (f32[128,1024]{1,0:T(8,128)S(1)}, bf16[256,1024]{1,0:T(8,128)(2,1)S(1)}, f32[128,128]{1,0:T(8,128)S(1)}, f32[128,128]{1,0:T(8,128)S(1)}, f32[128...) custom-call(f32[128,1024]{1,0:T(8,128)S(1)} %shard_map.91.refs_0_, ...), custom_call_target="tpu_custom_call" | custom-call | bytes 1048576 | tf_op jit(solution)/shard_map/pallas_call | solution.py:48
  103.0 6.0 %collective-permute-start.33 = (f32[448,128]{1,0:T(8,128)S(1)}, f32[448,128]{1,0:T(8,128)S(1)}, u32[]{:S(2)}, u32[]{:S(2)}) collective-permute-start(f32[448,128]{1,0:T(8,128)S(1)} %get-tuple-element.130), channel_id=1, source_target_pairs={{0,8},{4,12},{8,0},{12,4},{16,24},{20,28},{24,16},{28,20},{1,9},{5... | collective-permute-start | bytes 688136 | tf_op jit(solution)/shard_map/ppermute | solution.py:69
  109.0 3.5 %collective-permute-start.35 = (f32[448,128]{1,0:T(8,128)S(1)}, f32[448,128]{1,0:T(8,128)S(1)}, u32[]{:S(2)}, u32[]{:S(2)}) collective-permute-start(f32[448,128]{1,0:T(8,128)S(1)} %get-tuple-element.132), channel_id=1, source_target_pairs={{0,24},{4,28},{8,16},{12,20},{16,8},{20,12},{24,0},{28,4},{1,25},{... | collective-permute-start | bytes 688136 | tf_op jit(solution)/shard_map/ppermute | solution.py:69
  112.5 2.2 %collective-permute-start.34 = (f32[320,128]{1,0:T(8,128)S(1)}, f32[320,128]{1,0:T(8,128)S(1)}, u32[]{:S(2)}, u32[]{:S(2)}) collective-permute-start(f32[320,128]{1,0:T(8,128)S(1)} %get-tuple-element.131), channel_id=1, source_target_pairs={{0,28},{4,8},{8,4},{12,16},{16,12},{20,24},{24,20},{28,0},{1,29},{... | collective-permute-start | bytes 491528 | tf_op jit(solution)/shard_map/ppermute | solution.py:69
  115.6 7.7 %collective-permute-done.34.refs_6_ = f32[320,128]{1,0:T(8,128)S(1)} collective-permute-done((f32[320,128]{1,0:T(8,128)S(1)}, f32[320,128]{1,0:T(8,128)S(1)}, u32[]{:S(2)}, u32[]{:S(2)}) %collective-permute-start.34) | collective-permute-done | bytes 163872 | tf_op jit(solution)/shard_map/ppermute | solution.py:69
  123.3 1.9 %shard_map.94 = (f32[64,1024]{1,0:T(8,128)}, bf16[128,1024]{1,0:T(8,128)(2,1)S(1)}, f32[128,128]{1,0:T(8,128)S(1)}, f32[128,128]{1,0:T(8,128)S(1)}, f32[5,128,12...) custom-call(f32[64,1024]{1,0:T(8,128)S(1)} %shard_map.93.refs_0_, ...), custom_call_target="tpu_custom_call" | custom-call | bytes 1048576 | tf_op jit(solution)/shard_map/pallas_call | solution.py:48
  126.2 2.1 %collective-permute-start.39 = (f32[256,128]{1,0:T(8,128)S(1)}, f32[256,128]{1,0:T(8,128)S(1)}, u32[]{:S(2)}, u32[]{:S(2)}) collective-permute-start(f32[256,128]{1,0:T(8,128)S(1)} %get-tuple-element.141), channel_id=1, source_target_pairs={{0,24},{4,28},{8,16},{12,20},{16,8},{20,12},{24,0},{28,4},{1,25},{... | collective-permute-start | bytes 393224 | tf_op jit(solution)/shard_map/ppermute | solution.py:69
  128.3 2.2 %collective-permute-start.38 = (f32[192,128]{1,0:T(8,128)S(1)}, f32[192,128]{1,0:T(8,128)S(1)}, u32[]{:S(2)}, u32[]{:S(2)}) collective-permute-start(f32[192,128]{1,0:T(8,128)S(1)} %get-tuple-element.140), channel_id=1, source_target_pairs={{0,28},{4,8},{8,4},{12,16},{16,12},{20,24},{24,20},{28,0},{1,29},{... | collective-permute-start | bytes 294920 | tf_op jit(solution)/shard_map/ppermute | solution.py:69
  131.4 4.3 %collective-permute-done.38.refs_5_ = f32[192,128]{1,0:T(8,128)S(1)} collective-permute-done((f32[192,128]{1,0:T(8,128)S(1)}, f32[192,128]{1,0:T(8,128)S(1)}, u32[]{:S(2)}, u32[]{:S(2)}) %collective-permute-start.38) | collective-permute-done | bytes 98336 | tf_op jit(solution)/shard_map/ppermute | solution.py:69
  136.1 2.5 %shard_map.96 = (f32[64,1024]{1,0:T(8,128)}, f32[9,256,64]{2,1,0:T(8,128)S(1)}) custom-call(f32[64,1024]{1,0:T(8,128)S(1)} %shard_map.95.refs_0_, s32[4]{0:T(128)S(1)} %pad_add_fusion.refs_1_.refs_0_, bf16[1536,1024]{1,0:T(8,128)(2,1)S(1)} %get-tuple-element.74.refs_4_.refs_3_.refs_2_, bf16[1536,1024]{1,0:T(8,128)(2,1)S(1)} %get-tuple-element.75.refs_5_.refs_4_.refs_3_, ...), custom_call_target="tpu_custom_call" | custom-call | bytes 1048576 | tf_op jit(solution)/shard_map/pallas_call | solution.py:48
  138.6 1.2 copy.8
  (68 shorter events, 17.8 us)
Async XLA Ops:
  0.6 12.9 %collective-permute-start = (bf16[64,1024]{1,0:T(8,128)(2,1)}, bf16[64,1024]{1,0:T(8,128)(2,1)S(1)}, u32[]{:S(2)}, u32[]{:S(2)}) collective-permute-start(bf16[64,1024]{1,0:T(8,128)(2,1)} %refs_0_.1), channel_id=1, source_target_pairs={{0,2},{1,3},{2,0},{3,1},{4,6},{5,7},{6,4},{7,5},{8,10},{9,11},{10,... | collective-permute-start | bytes 393224 | tf_op jit(solution)/shard_map/ppermute | solution.py:97
  3.6 10.5 %collective-permute-start.1 = (bf16[64,1024]{1,0:T(8,128)(2,1)}, bf16[64,1024]{1,0:T(8,128)(2,1)S(1)}, u32[]{:S(2)}, u32[]{:S(2)}) collective-permute-start(bf16[64,1024]{1,0:T(8,128)(2,1)} %refs_0_.1), channel_id=1, source_target_pairs={{0,1},{1,0},{2,3},{3,2},{4,5},{5,4},{6,7},{7,6},{8,9},{9,8},{10,11... | collective-permute-start | bytes 393224 | tf_op jit(solution)/shard_map/ppermute | solution.py:97
  4.5 2.2 %copy-start = (f32[64,128,128]{2,1,0:T(8,128)S(1)}, f32[64,128,128]{2,1,0:T(8,128)}, u32[]{:S(2)}) copy-start(f32[64,128,128]{2,1,0:T(8,128)} %refs_3_.1) | copy-start | bytes 12582916
  6.7 0.7 copy-start.3
  7.4 6.8 %copy-start.4 = (bf16[9,64,256]{2,1,0:T(8,128)(2,1)S(1)}, bf16[9,64,256]{2,1,0:T(8,128)(2,1)}, u32[]{:S(2)}) copy-start(bf16[9,64,256]{2,1,0:T(8,128)(2,1)} %param.8) | copy-start | bytes 884740
  7.4 7.8 %copy-start.1 = (bf16[64,1024]{1,0:T(8,128)(2,1)S(1)}, bf16[64,1024]{1,0:T(8,128)(2,1)}, u32[]{:S(2)}) copy-start(bf16[64,1024]{1,0:T(8,128)(2,1)} %refs_1_.2) | copy-start | bytes 393220
  7.4 7.8 %copy-start.2 = (bf16[64,1024]{1,0:T(8,128)(2,1)S(1)}, bf16[64,1024]{1,0:T(8,128)(2,1)}, u32[]{:S(2)}) copy-start(bf16[64,1024]{1,0:T(8,128)(2,1)} %refs_0_.1) | copy-start | bytes 393220
  13.6 1.6 %collective-permute-start.2 = (bf16[64,1024]{1,0:T(8,128)(2,1)S(1)}, bf16[64,1024]{1,0:T(8,128)(2,1)S(1)}, u32[]{:S(2)}, u32[]{:S(2)}) collective-permute-start(bf16[64,1024]{1,0:T(8,128)(2,1)S(1)} %collective-permute-done.refs_7_), channel_id=1, source_target_pairs={{0,1},{1,0},{2,3},{3,2},{4,5},{5,4},{6,7},{7,6},{8,9},{9,8},{10,11... | collective-permute-start | bytes 393224 | tf_op jit(solution)/shard_map/ppermute | solution.py:97
  16.9 9.2 %collective-permute-start.3 = (f32[192,128]{1,0:T(8,128)S(1)}, f32[192,128]{1,0:T(8,128)S(1)}, u32[]{:S(2)}, u32[]{:S(2)}) collective-permute-start(f32[192,128]{1,0:T(8,128)S(1)} %get-tuple-element.81), channel_id=1, source_target_pairs={{0,8},{4,12},{8,0},{12,4},{16,24},{20,28},{24,16},{28,20},{1,9},{5... | collective-permute-start | bytes 294920 | tf_op jit(solution)/shard_map/ppermute | solution.py:69
  18.6 9.3 %collective-permute-start.4 = (f32[192,128]{1,0:T(8,128)S(1)}, f32[192,128]{1,0:T(8,128)S(1)}, u32[]{:S(2)}, u32[]{:S(2)}) collective-permute-start(f32[192,128]{1,0:T(8,128)S(1)} %get-tuple-element.82), channel_id=1, source_target_pairs={{0,28},{4,8},{8,4},{12,16},{16,12},{20,24},{24,20},{28,0},{1,29},{... | collective-permute-start | bytes 294920 | tf_op jit(solution)/shard_map/ppermute | solution.py:69
  22.0 6.4 %collective-permute-start.5 = (f32[192,128]{1,0:T(8,128)S(1)}, f32[192,128]{1,0:T(8,128)S(1)}, u32[]{:S(2)}, u32[]{:S(2)}) collective-permute-start(f32[192,128]{1,0:T(8,128)S(1)} %get-tuple-element.83), channel_id=1, source_target_pairs={{0,24},{4,28},{8,16},{12,20},{16,8},{20,12},{24,0},{28,4},{1,25},{... | collective-permute-start | bytes 294920 | tf_op jit(solution)/shard_map/ppermute | solution.py:69
  23.6 5.7 %collective-permute-start.6 = (f32[192,128]{1,0:T(8,128)S(1)}, f32[192,128]{1,0:T(8,128)S(1)}, u32[]{:S(2)}, u32[]{:S(2)}) collective-permute-start(f32[192,128]{1,0:T(8,128)S(1)} %get-tuple-element.84), channel_id=1, source_target_pairs={{0,4},{4,0},{8,12},{12,8},{16,20},{20,16},{24,28},{28,24},{1,5},{5... | collective-permute-start | bytes 294920 | tf_op jit(solution)/shard_map/ppermute | solution.py:69
  31.6 7.8 %collective-permute-start.7 = (f32[192,128]{1,0:T(8,128)S(1)}, f32[192,128]{1,0:T(8,128)S(1)}, u32[]{:S(2)}, u32[]{:S(2)}) collective-permute-start(f32[192,128]{1,0:T(8,128)S(1)} %get-tuple-element.90), channel_id=1, source_target_pairs={{0,8},{4,12},{8,0},{12,4},{16,24},{20,28},{24,16},{28,20},{1,9},{5... | collective-permute-start | bytes 294920 | tf_op jit(solution)/shard_map/ppermute | solution.py:69
  31.7 8.6 %collective-permute-start.8 = (f32[192,128]{1,0:T(8,128)S(1)}, f32[192,128]{1,0:T(8,128)S(1)}, u32[]{:S(2)}, u32[]{:S(2)}) collective-permute-start(f32[192,128]{1,0:T(8,128)S(1)} %get-tuple-element.91), channel_id=1, source_target_pairs={{0,28},{4,8},{8,4},{12,16},{16,12},{20,24},{24,20},{28,0},{1,29},{... | collective-permute-start | bytes 294920 | tf_op jit(solution)/shard_map/ppermute | solution.py:69
  34.9 6.5 %collective-permute-start.9 = (f32[192,128]{1,0:T(8,128)S(1)}, f32[192,128]{1,0:T(8,128)S(1)}, u32[]{:S(2)}, u32[]{:S(2)}) collective-permute-start(f32[192,128]{1,0:T(8,128)S(1)} %get-tuple-element.92), channel_id=1, source_target_pairs={{0,24},{4,28},{8,16},{12,20},{16,8},{20,12},{24,0},{28,4},{1,25},{... | collective-permute-start | bytes 294920 | tf_op jit(solution)/shard_map/ppermute | solution.py:69
  36.1 5.5 %collective-permute-start.10 = (f32[192,128]{1,0:T(8,128)S(1)}, f32[192,128]{1,0:T(8,128)S(1)}, u32[]{:S(2)}, u32[]{:S(2)}) collective-permute-start(f32[192,128]{1,0:T(8,128)S(1)} %get-tuple-element.93), channel_id=1, source_target_pairs={{0,4},{4,0},{8,12},{12,8},{16,20},{20,16},{24,28},{28,24},{1,5},{5... | collective-permute-start | bytes 294920 | tf_op jit(solution)/shard_map/ppermute | solution.py:69
  44.6 9.2 %collective-permute-start.22 = (bf16[128,1024]{1,0:T(8,128)(2,1)S(1)}, bf16[128,1024]{1,0:T(8,128)(2,1)S(1)}, u32[]{:S(2)}, u32[]{:S(2)}) collective-permute-start(bf16[128,1024]{1,0:T(8,128)(2,1)S(1)} %get-tuple-element.110.refs_5_), channel_id=1, source_target_pairs={{0,2},{1,3},{2,0},{3,1},{4,6},{5,7},{6,4},{7,5},{8,10},{9,11},{10,... | collective-permute-start | bytes 786440 | tf_op jit(solution)/shard_map/ppermute | solution.py:97
  45.2 10.0 %collective-permute-start.19 = (bf16[64,1024]{1,0:T(8,128)(2,1)S(1)}, bf16[64,1024]{1,0:T(8,128)(2,1)S(1)}, u32[]{:S(2)}, u32[]{:S(2)}) collective-permute-start(bf16[64,1024]{1,0:T(8,128)(2,1)S(1)} %copy-done.1), channel_id=1, source_target_pairs={{0,2},{1,3},{2,0},{3,1},{4,6},{5,7},{6,4},{7,5},{8,10},{9,11},{10,... | collective-permute-start | bytes 393224 | tf_op jit(solution)/shard_map/ppermute | solution.py:97
  46.7 24.0 %collective-permute-start.23 = (bf16[128,1024]{1,0:T(8,128)(2,1)S(1)}, bf16[128,1024]{1,0:T(8,128)(2,1)S(1)}, u32[]{:S(2)}, u32[]{:S(2)}) collective-permute-start(bf16[128,1024]{1,0:T(8,128)(2,1)S(1)} %get-tuple-element.110.refs_5_), channel_id=1, source_target_pairs={{0,1},{1,0},{2,3},{3,2},{4,5},{5,4},{6,7},{7,6},{8,9},{9,8},{10,11... | collective-permute-start | bytes 786440 | tf_op jit(solution)/shard_map/ppermute | solution.py:97
  46.7 9.2 %collective-permute-start.11 = (f32[128,128]{1,0:T(8,128)S(1)}, f32[128,128]{1,0:T(8,128)S(1)}, u32[]{:S(2)}, u32[]{:S(2)}) collective-permute-start(f32[128,128]{1,0:T(8,128)S(1)} %get-tuple-element.99), channel_id=1, source_target_pairs={{0,8},{4,12},{8,0},{12,4},{16,24},{20,28},{24,16},{28,20},{1,9},{5... | collective-permute-start | bytes 196616 | tf_op jit(solution)/shard_map/ppermute | solution.py:69
  47.6 8.2 %collective-permute-start.12 = (f32[128,128]{1,0:T(8,128)S(1)}, f32[128,128]{1,0:T(8,128)S(1)}, u32[]{:S(2)}, u32[]{:S(2)}) collective-permute-start(f32[128,128]{1,0:T(8,128)S(1)} %get-tuple-element.100), channel_id=1, source_target_pairs={{0,28},{4,8},{8,4},{12,16},{16,12},{20,24},{24,20},{28,0},{1,29},{... | collective-permute-start | bytes 196616 | tf_op jit(solution)/shard_map/ppermute | solution.py:69
  53.8 19.7 %collective-permute-start.24 = (bf16[128,1024]{1,0:T(8,128)(2,1)S(1)}, bf16[128,1024]{1,0:T(8,128)(2,1)S(1)}, u32[]{:S(2)}, u32[]{:S(2)}) collective-permute-start(bf16[128,1024]{1,0:T(8,128)(2,1)S(1)} %collective-permute-done.22.refs_6_), channel_id=1, source_target_pairs={{0,1},{1,0},{2,3},{3,2},{4,5},{5,4},{6,7},{7,6},{8,9},{9,8},{10,11... | collective-permute-start | bytes 786440 | tf_op jit(solution)/shard_map/ppermute | solution.py:97
  55.2 6.1 %collective-permute-start.13 = (f32[128,128]{1,0:T(8,128)S(1)}, f32[128,128]{1,0:T(8,128)S(1)}, u32[]{:S(2)}, u32[]{:S(2)}) collective-permute-start(f32[128,128]{1,0:T(8,128)S(1)} %get-tuple-element.101), channel_id=1, source_target_pairs={{0,24},{4,28},{8,16},{12,20},{16,8},{20,12},{24,0},{28,4},{1,25},{... | collective-permute-start | bytes 196616 | tf_op jit(solution)/shard_map/ppermute | solution.py:69
  55.9 11.1 %collective-permute-start.20 = (bf16[64,1024]{1,0:T(8,128)(2,1)S(1)}, bf16[64,1024]{1,0:T(8,128)(2,1)S(1)}, u32[]{:S(2)}, u32[]{:S(2)}) collective-permute-start(bf16[64,1024]{1,0:T(8,128)(2,1)S(1)} %copy-done.1), channel_id=1, source_target_pairs={{0,1},{1,0},{2,3},{3,2},{4,5},{5,4},{6,7},{7,6},{8,9},{9,8},{10,11... | collective-permute-start | bytes 393224 | tf_op jit(solution)/shard_map/ppermute | solution.py:97
  55.9 12.9 %collective-permute-start.21 = (bf16[64,1024]{1,0:T(8,128)(2,1)S(1)}, bf16[64,1024]{1,0:T(8,128)(2,1)S(1)}, u32[]{:S(2)}, u32[]{:S(2)}) collective-permute-start(bf16[64,1024]{1,0:T(8,128)(2,1)S(1)} %collective-permute-done.19.refs_2_), channel_id=1, source_target_pairs={{0,1},{1,0},{2,3},{3,2},{4,5},{5,4},{6,7},{7,6},{8,9},{9,8},{10,11... | collective-permute-start | bytes 393224 | tf_op jit(solution)/shard_map/ppermute | solution.py:97
  61.3 4.3 %collective-permute-start.14 = (f32[128,128]{1,0:T(8,128)S(1)}, f32[128,128]{1,0:T(8,128)S(1)}, u32[]{:S(2)}, u32[]{:S(2)}) collective-permute-start(f32[128,128]{1,0:T(8,128)S(1)} %get-tuple-element.102), channel_id=1, source_target_pairs={{0,4},{4,0},{8,12},{12,8},{16,20},{20,16},{24,28},{28,24},{1,5},{5... | collective-permute-start | bytes 196616 | tf_op jit(solution)/shard_map/ppermute | solution.py:69
  66.9 8.9 %collective-permute-start.15 = (f32[128,128]{1,0:T(8,128)S(1)}, f32[128,128]{1,0:T(8,128)S(1)}, u32[]{:S(2)}, u32[]{:S(2)}) collective-permute-start(f32[128,128]{1,0:T(8,128)S(1)} %get-tuple-element.105), channel_id=1, source_target_pairs={{0,8},{4,12},{8,0},{12,4},{16,24},{20,28},{24,16},{28,20},{1,9},{5... | collective-permute-start | bytes 196616 | tf_op jit(solution)/shard_map/ppermute | solution.py:69
  67.0 8.8 %collective-permute-start.16 = (f32[128,128]{1,0:T(8,128)S(1)}, f32[128,128]{1,0:T(8,128)S(1)}, u32[]{:S(2)}, u32[]{:S(2)}) collective-permute-start(f32[128,128]{1,0:T(8,128)S(1)} %get-tuple-element.106), channel_id=1, source_target_pairs={{0,28},{4,8},{8,4},{12,16},{16,12},{20,24},{24,20},{28,0},{1,29},{... | collective-permute-start | bytes 196616 | tf_op jit(solution)/shard_map/ppermute | solution.py:69
  68.7 7.1 %collective-permute-start.17 = (f32[128,128]{1,0:T(8,128)S(1)}, f32[128,128]{1,0:T(8,128)S(1)}, u32[]{:S(2)}, u32[]{:S(2)}) collective-permute-start(f32[128,128]{1,0:T(8,128)S(1)} %get-tuple-element.107), channel_id=1, source_target_pairs={{0,24},{4,28},{8,16},{12,20},{16,8},{20,12},{24,0},{28,4},{1,25},{... | collective-permute-start | bytes 196616 | tf_op jit(solution)/shard_map/ppermute | solution.py:69
  70.7 5.2 %collective-permute-start.18 = (f32[128,128]{1,0:T(8,128)S(1)}, f32[128,128]{1,0:T(8,128)S(1)}, u32[]{:S(2)}, u32[]{:S(2)}) collective-permute-start(f32[128,128]{1,0:T(8,128)S(1)} %get-tuple-element.108), channel_id=1, source_target_pairs={{0,4},{4,0},{8,12},{12,8},{16,20},{20,16},{24,28},{28,24},{1,5},{5... | collective-permute-start | bytes 196616 | tf_op jit(solution)/shard_map/ppermute | solution.py:69
  78.2 9.2 %collective-permute-start.25 = (f32[320,128]{1,0:T(8,128)S(1)}, f32[320,128]{1,0:T(8,128)S(1)}, u32[]{:S(2)}, u32[]{:S(2)}) collective-permute-start(f32[320,128]{1,0:T(8,128)S(1)} %get-tuple-element.116), channel_id=1, source_target_pairs={{0,8},{4,12},{8,0},{12,4},{16,24},{20,28},{24,16},{28,20},{1,9},{5... | collective-permute-start | bytes 491528 | tf_op jit(solution)/shard_map/ppermute | solution.py:69
  78.3 9.1 %collective-permute-start.27 = (f32[320,128]{1,0:T(8,128)S(1)}, f32[320,128]{1,0:T(8,128)S(1)}, u32[]{:S(2)}, u32[]{:S(2)}) collective-permute-start(f32[320,128]{1,0:T(8,128)S(1)} %get-tuple-element.118), channel_id=1, source_target_pairs={{0,24},{4,28},{8,16},{12,20},{16,8},{20,12},{24,0},{28,4},{1,25},{... | collective-permute-start | bytes 491528 | tf_op jit(solution)/shard_map/ppermute | solution.py:69
  80.3 7.1 %collective-permute-start.26 = (f32[128,128]{1,0:T(8,128)S(1)}, f32[128,128]{1,0:T(8,128)S(1)}, u32[]{:S(2)}, u32[]{:S(2)}) collective-permute-start(f32[128,128]{1,0:T(8,128)S(1)} %get-tuple-element.117), channel_id=1, source_target_pairs={{0,28},{4,8},{8,4},{12,16},{16,12},{20,24},{24,20},{28,0},{1,29},{... | collective-permute-start | bytes 196616 | tf_op jit(solution)/shard_map/ppermute | solution.py:69
  82.4 5.0 %collective-permute-start.28 = (f32[128,128]{1,0:T(8,128)S(1)}, f32[128,128]{1,0:T(8,128)S(1)}, u32[]{:S(2)}, u32[]{:S(2)}) collective-permute-start(f32[128,128]{1,0:T(8,128)S(1)} %get-tuple-element.119), channel_id=1, source_target_pairs={{0,4},{4,0},{8,12},{12,8},{16,20},{20,16},{24,28},{28,24},{1,5},{5... | collective-permute-start | bytes 196616 | tf_op jit(solution)/shard_map/ppermute | solution.py:69
  89.7 6.5 %collective-permute-start.29 = (f32[384,128]{1,0:T(8,128)S(1)}, f32[384,128]{1,0:T(8,128)S(1)}, u32[]{:S(2)}, u32[]{:S(2)}) collective-permute-start(f32[384,128]{1,0:T(8,128)S(1)} %get-tuple-element.123), channel_id=1, source_target_pairs={{0,8},{4,12},{8,0},{12,4},{16,24},{20,28},{24,16},{28,20},{1,9},{5... | collective-permute-start | bytes 589832 | tf_op jit(solution)/shard_map/ppermute | solution.py:69
  89.8 8.6 %collective-permute-start.30 = (f32[384,128]{1,0:T(8,128)S(1)}, f32[384,128]{1,0:T(8,128)S(1)}, u32[]{:S(2)}, u32[]{:S(2)}) collective-permute-start(f32[384,128]{1,0:T(8,128)S(1)} %get-tuple-element.124), channel_id=1, source_target_pairs={{0,28},{4,8},{8,4},{12,16},{16,12},{20,24},{24,20},{28,0},{1,29},{... | collective-permute-start | bytes 589832 | tf_op jit(solution)/shard_map/ppermute | solution.py:69
  92.4 8.3 %collective-permute-start.31 = (f32[384,128]{1,0:T(8,128)S(1)}, f32[384,128]{1,0:T(8,128)S(1)}, u32[]{:S(2)}, u32[]{:S(2)}) collective-permute-start(f32[384,128]{1,0:T(8,128)S(1)} %get-tuple-element.125), channel_id=1, source_target_pairs={{0,24},{4,28},{8,16},{12,20},{16,8},{20,12},{24,0},{28,4},{1,25},{... | collective-permute-start | bytes 589832 | tf_op jit(solution)/shard_map/ppermute | solution.py:69
  94.4 6.3 %collective-permute-start.32 = (f32[384,128]{1,0:T(8,128)S(1)}, f32[384,128]{1,0:T(8,128)S(1)}, u32[]{:S(2)}, u32[]{:S(2)}) collective-permute-start(f32[384,128]{1,0:T(8,128)S(1)} %get-tuple-element.126), channel_id=1, source_target_pairs={{0,4},{4,0},{8,12},{12,8},{16,20},{20,16},{24,28},{28,24},{1,5},{5... | collective-permute-start | bytes 589832 | tf_op jit(solution)/shard_map/ppermute | solution.py:69
  103.0 20.3 %collective-permute-start.33 = (f32[448,128]{1,0:T(8,128)S(1)}, f32[448,128]{1,0:T(8,128)S(1)}, u32[]{:S(2)}, u32[]{:S(2)}) collective-permute-start(f32[448,128]{1,0:T(8,128)S(1)} %get-tuple-element.130), channel_id=1, source_target_pairs={{0,8},{4,12},{8,0},{12,4},{16,24},{20,28},{24,16},{28,20},{1,9},{5... | collective-permute-start | bytes 688136 | tf_op jit(solution)/shard_map/ppermute | solution.py:69
  109.0 14.3 %collective-permute-start.35 = (f32[448,128]{1,0:T(8,128)S(1)}, f32[448,128]{1,0:T(8,128)S(1)}, u32[]{:S(2)}, u32[]{:S(2)}) collective-permute-start(f32[448,128]{1,0:T(8,128)S(1)} %get-tuple-element.132), channel_id=1, source_target_pairs={{0,24},{4,28},{8,16},{12,20},{16,8},{20,12},{24,0},{28,4},{1,25},{... | collective-permute-start | bytes 688136 | tf_op jit(solution)/shard_map/ppermute | solution.py:69
  112.5 10.8 %collective-permute-start.34 = (f32[320,128]{1,0:T(8,128)S(1)}, f32[320,128]{1,0:T(8,128)S(1)}, u32[]{:S(2)}, u32[]{:S(2)}) collective-permute-start(f32[320,128]{1,0:T(8,128)S(1)} %get-tuple-element.131), channel_id=1, source_target_pairs={{0,28},{4,8},{8,4},{12,16},{16,12},{20,24},{24,20},{28,0},{1,29},{... | collective-permute-start | bytes 491528 | tf_op jit(solution)/shard_map/ppermute | solution.py:69
  114.7 8.6 %collective-permute-start.36 = (f32[320,128]{1,0:T(8,128)S(1)}, f32[320,128]{1,0:T(8,128)S(1)}, u32[]{:S(2)}, u32[]{:S(2)}) collective-permute-start(f32[320,128]{1,0:T(8,128)S(1)} %get-tuple-element.133), channel_id=1, source_target_pairs={{0,4},{4,0},{8,12},{12,8},{16,20},{20,16},{24,28},{28,24},{1,5},{5... | collective-permute-start | bytes 491528 | tf_op jit(solution)/shard_map/ppermute | solution.py:69
  125.2 11.0 %collective-permute-start.37 = (f32[256,128]{1,0:T(8,128)S(1)}, f32[256,128]{1,0:T(8,128)S(1)}, u32[]{:S(2)}, u32[]{:S(2)}) collective-permute-start(f32[256,128]{1,0:T(8,128)S(1)} %get-tuple-element.139), channel_id=1, source_target_pairs={{0,8},{4,12},{8,0},{12,4},{16,24},{20,28},{24,16},{28,20},{1,9},{5... | collective-permute-start | bytes 393224 | tf_op jit(solution)/shard_map/ppermute | solution.py:69
  126.2 9.9 %collective-permute-start.39 = (f32[256,128]{1,0:T(8,128)S(1)}, f32[256,128]{1,0:T(8,128)S(1)}, u32[]{:S(2)}, u32[]{:S(2)}) collective-permute-start(f32[256,128]{1,0:T(8,128)S(1)} %get-tuple-element.141), channel_id=1, source_target_pairs={{0,24},{4,28},{8,16},{12,20},{16,8},{20,12},{24,0},{28,4},{1,25},{... | collective-permute-start | bytes 393224 | tf_op jit(solution)/shard_map/ppermute | solution.py:69
  128.3 7.4 %collective-permute-start.38 = (f32[192,128]{1,0:T(8,128)S(1)}, f32[192,128]{1,0:T(8,128)S(1)}, u32[]{:S(2)}, u32[]{:S(2)}) collective-permute-start(f32[192,128]{1,0:T(8,128)S(1)} %get-tuple-element.140), channel_id=1, source_target_pairs={{0,28},{4,8},{8,4},{12,16},{16,12},{20,24},{24,20},{28,0},{1,29},{... | collective-permute-start | bytes 294920 | tf_op jit(solution)/shard_map/ppermute | solution.py:69
  130.5 5.7 %collective-permute-start.40 = (f32[192,128]{1,0:T(8,128)S(1)}, f32[192,128]{1,0:T(8,128)S(1)}, u32[]{:S(2)}, u32[]{:S(2)}) collective-permute-start(f32[192,128]{1,0:T(8,128)S(1)} %get-tuple-element.142), channel_id=1, source_target_pairs={{0,4},{4,0},{8,12},{12,8},{16,20},{20,16},{24,28},{28,24},{1,5},{5... | collective-permute-start | bytes 294920 | tf_op jit(solution)/shard_map/ppermute | solution.py:69
where the time goes:
time: 140 us
  starting transfers between devices  54.7 us (39%)
  waiting for transfers between devices  41.3 us (30%)
  Pallas kernels  38 us (27%)
  local copies, waits for them, and re-layouts  4.84 us (3%)
    ppermute x32, starting transfers between devices, exchange(): lax.ppermute(block, 'dom', pairs[kind])  48.5 us
    pallas_call x20, Pallas kernels, call(): pl.pallas_call(kernel, out_shape=shapes, in_specs=specs, out_specs=[pl.Bl...  38 us
    ppermute x32, waiting for transfers between devices, exchange(): lax.ppermute(block, 'dom', pairs[kind])  34.2 us
    ppermute x9, waiting for transfers between devices, gather(): lax.ppermute(block, 'chan', [(c, c ^ bit) for c in range(size)])  7.11 us
    ppermute x9, starting transfers between devices, gather(): lax.ppermute(block, 'chan', [(c, c ^ bit) for c in range(size)])  6.18 us
    unnamed x10, local copies, waits for them, and re-layouts  2.88 us
  transfers between devices with their start and end apart: 41, of which 17 were waited for; matrix products, arithmetic and copies ran while one was open for 1% of the time, Pallas kernels for 14%

commit v1 on v0

v1 whole, which is shorter than its diff:
```python
import types

import jax
import jax.numpy as jnp
from jax import lax
from jax.experimental import pallas as pl
from jax.experimental.pallas import tpu as pltpu
from jax.sharding import PartitionSpec as P

F32, BF16 = jnp.float32, jnp.bfloat16
SLOTS = 4
WIDE = 256
MIB = 1 << 20
RING = 8
KINDS = (2, 0, 3, 1)


def dot(a, b, contract=(1, 0)):
    return lax.dot_general(
        a, b, (((contract[0],), (contract[1],)), ((), ())), preferred_element_type=F32
    )


def halves(x):
    high = x.astype(BF16)
    return high, (x - high.astype(F32)).astype(BF16)


def call(body, ins, outs, scratch=(), flops=0):
    specs, operands = [], []
    for value in ins.values():
        x, place = value if isinstance(value, tuple) else (value, "vmem")
        if place:
            x = pltpu.with_memory_space_constraint(x, pltpu.VMEM if place == "vmem" else pltpu.HBM)
        specs.append(pl.BlockSpec(memory_space={"smem": pltpu.SMEM, "hbm": pltpu.HBM}.get(place, pltpu.VMEM)))
        operands.append(x)
    shapes = [
        pltpu.VMEM(shape, dtype) if kept else jax.ShapeDtypeStruct(shape, dtype)
        for shape, dtype, kept in outs.values()
    ]

    def kernel(*refs):
        n, m = len(ins), len(outs)
        i = types.SimpleNamespace(**dict(zip(ins, refs[:n])))
        o = types.SimpleNamespace(**dict(zip(outs, refs[n : n + m])))
        body(i, o, *refs[n + m :])

    got = pl.pallas_call(
        kernel,
        out_shape=shapes,
        in_specs=specs,
        out_specs=[pl.BlockSpec(memory_space=pltpu.VMEM)] * len(outs),
        scratch_shapes=list(scratch),
        compiler_params=pltpu.CompilerParams(vmem_limit_bytes=32 * MIB),
        cost_estimate=pl.CostEstimate(flops=flops, bytes_accessed=MIB, transcendentals=0),
    )(*operands)
    return dict(zip(outs, got))


def exchange(blocks):
    size = lax.axis_size("dom")
    pairs = [[], [], [], []]
    for p in range(size):
        odd, far = p % 2, (p // 2) % 2
        pairs[0].append((p, (p + 1) % size if odd else (p - 1) % size))
        pairs[1].append((p, (p - 1) % size if odd else (p + 1) % size))
        pairs[2].append((p, (p - 2) % size if far else (p + 2) % size))
        pairs[3].append((p, (p + 2) % size if far else (p - 2) % size))
    return [lax.ppermute(block, "dom", pairs[kind]) for block, kind in zip(blocks, KINDS)]


def sides():
    me = lax.axis_index("dom")
    return lax.rem(me, 2), lax.rem(lax.div(me, 2), 2)


def pairs_of_two(forth, back):
    far = sides()[1] == 1
    return {2: jnp.where(far, back, forth), 3: jnp.where(far, forth, back)}


def from_pairs(got):
    odd, far = sides()
    odd, far = odd == 1, far == 1
    near = (None, None)
    if 0 in got:
        near = (jnp.where(odd, got[1], got[0]), jnp.where(odd, got[0], got[1]))
    return *near, jnp.where(far, got[2], got[3]), jnp.where(far, got[3], got[2])


LAYOUT = {
    4: {1: (256,)},
    5: {1: (192,), 2: (128,), 3: (128,)},
    6: {1: (128,), 2: (128, 96), 3: (128, 96)},
    7: {0: (128,), 1: (256, 128), 2: (96, 64, 128), 3: (96, 64, 128)},
    8: {1: (192,), 2: (64, 128), 3: (64, 128)},
}


def carried(i, step, base, kind, index):
    rows = LAYOUT[step][kind]
    start = base + sum(rows[:index])
    return getattr(i, f"halo{KINDS.index(kind)}")[start : start + rows[index], :]


def parted(group):
    odd = sides()[0] == 1
    half = group.shape[0] // 2
    return jnp.where(odd, group[half:], group[:half]), jnp.where(odd, group[:half], group[half:])


def joined(own, other):
    odd = sides()[0] == 1
    return jnp.concatenate([jnp.where(odd, other, own), jnp.where(odd, own, other)], axis=0)


def added(rows, first, second):
    half = rows.shape[0] // 2
    return jnp.concatenate([rows[:half] + first, rows[half:] + second], axis=0)


def gather(x, hold=lambda block: block):
    size = lax.axis_size("chan")
    bit, blocks = size // 2, [x]
    while bit:
        blocks = blocks + [
            lax.ppermute(block, "chan", [(c, c ^ bit) for c in range(size)]) for block in blocks
        ]
        if bit == size // 2:
            blocks[1] = hold(blocks[1])
        bit //= 2
    return blocks


def collect(blocks, out):
    masks, bit = [0], len(blocks) // 2
    while bit:
        masks = masks + [m ^ bit for m in masks]
        bit //= 2
    place = lax.axis_index("chan")
    for mask, block in zip(masks, blocks):
        rows = block.shape[0]
        out[pl.ds(pl.multiple_of((place ^ mask) * rows, rows), rows), :] = block


def stack(i, o, sems):
    local = i.upper.shape[0]
    copies = [
        pltpu.make_async_copy(i.upper, o.both.at[pl.ds(0, local)], sems.at[0]),
        pltpu.make_async_copy(i.lower, o.both.at[pl.ds(local, local)], sems.at[1]),
    ]
    for copy in copies:
        copy.start()
    for copy in copies:
        copy.wait()


def prepare(i, o, total, held, sems):
    count, tile, _ = held.shape
    nodes = o.pick.shape[0]
    blocks = nodes // tile
    per_row = count // blocks
    copies = [
        pltpu.make_async_copy(
            i.tiles.at[pl.ds(r * per_row, per_row)], held.at[pl.ds(r * per_row, per_row)], sems.at[r]
        )
        for r in range(blocks)
    ]
    for copy in copies:
        copy.start()
    odd, far = sides()
    rows = lax.broadcasted_iota(jnp.int32, (nodes, tile), 0)
    lists = i.lists[0]
    near = jnp.where(odd == 1, lists[0:1], lists[1:2]), jnp.where(odd == 1, lists[1:2], lists[0:1])
    order = [*near, *pairs_of_two(lists[2:3], lists[3:4]).values()]
    for k, kind in enumerate(KINDS):
        hit = rows == jnp.broadcast_to(order[kind], rows.shape)
        o.pick[:, k * tile : (k + 1) * tile] = hit.astype(F32).astype(BF16)
    total[...] = jnp.zeros_like(total)
    for r, copy in enumerate(copies):
        copy.wait()
        here = slice(r * tile, (r + 1) * tile)
        for j in range(per_row):
            col = i.cols[0, r, j]
            slot = col - blocks
            kind = jnp.where(slot < 2, slot ^ odd, slot ^ (1 - far))
            place = sum(jnp.where(kind == k, KINDS.index(k), 0) for k in range(SLOTS))
            col = jnp.where(slot >= 0, blocks + place, col)
            at = pl.ds(pl.multiple_of(col * tile, tile), tile)
            total[at, here] += held[r * per_row + j]
        high, low = halves(total[:, here])
        o.high[:, here] = high
        o.low[:, here] = low
    channels = i.stacked.shape[0] // 2
    feat = i.stacked[channels:]
    o.back[...] = dot(feat, o.high[nodes:, :], (1, 1)) + dot(feat, o.low[nodes:, :], (1, 1))
    o.sent[...] = dot(i.stacked[:channels], o.pick[...])


def summed(both):
    rows = both.shape[0] // 2
    return both[:rows] + both[rows:]


def write_sends(o, parts, extra=None):
    for k, kind in enumerate(KINDS):
        ref = getattr(o, f"send{k}")
        at, width = 0, ref.shape[1]
        for part in parts:
            ref[at : at + part.shape[0], :] = part[:, k * width : (k + 1) * width]
            at += part.shape[0]
        for block in (extra or {}).get(kind, ()):
            ref[at : at + block.shape[0], :] = block
            at += block.shape[0]


def back_halo(both, i, nodes):
    rows = both.shape[0] // 2
    return summed(dot(both, i.high[nodes:, :], (1, 1))) + dot(both[:rows], i.low[nodes:, :], (1, 1))


def correlate(u_high, u_low, g_high, g_low=None):
    if u_low is None:
        total = dot(u_high, g_high)
    else:
        total = summed(dot(jnp.concatenate([u_high, u_low], axis=0), g_high))
    if g_low is not None:
        total += dot(u_high, g_low)
    half = total.shape[1] // 2
    return jnp.concatenate([total[:, :half], total[:, half:]], axis=0)


def transposed(x):
    return x.astype(F32).T.astype(BF16)


def begin(i, o):
    local = i.weight.shape[0]
    own = i.stacked[:local]
    collect([own] + [ref[:local, :] for name, ref in vars(i).items() if name.startswith("block")], o.gathered)
    first = dot(i.weight[...], o.gathered[...])
    o.state[:local] = first
    o.state[local:] = own.astype(F32)
    high, low = halves(first)
    o.both[:local] = high
    o.both[local : 2 * local] = own
    o.both[2 * local : 3 * local] = low
    o.both[3 * local :] = jnp.zeros_like(low)
    parts = summed(dot(jnp.concatenate([high, low], axis=0), i.pick[...])), i.sent[...], i.back[...]
    write_sends(o, parts)


def make_inner(step, top, chains):
    def inner(i, o):
        rows, nodes = o.part.shape
        local = rows // chains
        scale = 1.0 if step == top else 2.0
        width = i.both.shape[0] // 2
        lhs = jnp.concatenate([i.both[:rows], i.both[width : width + rows]], axis=0)
        for start in range(0, nodes, WIDE):
            here = slice(start, start + WIDE)
            total = summed(dot(lhs, i.high[:nodes, here])) + dot(lhs[:rows], i.low[:nodes, here])
            mixed = dot(i.weight[...], i.gathered[:, here])
            value = scale * total[:local] + mixed
            if step > 1:
                value -= i.before[:local, here]
            o.part[:local, here] = value
            if chains > 1:
                value = (1.0 if step == 1 else 2.0) * total[local:]
                if step > 1:
                    value -= i.before[local:, here]
                o.part[local:, here] = value
        if step == 1:
            feat = i.stacked[local:]
            for start in range(0, nodes, WIDE):
                here = slice(start, start + WIDE)
                o.fpart[:, here] = dot(feat, i.high[here, :], (1, 1)) + dot(feat, i.low[here, :], (1, 1))
        if step == 2:
            for start in range(0, nodes, WIDE):
                here = slice(start, start + WIDE)
                total = summed(dot(i.fboth[...], i.high[here, :], (1, 1)))
                total += dot(i.fboth[:local], i.low[here, :], (1, 1))
                o.fpart[:, here] = 2.0 * total - i.stacked[local:, here].astype(F32)
        if step <= 3:
            u_low = None if step == 1 else i.both[width + local : width + 2 * local]
            o.grad[...] = correlate(i.both[local : 2 * local], u_low, i.feat_t[...])

    return inner


def halo_product(i, lhs, rows, here, nodes):
    return summed(dot(lhs, i.high[nodes:, here])) + dot(lhs[:rows], i.low[nodes:, here])


def split_halos(i, rows):
    got = [getattr(i, f"halo{k}") for k in range(SLOTS)]
    high, low = halves(jnp.concatenate([ref[:rows, :] for ref in got], axis=1))
    return jnp.concatenate([high, low], axis=0)


def make_outer(step, chains, following, ring):
    def outer(i, o):
        rows, nodes = i.part.shape
        local = rows // chains
        lhs = split_halos(i, rows)
        for start in range(0, nodes, WIDE):
            here = slice(start, start + WIDE)
            total = halo_product(i, lhs, rows, here, nodes)
            for chain in range(chains):
                mine = slice(chain * local, (chain + 1) * local)
                state = i.part[mine, here] + (1.0 if chain == 1 and step == 1 else 2.0) * total[mine]
                o.state[mine, here] = state
                high, low = halves(state)
                o.both[mine, here] = high
                o.both[rows + chain * local : rows + (chain + 1) * local, here] = low
        live = following * local
        moving = o.both[...]
        if following < chains:
            moving = jnp.concatenate([o.both[:live], o.both[rows : rows + live]], axis=0)
        parts, extra = [summed(dot(moving, i.pick[...]))], []
        if step <= 2:
            got = [getattr(i, f"halo{k}")[rows : rows + local, :] for k in range(SLOTS)]
            high, low = halves(jnp.concatenate(got, axis=1))
            lhs = jnp.concatenate([high, low], axis=0)
            for start in range(0, nodes, WIDE):
                here = slice(start, start + WIDE)
                total = summed(dot(lhs, i.pick[here, :], (1, 1)))
                high, low = halves(i.fpart[:, here] + (1.0 if step == 1 else 2.0) * total)
                o.fboth[:local, here] = high
                o.fboth[local:, here] = low
            if step == 1:
                parts.append(back_halo(o.fboth[...], i, nodes))
        extra = None
        if ring:
            if chains > 1:
                state = o.both[local : 2 * local], o.both[rows + local : rows + 2 * local]

            def got(kind, index):
                return carried(i, step, rows, kind, index)

            def newest(old):
                return 2.0 * correlate(*state, i.g_high[...], i.g_low[...]) - old

            if step == 3:
                o.third[...] = correlate(*state, i.feat_t[...])
                group = jnp.concatenate([i.grad0[...], i.grad1[...], i.grad2[...], o.third[...]], axis=0)
                o.one[...], away = parted(group)
                extra = {1: [away]}
            if step == 4:
                one = i.one[...] + got(1, 0)
                half = one.shape[0] // 2
                o.one[...] = one
                o.fourth[...] = correlate(*state, i.feat_t[...])
                group = jnp.concatenate([o.fourth[...], i.fifth[...], newest(i.grad2[...])], axis=0)
                o.two[...], away = parted(group)
                extra = {1: [away], 2: [one[:half]], 3: [one[half:]]}
            if step == 5:
                one = added(i.one[...], got(2, 0), got(3, 0))
                two = i.two[...] + got(1, 0)
                half, quarter = one.shape[0] // 2, two.shape[0] // 2
                o.one[...], o.two[...] = one, two
                o.seven[...] = newest(i.third[...])
                extra = {1: [o.seven[...]], 2: [one[half:], two[:quarter]], 3: [one[:half], two[quarter:]]}
            if step == 6:
                one = added(i.one[...], got(3, 0), got(2, 0))
                two = added(i.two[...], got(2, 1), got(3, 1))
                seven = i.seven[...] + got(1, 0)
                eight = newest(i.fourth[...])
                half, quarter = seven.shape[0] // 2, two.shape[0] // 2
                o.one[...], o.two[...], o.seven[...], o.eight[...] = one, two, seven, eight
                extra = {
                    0: [eight],
                    1: [one, eight],
                    2: [two[quarter:], seven[:half], eight],
                    3: [two[:quarter], seven[half:], eight],
                }
            if step == 7:
                o.one[...] = joined(i.one[...], got(1, 0))
                two = added(i.two[...], got(3, 0), got(2, 0))
                seven = added(i.seven[...], got(2, 1), got(3, 1))
                m1, p1, m2, p2 = from_pairs({0: got(0, 0), 1: got(1, 1), 2: got(2, 2), 3: got(3, 2)})
                half = seven.shape[0] // 2
                o.two[...], o.seven[...] = two, seven
                o.eight[...] = i.eight[...] + m1 + p1 + m2 + p2
                on = pairs_of_two(m1, p1 + p2)
                extra = {1: [two], 2: [seven[half:], on[2]], 3: [seven[:half], on[3]]}
        write_sends(o, parts, extra)

    return outer


def settle(i, o):
    blocks = [ref for name, ref in vars(i).items() if name.startswith("block")]
    rows = blocks[0].shape[0] // 2
    for half, out in ((slice(0, rows), o.g_high), (slice(rows, None), o.g_low)):
        collect([ref[half, :] for ref in blocks], o.whole)
        out[...] = transposed(o.whole[...])
    local = i.both.shape[0] // 4
    o.fifth[...] = 2.0 * correlate(
        i.both[local : 2 * local], i.both[3 * local :], o.g_high[...], o.g_low[...]
    ) - i.grad1[...]


def make_last(step, scale, ring):
    def last(i, o):
        rows, nodes = i.part.shape
        lhs = split_halos(i, rows)
        for start in range(0, nodes, WIDE):
            here = slice(start, start + WIDE)
            o.result[:, here] = i.part[:, here] + halo_product(i, lhs, rows, here, nodes)
        if not ring:
            return

        def got(kind, index):
            return carried(i, step, rows, kind, index)

        def put(k, chunk):
            size = chunk.shape[0] // 2
            o.grads[k] = scale * jnp.concatenate([chunk[:size], chunk[size:]], axis=1)

        size = i.eight.shape[0]
        one, two = i.one[...], joined(i.two[...], got(1, 0))
        for k in range(4):
            put(k, one[k * size : (k + 1) * size])
        for k in range(3):
            put(4 + k, two[k * size : (k + 1) * size])
        put(7, added(i.seven[...], got(3, 0), got(2, 0)))
        _, _, m2, p2 = from_pairs({2: got(2, 1), 3: got(3, 1)})
        put(8, i.eight[...] + m2 + p2)

    return last


def after(x, marker):
    return lax.optimization_barrier((x, marker))


def local(features, cotangent, weights, tile_values, tile_cols, send_list):
    top = weights.shape[0] - 1
    channels, nodes = features.shape
    tile = tile_values.shape[-1]
    every = weights.shape[2]
    wide = nodes + SLOTS * tile
    parts = lax.axis_size("dom")
    ring = parts == RING and top == RING and channels * every == tile * tile and tile == 128
    scale = float(parts * nodes) ** (-0.5)
    sent_shape = ((channels, SLOTS * tile), F32, True)
    whole = ((every, nodes), BF16, True)
    turned = ((nodes, every), BF16, True)
    chunk = ((2 * channels, every // 2), F32, True)

    stacked = call(
        stack,
        dict(upper=(cotangent, "hbm"), lower=(features, "hbm")),
        dict(both=((2 * channels, nodes), BF16, True)),
        [pltpu.SemaphoreType.DMA((2,))],
    )["both"]
    ready = call(
        prepare,
        dict(
            cols=(tile_cols, "smem"),
            lists=(send_list, "load"),
            tiles=(tile_values, "hbm"),
            stacked=stacked,
        ),
        dict(
            high=((wide, nodes), BF16, True),
            low=((wide, nodes), BF16, True),
            pick=((nodes, SLOTS * tile), BF16, True),
            back=sent_shape,
            sent=sent_shape,
        ),
        [
            pltpu.VMEM((wide, nodes), F32),
            pltpu.VMEM(tile_values.shape, F32),
            pltpu.SemaphoreType.DMA((nodes // tile,)),
        ],
        flops=10**10,
    )
    matrix = dict(high=ready["high"], low=ready["low"])
    pick = dict(pick=ready["pick"])
    blocks = gather(stacked, lambda block: after(block, ready["back"])[0])

    def messages(rows, step):
        extra = LAYOUT.get(step, {}) if ring else {}
        return {
            f"send{k}": ((rows + sum(extra.get(kind, ())), tile), F32, False) for k, kind in enumerate(KINDS)
        }

    def state_outs(chains):
        rows = chains * channels
        return dict(state=((rows, nodes), F32, True), both=((2 * rows, nodes), BF16, True))

    named = {f"block{k}": (block, "") for k, block in enumerate(blocks[1:])}
    got = call(
        begin,
        dict(
            stacked=stacked,
            weight=(weights[top], ""),
            **pick,
            sent=ready["sent"],
            back=ready["back"],
            **named,
        ),
        dict(gathered=whole, **state_outs(2), **messages(3 * channels, 1)),
    )
    gathered = got["gathered"]

    def turn(i, o):
        rows = [ref[channels:, :] for name, ref in vars(i).items() if name.startswith("block")]
        collect([i.stacked[channels:]] + rows, o.whole)
        o.feat_t[...] = transposed(o.whole[...])

    feat_t = call(turn, dict(stacked=stacked, **named), dict(whole=whole, feat_t=turned))["feat_t"]
    before, boths, grads, back = None, {}, {}, None
    for step in range(1, top + 1):
        chains = 2 if step <= top - 2 else 1
        following = 2 if step + 1 <= top - 2 else 1
        halos = {f"halo{k}": (x, "") for k, x in enumerate(exchange([got[f"send{k}"] for k in range(SLOTS)]))}
        ins = dict(both=got["both"], weight=(weights[top - step], ""), gathered=gathered, **matrix)
        outs = dict(part=((chains * channels, nodes), F32, True))
        if step > 1:
            ins["before"] = before
        if step <= 2:
            ins["stacked"] = stacked
            outs["fpart"] = ((channels, nodes), F32, True)
        if step == 2:
            ins["fboth"] = got["fboth"]
        if step <= 3:
            ins["feat_t"] = feat_t
            outs["grad"] = chunk
        inside = call(
            make_inner(step, top, chains), ins, outs, flops=2 * chains * channels * nodes * nodes * 3
        )
        part = inside["part"]
        if step <= 3:
            grads[step - 1] = inside["grad"]
        if step == 3:
            back_blocks = gather(got["fboth"])
        if step == 4:
            back = call(
                settle,
                dict(
                    **{f"block{k}": (x, "") for k, x in enumerate(back_blocks)}, both=boths[3], grad1=grads[1]
                ),
                dict(g_high=turned, g_low=turned, whole=whole, fifth=chunk),
            )
        ins = dict(part=part, **matrix, **halos)
        if step == top:
            outs = dict(result=((channels, nodes), F32, False))
            if ring:
                ins.update({k: got[k] for k in ("one", "two", "seven", "eight")})
                outs["grads"] = ((top + 1, channels, every), F32, False)
            got = call(make_last(step, scale, ring), ins, outs)
            break
        ins.update(pick)
        outs = state_outs(chains)
        if step <= 2:
            ins["fpart"] = inside["fpart"]
            outs["fboth"] = ((2 * channels, nodes), BF16, True)
        if ring and step >= 3:
            one = ((4 * channels, every // 2), F32, True)
            two = ((3 * channels, every // 2), F32, True)
            if step in (3, 4):
                ins["feat_t"] = feat_t
            if step in (4, 5, 6):
                ins.update(g_high=back["g_high"], g_low=back["g_low"])
            if step == 3:
                ins.update({f"grad{k}": grads[k] for k in range(3)})
                outs.update(one=one, third=chunk)
            if step == 4:
                grads[3] = got["third"]
                ins.update(one=got["one"], grad2=grads[2], fifth=back["fifth"])
                outs.update(one=one, two=two, fourth=chunk)
            if step == 5:
                grads[4] = got["fourth"]
                ins.update(one=got["one"], two=got["two"], third=grads[3])
                outs.update(one=one, two=two, seven=chunk)
            if step == 6:
                ins.update({k: got[k] for k in ("one", "two", "seven")}, fourth=grads[4])
                outs.update(one=one, two=two, seven=chunk, eight=chunk)
            if step == 7:
                ins.update({k: got[k] for k in ("one", "two", "seven", "eight")})
                outs.update(one=((8 * channels, every // 2), F32, True), two=two, seven=chunk, eight=chunk)
        sent = following + (1 if step == 1 else 0)
        outs.update(messages(sent * channels, step + 1))
        before = got["state"]
        got = call(make_outer(step, chains, following, ring and step >= 3), ins, outs)
        boths[step] = got["both"]
    if ring:
        return got["result"], jnp.swapaxes(got["grads"], 1, 2)

    def rest(i, o):
        for k in range(3):
            o.out[k] = getattr(i, f"grad{k}")[...]
        o.out[5] = i.fifth[...]
        for k in range(3, 7):
            ref = getattr(i, f"both{k}")
            state = ref[channels : 2 * channels], ref[3 * channels :]
            if k <= 4:
                o.out[k] = correlate(*state, i.feat_t[...])
            if k >= 4:
                o.out[k + 2] = 2.0 * correlate(*state, i.g_high[...], i.g_low[...]) - o.out[k - 2]

    total = call(
        rest,
        dict(
            feat_t=feat_t,
            fifth=back["fifth"],
            g_high=back["g_high"],
            g_low=back["g_low"],
            **{f"grad{k}": grads[k] for k in range(3)},
            **{f"both{k}": boths[k] for k in range(3, 7)},
        ),
        dict(out=((top + 1, 2 * channels, every // 2), F32, True)),
    )["out"]
    total = lax.psum(total, "dom").reshape(top + 1, 2, channels, every // 2)
    return got["result"], total.transpose(0, 1, 3, 2).reshape(top + 1, every, channels) * scale


def solution(mesh):
    placed = (
        P("chan", "dom"),
        P("chan", "dom"),
        P(None, "chan", None),
        P("dom", None, None),
        P("dom", None, None),
        P("dom", None, None),
    )
    return jax.shard_map(
        local,
        mesh=mesh,
        in_specs=placed,
        out_specs=(P("chan", "dom"), P(None, None, "chan")),
        check_vma=False,
    )
```

time: 140 us -> 112 us (0.80)
  waiting for transfers between devices: 41.3 us -> 29.1 us
  Pallas kernels: 38 us -> 31.5 us
  local copies, waits for them, and re-layouts: 4.84 us -> 0.03 us
  starting transfers between devices: 54.7 us -> 50.4 us
    pallas_call x20 -> x21, Pallas kernels: 38 us -> 31.5 us  [call(): pl.pallas_call(kernel, out_shape=shapes, in_specs=specs, out_specs=[pl.Bl...]
    ppermute x32, waiting for transfers between devices: 34.2 us -> 27.7 us  [exchange(): lax.ppermute(block, 'dom', pairs[kind])]
    ppermute x9 -> x6, waiting for transfers between devices: 7.11 us -> 1.35 us  [gather(): lax.ppermute(block, 'chan', [(c, c ^ bit) for c in range(size)])]
    unnamed x10 -> x2, local copies, waits for them, and re-layouts: 2.88 us -> 0.01 us
    ppermute x32, starting transfers between devices: 48.5 us -> 45.6 us  [exchange(): lax.ppermute(block, 'dom', pairs[kind])]
    ppermute x9 -> x6, starting transfers between devices: 6.18 us -> 4.8 us  [gather(): lax.ppermute(block, 'chan', [(c, c ^ bit) for c in range(size)])]
  transfers between devices with their start and end apart: 41 -> 38, of which waited for: 17 -> 14; matrix products, arithmetic and copies ran while one was open for 1% -> 0% of each run, Pallas kernels for 14% -> 19%
where the time goes in v1:
time: 112 us
  starting transfers between devices  50.4 us (45%)
  Pallas kernels  31.5 us (28%)
  waiting for transfers between devices  29.1 us (26%)
    ppermute x32, starting transfers between devices, exchange(): lax.ppermute(block, 'dom', pairs[kind])  45.6 us
    pallas_call x21, Pallas kernels, call(): pl.pallas_call(kernel, out_shape=shapes, in_specs=specs, out_specs=[pl.Bl...  31.5 us
    ppermute x32, waiting for transfers between devices, exchange(): lax.ppermute(block, 'dom', pairs[kind])  27.7 us
    ppermute x6, starting transfers between devices, gather(): lax.ppermute(block, 'chan', [(c, c ^ bit) for c in range(size)])  4.8 us
  transfers between devices with their start and end apart: 38, of which 14 were waited for; matrix products, arithmetic and copies ran while one was open for 0% of the time, Pallas kernels for 19%

profile of v1, /device:TPU:0, one launch (start us, length us, event | category | flops | bytes accessed | tf_op | source)
XLA Modules:
  0.0 111.8 jit_solution(11847777399423308689)
XLA Ops:
  0.6 1.0 shard_map.77.refs_3_.refs_0_.refs_5_.refs_6_
  2.2 2.6 %collective-permute-start = (bf16[128,1024]{1,0:T(8,128)(2,1)S(1)}, bf16[128,1024]{1,0:T(8,128)(2,1)S(1)}, u32[]{:S(2)}, u32[]{:S(2)}) collective-permute-start(bf16[128,1024]{1,0:T(8,128)(2,1)S(1)} %shard_map.77.refs_3_.refs_0_.refs_5_.refs_6_), channel_id=1, source_target_pairs={{0,2},{1,3},{2,0},{3,1},{4,6},{5,7},{6,4},{7,5},{8,10},{9,11},{10,... | collective-permute-start | bytes 786440 | tf_op jit(solution)/shard_map/ppermute | solution.py:127
  4.7 7.1 %shard_map.78 = (bf16[1536,1024]{1,0:T(8,128)(2,1)S(1)}, bf16[1536,1024]{1,0:T(8,128)(2,1)S(1)}, bf16[1024,512]{1,0:T(8,128)(2,1)S(1)}, f32[64,512]{1,0:T(8,128)S(1)}, f32[64,512]{1,0:T(8,128)S(1)}) custom-call(s32[1,8,8]{2,1,0:T(8,128)} %refs_0_.3, s32[1,4,128]{2,1,0:T(4,128)} %refs_1_.3, f32[64,128,128]{2,1,0:T(8,128)} %refs_2_.1, ...), custom_call_target="tpu_custom_call" | custom-call | flops 10000000000 | bytes 1048576 | tf_op jit(solution)/shard_map/pallas_call | solution.py:48
  12.1 1.3 %collective-permute-done.2.refs_7_.refs_3_ = bf16[128,1024]{1,0:T(8,128)(2,1)S(1)} collective-permute-done((bf16[128,1024]{1,0:T(8,128)(2,1)S(1)}, bf16[128,1024]{1,0:T(8,128)(2,1)S(1)}, u32[]{:S(2)}, u32[]{:S(2)}) %collective-permute-start.2) | collective-permute-done | bytes 262176 | tf_op jit(solution)/shard_map/ppermute | solution.py:127
  14.0 1.6 %collective-permute-start.3 = (f32[192,128]{1,0:T(8,128)S(1)}, f32[192,128]{1,0:T(8,128)S(1)}, u32[]{:S(2)}, u32[]{:S(2)}) collective-permute-start(f32[192,128]{1,0:T(8,128)S(1)} %get-tuple-element.98), channel_id=1, source_target_pairs={{0,8},{4,12},{8,0},{12,4},{16,24},{20,28},{24,16},{28,20},{1,9},{5... | collective-permute-start | bytes 294920 | tf_op jit(solution)/shard_map/ppermute | solution.py:69
  15.6 3.4 %collective-permute-start.4 = (f32[192,128]{1,0:T(8,128)S(1)}, f32[192,128]{1,0:T(8,128)S(1)}, u32[]{:S(2)}, u32[]{:S(2)}) collective-permute-start(f32[192,128]{1,0:T(8,128)S(1)} %get-tuple-element.99), channel_id=1, source_target_pairs={{0,28},{4,8},{8,4},{12,16},{16,12},{20,24},{24,20},{28,0},{1,29},{... | collective-permute-start | bytes 294920 | tf_op jit(solution)/shard_map/ppermute | solution.py:69
  19.0 1.6 %collective-permute-start.5 = (f32[192,128]{1,0:T(8,128)S(1)}, f32[192,128]{1,0:T(8,128)S(1)}, u32[]{:S(2)}, u32[]{:S(2)}) collective-permute-start(f32[192,128]{1,0:T(8,128)S(1)} %get-tuple-element.100), channel_id=1, source_target_pairs={{0,24},{4,28},{8,16},{12,20},{16,8},{20,12},{24,0},{28,4},{1,25},{... | collective-permute-start | bytes 294920 | tf_op jit(solution)/shard_map/ppermute | solution.py:69
  21.7 2.4 %shard_map.81 = (f32[128,1024]{1,0:T(8,128)S(1)}, f32[64,1024]{1,0:T(8,128)S(1)}, f32[128,128]{1,0:T(8,128)S(1)}) custom-call(bf16[256,1024]{1,0:T(8,128)(2,1)S(1)} %get-tuple-element.92.refs_0_, bf16[64,256]{1,0:T(8,128)(2,1)S(1)} %get-tuple-element.180.refs_1_, bf16[256,1024]{1,0:T(8,128)(2,1)S(1)} %get-tuple-element.93.refs_2_, ...), custom_call_target="tpu_custom_call" | custom-call | flops 805306368 | bytes 1048576 | tf_op jit(solution)/shard_map/pallas_call | solution.py:48
  26.0 1.8 %shard_map.82 = (f32[128,1024]{1,0:T(8,128)S(1)}, bf16[256,1024]{1,0:T(8,128)(2,1)S(1)}, bf16[128,1024]{1,0:T(8,128)(2,1)S(1)}, f32[192,128]{1,0:T(8,128)S(1)}, ...) custom-call(f32[128,1024]{1,0:T(8,128)S(1)} %get-tuple-element.97.refs_0_, ...), custom_call_target="tpu_custom_call" | custom-call | bytes 1048576 | tf_op jit(solution)/shard_map/pallas_call | solution.py:48
  27.9 3.3 %collective-permute-start.8 = (f32[192,128]{1,0:T(8,128)S(1)}, f32[192,128]{1,0:T(8,128)S(1)}, u32[]{:S(2)}, u32[]{:S(2)}) collective-permute-start(f32[192,128]{1,0:T(8,128)S(1)} %get-tuple-element.108), channel_id=1, source_target_pairs={{0,28},{4,8},{8,4},{12,16},{16,12},{20,24},{24,20},{28,0},{1,29},{... | collective-permute-start | bytes 294920 | tf_op jit(solution)/shard_map/ppermute | solution.py:69
  31.2 1.2 %collective-permute-start.9 = (f32[192,128]{1,0:T(8,128)S(1)}, f32[192,128]{1,0:T(8,128)S(1)}, u32[]{:S(2)}, u32[]{:S(2)}) collective-permute-start(f32[192,128]{1,0:T(8,128)S(1)} %get-tuple-element.109), channel_id=1, source_target_pairs={{0,24},{4,28},{8,16},{12,20},{16,8},{20,12},{24,0},{28,4},{1,25},{... | collective-permute-start | bytes 294920 | tf_op jit(solution)/shard_map/ppermute | solution.py:69
  33.3 2.4 %shard_map.83 = (f32[128,1024]{1,0:T(8,128)S(1)}, f32[64,1024]{1,0:T(8,128)S(1)}, f32[128,128]{1,0:T(8,128)S(1)}) custom-call(bf16[256,1024]{1,0:T(8,128)(2,1)S(1)} %get-tuple-element.103.refs_0_, bf16[64,256]{1,0:T(8,128)(2,1)S(1)} %get-tuple-element.179.refs_1_, bf16[256,1024]{1,0:T(8,128)(2,1)S(1)} %get-tuple-element.93.refs_2_, ...), custom_call_target="tpu_custom_call" | custom-call | flops 805306368 | bytes 1048576 | tf_op jit(solution)/shard_map/pallas_call | solution.py:48
  35.7 1.4 %collective-permute-done.8.refs_4_ = f32[192,128]{1,0:T(8,128)S(1)} collective-permute-done((f32[192,128]{1,0:T(8,128)S(1)}, f32[192,128]{1,0:T(8,128)S(1)}, u32[]{:S(2)}, u32[]{:S(2)}) %collective-permute-start.8) | collective-permute-done | bytes 98336 | tf_op jit(solution)/shard_map/ppermute | solution.py:69
  37.7 1.1 %shard_map.84 = (f32[128,1024]{1,0:T(8,128)S(1)}, bf16[256,1024]{1,0:T(8,128)(2,1)S(1)}, bf16[128,1024]{1,0:T(8,128)(2,1)S(1)}, f32[128,128]{1,0:T(8,128)S(1)}, ...) custom-call(f32[128,1024]{1,0:T(8,128)S(1)} %get-tuple-element.106.refs_0_, ...), custom_call_target="tpu_custom_call" | custom-call | bytes 1048576 | tf_op jit(solution)/shard_map/pallas_call | solution.py:48
  38.8 1.5 %collective-permute-start.19 = (bf16[128,1024]{1,0:T(8,128)(2,1)S(1)}, bf16[128,1024]{1,0:T(8,128)(2,1)S(1)}, u32[]{:S(2)}, u32[]{:S(2)}) collective-permute-start(bf16[128,1024]{1,0:T(8,128)(2,1)S(1)} %get-tuple-element.128.refs_0_), channel_id=1, source_target_pairs={{0,2},{1,3},{2,0},{3,1},{4,6},{5,7},{6,4},{7,5},{8,10},{9,11},{10,... | collective-permute-start | bytes 786440 | tf_op jit(solution)/shard_map/ppermute | solution.py:127
  41.3 1.4 %collective-permute-start.12 = (f32[128,128]{1,0:T(8,128)S(1)}, f32[128,128]{1,0:T(8,128)S(1)}, u32[]{:S(2)}, u32[]{:S(2)}) collective-permute-start(f32[128,128]{1,0:T(8,128)S(1)} %get-tuple-element.116), channel_id=1, source_target_pairs={{0,28},{4,8},{8,4},{12,16},{16,12},{20,24},{24,20},{28,0},{1,29},{... | collective-permute-start | bytes 196616 | tf_op jit(solution)/shard_map/ppermute | solution.py:69
  42.7 2.0 %collective-permute-start.13 = (f32[128,128]{1,0:T(8,128)S(1)}, f32[128,128]{1,0:T(8,128)S(1)}, u32[]{:S(2)}, u32[]{:S(2)}) collective-permute-start(f32[128,128]{1,0:T(8,128)S(1)} %get-tuple-element.117), channel_id=1, source_target_pairs={{0,24},{4,28},{8,16},{12,20},{16,8},{20,12},{24,0},{28,4},{1,25},{... | collective-permute-start | bytes 196616 | tf_op jit(solution)/shard_map/ppermute | solution.py:69
  44.7 1.9 %collective-permute-start.14 = (f32[128,128]{1,0:T(8,128)S(1)}, f32[128,128]{1,0:T(8,128)S(1)}, u32[]{:S(2)}, u32[]{:S(2)}) collective-permute-start(f32[128,128]{1,0:T(8,128)S(1)} %get-tuple-element.118), channel_id=1, source_target_pairs={{0,4},{4,0},{8,12},{12,8},{16,20},{20,16},{24,28},{28,24},{1,5},{5... | collective-permute-start | bytes 196616 | tf_op jit(solution)/shard_map/ppermute | solution.py:69
  46.6 1.1 %shard_map.85 = (f32[128,1024]{1,0:T(8,128)S(1)}, f32[128,128]{1,0:T(8,128)S(1)}) custom-call(bf16[256,1024]{1,0:T(8,128)(2,1)S(1)} %get-tuple-element.112.refs_0_, bf16[64,256]{1,0:T(8,128)(2,1)S(1)} %get-tuple-element.178.refs_1_, bf16[256,1024]{1,0:T(8,128)(2,1)S(1)} %get-tuple-element.93.refs_2_, ...), custom_call_target="tpu_custom_call" | custom-call | flops 805306368 | bytes 1048576 | tf_op jit(solution)/shard_map/pallas_call | solution.py:48
  47.7 1.2 %collective-permute-done.12.refs_4_ = f32[128,128]{1,0:T(8,128)S(1)} collective-permute-done((f32[128,128]{1,0:T(8,128)S(1)}, f32[128,128]{1,0:T(8,128)S(1)}, u32[]{:S(2)}, u32[]{:S(2)}) %collective-permute-start.12) | collective-permute-done | bytes 65568 | tf_op jit(solution)/shard_map/ppermute | solution.py:69
  49.0 1.0 collective-permute-done.14.refs_6_
  50.0 1.0 shard_map.86
  51.8 1.1 collective-permute-start.15
  53.0 1.9 %collective-permute-start.16 = (f32[128,128]{1,0:T(8,128)S(1)}, f32[128,128]{1,0:T(8,128)S(1)}, u32[]{:S(2)}, u32[]{:S(2)}) collective-permute-start(f32[128,128]{1,0:T(8,128)S(1)} %get-tuple-element.125), channel_id=1, source_target_pairs={{0,28},{4,8},{8,4},{12,16},{16,12},{20,24},{24,20},{28,0},{1,29},{... | collective-permute-start | bytes 196616 | tf_op jit(solution)/shard_map/ppermute | solution.py:69
  55.3 1.1 shard_map.87.refs_0_
  56.4 1.2 %shard_map.88 = (bf16[1024,256]{1,0:T(8,128)(2,1)S(1)}, bf16[1024,256]{1,0:T(8,128)(2,1)S(1)}, bf16[256,1024]{1,0:T(8,128)(2,1)}, f32[128,128]{1,0:T(8,128)S(1)}) custom-call(bf16[128,1024]{1,0:T(8,128)(2,1)S(1)} %get-tuple-element.128.refs_0_, bf16[128,1024]{1,0:T(8,128)(2,1)S(1)} %collective-permute-done.19.refs_1_, ...), custom_call_target="tpu_custom_call" | custom-call | bytes 1048576 | tf_op jit(solution)/shard_map/pallas_call | solution.py:48
  57.7 2.4 %collective-permute-done.16.refs_4_ = f32[128,128]{1,0:T(8,128)S(1)} collective-permute-done((f32[128,128]{1,0:T(8,128)S(1)}, f32[128,128]{1,0:T(8,128)S(1)}, u32[]{:S(2)}, u32[]{:S(2)}) %collective-permute-start.16) | collective-permute-done | bytes 65568 | tf_op jit(solution)/shard_map/ppermute | solution.py:69
  60.9 1.1 %shard_map.89 = (f32[128,1024]{1,0:T(8,128)S(1)}, bf16[256,1024]{1,0:T(8,128)(2,1)S(1)}, f32[256,128]{1,0:T(8,128)S(1)}, f32[192,128]{1,0:T(8,128)S(1)}, f32[128...) custom-call(f32[128,1024]{1,0:T(8,128)S(1)} %shard_map.87.refs_0_, ...), custom_call_target="tpu_custom_call" | custom-call | bytes 1048576 | tf_op jit(solution)/shard_map/pallas_call | solution.py:48
  62.6 2.9 %collective-permute-start.24 = (f32[256,128]{1,0:T(8,128)S(1)}, f32[256,128]{1,0:T(8,128)S(1)}, u32[]{:S(2)}, u32[]{:S(2)}) collective-permute-start(f32[256,128]{1,0:T(8,128)S(1)} %get-tuple-element.137), channel_id=1, source_target_pairs={{0,24},{4,28},{8,16},{12,20},{16,8},{20,12},{24,0},{28,4},{1,25},{... | collective-permute-start | bytes 393224 | tf_op jit(solution)/shard_map/ppermute | solution.py:69
  65.5 1.9 %collective-permute-start.23 = (f32[128,128]{1,0:T(8,128)S(1)}, f32[128,128]{1,0:T(8,128)S(1)}, u32[]{:S(2)}, u32[]{:S(2)}) collective-permute-start(f32[128,128]{1,0:T(8,128)S(1)} %get-tuple-element.136), channel_id=1, source_target_pairs={{0,28},{4,8},{8,4},{12,16},{16,12},{20,24},{24,20},{28,0},{1,29},{... | collective-permute-start | bytes 196616 | tf_op jit(solution)/shard_map/ppermute | solution.py:69
  67.4 1.0 shard_map.90.refs_0_
  68.4 4.7 %collective-permute-done.23.refs_4_ = f32[128,128]{1,0:T(8,128)S(1)} collective-permute-done((f32[128,128]{1,0:T(8,128)S(1)}, f32[128,128]{1,0:T(8,128)S(1)}, u32[]{:S(2)}, u32[]{:S(2)}) %collective-permute-start.23) | collective-permute-done | bytes 65568 | tf_op jit(solution)/shard_map/ppermute | solution.py:69
  73.1 1.2 %shard_map.91 = (f32[128,1024]{1,0:T(8,128)S(1)}, bf16[256,1024]{1,0:T(8,128)(2,1)S(1)}, f32[256,128]{1,0:T(8,128)S(1)}, f32[192,128]{1,0:T(8,128)S(1)}, f32[128...) custom-call(f32[128,1024]{1,0:T(8,128)S(1)} %shard_map.90.refs_0_, ...), custom_call_target="tpu_custom_call" | custom-call | bytes 1048576 | tf_op jit(solution)/shard_map/pallas_call | solution.py:48
  74.4 2.4 %collective-permute-start.28 = (f32[352,128]{1,0:T(8,128)S(1)}, f32[352,128]{1,0:T(8,128)S(1)}, u32[]{:S(2)}, u32[]{:S(2)}) collective-permute-start(f32[352,128]{1,0:T(8,128)S(1)} %get-tuple-element.146), channel_id=1, source_target_pairs={{0,24},{4,28},{8,16},{12,20},{16,8},{20,12},{24,0},{28,4},{1,25},{... | collective-permute-start | bytes 540680 | tf_op jit(solution)/shard_map/ppermute | solution.py:69
  76.8 2.9 %collective-permute-start.27 = (f32[128,128]{1,0:T(8,128)S(1)}, f32[128,128]{1,0:T(8,128)S(1)}, u32[]{:S(2)}, u32[]{:S(2)}) collective-permute-start(f32[128,128]{1,0:T(8,128)S(1)} %get-tuple-element.145), channel_id=1, source_target_pairs={{0,28},{4,8},{8,4},{12,16},{16,12},{20,24},{24,20},{28,0},{1,29},{... | collective-permute-start | bytes 196616 | tf_op jit(solution)/shard_map/ppermute | solution.py:69
  79.7 1.1 shard_map.92.refs_0_
  80.8 3.4 %collective-permute-done.27.refs_4_ = f32[128,128]{1,0:T(8,128)S(1)} collective-permute-done((f32[128,128]{1,0:T(8,128)S(1)}, f32[128,128]{1,0:T(8,128)S(1)}, u32[]{:S(2)}, u32[]{:S(2)}) %collective-permute-start.27) | collective-permute-done | bytes 65568 | tf_op jit(solution)/shard_map/ppermute | solution.py:69
  84.3 1.1 %shard_map.93 = (f32[128,1024]{1,0:T(8,128)S(1)}, bf16[256,1024]{1,0:T(8,128)(2,1)S(1)}, f32[256,128]{1,0:T(8,128)S(1)}, f32[192,128]{1,0:T(8,128)S(1)}, f32[128...) custom-call(f32[128,1024]{1,0:T(8,128)S(1)} %shard_map.92.refs_0_, ...), custom_call_target="tpu_custom_call" | custom-call | bytes 1048576 | tf_op jit(solution)/shard_map/pallas_call | solution.py:48
  85.4 1.6 %collective-permute-start.33 = (f32[448,128]{1,0:T(8,128)S(1)}, f32[448,128]{1,0:T(8,128)S(1)}, u32[]{:S(2)}, u32[]{:S(2)}) collective-permute-start(f32[448,128]{1,0:T(8,128)S(1)} %get-tuple-element.157), channel_id=1, source_target_pairs={{0,4},{4,0},{8,12},{12,8},{16,20},{20,16},{24,28},{28,24},{1,5},{5... | collective-permute-start | bytes 688136 | tf_op jit(solution)/shard_map/ppermute | solution.py:69
  87.0 1.6 %collective-permute-start.30 = (f32[352,128]{1,0:T(8,128)S(1)}, f32[352,128]{1,0:T(8,128)S(1)}, u32[]{:S(2)}, u32[]{:S(2)}) collective-permute-start(f32[352,128]{1,0:T(8,128)S(1)} %get-tuple-element.154), channel_id=1, source_target_pairs={{0,8},{4,12},{8,0},{12,4},{16,24},{20,28},{24,16},{28,20},{1,9},{5... | collective-permute-start | bytes 540680 | tf_op jit(solution)/shard_map/ppermute | solution.py:69
  89.0 2.9 %collective-permute-start.31 = (f32[192,128]{1,0:T(8,128)S(1)}, f32[192,128]{1,0:T(8,128)S(1)}, u32[]{:S(2)}, u32[]{:S(2)}) collective-permute-start(f32[192,128]{1,0:T(8,128)S(1)} %get-tuple-element.155), channel_id=1, source_target_pairs={{0,28},{4,8},{8,4},{12,16},{16,12},{20,24},{24,20},{28,0},{1,29},{... | collective-permute-start | bytes 294920 | tf_op jit(solution)/shard_map/ppermute | solution.py:69
  92.8 6.3 %collective-permute-done.31.refs_4_ = f32[192,128]{1,0:T(8,128)S(1)} collective-permute-done((f32[192,128]{1,0:T(8,128)S(1)}, f32[192,128]{1,0:T(8,128)S(1)}, u32[]{:S(2)}, u32[]{:S(2)}) %collective-permute-start.31) | collective-permute-done | bytes 98336 | tf_op jit(solution)/shard_map/ppermute | solution.py:69
  99.1 1.3 %shard_map.95 = (f32[64,1024]{1,0:T(8,128)}, bf16[128,1024]{1,0:T(8,128)(2,1)S(1)}, f32[512,128]{1,0:T(8,128)S(1)}, f32[192,128]{1,0:T(8,128)S(1)}, f32[128,128]...) custom-call(f32[64,1024]{1,0:T(8,128)S(1)} %shard_map.94.refs_0_, ...), custom_call_target="tpu_custom_call" | custom-call | bytes 1048576 | tf_op jit(solution)/shard_map/pallas_call | solution.py:48
  100.5 2.0 %collective-permute-start.36 = (f32[256,128]{1,0:T(8,128)S(1)}, f32[256,128]{1,0:T(8,128)S(1)}, u32[]{:S(2)}, u32[]{:S(2)}) collective-permute-start(f32[256,128]{1,0:T(8,128)S(1)} %get-tuple-element.166), channel_id=1, source_target_pairs={{0,24},{4,28},{8,16},{12,20},{16,8},{20,12},{24,0},{28,4},{1,25},{... | collective-permute-start | bytes 393224 | tf_op jit(solution)/shard_map/ppermute | solution.py:69
  102.5 1.4 %collective-permute-start.37 = (f32[256,128]{1,0:T(8,128)S(1)}, f32[256,128]{1,0:T(8,128)S(1)}, u32[]{:S(2)}, u32[]{:S(2)}) collective-permute-start(f32[256,128]{1,0:T(8,128)S(1)} %get-tuple-element.167), channel_id=1, source_target_pairs={{0,4},{4,0},{8,12},{12,8},{16,20},{20,16},{24,28},{28,24},{1,5},{5... | collective-permute-start | bytes 393224 | tf_op jit(solution)/shard_map/ppermute | solution.py:69
  103.9 1.9 %collective-permute-start.35 = (f32[64,128]{1,0:T(8,128)S(1)}, f32[64,128]{1,0:T(8,128)S(1)}, u32[]{:S(2)}, u32[]{:S(2)}) collective-permute-start(f32[64,128]{1,0:T(8,128)S(1)} %get-tuple-element.165), channel_id=1, source_target_pairs={{0,28},{4,8},{8,4},{12,16},{16,12},{20,24},{24,20},{28,0},{1,29},{... | collective-permute-start | bytes 98312 | tf_op jit(solution)/shard_map/ppermute | solution.py:69
  106.7 3.9 %collective-permute-done.35.refs_4_ = f32[64,128]{1,0:T(8,128)S(1)} collective-permute-done((f32[64,128]{1,0:T(8,128)S(1)}, f32[64,128]{1,0:T(8,128)S(1)}, u32[]{:S(2)}, u32[]{:S(2)}) %collective-permute-start.35) | collective-permute-done | bytes 32800 | tf_op jit(solution)/shard_map/ppermute | solution.py:69
  110.5 1.3 %shard_map.97 = (f32[64,1024]{1,0:T(8,128)}, f32[9,64,256]{2,1,0:T(8,128)}) custom-call(f32[64,1024]{1,0:T(8,128)S(1)} %shard_map.96.refs_0_, bf16[1536,1024]{1,0:T(8,128)(2,1)S(1)} %get-tuple-element.94.refs_3_.refs_1_, bf16[1536,1024]{1,0:T(8,128)(2,1)S(1)} %get-tuple-element.95.refs_4_.refs_2_, f32[256,128]{1,0:T(8,128)S(1)} %collective-permute-done.34.refs_3_, ...), custom_call_target="tpu_custom_call" | custom-call | bytes 1048576 | tf_op jit(solution)/shard_map/pallas_call | solution.py:48
  (52 shorter events, 11.9 us)
Async XLA Ops:
  1.6 10.5 %copy-start = (bf16[9,64,256]{2,1,0:T(8,128)(2,1)S(1)}, bf16[9,64,256]{2,1,0:T(8,128)(2,1)}, u32[]{:S(2)}) copy-start(bf16[9,64,256]{2,1,0:T(8,128)(2,1)} %param.8) | copy-start | bytes 884740
  1.6 10.5 %collective-permute-start.1 = (bf16[128,1024]{1,0:T(8,128)(2,1)S(1)}, bf16[128,1024]{1,0:T(8,128)(2,1)S(1)}, u32[]{:S(2)}, u32[]{:S(2)}) collective-permute-start(bf16[128,1024]{1,0:T(8,128)(2,1)S(1)} %shard_map.77.refs_3_.refs_0_.refs_5_.refs_6_), channel_id=1, source_target_pairs={{0,1},{1,0},{2,3},{3,2},{4,5},{5,4},{6,7},{7,6},{8,9},{9,8},{10,11... | collective-permute-start | bytes 786440 | tf_op jit(solution)/shard_map/ppermute | solution.py:127
  2.2 9.7 %collective-permute-start = (bf16[128,1024]{1,0:T(8,128)(2,1)S(1)}, bf16[128,1024]{1,0:T(8,128)(2,1)S(1)}, u32[]{:S(2)}, u32[]{:S(2)}) collective-permute-start(bf16[128,1024]{1,0:T(8,128)(2,1)S(1)} %shard_map.77.refs_3_.refs_0_.refs_5_.refs_6_), channel_id=1, source_target_pairs={{0,2},{1,3},{2,0},{3,1},{4,6},{5,7},{6,4},{7,5},{8,10},{9,11},{10,... | collective-permute-start | bytes 786440 | tf_op jit(solution)/shard_map/ppermute | solution.py:127
  11.9 1.6 %collective-permute-start.2 = (bf16[128,1024]{1,0:T(8,128)(2,1)S(1)}, bf16[128,1024]{1,0:T(8,128)(2,1)S(1)}, u32[]{:S(2)}, u32[]{:S(2)}) collective-permute-start(bf16[128,1024]{1,0:T(8,128)(2,1)S(1)} %collective-permute-done.refs_5_.refs_1_), channel_id=1, source_target_pairs={{0,1},{1,0},{2,3},{3,2},{4,5},{5,4},{6,7},{7,6},{8,9},{9,8},{10,11... | collective-permute-start | bytes 786440 | tf_op jit(solution)/shard_map/ppermute | solution.py:127
  14.0 10.2 %collective-permute-start.3 = (f32[192,128]{1,0:T(8,128)S(1)}, f32[192,128]{1,0:T(8,128)S(1)}, u32[]{:S(2)}, u32[]{:S(2)}) collective-permute-start(f32[192,128]{1,0:T(8,128)S(1)} %get-tuple-element.98), channel_id=1, source_target_pairs={{0,8},{4,12},{8,0},{12,4},{16,24},{20,28},{24,16},{28,20},{1,9},{5... | collective-permute-start | bytes 294920 | tf_op jit(solution)/shard_map/ppermute | solution.py:69
  15.6 9.2 %collective-permute-start.4 = (f32[192,128]{1,0:T(8,128)S(1)}, f32[192,128]{1,0:T(8,128)S(1)}, u32[]{:S(2)}, u32[]{:S(2)}) collective-permute-start(f32[192,128]{1,0:T(8,128)S(1)} %get-tuple-element.99), channel_id=1, source_target_pairs={{0,28},{4,8},{8,4},{12,16},{16,12},{20,24},{24,20},{28,0},{1,29},{... | collective-permute-start | bytes 294920 | tf_op jit(solution)/shard_map/ppermute | solution.py:69
  19.0 6.4 %collective-permute-start.5 = (f32[192,128]{1,0:T(8,128)S(1)}, f32[192,128]{1,0:T(8,128)S(1)}, u32[]{:S(2)}, u32[]{:S(2)}) collective-permute-start(f32[192,128]{1,0:T(8,128)S(1)} %get-tuple-element.100), channel_id=1, source_target_pairs={{0,24},{4,28},{8,16},{12,20},{16,8},{20,12},{24,0},{28,4},{1,25},{... | collective-permute-start | bytes 294920 | tf_op jit(solution)/shard_map/ppermute | solution.py:69
  20.6 5.4 %collective-permute-start.6 = (f32[192,128]{1,0:T(8,128)S(1)}, f32[192,128]{1,0:T(8,128)S(1)}, u32[]{:S(2)}, u32[]{:S(2)}) collective-permute-start(f32[192,128]{1,0:T(8,128)S(1)} %get-tuple-element.101), channel_id=1, source_target_pairs={{0,4},{4,0},{8,12},{12,8},{16,20},{20,16},{24,28},{28,24},{1,5},{5... | collective-permute-start | bytes 294920 | tf_op jit(solution)/shard_map/ppermute | solution.py:69
  27.8 7.8 %collective-permute-start.7 = (f32[192,128]{1,0:T(8,128)S(1)}, f32[192,128]{1,0:T(8,128)S(1)}, u32[]{:S(2)}, u32[]{:S(2)}) collective-permute-start(f32[192,128]{1,0:T(8,128)S(1)} %get-tuple-element.107), channel_id=1, source_target_pairs={{0,8},{4,12},{8,0},{12,4},{16,24},{20,28},{24,16},{28,20},{1,9},{5... | collective-permute-start | bytes 294920 | tf_op jit(solution)/shard_map/ppermute | solution.py:69
  27.9 9.2 %collective-permute-start.8 = (f32[192,128]{1,0:T(8,128)S(1)}, f32[192,128]{1,0:T(8,128)S(1)}, u32[]{:S(2)}, u32[]{:S(2)}) collective-permute-start(f32[192,128]{1,0:T(8,128)S(1)} %get-tuple-element.108), channel_id=1, source_target_pairs={{0,28},{4,8},{8,4},{12,16},{16,12},{20,24},{24,20},{28,0},{1,29},{... | collective-permute-start | bytes 294920 | tf_op jit(solution)/shard_map/ppermute | solution.py:69
  31.2 6.5 %collective-permute-start.9 = (f32[192,128]{1,0:T(8,128)S(1)}, f32[192,128]{1,0:T(8,128)S(1)}, u32[]{:S(2)}, u32[]{:S(2)}) collective-permute-start(f32[192,128]{1,0:T(8,128)S(1)} %get-tuple-element.109), channel_id=1, source_target_pairs={{0,24},{4,28},{8,16},{12,20},{16,8},{20,12},{24,0},{28,4},{1,25},{... | collective-permute-start | bytes 294920 | tf_op jit(solution)/shard_map/ppermute | solution.py:69
  32.4 5.3 %collective-permute-start.10 = (f32[192,128]{1,0:T(8,128)S(1)}, f32[192,128]{1,0:T(8,128)S(1)}, u32[]{:S(2)}, u32[]{:S(2)}) collective-permute-start(f32[192,128]{1,0:T(8,128)S(1)} %get-tuple-element.110), channel_id=1, source_target_pairs={{0,4},{4,0},{8,12},{12,8},{16,20},{20,16},{24,28},{28,24},{1,5},{5... | collective-permute-start | bytes 294920 | tf_op jit(solution)/shard_map/ppermute | solution.py:69
  38.8 7.7 %collective-permute-start.19 = (bf16[128,1024]{1,0:T(8,128)(2,1)S(1)}, bf16[128,1024]{1,0:T(8,128)(2,1)S(1)}, u32[]{:S(2)}, u32[]{:S(2)}) collective-permute-start(bf16[128,1024]{1,0:T(8,128)(2,1)S(1)} %get-tuple-element.128.refs_0_), channel_id=1, source_target_pairs={{0,2},{1,3},{2,0},{3,1},{4,6},{5,7},{6,4},{7,5},{8,10},{9,11},{10,... | collective-permute-start | bytes 786440 | tf_op jit(solution)/shard_map/ppermute | solution.py:127
  40.3 4.4 %collective-permute-start.11 = (f32[128,128]{1,0:T(8,128)S(1)}, f32[128,128]{1,0:T(8,128)S(1)}, u32[]{:S(2)}, u32[]{:S(2)}) collective-permute-start(f32[128,128]{1,0:T(8,128)S(1)} %get-tuple-element.115), channel_id=1, source_target_pairs={{0,8},{4,12},{8,0},{12,4},{16,24},{20,28},{24,16},{28,20},{1,9},{5... | collective-permute-start | bytes 196616 | tf_op jit(solution)/shard_map/ppermute | solution.py:69
  41.3 13.6 %collective-permute-start.20 = (bf16[128,1024]{1,0:T(8,128)(2,1)S(1)}, bf16[128,1024]{1,0:T(8,128)(2,1)S(1)}, u32[]{:S(2)}, u32[]{:S(2)}) collective-permute-start(bf16[128,1024]{1,0:T(8,128)(2,1)S(1)} %get-tuple-element.128.refs_0_), channel_id=1, source_target_pairs={{0,1},{1,0},{2,3},{3,2},{4,5},{5,4},{6,7},{7,6},{8,9},{9,8},{10,11... | collective-permute-start | bytes 786440 | tf_op jit(solution)/shard_map/ppermute | solution.py:127
  41.3 7.7 %collective-permute-start.12 = (f32[128,128]{1,0:T(8,128)S(1)}, f32[128,128]{1,0:T(8,128)S(1)}, u32[]{:S(2)}, u32[]{:S(2)}) collective-permute-start(f32[128,128]{1,0:T(8,128)S(1)} %get-tuple-element.116), channel_id=1, source_target_pairs={{0,28},{4,8},{8,4},{12,16},{16,12},{20,24},{24,20},{28,0},{1,29},{... | collective-permute-start | bytes 196616 | tf_op jit(solution)/shard_map/ppermute | solution.py:69
  42.7 6.3 %collective-permute-start.13 = (f32[128,128]{1,0:T(8,128)S(1)}, f32[128,128]{1,0:T(8,128)S(1)}, u32[]{:S(2)}, u32[]{:S(2)}) collective-permute-start(f32[128,128]{1,0:T(8,128)S(1)} %get-tuple-element.117), channel_id=1, source_target_pairs={{0,24},{4,28},{8,16},{12,20},{16,8},{20,12},{24,0},{28,4},{1,25},{... | collective-permute-start | bytes 196616 | tf_op jit(solution)/shard_map/ppermute | solution.py:69
  44.7 5.3 %collective-permute-start.14 = (f32[128,128]{1,0:T(8,128)S(1)}, f32[128,128]{1,0:T(8,128)S(1)}, u32[]{:S(2)}, u32[]{:S(2)}) collective-permute-start(f32[128,128]{1,0:T(8,128)S(1)} %get-tuple-element.118), channel_id=1, source_target_pairs={{0,4},{4,0},{8,12},{12,8},{16,20},{20,16},{24,28},{28,24},{1,5},{5... | collective-permute-start | bytes 196616 | tf_op jit(solution)/shard_map/ppermute | solution.py:69
  46.6 9.8 %collective-permute-start.21 = (bf16[128,1024]{1,0:T(8,128)(2,1)S(1)}, bf16[128,1024]{1,0:T(8,128)(2,1)S(1)}, u32[]{:S(2)}, u32[]{:S(2)}) collective-permute-start(bf16[128,1024]{1,0:T(8,128)(2,1)S(1)} %collective-permute-done.19.refs_1_), channel_id=1, source_target_pairs={{0,1},{1,0},{2,3},{3,2},{4,5},{5,4},{6,7},{7,6},{8,9},{9,8},{10,11... | collective-permute-start | bytes 786440 | tf_op jit(solution)/shard_map/ppermute | solution.py:127
  50.9 10.0 %collective-permute-start.18 = (f32[384,128]{1,0:T(8,128)S(1)}, f32[384,128]{1,0:T(8,128)S(1)}, u32[]{:S(2)}, u32[]{:S(2)}) collective-permute-start(f32[384,128]{1,0:T(8,128)S(1)} %get-tuple-element.127), channel_id=1, source_target_pairs={{0,4},{4,0},{8,12},{12,8},{16,20},{20,16},{24,28},{28,24},{1,5},{5... | collective-permute-start | bytes 589832 | tf_op jit(solution)/shard_map/ppermute | solution.py:69
  51.8 5.8 %collective-permute-start.15 = (f32[128,128]{1,0:T(8,128)S(1)}, f32[128,128]{1,0:T(8,128)S(1)}, u32[]{:S(2)}, u32[]{:S(2)}) collective-permute-start(f32[128,128]{1,0:T(8,128)S(1)} %get-tuple-element.124), channel_id=1, source_target_pairs={{0,8},{4,12},{8,0},{12,4},{16,24},{20,28},{24,16},{28,20},{1,9},{5... | collective-permute-start | bytes 196616 | tf_op jit(solution)/shard_map/ppermute | solution.py:69
  53.0 7.1 %collective-permute-start.16 = (f32[128,128]{1,0:T(8,128)S(1)}, f32[128,128]{1,0:T(8,128)S(1)}, u32[]{:S(2)}, u32[]{:S(2)}) collective-permute-start(f32[128,128]{1,0:T(8,128)S(1)} %get-tuple-element.125), channel_id=1, source_target_pairs={{0,28},{4,8},{8,4},{12,16},{16,12},{20,24},{24,20},{28,0},{1,29},{... | collective-permute-start | bytes 196616 | tf_op jit(solution)/shard_map/ppermute | solution.py:69
  54.8 6.1 %collective-permute-start.17 = (f32[128,128]{1,0:T(8,128)S(1)}, f32[128,128]{1,0:T(8,128)S(1)}, u32[]{:S(2)}, u32[]{:S(2)}) collective-permute-start(f32[128,128]{1,0:T(8,128)S(1)} %get-tuple-element.126), channel_id=1, source_target_pairs={{0,24},{4,28},{8,16},{12,20},{16,8},{20,12},{24,0},{28,4},{1,25},{... | collective-permute-start | bytes 196616 | tf_op jit(solution)/shard_map/ppermute | solution.py:69
  62.0 11.1 %collective-permute-start.25 = (f32[320,128]{1,0:T(8,128)S(1)}, f32[320,128]{1,0:T(8,128)S(1)}, u32[]{:S(2)}, u32[]{:S(2)}) collective-permute-start(f32[320,128]{1,0:T(8,128)S(1)} %get-tuple-element.138), channel_id=1, source_target_pairs={{0,4},{4,0},{8,12},{12,8},{16,20},{20,16},{24,28},{28,24},{1,5},{5... | collective-permute-start | bytes 491528 | tf_op jit(solution)/shard_map/ppermute | solution.py:69
  62.6 10.5 %collective-permute-start.22 = (f32[256,128]{1,0:T(8,128)S(1)}, f32[256,128]{1,0:T(8,128)S(1)}, u32[]{:S(2)}, u32[]{:S(2)}) collective-permute-start(f32[256,128]{1,0:T(8,128)S(1)} %get-tuple-element.135), channel_id=1, source_target_pairs={{0,8},{4,12},{8,0},{12,4},{16,24},{20,28},{24,16},{28,20},{1,9},{5... | collective-permute-start | bytes 393224 | tf_op jit(solution)/shard_map/ppermute | solution.py:69
  62.6 10.5 %collective-permute-start.24 = (f32[256,128]{1,0:T(8,128)S(1)}, f32[256,128]{1,0:T(8,128)S(1)}, u32[]{:S(2)}, u32[]{:S(2)}) collective-permute-start(f32[256,128]{1,0:T(8,128)S(1)} %get-tuple-element.137), channel_id=1, source_target_pairs={{0,24},{4,28},{8,16},{12,20},{16,8},{20,12},{24,0},{28,4},{1,25},{... | collective-permute-start | bytes 393224 | tf_op jit(solution)/shard_map/ppermute | solution.py:69
  65.5 7.6 %collective-permute-start.23 = (f32[128,128]{1,0:T(8,128)S(1)}, f32[128,128]{1,0:T(8,128)S(1)}, u32[]{:S(2)}, u32[]{:S(2)}) collective-permute-start(f32[128,128]{1,0:T(8,128)S(1)} %get-tuple-element.136), channel_id=1, source_target_pairs={{0,28},{4,8},{8,4},{12,16},{16,12},{20,24},{24,20},{28,0},{1,29},{... | collective-permute-start | bytes 196616 | tf_op jit(solution)/shard_map/ppermute | solution.py:69
  74.3 9.9 %collective-permute-start.26 = (f32[352,128]{1,0:T(8,128)S(1)}, f32[352,128]{1,0:T(8,128)S(1)}, u32[]{:S(2)}, u32[]{:S(2)}) collective-permute-start(f32[352,128]{1,0:T(8,128)S(1)} %get-tuple-element.144), channel_id=1, source_target_pairs={{0,8},{4,12},{8,0},{12,4},{16,24},{20,28},{24,16},{28,20},{1,9},{5... | collective-permute-start | bytes 540680 | tf_op jit(solution)/shard_map/ppermute | solution.py:69
  74.4 9.9 %collective-permute-start.28 = (f32[352,128]{1,0:T(8,128)S(1)}, f32[352,128]{1,0:T(8,128)S(1)}, u32[]{:S(2)}, u32[]{:S(2)}) collective-permute-start(f32[352,128]{1,0:T(8,128)S(1)} %get-tuple-element.146), channel_id=1, source_target_pairs={{0,24},{4,28},{8,16},{12,20},{16,8},{20,12},{24,0},{28,4},{1,25},{... | collective-permute-start | bytes 540680 | tf_op jit(solution)/shard_map/ppermute | solution.py:69
  76.8 7.4 %collective-permute-start.29 = (f32[256,128]{1,0:T(8,128)S(1)}, f32[256,128]{1,0:T(8,128)S(1)}, u32[]{:S(2)}, u32[]{:S(2)}) collective-permute-start(f32[256,128]{1,0:T(8,128)S(1)} %get-tuple-element.147), channel_id=1, source_target_pairs={{0,4},{4,0},{8,12},{12,8},{16,20},{20,16},{24,28},{28,24},{1,5},{5... | collective-permute-start | bytes 393224 | tf_op jit(solution)/shard_map/ppermute | solution.py:69
  76.8 7.4 %collective-permute-start.27 = (f32[128,128]{1,0:T(8,128)S(1)}, f32[128,128]{1,0:T(8,128)S(1)}, u32[]{:S(2)}, u32[]{:S(2)}) collective-permute-start(f32[128,128]{1,0:T(8,128)S(1)} %get-tuple-element.145), channel_id=1, source_target_pairs={{0,28},{4,8},{8,4},{12,16},{16,12},{20,24},{24,20},{28,0},{1,29},{... | collective-permute-start | bytes 196616 | tf_op jit(solution)/shard_map/ppermute | solution.py:69
  85.4 13.7 %collective-permute-start.33 = (f32[448,128]{1,0:T(8,128)S(1)}, f32[448,128]{1,0:T(8,128)S(1)}, u32[]{:S(2)}, u32[]{:S(2)}) collective-permute-start(f32[448,128]{1,0:T(8,128)S(1)} %get-tuple-element.157), channel_id=1, source_target_pairs={{0,4},{4,0},{8,12},{12,8},{16,20},{20,16},{24,28},{28,24},{1,5},{5... | collective-permute-start | bytes 688136 | tf_op jit(solution)/shard_map/ppermute | solution.py:69
  87.0 12.1 %collective-permute-start.30 = (f32[352,128]{1,0:T(8,128)S(1)}, f32[352,128]{1,0:T(8,128)S(1)}, u32[]{:S(2)}, u32[]{:S(2)}) collective-permute-start(f32[352,128]{1,0:T(8,128)S(1)} %get-tuple-element.154), channel_id=1, source_target_pairs={{0,8},{4,12},{8,0},{12,4},{16,24},{20,28},{24,16},{28,20},{1,9},{5... | collective-permute-start | bytes 540680 | tf_op jit(solution)/shard_map/ppermute | solution.py:69
  88.6 10.5 %collective-permute-start.32 = (f32[352,128]{1,0:T(8,128)S(1)}, f32[352,128]{1,0:T(8,128)S(1)}, u32[]{:S(2)}, u32[]{:S(2)}) collective-permute-start(f32[352,128]{1,0:T(8,128)S(1)} %get-tuple-element.156), channel_id=1, source_target_pairs={{0,24},{4,28},{8,16},{12,20},{16,8},{20,12},{24,0},{28,4},{1,25},{... | collective-permute-start | bytes 540680 | tf_op jit(solution)/shard_map/ppermute | solution.py:69
  89.0 10.1 %collective-permute-start.31 = (f32[192,128]{1,0:T(8,128)S(1)}, f32[192,128]{1,0:T(8,128)S(1)}, u32[]{:S(2)}, u32[]{:S(2)}) collective-permute-start(f32[192,128]{1,0:T(8,128)S(1)} %get-tuple-element.155), channel_id=1, source_target_pairs={{0,28},{4,8},{8,4},{12,16},{16,12},{20,24},{24,20},{28,0},{1,29},{... | collective-permute-start | bytes 294920 | tf_op jit(solution)/shard_map/ppermute | solution.py:69
  100.5 10.0 %collective-permute-start.34 = (f32[256,128]{1,0:T(8,128)S(1)}, f32[256,128]{1,0:T(8,128)S(1)}, u32[]{:S(2)}, u32[]{:S(2)}) collective-permute-start(f32[256,128]{1,0:T(8,128)S(1)} %get-tuple-element.164), channel_id=1, source_target_pairs={{0,8},{4,12},{8,0},{12,4},{16,24},{20,28},{24,16},{28,20},{1,9},{5... | collective-permute-start | bytes 393224 | tf_op jit(solution)/shard_map/ppermute | solution.py:69
  100.5 10.0 %collective-permute-start.36 = (f32[256,128]{1,0:T(8,128)S(1)}, f32[256,128]{1,0:T(8,128)S(1)}, u32[]{:S(2)}, u32[]{:S(2)}) collective-permute-start(f32[256,128]{1,0:T(8,128)S(1)} %get-tuple-element.166), channel_id=1, source_target_pairs={{0,24},{4,28},{8,16},{12,20},{16,8},{20,12},{24,0},{28,4},{1,25},{... | collective-permute-start | bytes 393224 | tf_op jit(solution)/shard_map/ppermute | solution.py:69
  102.5 8.0 %collective-permute-start.37 = (f32[256,128]{1,0:T(8,128)S(1)}, f32[256,128]{1,0:T(8,128)S(1)}, u32[]{:S(2)}, u32[]{:S(2)}) collective-permute-start(f32[256,128]{1,0:T(8,128)S(1)} %get-tuple-element.167), channel_id=1, source_target_pairs={{0,4},{4,0},{8,12},{12,8},{16,20},{20,16},{24,28},{28,24},{1,5},{5... | collective-permute-start | bytes 393224 | tf_op jit(solution)/shard_map/ppermute | solution.py:69
  103.9 6.6 %collective-permute-start.35 = (f32[64,128]{1,0:T(8,128)S(1)}, f32[64,128]{1,0:T(8,128)S(1)}, u32[]{:S(2)}, u32[]{:S(2)}) collective-permute-start(f32[64,128]{1,0:T(8,128)S(1)} %get-tuple-element.165), channel_id=1, source_target_pairs={{0,28},{4,8},{8,4},{12,16},{16,12},{20,24},{24,20},{28,0},{1,29},{... | collective-permute-start | bytes 98312 | tf_op jit(solution)/shard_map/ppermute | solution.py:69

commit v2 on v1

--- a/solution.py
+++ b/solution.py
@@ -92,8 +92,8 @@
     4: {1: (256,)},
     5: {1: (192,), 2: (128,), 3: (128,)},
     6: {1: (128,), 2: (128, 96), 3: (128, 96)},
-    7: {0: (128,), 1: (256, 128), 2: (96, 64, 128), 3: (96, 64, 128)},
-    8: {1: (192,), 2: (64, 128), 3: (64, 128)},
+    7: {0: (128,), 1: (128,), 2: (96, 64, 128), 3: (96, 64, 128)},
+    8: {1: (192, 256), 2: (64, 128), 3: (64, 128)},
 }
 
 
@@ -119,15 +119,15 @@
     return jnp.concatenate([rows[:half] + first, rows[half:] + second], axis=0)
 
 
-def gather(x, hold=lambda block: block):
-    size = lax.axis_size("chan")
-    bit, blocks = size // 2, [x]
+def hop(block, bit):
+    return lax.ppermute(block, "chan", [(c, c ^ bit) for c in range(lax.axis_size("chan"))])
+
+
+def gather(blocks, marker):
+    bit = lax.axis_size("chan") // 4
+    blocks = [*lax.optimization_barrier((*blocks, marker))[:2]]
     while bit:
-        blocks = blocks + [
-            lax.ppermute(block, "chan", [(c, c ^ bit) for c in range(size)]) for block in blocks
-        ]
-        if bit == size // 2:
-            blocks[1] = hold(blocks[1])
+        blocks = blocks + [hop(block, bit) for block in blocks]
         bit //= 2
     return blocks
 
@@ -370,20 +370,20 @@
                 o.one[...], o.two[...], o.seven[...], o.eight[...] = one, two, seven, eight
                 extra = {
                     0: [eight],
-                    1: [one, eight],
+                    1: [eight],
                     2: [two[quarter:], seven[:half], eight],
                     3: [two[:quarter], seven[half:], eight],
                 }
             if step == 7:
-                o.one[...] = joined(i.one[...], got(1, 0))
+                o.one[...] = i.one[...]
                 two = added(i.two[...], got(3, 0), got(2, 0))
                 seven = added(i.seven[...], got(2, 1), got(3, 1))
-                m1, p1, m2, p2 = from_pairs({0: got(0, 0), 1: got(1, 1), 2: got(2, 2), 3: got(3, 2)})
+                m1, p1, m2, p2 = from_pairs({0: got(0, 0), 1: got(1, 0), 2: got(2, 2), 3: got(3, 2)})
                 half = seven.shape[0] // 2
                 o.two[...], o.seven[...] = two, seven
                 o.eight[...] = i.eight[...] + m1 + p1 + m2 + p2
                 on = pairs_of_two(m1, p1 + p2)
-                extra = {1: [two], 2: [seven[half:], on[2]], 3: [seven[:half], on[3]]}
+                extra = {1: [two, i.one[...]], 2: [seven[half:], on[2]], 3: [seven[:half], on[3]]}
         write_sends(o, parts, extra)
 
     return outer
@@ -419,7 +419,7 @@
             o.grads[k] = scale * jnp.concatenate([chunk[:size], chunk[size:]], axis=1)
 
         size = i.eight.shape[0]
-        one, two = i.one[...], joined(i.two[...], got(1, 0))
+        one, two = joined(i.one[...], got(1, 1)), joined(i.two[...], got(1, 0))
         for k in range(4):
             put(k, one[k * size : (k + 1) * size])
         for k in range(3):
@@ -429,10 +429,6 @@
         put(8, i.eight[...] + m2 + p2)
 
     return last
-
-
-def after(x, marker):
-    return lax.optimization_barrier((x, marker))
 
 
 def local(features, cotangent, weights, tile_values, tile_cols, send_list):
@@ -479,7 +475,7 @@
     )
     matrix = dict(high=ready["high"], low=ready["low"])
     pick = dict(pick=ready["pick"])
-    blocks = gather(stacked, lambda block: after(block, ready["back"])[0])
+    blocks = gather((stacked, hop(stacked, lax.axis_size("chan") // 2)), ready["back"])
 
     def messages(rows, step):
         extra = LAYOUT.get(step, {}) if ring else {}
@@ -536,12 +532,12 @@
         if step <= 3:
             grads[step - 1] = inside["grad"]
         if step == 3:
-            back_blocks = gather(got["fboth"])
+            back_blocks = got["fboth"], hop(got["fboth"], lax.axis_size("chan") // 2)
         if step == 4:
             back = call(
                 settle,
                 dict(
-                    **{f"block{k}": (x, "") for k, x in enumerate(back_blocks)}, both=boths[3], grad1=grads[1]
+                    **{f"block{k}": (x, "") for k, x in enumerate(gather(back_blocks, got["send0"]))}, both=boths[3], grad1=grads[1]
                 ),
                 dict(g_high=turned, g_low=turned, whole=whole, fifth=chunk),
             )
@@ -581,7 +577,7 @@
                 outs.update(one=one, two=two, seven=chunk, eight=chunk)
             if step == 7:
                 ins.update({k: got[k] for k in ("one", "two", "seven", "eight")})
-                outs.update(one=((8 * channels, every // 2), F32, True), two=two, seven=chunk, eight=chunk)
+                outs.update(one=one, two=two, seven=chunk, eight=chunk)
         sent = following + (1 if step == 1 else 0)
         outs.update(messages(sent * channels, step + 1))
         before = got["state"]

time: 112 us -> 109 us (0.973)
  waiting for transfers between devices: 29.1 us -> 25.8 us
    ppermute x32, waiting for transfers between devices: 27.7 us -> 24.4 us  [exchange(): lax.ppermute(block, 'dom', pairs[kind])]
  transfers between devices with their start and end apart: 38 -> 38, of which waited for: 14 -> 17; matrix products, arithmetic and copies ran while one was open for 0% -> 0% of each run, Pallas kernels for 19% -> 19%
where the time goes in v2:
time: 109 us
  starting transfers between devices  50.4 us (46%)
  Pallas kernels  31.7 us (29%)
  waiting for transfers between devices  25.8 us (24%)
    ppermute x32, starting transfers between devices, exchange(): lax.ppermute(block, 'dom', pairs[kind])  45.3 us
    pallas_call x21, Pallas kernels, call(): pl.pallas_call(kernel, out_shape=shapes, in_specs=specs, out_specs=[pl.Bl...  31.7 us
    ppermute x32, waiting for transfers between devices, exchange(): lax.ppermute(block, 'dom', pairs[kind])  24.4 us
    ppermute x6, starting transfers between devices, hop(): lax.ppermute(block, 'chan', [(c, c ^ bit) for c in range(lax.axis_size('c...  5.03 us
  transfers between devices with their start and end apart: 38, of which 17 were waited for; matrix products, arithmetic and copies ran while one was open for 0% of the time, Pallas kernels for 19%

profile of v2, /device:TPU:0, one launch (start us, length us, event | category | flops | bytes accessed | tf_op | source)
XLA Modules:
  0.0 108.8 jit_solution(9697753376447476718)
XLA Ops:
  0.6 1.0 shard_map.77.refs_3_.refs_0_.refs_5_.refs_6_
  1.6 3.0 %collective-permute-start = (bf16[128,1024]{1,0:T(8,128)(2,1)S(1)}, bf16[128,1024]{1,0:T(8,128)(2,1)S(1)}, u32[]{:S(2)}, u32[]{:S(2)}) collective-permute-start(bf16[128,1024]{1,0:T(8,128)(2,1)S(1)} %shard_map.77.refs_3_.refs_0_.refs_5_.refs_6_), channel_id=1, source_target_pairs={{0,2},{1,3},{2,0},{3,1},{4,6},{5,7},{6,4},{7,5},{8,10},{9,11},{10,... | collective-permute-start | bytes 786440 | tf_op jit(solution)/shard_map/ppermute | solution.py:123
  4.6 7.1 %shard_map.78 = (bf16[1536,1024]{1,0:T(8,128)(2,1)S(1)}, bf16[1536,1024]{1,0:T(8,128)(2,1)S(1)}, bf16[1024,512]{1,0:T(8,128)(2,1)S(1)}, f32[64,512]{1,0:T(8,128)S(1)}, f32[64,512]{1,0:T(8,128)S(1)}) custom-call(s32[1,8,8]{2,1,0:T(8,128)} %refs_0_.3, s32[1,4,128]{2,1,0:T(4,128)} %refs_1_.3, f32[64,128,128]{2,1,0:T(8,128)} %refs_2_.1, ...), custom_call_target="tpu_custom_call" | custom-call | flops 10000000000 | bytes 1048576 | tf_op jit(solution)/shard_map/pallas_call | solution.py:48
  12.4 1.0 collective-permute-done.1.refs_6_.refs_2_
  14.3 1.6 %collective-permute-start.3 = (f32[192,128]{1,0:T(8,128)S(1)}, f32[192,128]{1,0:T(8,128)S(1)}, u32[]{:S(2)}, u32[]{:S(2)}) collective-permute-start(f32[192,128]{1,0:T(8,128)S(1)} %get-tuple-element.102), channel_id=1, source_target_pairs={{0,8},{4,12},{8,0},{12,4},{16,24},{20,28},{24,16},{28,20},{1,9},{5... | collective-permute-start | bytes 294920 | tf_op jit(solution)/shard_map/ppermute | solution.py:69
  15.9 3.4 %collective-permute-start.4 = (f32[192,128]{1,0:T(8,128)S(1)}, f32[192,128]{1,0:T(8,128)S(1)}, u32[]{:S(2)}, u32[]{:S(2)}) collective-permute-start(f32[192,128]{1,0:T(8,128)S(1)} %get-tuple-element.103), channel_id=1, source_target_pairs={{0,28},{4,8},{8,4},{12,16},{16,12},{20,24},{24,20},{28,0},{1,29},{... | collective-permute-start | bytes 294920 | tf_op jit(solution)/shard_map/ppermute | solution.py:69
  19.3 1.6 %collective-permute-start.5 = (f32[192,128]{1,0:T(8,128)S(1)}, f32[192,128]{1,0:T(8,128)S(1)}, u32[]{:S(2)}, u32[]{:S(2)}) collective-permute-start(f32[192,128]{1,0:T(8,128)S(1)} %get-tuple-element.104), channel_id=1, source_target_pairs={{0,24},{4,28},{8,16},{12,20},{16,8},{20,12},{24,0},{28,4},{1,25},{... | collective-permute-start | bytes 294920 | tf_op jit(solution)/shard_map/ppermute | solution.py:69
  22.0 2.4 %shard_map.81 = (f32[128,1024]{1,0:T(8,128)S(1)}, f32[64,1024]{1,0:T(8,128)S(1)}, f32[128,128]{1,0:T(8,128)S(1)}) custom-call(bf16[256,1024]{1,0:T(8,128)(2,1)S(1)} %get-tuple-element.96.refs_0_, bf16[64,256]{1,0:T(8,128)(2,1)S(1)} %get-tuple-element.186.refs_1_, bf16[256,1024]{1,0:T(8,128)(2,1)S(1)} %get-tuple-element.97.refs_2_, ...), custom_call_target="tpu_custom_call" | custom-call | flops 805306368 | bytes 1048576 | tf_op jit(solution)/shard_map/pallas_call | solution.py:48
  26.3 1.8 %shard_map.82 = (f32[128,1024]{1,0:T(8,128)S(1)}, bf16[256,1024]{1,0:T(8,128)(2,1)S(1)}, bf16[128,1024]{1,0:T(8,128)(2,1)S(1)}, f32[192,128]{1,0:T(8,128)S(1)}, ...) custom-call(f32[128,1024]{1,0:T(8,128)S(1)} %get-tuple-element.101.refs_0_, ...), custom_call_target="tpu_custom_call" | custom-call | bytes 1048576 | tf_op jit(solution)/shard_map/pallas_call | solution.py:48
  28.2 3.3 %collective-permute-start.8 = (f32[192,128]{1,0:T(8,128)S(1)}, f32[192,128]{1,0:T(8,128)S(1)}, u32[]{:S(2)}, u32[]{:S(2)}) collective-permute-start(f32[192,128]{1,0:T(8,128)S(1)} %get-tuple-element.112), channel_id=1, source_target_pairs={{0,28},{4,8},{8,4},{12,16},{16,12},{20,24},{24,20},{28,0},{1,29},{... | collective-permute-start | bytes 294920 | tf_op jit(solution)/shard_map/ppermute | solution.py:69
  31.5 1.2 %collective-permute-start.9 = (f32[192,128]{1,0:T(8,128)S(1)}, f32[192,128]{1,0:T(8,128)S(1)}, u32[]{:S(2)}, u32[]{:S(2)}) collective-permute-start(f32[192,128]{1,0:T(8,128)S(1)} %get-tuple-element.113), channel_id=1, source_target_pairs={{0,24},{4,28},{8,16},{12,20},{16,8},{20,12},{24,0},{28,4},{1,25},{... | collective-permute-start | bytes 294920 | tf_op jit(solution)/shard_map/ppermute | solution.py:69
  33.5 2.4 %shard_map.83 = (f32[128,1024]{1,0:T(8,128)S(1)}, f32[64,1024]{1,0:T(8,128)S(1)}, f32[128,128]{1,0:T(8,128)S(1)}) custom-call(bf16[256,1024]{1,0:T(8,128)(2,1)S(1)} %get-tuple-element.107.refs_0_, bf16[64,256]{1,0:T(8,128)(2,1)S(1)} %get-tuple-element.185.refs_1_, bf16[256,1024]{1,0:T(8,128)(2,1)S(1)} %get-tuple-element.97.refs_2_, ...), custom_call_target="tpu_custom_call" | custom-call | flops 805306368 | bytes 1048576 | tf_op jit(solution)/shard_map/pallas_call | solution.py:48
  35.9 1.4 %collective-permute-done.8.refs_4_ = f32[192,128]{1,0:T(8,128)S(1)} collective-permute-done((f32[192,128]{1,0:T(8,128)S(1)}, f32[192,128]{1,0:T(8,128)S(1)}, u32[]{:S(2)}, u32[]{:S(2)}) %collective-permute-start.8) | collective-permute-done | bytes 98336 | tf_op jit(solution)/shard_map/ppermute | solution.py:69
  38.0 1.2 %shard_map.84 = (f32[128,1024]{1,0:T(8,128)S(1)}, bf16[256,1024]{1,0:T(8,128)(2,1)S(1)}, bf16[128,1024]{1,0:T(8,128)(2,1)S(1)}, f32[128,128]{1,0:T(8,128)S(1)}, ...) custom-call(f32[128,1024]{1,0:T(8,128)S(1)} %get-tuple-element.110.refs_0_, ...), custom_call_target="tpu_custom_call" | custom-call | bytes 1048576 | tf_op jit(solution)/shard_map/pallas_call | solution.py:48
  40.0 0.9 collective-permute-start.11
  40.9 1.4 %collective-permute-start.12 = (f32[128,128]{1,0:T(8,128)S(1)}, f32[128,128]{1,0:T(8,128)S(1)}, u32[]{:S(2)}, u32[]{:S(2)}) collective-permute-start(f32[128,128]{1,0:T(8,128)S(1)} %get-tuple-element.120), channel_id=1, source_target_pairs={{0,28},{4,8},{8,4},{12,16},{16,12},{20,24},{24,20},{28,0},{1,29},{... | collective-permute-start | bytes 196616 | tf_op jit(solution)/shard_map/ppermute | solution.py:69
  42.3 2.0 %collective-permute-start.13 = (f32[128,128]{1,0:T(8,128)S(1)}, f32[128,128]{1,0:T(8,128)S(1)}, u32[]{:S(2)}, u32[]{:S(2)}) collective-permute-start(f32[128,128]{1,0:T(8,128)S(1)} %get-tuple-element.121), channel_id=1, source_target_pairs={{0,24},{4,28},{8,16},{12,20},{16,8},{20,12},{24,0},{28,4},{1,25},{... | collective-permute-start | bytes 196616 | tf_op jit(solution)/shard_map/ppermute | solution.py:69
  44.4 1.9 %collective-permute-start.14 = (f32[128,128]{1,0:T(8,128)S(1)}, f32[128,128]{1,0:T(8,128)S(1)}, u32[]{:S(2)}, u32[]{:S(2)}) collective-permute-start(f32[128,128]{1,0:T(8,128)S(1)} %get-tuple-element.122), channel_id=1, source_target_pairs={{0,4},{4,0},{8,12},{12,8},{16,20},{20,16},{24,28},{28,24},{1,5},{5... | collective-permute-start | bytes 196616 | tf_op jit(solution)/shard_map/ppermute | solution.py:69
  46.2 1.3 %shard_map.85 = (f32[128,1024]{1,0:T(8,128)S(1)}, f32[128,128]{1,0:T(8,128)S(1)}) custom-call(bf16[256,1024]{1,0:T(8,128)(2,1)S(1)} %get-tuple-element.116.refs_0_, bf16[64,256]{1,0:T(8,128)(2,1)S(1)} %get-tuple-element.184.refs_1_, bf16[256,1024]{1,0:T(8,128)(2,1)S(1)} %get-tuple-element.97.refs_2_, ...), custom_call_target="tpu_custom_call" | custom-call | flops 805306368 | bytes 1048576 | tf_op jit(solution)/shard_map/pallas_call | solution.py:48
  48.7 1.0 shard_map.86
  50.3 1.8 %collective-permute-start.18 = (f32[384,128]{1,0:T(8,128)S(1)}, f32[384,128]{1,0:T(8,128)S(1)}, u32[]{:S(2)}, u32[]{:S(2)}) collective-permute-start(f32[384,128]{1,0:T(8,128)S(1)} %get-tuple-element.131), channel_id=1, source_target_pairs={{0,4},{4,0},{8,12},{12,8},{16,20},{20,16},{24,28},{28,24},{1,5},{5... | collective-permute-start | bytes 589832 | tf_op jit(solution)/shard_map/ppermute | solution.py:69
  52.0 1.9 %collective-permute-start.16 = (f32[128,128]{1,0:T(8,128)S(1)}, f32[128,128]{1,0:T(8,128)S(1)}, u32[]{:S(2)}, u32[]{:S(2)}) collective-permute-start(f32[128,128]{1,0:T(8,128)S(1)} %get-tuple-element.129), channel_id=1, source_target_pairs={{0,28},{4,8},{8,4},{12,16},{16,12},{20,24},{24,20},{28,0},{1,29},{... | collective-permute-start | bytes 196616 | tf_op jit(solution)/shard_map/ppermute | solution.py:69
  54.0 1.5 %collective-permute-start.17 = (f32[128,128]{1,0:T(8,128)S(1)}, f32[128,128]{1,0:T(8,128)S(1)}, u32[]{:S(2)}, u32[]{:S(2)}) collective-permute-start(f32[128,128]{1,0:T(8,128)S(1)} %get-tuple-element.130), channel_id=1, source_target_pairs={{0,24},{4,28},{8,16},{12,20},{16,8},{20,12},{24,0},{28,4},{1,25},{... | collective-permute-start | bytes 196616 | tf_op jit(solution)/shard_map/ppermute | solution.py:69
  55.5 1.1 shard_map.87.refs_0_
  56.5 1.2 %shard_map.88 = (bf16[1024,256]{1,0:T(8,128)(2,1)S(1)}, bf16[1024,256]{1,0:T(8,128)(2,1)S(1)}, bf16[256,1024]{1,0:T(8,128)(2,1)}, f32[128,128]{1,0:T(8,128)S(1)}) custom-call(bf16[128,1024]{1,0:T(8,128)(2,1)S(1)} %get-tuple-element.133.refs_0_, bf16[128,1024]{1,0:T(8,128)(2,1)S(1)} %collective-permute-done.19.refs_1_, ...), custom_call_target="tpu_custom_call" | custom-call | bytes 1048576 | tf_op jit(solution)/shard_map/pallas_call | solution.py:48
  57.8 1.7 %collective-permute-done.16.refs_4_ = f32[128,128]{1,0:T(8,128)S(1)} collective-permute-done((f32[128,128]{1,0:T(8,128)S(1)}, f32[128,128]{1,0:T(8,128)S(1)}, u32[]{:S(2)}, u32[]{:S(2)}) %collective-permute-start.16) | collective-permute-done | bytes 65568 | tf_op jit(solution)/shard_map/ppermute | solution.py:69
  60.1 1.1 %shard_map.89 = (f32[128,1024]{1,0:T(8,128)S(1)}, bf16[256,1024]{1,0:T(8,128)(2,1)S(1)}, f32[256,128]{1,0:T(8,128)S(1)}, f32[192,128]{1,0:T(8,128)S(1)}, f32[128...) custom-call(f32[128,1024]{1,0:T(8,128)S(1)} %shard_map.87.refs_0_, ...), custom_call_target="tpu_custom_call" | custom-call | bytes 1048576 | tf_op jit(solution)/shard_map/pallas_call | solution.py:48
  61.2 1.7 %collective-permute-start.25 = (f32[320,128]{1,0:T(8,128)S(1)}, f32[320,128]{1,0:T(8,128)S(1)}, u32[]{:S(2)}, u32[]{:S(2)}) collective-permute-start(f32[320,128]{1,0:T(8,128)S(1)} %get-tuple-element.144), channel_id=1, source_target_pairs={{0,4},{4,0},{8,12},{12,8},{16,20},{20,16},{24,28},{28,24},{1,5},{5... | collective-permute-start | bytes 491528 | tf_op jit(solution)/shard_map/ppermute | solution.py:69
  63.7 0.9 collective-permute-start.24
  64.6 2.4 %collective-permute-start.23 = (f32[128,128]{1,0:T(8,128)S(1)}, f32[128,128]{1,0:T(8,128)S(1)}, u32[]{:S(2)}, u32[]{:S(2)}) collective-permute-start(f32[128,128]{1,0:T(8,128)S(1)} %get-tuple-element.142), channel_id=1, source_target_pairs={{0,28},{4,8},{8,4},{12,16},{16,12},{20,24},{24,20},{28,0},{1,29},{... | collective-permute-start | bytes 196616 | tf_op jit(solution)/shard_map/ppermute | solution.py:69
  67.0 1.1 shard_map.90.refs_0_
  68.1 3.8 %collective-permute-done.23.refs_4_ = f32[128,128]{1,0:T(8,128)S(1)} collective-permute-done((f32[128,128]{1,0:T(8,128)S(1)}, f32[128,128]{1,0:T(8,128)S(1)}, u32[]{:S(2)}, u32[]{:S(2)}) %collective-permute-start.23) | collective-permute-done | bytes 65568 | tf_op jit(solution)/shard_map/ppermute | solution.py:69
  71.9 1.2 %shard_map.91 = (f32[128,1024]{1,0:T(8,128)S(1)}, bf16[256,1024]{1,0:T(8,128)(2,1)S(1)}, f32[256,128]{1,0:T(8,128)S(1)}, f32[192,128]{1,0:T(8,128)S(1)}, f32[128...) custom-call(f32[128,1024]{1,0:T(8,128)S(1)} %shard_map.90.refs_0_, ...), custom_call_target="tpu_custom_call" | custom-call | bytes 1048576 | tf_op jit(solution)/shard_map/pallas_call | solution.py:48
  73.2 2.6 %collective-permute-start.28 = (f32[352,128]{1,0:T(8,128)S(1)}, f32[352,128]{1,0:T(8,128)S(1)}, u32[]{:S(2)}, u32[]{:S(2)}) collective-permute-start(f32[352,128]{1,0:T(8,128)S(1)} %get-tuple-element.152), channel_id=1, source_target_pairs={{0,24},{4,28},{8,16},{12,20},{16,8},{20,12},{24,0},{28,4},{1,25},{... | collective-permute-start | bytes 540680 | tf_op jit(solution)/shard_map/ppermute | solution.py:69
  76.6 2.1 %collective-permute-start.27 = (f32[128,128]{1,0:T(8,128)S(1)}, f32[128,128]{1,0:T(8,128)S(1)}, u32[]{:S(2)}, u32[]{:S(2)}) collective-permute-start(f32[128,128]{1,0:T(8,128)S(1)} %get-tuple-element.151), channel_id=1, source_target_pairs={{0,28},{4,8},{8,4},{12,16},{16,12},{20,24},{24,20},{28,0},{1,29},{... | collective-permute-start | bytes 196616 | tf_op jit(solution)/shard_map/ppermute | solution.py:69
  78.6 1.1 shard_map.92.refs_0_
  79.7 4.4 %collective-permute-done.27.refs_4_ = f32[128,128]{1,0:T(8,128)S(1)} collective-permute-done((f32[128,128]{1,0:T(8,128)S(1)}, f32[128,128]{1,0:T(8,128)S(1)}, u32[]{:S(2)}, u32[]{:S(2)}) %collective-permute-start.27) | collective-permute-done | bytes 65568 | tf_op jit(solution)/shard_map/ppermute | solution.py:69
  84.1 1.1 %shard_map.93 = (f32[128,1024]{1,0:T(8,128)S(1)}, bf16[256,1024]{1,0:T(8,128)(2,1)S(1)}, f32[256,128]{1,0:T(8,128)S(1)}, f32[192,128]{1,0:T(8,128)S(1)}, f32[128...) custom-call(f32[128,1024]{1,0:T(8,128)S(1)} %shard_map.92.refs_0_, ...), custom_call_target="tpu_custom_call" | custom-call | bytes 1048576 | tf_op jit(solution)/shard_map/pallas_call | solution.py:48
  85.3 2.6 %collective-permute-start.32 = (f32[352,128]{1,0:T(8,128)S(1)}, f32[352,128]{1,0:T(8,128)S(1)}, u32[]{:S(2)}, u32[]{:S(2)}) collective-permute-start(f32[352,128]{1,0:T(8,128)S(1)} %get-tuple-element.162), channel_id=1, source_target_pairs={{0,24},{4,28},{8,16},{12,20},{16,8},{20,12},{24,0},{28,4},{1,25},{... | collective-permute-start | bytes 540680 | tf_op jit(solution)/shard_map/ppermute | solution.py:69
  87.9 2.2 %collective-permute-start.31 = (f32[192,128]{1,0:T(8,128)S(1)}, f32[192,128]{1,0:T(8,128)S(1)}, u32[]{:S(2)}, u32[]{:S(2)}) collective-permute-start(f32[192,128]{1,0:T(8,128)S(1)} %get-tuple-element.161), channel_id=1, source_target_pairs={{0,28},{4,8},{8,4},{12,16},{16,12},{20,24},{24,20},{28,0},{1,29},{... | collective-permute-start | bytes 294920 | tf_op jit(solution)/shard_map/ppermute | solution.py:69
  91.0 4.4 %collective-permute-done.31.refs_4_ = f32[192,128]{1,0:T(8,128)S(1)} collective-permute-done((f32[192,128]{1,0:T(8,128)S(1)}, f32[192,128]{1,0:T(8,128)S(1)}, u32[]{:S(2)}, u32[]{:S(2)}) %collective-permute-start.31) | collective-permute-done | bytes 98336 | tf_op jit(solution)/shard_map/ppermute | solution.py:69
  95.3 1.2 %collective-permute-done.33.refs_6_ = f32[192,128]{1,0:T(8,128)S(1)} collective-permute-done((f32[192,128]{1,0:T(8,128)S(1)}, f32[192,128]{1,0:T(8,128)S(1)}, u32[]{:S(2)}, u32[]{:S(2)}) %collective-permute-start.33) | collective-permute-done | bytes 98336 | tf_op jit(solution)/shard_map/ppermute | solution.py:69
  96.6 1.3 %shard_map.95 = (f32[64,1024]{1,0:T(8,128)}, bf16[128,1024]{1,0:T(8,128)(2,1)S(1)}, f32[256,128]{1,0:T(8,128)S(1)}, f32[192,128]{1,0:T(8,128)S(1)}, f32[128,128]...) custom-call(f32[64,1024]{1,0:T(8,128)S(1)} %shard_map.94.refs_0_, ...), custom_call_target="tpu_custom_call" | custom-call | bytes 1048576 | tf_op jit(solution)/shard_map/pallas_call | solution.py:48
  97.9 1.3 %collective-permute-start.34 = (f32[256,128]{1,0:T(8,128)S(1)}, f32[256,128]{1,0:T(8,128)S(1)}, u32[]{:S(2)}, u32[]{:S(2)}) collective-permute-start(f32[256,128]{1,0:T(8,128)S(1)} %get-tuple-element.170), channel_id=1, source_target_pairs={{0,8},{4,12},{8,0},{12,4},{16,24},{20,28},{24,16},{28,20},{1,9},{5... | collective-permute-start | bytes 393224 | tf_op jit(solution)/shard_map/ppermute | solution.py:69
  99.2 1.4 %collective-permute-start.36 = (f32[256,128]{1,0:T(8,128)S(1)}, f32[256,128]{1,0:T(8,128)S(1)}, u32[]{:S(2)}, u32[]{:S(2)}) collective-permute-start(f32[256,128]{1,0:T(8,128)S(1)} %get-tuple-element.172), channel_id=1, source_target_pairs={{0,24},{4,28},{8,16},{12,20},{16,8},{20,12},{24,0},{28,4},{1,25},{... | collective-permute-start | bytes 393224 | tf_op jit(solution)/shard_map/ppermute | solution.py:69
  100.6 2.6 %collective-permute-start.35 = (f32[64,128]{1,0:T(8,128)S(1)}, f32[64,128]{1,0:T(8,128)S(1)}, u32[]{:S(2)}, u32[]{:S(2)}) collective-permute-start(f32[64,128]{1,0:T(8,128)S(1)} %get-tuple-element.171), channel_id=1, source_target_pairs={{0,28},{4,8},{8,4},{12,16},{16,12},{20,24},{24,20},{28,0},{1,29},{... | collective-permute-start | bytes 98312 | tf_op jit(solution)/shard_map/ppermute | solution.py:69
  104.1 3.3 %collective-permute-done.35.refs_4_ = f32[64,128]{1,0:T(8,128)S(1)} collective-permute-done((f32[64,128]{1,0:T(8,128)S(1)}, f32[64,128]{1,0:T(8,128)S(1)}, u32[]{:S(2)}, u32[]{:S(2)}) %collective-permute-start.35) | collective-permute-done | bytes 32800 | tf_op jit(solution)/shard_map/ppermute | solution.py:69
  107.4 1.4 %shard_map.97 = (f32[64,1024]{1,0:T(8,128)}, f32[9,64,256]{2,1,0:T(8,128)}) custom-call(f32[64,1024]{1,0:T(8,128)S(1)} %shard_map.96.refs_0_, bf16[1536,1024]{1,0:T(8,128)(2,1)S(1)} %get-tuple-element.98.refs_3_.refs_1_, bf16[1536,1024]{1,0:T(8,128)(2,1)S(1)} %get-tuple-element.99.refs_4_.refs_2_, f32[256,128]{1,0:T(8,128)S(1)} %collective-permute-done.34.refs_3_, ...), custom_call_target="tpu_custom_call" | custom-call | bytes 1048576 | tf_op jit(solution)/shard_map/pallas_call | solution.py:48
  (52 shorter events, 12.7 us)
Async XLA Ops:
  1.6 10.7 %copy-start = (bf16[9,64,256]{2,1,0:T(8,128)(2,1)S(1)}, bf16[9,64,256]{2,1,0:T(8,128)(2,1)}, u32[]{:S(2)}) copy-start(bf16[9,64,256]{2,1,0:T(8,128)(2,1)} %param.8) | copy-start | bytes 884740
  1.6 10.2 %collective-permute-start = (bf16[128,1024]{1,0:T(8,128)(2,1)S(1)}, bf16[128,1024]{1,0:T(8,128)(2,1)S(1)}, u32[]{:S(2)}, u32[]{:S(2)}) collective-permute-start(bf16[128,1024]{1,0:T(8,128)(2,1)S(1)} %shard_map.77.refs_3_.refs_0_.refs_5_.refs_6_), channel_id=1, source_target_pairs={{0,2},{1,3},{2,0},{3,1},{4,6},{5,7},{6,4},{7,5},{8,10},{9,11},{10,... | collective-permute-start | bytes 786440 | tf_op jit(solution)/shard_map/ppermute | solution.py:123
  11.8 1.6 %collective-permute-start.1 = (bf16[128,1024]{1,0:T(8,128)(2,1)S(1)}, bf16[128,1024]{1,0:T(8,128)(2,1)S(1)}, u32[]{:S(2)}, u32[]{:S(2)}) collective-permute-start(bf16[128,1024]{1,0:T(8,128)(2,1)S(1)} %shard_map.77.refs_3_.refs_0_.refs_5_.refs_6_), channel_id=1, source_target_pairs={{0,1},{1,0},{2,3},{3,2},{4,5},{5,4},{6,7},{7,6},{8,9},{9,8},{10,11... | collective-permute-start | bytes 786440 | tf_op jit(solution)/shard_map/ppermute | solution.py:123
  11.9 1.9 %collective-permute-start.2 = (bf16[128,1024]{1,0:T(8,128)(2,1)S(1)}, bf16[128,1024]{1,0:T(8,128)(2,1)S(1)}, u32[]{:S(2)}, u32[]{:S(2)}) collective-permute-start(bf16[128,1024]{1,0:T(8,128)(2,1)S(1)} %collective-permute-done.refs_5_.refs_1_), channel_id=1, source_target_pairs={{0,1},{1,0},{2,3},{3,2},{4,5},{5,4},{6,7},{7,6},{8,9},{9,8},{10,11... | collective-permute-start | bytes 786440 | tf_op jit(solution)/shard_map/ppermute | solution.py:123
  14.3 10.2 %collective-permute-start.3 = (f32[192,128]{1,0:T(8,128)S(1)}, f32[192,128]{1,0:T(8,128)S(1)}, u32[]{:S(2)}, u32[]{:S(2)}) collective-permute-start(f32[192,128]{1,0:T(8,128)S(1)} %get-tuple-element.102), channel_id=1, source_target_pairs={{0,8},{4,12},{8,0},{12,4},{16,24},{20,28},{24,16},{28,20},{1,9},{5... | collective-permute-start | bytes 294920 | tf_op jit(solution)/shard_map/ppermute | solution.py:69
  15.9 9.3 %collective-permute-start.4 = (f32[192,128]{1,0:T(8,128)S(1)}, f32[192,128]{1,0:T(8,128)S(1)}, u32[]{:S(2)}, u32[]{:S(2)}) collective-permute-start(f32[192,128]{1,0:T(8,128)S(1)} %get-tuple-element.103), channel_id=1, source_target_pairs={{0,28},{4,8},{8,4},{12,16},{16,12},{20,24},{24,20},{28,0},{1,29},{... | collective-permute-start | bytes 294920 | tf_op jit(solution)/shard_map/ppermute | solution.py:69
  19.3 6.4 %collective-permute-start.5 = (f32[192,128]{1,0:T(8,128)S(1)}, f32[192,128]{1,0:T(8,128)S(1)}, u32[]{:S(2)}, u32[]{:S(2)}) collective-permute-start(f32[192,128]{1,0:T(8,128)S(1)} %get-tuple-element.104), channel_id=1, source_target_pairs={{0,24},{4,28},{8,16},{12,20},{16,8},{20,12},{24,0},{28,4},{1,25},{... | collective-permute-start | bytes 294920 | tf_op jit(solution)/shard_map/ppermute | solution.py:69
  20.9 5.4 %collective-permute-start.6 = (f32[192,128]{1,0:T(8,128)S(1)}, f32[192,128]{1,0:T(8,128)S(1)}, u32[]{:S(2)}, u32[]{:S(2)}) collective-permute-start(f32[192,128]{1,0:T(8,128)S(1)} %get-tuple-element.105), channel_id=1, source_target_pairs={{0,4},{4,0},{8,12},{12,8},{16,20},{20,16},{24,28},{28,24},{1,5},{5... | collective-permute-start | bytes 294920 | tf_op jit(solution)/shard_map/ppermute | solution.py:69
  28.1 7.8 %collective-permute-start.7 = (f32[192,128]{1,0:T(8,128)S(1)}, f32[192,128]{1,0:T(8,128)S(1)}, u32[]{:S(2)}, u32[]{:S(2)}) collective-permute-start(f32[192,128]{1,0:T(8,128)S(1)} %get-tuple-element.111), channel_id=1, source_target_pairs={{0,8},{4,12},{8,0},{12,4},{16,24},{20,28},{24,16},{28,20},{1,9},{5... | collective-permute-start | bytes 294920 | tf_op jit(solution)/shard_map/ppermute | solution.py:69
  28.2 9.1 %collective-permute-start.8 = (f32[192,128]{1,0:T(8,128)S(1)}, f32[192,128]{1,0:T(8,128)S(1)}, u32[]{:S(2)}, u32[]{:S(2)}) collective-permute-start(f32[192,128]{1,0:T(8,128)S(1)} %get-tuple-element.112), channel_id=1, source_target_pairs={{0,28},{4,8},{8,4},{12,16},{16,12},{20,24},{24,20},{28,0},{1,29},{... | collective-permute-start | bytes 294920 | tf_op jit(solution)/shard_map/ppermute | solution.py:69
  31.5 6.5 %collective-permute-start.9 = (f32[192,128]{1,0:T(8,128)S(1)}, f32[192,128]{1,0:T(8,128)S(1)}, u32[]{:S(2)}, u32[]{:S(2)}) collective-permute-start(f32[192,128]{1,0:T(8,128)S(1)} %get-tuple-element.113), channel_id=1, source_target_pairs={{0,24},{4,28},{8,16},{12,20},{16,8},{20,12},{24,0},{28,4},{1,25},{... | collective-permute-start | bytes 294920 | tf_op jit(solution)/shard_map/ppermute | solution.py:69
  32.7 5.3 %collective-permute-start.10 = (f32[192,128]{1,0:T(8,128)S(1)}, f32[192,128]{1,0:T(8,128)S(1)}, u32[]{:S(2)}, u32[]{:S(2)}) collective-permute-start(f32[192,128]{1,0:T(8,128)S(1)} %get-tuple-element.114), channel_id=1, source_target_pairs={{0,4},{4,0},{8,12},{12,8},{16,20},{20,16},{24,28},{28,24},{1,5},{5... | collective-permute-start | bytes 294920 | tf_op jit(solution)/shard_map/ppermute | solution.py:69
  39.1 10.6 %collective-permute-start.19 = (bf16[128,1024]{1,0:T(8,128)(2,1)S(1)}, bf16[128,1024]{1,0:T(8,128)(2,1)S(1)}, u32[]{:S(2)}, u32[]{:S(2)}) collective-permute-start(bf16[128,1024]{1,0:T(8,128)(2,1)S(1)} %get-tuple-element.133.refs_0_), channel_id=1, source_target_pairs={{0,2},{1,3},{2,0},{3,1},{4,6},{5,7},{6,4},{7,5},{8,10},{9,11},{10,... | collective-permute-start | bytes 786440 | tf_op jit(solution)/shard_map/ppermute | solution.py:123
  40.0 7.6 %collective-permute-start.11 = (f32[128,128]{1,0:T(8,128)S(1)}, f32[128,128]{1,0:T(8,128)S(1)}, u32[]{:S(2)}, u32[]{:S(2)}) collective-permute-start(f32[128,128]{1,0:T(8,128)S(1)} %get-tuple-element.119), channel_id=1, source_target_pairs={{0,8},{4,12},{8,0},{12,4},{16,24},{20,28},{24,16},{28,20},{1,9},{5... | collective-permute-start | bytes 196616 | tf_op jit(solution)/shard_map/ppermute | solution.py:69
  40.9 7.1 %collective-permute-start.12 = (f32[128,128]{1,0:T(8,128)S(1)}, f32[128,128]{1,0:T(8,128)S(1)}, u32[]{:S(2)}, u32[]{:S(2)}) collective-permute-start(f32[128,128]{1,0:T(8,128)S(1)} %get-tuple-element.120), channel_id=1, source_target_pairs={{0,28},{4,8},{8,4},{12,16},{16,12},{20,24},{24,20},{28,0},{1,29},{... | collective-permute-start | bytes 196616 | tf_op jit(solution)/shard_map/ppermute | solution.py:69
  42.3 6.1 %collective-permute-start.13 = (f32[128,128]{1,0:T(8,128)S(1)}, f32[128,128]{1,0:T(8,128)S(1)}, u32[]{:S(2)}, u32[]{:S(2)}) collective-permute-start(f32[128,128]{1,0:T(8,128)S(1)} %get-tuple-element.121), channel_id=1, source_target_pairs={{0,24},{4,28},{8,16},{12,20},{16,8},{20,12},{24,0},{28,4},{1,25},{... | collective-permute-start | bytes 196616 | tf_op jit(solution)/shard_map/ppermute | solution.py:69
  44.4 4.4 %collective-permute-start.14 = (f32[128,128]{1,0:T(8,128)S(1)}, f32[128,128]{1,0:T(8,128)S(1)}, u32[]{:S(2)}, u32[]{:S(2)}) collective-permute-start(f32[128,128]{1,0:T(8,128)S(1)} %get-tuple-element.122), channel_id=1, source_target_pairs={{0,4},{4,0},{8,12},{12,8},{16,20},{20,16},{24,28},{28,24},{1,5},{5... | collective-permute-start | bytes 196616 | tf_op jit(solution)/shard_map/ppermute | solution.py:69
  49.7 4.3 %collective-permute-start.20 = (bf16[128,1024]{1,0:T(8,128)(2,1)S(1)}, bf16[128,1024]{1,0:T(8,128)(2,1)S(1)}, u32[]{:S(2)}, u32[]{:S(2)}) collective-permute-start(bf16[128,1024]{1,0:T(8,128)(2,1)S(1)} %get-tuple-element.133.refs_0_), channel_id=1, source_target_pairs={{0,1},{1,0},{2,3},{3,2},{4,5},{5,4},{6,7},{7,6},{8,9},{9,8},{10,11... | collective-permute-start | bytes 786440 | tf_op jit(solution)/shard_map/ppermute | solution.py:123
  49.8 6.8 %collective-permute-start.21 = (bf16[128,1024]{1,0:T(8,128)(2,1)S(1)}, bf16[128,1024]{1,0:T(8,128)(2,1)S(1)}, u32[]{:S(2)}, u32[]{:S(2)}) collective-permute-start(bf16[128,1024]{1,0:T(8,128)(2,1)S(1)} %collective-permute-done.19.refs_1_), channel_id=1, source_target_pairs={{0,1},{1,0},{2,3},{3,2},{4,5},{5,4},{6,7},{7,6},{8,9},{9,8},{10,11... | collective-permute-start | bytes 786440 | tf_op jit(solution)/shard_map/ppermute | solution.py:123
  50.3 9.8 %collective-permute-start.18 = (f32[384,128]{1,0:T(8,128)S(1)}, f32[384,128]{1,0:T(8,128)S(1)}, u32[]{:S(2)}, u32[]{:S(2)}) collective-permute-start(f32[384,128]{1,0:T(8,128)S(1)} %get-tuple-element.131), channel_id=1, source_target_pairs={{0,4},{4,0},{8,12},{12,8},{16,20},{20,16},{24,28},{28,24},{1,5},{5... | collective-permute-start | bytes 589832 | tf_op jit(solution)/shard_map/ppermute | solution.py:69
  52.0 8.0 %collective-permute-start.15 = (f32[128,128]{1,0:T(8,128)S(1)}, f32[128,128]{1,0:T(8,128)S(1)}, u32[]{:S(2)}, u32[]{:S(2)}) collective-permute-start(f32[128,128]{1,0:T(8,128)S(1)} %get-tuple-element.128), channel_id=1, source_target_pairs={{0,8},{4,12},{8,0},{12,4},{16,24},{20,28},{24,16},{28,20},{1,9},{5... | collective-permute-start | bytes 196616 | tf_op jit(solution)/shard_map/ppermute | solution.py:69
  52.0 7.4 %collective-permute-start.16 = (f32[128,128]{1,0:T(8,128)S(1)}, f32[128,128]{1,0:T(8,128)S(1)}, u32[]{:S(2)}, u32[]{:S(2)}) collective-permute-start(f32[128,128]{1,0:T(8,128)S(1)} %get-tuple-element.129), channel_id=1, source_target_pairs={{0,28},{4,8},{8,4},{12,16},{16,12},{20,24},{24,20},{28,0},{1,29},{... | collective-permute-start | bytes 196616 | tf_op jit(solution)/shard_map/ppermute | solution.py:69
  54.0 6.1 %collective-permute-start.17 = (f32[128,128]{1,0:T(8,128)S(1)}, f32[128,128]{1,0:T(8,128)S(1)}, u32[]{:S(2)}, u32[]{:S(2)}) collective-permute-start(f32[128,128]{1,0:T(8,128)S(1)} %get-tuple-element.130), channel_id=1, source_target_pairs={{0,24},{4,28},{8,16},{12,20},{16,8},{20,12},{24,0},{28,4},{1,25},{... | collective-permute-start | bytes 196616 | tf_op jit(solution)/shard_map/ppermute | solution.py:69
  61.2 10.7 %collective-permute-start.25 = (f32[320,128]{1,0:T(8,128)S(1)}, f32[320,128]{1,0:T(8,128)S(1)}, u32[]{:S(2)}, u32[]{:S(2)}) collective-permute-start(f32[320,128]{1,0:T(8,128)S(1)} %get-tuple-element.144), channel_id=1, source_target_pairs={{0,4},{4,0},{8,12},{12,8},{16,20},{20,16},{24,28},{28,24},{1,5},{5... | collective-permute-start | bytes 491528 | tf_op jit(solution)/shard_map/ppermute | solution.py:69
  62.9 8.9 %collective-permute-start.22 = (f32[256,128]{1,0:T(8,128)S(1)}, f32[256,128]{1,0:T(8,128)S(1)}, u32[]{:S(2)}, u32[]{:S(2)}) collective-permute-start(f32[256,128]{1,0:T(8,128)S(1)} %get-tuple-element.141), channel_id=1, source_target_pairs={{0,8},{4,12},{8,0},{12,4},{16,24},{20,28},{24,16},{28,20},{1,9},{5... | collective-permute-start | bytes 393224 | tf_op jit(solution)/shard_map/ppermute | solution.py:69
  63.7 8.2 %collective-permute-start.24 = (f32[256,128]{1,0:T(8,128)S(1)}, f32[256,128]{1,0:T(8,128)S(1)}, u32[]{:S(2)}, u32[]{:S(2)}) collective-permute-start(f32[256,128]{1,0:T(8,128)S(1)} %get-tuple-element.143), channel_id=1, source_target_pairs={{0,24},{4,28},{8,16},{12,20},{16,8},{20,12},{24,0},{28,4},{1,25},{... | collective-permute-start | bytes 393224 | tf_op jit(solution)/shard_map/ppermute | solution.py:69
  64.6 7.2 %collective-permute-start.23 = (f32[128,128]{1,0:T(8,128)S(1)}, f32[128,128]{1,0:T(8,128)S(1)}, u32[]{:S(2)}, u32[]{:S(2)}) collective-permute-start(f32[128,128]{1,0:T(8,128)S(1)} %get-tuple-element.142), channel_id=1, source_target_pairs={{0,28},{4,8},{8,4},{12,16},{16,12},{20,24},{24,20},{28,0},{1,29},{... | collective-permute-start | bytes 196616 | tf_op jit(solution)/shard_map/ppermute | solution.py:69
  73.1 11.0 %collective-permute-start.26 = (f32[352,128]{1,0:T(8,128)S(1)}, f32[352,128]{1,0:T(8,128)S(1)}, u32[]{:S(2)}, u32[]{:S(2)}) collective-permute-start(f32[352,128]{1,0:T(8,128)S(1)} %get-tuple-element.150), channel_id=1, source_target_pairs={{0,8},{4,12},{8,0},{12,4},{16,24},{20,28},{24,16},{28,20},{1,9},{5... | collective-permute-start | bytes 540680 | tf_op jit(solution)/shard_map/ppermute | solution.py:69
  73.2 10.9 %collective-permute-start.28 = (f32[352,128]{1,0:T(8,128)S(1)}, f32[352,128]{1,0:T(8,128)S(1)}, u32[]{:S(2)}, u32[]{:S(2)}) collective-permute-start(f32[352,128]{1,0:T(8,128)S(1)} %get-tuple-element.152), channel_id=1, source_target_pairs={{0,24},{4,28},{8,16},{12,20},{16,8},{20,12},{24,0},{28,4},{1,25},{... | collective-permute-start | bytes 540680 | tf_op jit(solution)/shard_map/ppermute | solution.py:69
  75.8 8.3 %collective-permute-start.29 = (f32[256,128]{1,0:T(8,128)S(1)}, f32[256,128]{1,0:T(8,128)S(1)}, u32[]{:S(2)}, u32[]{:S(2)}) collective-permute-start(f32[256,128]{1,0:T(8,128)S(1)} %get-tuple-element.153), channel_id=1, source_target_pairs={{0,4},{4,0},{8,12},{12,8},{16,20},{20,16},{24,28},{28,24},{1,5},{5... | collective-permute-start | bytes 393224 | tf_op jit(solution)/shard_map/ppermute | solution.py:69
  76.6 7.5 %collective-permute-start.27 = (f32[128,128]{1,0:T(8,128)S(1)}, f32[128,128]{1,0:T(8,128)S(1)}, u32[]{:S(2)}, u32[]{:S(2)}) collective-permute-start(f32[128,128]{1,0:T(8,128)S(1)} %get-tuple-element.151), channel_id=1, source_target_pairs={{0,28},{4,8},{8,4},{12,16},{16,12},{20,24},{24,20},{28,0},{1,29},{... | collective-permute-start | bytes 196616 | tf_op jit(solution)/shard_map/ppermute | solution.py:69
  85.2 11.4 %collective-permute-start.30 = (f32[352,128]{1,0:T(8,128)S(1)}, f32[352,128]{1,0:T(8,128)S(1)}, u32[]{:S(2)}, u32[]{:S(2)}) collective-permute-start(f32[352,128]{1,0:T(8,128)S(1)} %get-tuple-element.160), channel_id=1, source_target_pairs={{0,8},{4,12},{8,0},{12,4},{16,24},{20,28},{24,16},{28,20},{1,9},{5... | collective-permute-start | bytes 540680 | tf_op jit(solution)/shard_map/ppermute | solution.py:69
  85.3 11.3 %collective-permute-start.32 = (f32[352,128]{1,0:T(8,128)S(1)}, f32[352,128]{1,0:T(8,128)S(1)}, u32[]{:S(2)}, u32[]{:S(2)}) collective-permute-start(f32[352,128]{1,0:T(8,128)S(1)} %get-tuple-element.162), channel_id=1, source_target_pairs={{0,24},{4,28},{8,16},{12,20},{16,8},{20,12},{24,0},{28,4},{1,25},{... | collective-permute-start | bytes 540680 | tf_op jit(solution)/shard_map/ppermute | solution.py:69
  87.9 7.4 %collective-permute-start.31 = (f32[192,128]{1,0:T(8,128)S(1)}, f32[192,128]{1,0:T(8,128)S(1)}, u32[]{:S(2)}, u32[]{:S(2)}) collective-permute-start(f32[192,128]{1,0:T(8,128)S(1)} %get-tuple-element.161), channel_id=1, source_target_pairs={{0,28},{4,8},{8,4},{12,16},{16,12},{20,24},{24,20},{28,0},{1,29},{... | collective-permute-start | bytes 294920 | tf_op jit(solution)/shard_map/ppermute | solution.py:69
  90.1 6.4 %collective-permute-start.33 = (f32[192,128]{1,0:T(8,128)S(1)}, f32[192,128]{1,0:T(8,128)S(1)}, u32[]{:S(2)}, u32[]{:S(2)}) collective-permute-start(f32[192,128]{1,0:T(8,128)S(1)} %get-tuple-element.163), channel_id=1, source_target_pairs={{0,4},{4,0},{8,12},{12,8},{16,20},{20,16},{24,28},{28,24},{1,5},{5... | collective-permute-start | bytes 294920 | tf_op jit(solution)/shard_map/ppermute | solution.py:69
  97.9 9.5 %collective-permute-start.37 = (f32[512,128]{1,0:T(8,128)S(1)}, f32[512,128]{1,0:T(8,128)S(1)}, u32[]{:S(2)}, u32[]{:S(2)}) collective-permute-start(f32[512,128]{1,0:T(8,128)S(1)} %get-tuple-element.173), channel_id=1, source_target_pairs={{0,4},{4,0},{8,12},{12,8},{16,20},{20,16},{24,28},{28,24},{1,5},{5... | collective-permute-start | bytes 786440 | tf_op jit(solution)/shard_map/ppermute | solution.py:69
  97.9 9.5 %collective-permute-start.34 = (f32[256,128]{1,0:T(8,128)S(1)}, f32[256,128]{1,0:T(8,128)S(1)}, u32[]{:S(2)}, u32[]{:S(2)}) collective-permute-start(f32[256,128]{1,0:T(8,128)S(1)} %get-tuple-element.170), channel_id=1, source_target_pairs={{0,8},{4,12},{8,0},{12,4},{16,24},{20,28},{24,16},{28,20},{1,9},{5... | collective-permute-start | bytes 393224 | tf_op jit(solution)/shard_map/ppermute | solution.py:69
  99.2 8.1 %collective-permute-start.36 = (f32[256,128]{1,0:T(8,128)S(1)}, f32[256,128]{1,0:T(8,128)S(1)}, u32[]{:S(2)}, u32[]{:S(2)}) collective-permute-start(f32[256,128]{1,0:T(8,128)S(1)} %get-tuple-element.172), channel_id=1, source_target_pairs={{0,24},{4,28},{8,16},{12,20},{16,8},{20,12},{24,0},{28,4},{1,25},{... | collective-permute-start | bytes 393224 | tf_op jit(solution)/shard_map/ppermute | solution.py:69
  100.6 6.7 %collective-permute-start.35 = (f32[64,128]{1,0:T(8,128)S(1)}, f32[64,128]{1,0:T(8,128)S(1)}, u32[]{:S(2)}, u32[]{:S(2)}) collective-permute-start(f32[64,128]{1,0:T(8,128)S(1)} %get-tuple-element.171), channel_id=1, source_target_pairs={{0,28},{4,8},{8,4},{12,16},{16,12},{20,24},{24,20},{28,0},{1,29},{... | collective-permute-start | bytes 98312 | tf_op jit(solution)/shard_map/ppermute | solution.py:69

commit v3 on v2

--- a/solution.py
+++ b/solution.py
@@ -12,6 +12,7 @@
 WIDE = 256
 MIB = 1 << 20
 RING = 8
+QUICK = (1, 2, 7)
 KINDS = (2, 0, 3, 1)
 
 
@@ -281,11 +282,48 @@
                 total = summed(dot(i.fboth[...], i.high[here, :], (1, 1)))
                 total += dot(i.fboth[:local], i.low[here, :], (1, 1))
                 o.fpart[:, here] = 2.0 * total - i.stacked[local:, here].astype(F32)
-        if step <= 3:
-            u_low = None if step == 1 else i.both[width + local : width + 2 * local]
-            o.grad[...] = correlate(i.both[local : 2 * local], u_low, i.feat_t[...])
+        if step in QUICK:
+            o.picked[...] = summed(dot(jnp.concatenate(halves(o.part[...]), axis=0), i.pick[...]))
+        if step == 1:
+            o.back[...] = back_halo(jnp.concatenate(halves(o.fpart[...]), axis=0), i, nodes)
 
     return inner
+
+
+def make_quick(step, ring):
+    def quick(i, o):
+        rows = i.picked.shape[0]
+        both = split_halos(i, rows)
+        total = summed(dot(both, i.through_high[...])) + dot(both[:rows], i.through_low[...])
+        if step == 1:
+            half = rows // 2
+            total = jnp.concatenate([2.0 * total[:half], total[half:]], axis=0)
+        else:
+            total = 2.0 * total
+        parts = [i.picked[...] + total]
+        if step == 1:
+            local = i.back.shape[0]
+            got = [getattr(i, f"halo{k}")[rows : rows + local, :] for k in range(SLOTS)]
+            both = jnp.concatenate(halves(jnp.concatenate(got, axis=1)), axis=0)
+            total = summed(dot(both, i.through_high[...], (1, 1)))
+            parts.append(i.back[...] + total + dot(both[:local], i.through_low[...], (1, 1)))
+        extra = None
+        if step == 7 and ring:
+
+            def got(kind, index):
+                return carried(i, step, rows, kind, index)
+
+            two = added(i.two[...], got(3, 0), got(2, 0))
+            seven = added(i.seven[...], got(2, 1), got(3, 1))
+            m1, p1, m2, p2 = from_pairs({0: got(0, 0), 1: got(1, 0), 2: got(2, 2), 3: got(3, 2)})
+            half = seven.shape[0] // 2
+            o.two[...], o.seven[...] = two, seven
+            o.eight[...] = i.eight[...] + m1 + p1 + m2 + p2
+            on = pairs_of_two(m1, p1 + p2)
+            extra = {1: [two, i.one[...]], 2: [seven[half:], on[2]], 3: [seven[:half], on[3]]}
+        write_sends(o, parts, extra)
+
+    return quick
 
 
 def halo_product(i, lhs, rows, here, nodes):
@@ -317,7 +355,8 @@
         moving = o.both[...]
         if following < chains:
             moving = jnp.concatenate([o.both[:live], o.both[rows : rows + live]], axis=0)
-        parts, extra = [summed(dot(moving, i.pick[...]))], []
+        if step not in QUICK:
+            parts = [summed(dot(moving, i.pick[...]))]
         if step <= 2:
             got = [getattr(i, f"halo{k}")[rows : rows + local, :] for k in range(SLOTS)]
             high, low = halves(jnp.concatenate(got, axis=1))
@@ -328,8 +367,8 @@
                 high, low = halves(i.fpart[:, here] + (1.0 if step == 1 else 2.0) * total)
                 o.fboth[:local, here] = high
                 o.fboth[local:, here] = low
-            if step == 1:
-                parts.append(back_halo(o.fboth[...], i, nodes))
+        if step in QUICK:
+            return
         extra = None
         if ring:
             if chains > 1:
@@ -374,16 +413,6 @@
                     2: [two[quarter:], seven[:half], eight],
                     3: [two[:quarter], seven[half:], eight],
                 }
-            if step == 7:
-                o.one[...] = i.one[...]
-                two = added(i.two[...], got(3, 0), got(2, 0))
-                seven = added(i.seven[...], got(2, 1), got(3, 1))
-                m1, p1, m2, p2 = from_pairs({0: got(0, 0), 1: got(1, 0), 2: got(2, 2), 3: got(3, 2)})
-                half = seven.shape[0] // 2
-                o.two[...], o.seven[...] = two, seven
-                o.eight[...] = i.eight[...] + m1 + p1 + m2 + p2
-                on = pairs_of_two(m1, p1 + p2)
-                extra = {1: [two, i.one[...]], 2: [seven[half:], on[2]], 3: [seven[:half], on[3]]}
         write_sends(o, parts, extra)
 
     return outer
@@ -502,12 +531,21 @@
     )
     gathered = got["gathered"]
 
-    def turn(i, o):
+    def pass_through(i, o):
+        for matrix, out in ((i.high, o.through_high), (i.low, o.through_low)):
+            out[...] = dot(matrix[nodes:, :], i.pick[...]).astype(BF16)
+
+    through = ((SLOTS * tile, SLOTS * tile), BF16, True)
+    through = call(pass_through, dict(**matrix, **pick), dict(through_high=through, through_low=through))
+
+    def opening(i, o):
         rows = [ref[channels:, :] for name, ref in vars(i).items() if name.startswith("block")]
         collect([i.stacked[channels:]] + rows, o.whole)
         o.feat_t[...] = transposed(o.whole[...])
-
-    feat_t = call(turn, dict(stacked=stacked, **named), dict(whole=whole, feat_t=turned))["feat_t"]
+        o.grad0[...] = correlate(i.stacked[:channels], None, o.feat_t[...])
+        for ref, out in ((i.both1, o.grad1), (i.both2, o.grad2)):
+            out[...] = correlate(ref[channels : 2 * channels], ref[3 * channels :], o.feat_t[...])
+
     before, boths, grads, back = None, {}, {}, None
     for step in range(1, top + 1):
         chains = 2 if step <= top - 2 else 1
@@ -517,20 +555,27 @@
         outs = dict(part=((chains * channels, nodes), F32, True))
         if step > 1:
             ins["before"] = before
+        if step in QUICK:
+            ins.update(pick)
+            outs["picked"] = ((chains * channels, SLOTS * tile), F32, True)
+        if step == 1:
+            outs["back"] = sent_shape
         if step <= 2:
             ins["stacked"] = stacked
             outs["fpart"] = ((channels, nodes), F32, True)
         if step == 2:
             ins["fboth"] = got["fboth"]
-        if step <= 3:
-            ins["feat_t"] = feat_t
-            outs["grad"] = chunk
         inside = call(
             make_inner(step, top, chains), ins, outs, flops=2 * chains * channels * nodes * nodes * 3
         )
         part = inside["part"]
-        if step <= 3:
-            grads[step - 1] = inside["grad"]
+        if step == 3:
+            opened = call(
+                opening,
+                dict(stacked=stacked, **named, both1=boths[1], both2=boths[2]),
+                dict(whole=whole, feat_t=turned, **{f"grad{k}": chunk for k in range(3)}),
+            )
+            feat_t, grads = opened["feat_t"], {k: opened[f"grad{k}"] for k in range(3)}
         if step == 3:
             back_blocks = got["fboth"], hop(got["fboth"], lax.axis_size("chan") // 2)
         if step == 4:
@@ -575,13 +620,23 @@
             if step == 6:
                 ins.update({k: got[k] for k in ("one", "two", "seven")}, fourth=grads[4])
                 outs.update(one=one, two=two, seven=chunk, eight=chunk)
-            if step == 7:
-                ins.update({k: got[k] for k in ("one", "two", "seven", "eight")})
-                outs.update(one=one, two=two, seven=chunk, eight=chunk)
         sent = following + (1 if step == 1 else 0)
-        outs.update(messages(sent * channels, step + 1))
+        sends = messages(sent * channels, step + 1)
+        ready = {}
+        if step in QUICK:
+            told = dict(picked=inside["picked"], **through, **halos)
+            if step == 1:
+                told["back"] = inside["back"]
+            if step == 7 and ring:
+                told.update({k: got[k] for k in ("one", "two", "seven", "eight")})
+                sends.update(two=two, seven=chunk, eight=chunk)
+                ready["one"] = got["one"]
+            ready.update(call(make_quick(step, ring), told, sends))
+        else:
+            outs.update(sends)
         before = got["state"]
         got = call(make_outer(step, chains, following, ring and step >= 3), ins, outs)
+        got.update(ready)
         boths[step] = got["both"]
     if ring:
         return got["result"], jnp.swapaxes(got["grads"], 1, 2)

time: 109 us -> 107 us (0.982)
  waiting for transfers between devices: 25.8 us -> 20.1 us
  Pallas kernels: 31.7 us -> 34.7 us
    ppermute x32, waiting for transfers between devices: 24.4 us -> 18.7 us  [exchange(): lax.ppermute(block, 'dom', pairs[kind])]
    pallas_call x21 -> x25, Pallas kernels: 31.7 us -> 34.7 us  [call(): pl.pallas_call(kernel, out_shape=shapes, in_specs=specs, out_specs=[pl.Bl...]
  transfers between devices with their start and end apart: 38 -> 38, of which waited for: 17 -> 14; matrix products, arithmetic and copies ran while one was open for 0% -> 0% of each run, Pallas kernels for 19% -> 25%
where the time goes in v3:
time: 107 us
  starting transfers between devices  51.1 us (48%)
  Pallas kernels  34.7 us (32%)
  waiting for transfers between devices  20.1 us (19%)
    ppermute x32, starting transfers between devices, exchange(): lax.ppermute(block, 'dom', pairs[kind])  46 us
    pallas_call x25, Pallas kernels, call(): pl.pallas_call(kernel, out_shape=shapes, in_specs=specs, out_specs=[pl.Bl...  34.7 us
    ppermute x32, waiting for transfers between devices, exchange(): lax.ppermute(block, 'dom', pairs[kind])  18.7 us
    ppermute x6, starting transfers between devices, hop(): lax.ppermute(block, 'chan', [(c, c ^ bit) for c in range(lax.axis_size('c...  5.05 us
  transfers between devices with their start and end apart: 38, of which 14 were waited for; matrix products, arithmetic and copies ran while one was open for 0% of the time, Pallas kernels for 25%

profile of v3, /device:TPU:0, one launch (start us, length us, event | category | flops | bytes accessed | tf_op | source)
XLA Modules:
  0.0 106.8 jit_solution(6111752287118325356)
XLA Ops:
  0.6 1.0 shard_map.77.refs_3_.refs_0_.refs_6_.refs_7_
  1.6 3.0 %collective-permute-start = (bf16[128,1024]{1,0:T(8,128)(2,1)S(1)}, bf16[128,1024]{1,0:T(8,128)(2,1)S(1)}, u32[]{:S(2)}, u32[]{:S(2)}) collective-permute-start(bf16[128,1024]{1,0:T(8,128)(2,1)S(1)} %shard_map.77.refs_3_.refs_0_.refs_6_.refs_7_), channel_id=1, source_target_pairs={{0,2},{1,3},{2,0},{3,1},{4,6},{5,7},{6,4},{7,5},{8,10},{9,11},{10,... | collective-permute-start | bytes 786440 | tf_op jit(solution)/shard_map/ppermute | solution.py:124
  4.6 7.1 %shard_map.78 = (bf16[1536,1024]{1,0:T(8,128)(2,1)S(1)}, bf16[1536,1024]{1,0:T(8,128)(2,1)S(1)}, bf16[1024,512]{1,0:T(8,128)(2,1)S(1)}, f32[64,512]{1,0:T(8,128)S(1)}, f32[64,512]{1,0:T(8,128)S(1)}) custom-call(s32[1,8,8]{2,1,0:T(8,128)} %refs_0_.3, s32[1,4,128]{2,1,0:T(4,128)} %refs_1_.3, f32[64,128,128]{2,1,0:T(8,128)} %refs_2_.1, ...), custom_call_target="tpu_custom_call" | custom-call | flops 10000000000 | bytes 1048576 | tf_op jit(solution)/shard_map/pallas_call | solution.py:49
  12.4 1.0 collective-permute-done.1.refs_6_.refs_2_
  14.3 1.6 %collective-permute-start.3 = (f32[192,128]{1,0:T(8,128)S(1)}, f32[192,128]{1,0:T(8,128)S(1)}, u32[]{:S(2)}, u32[]{:S(2)}) collective-permute-start(f32[192,128]{1,0:T(8,128)S(1)} %get-tuple-element.106), channel_id=1, source_target_pairs={{0,8},{4,12},{8,0},{12,4},{16,24},{20,28},{24,16},{28,20},{1,9},{5... | collective-permute-start | bytes 294920 | tf_op jit(solution)/shard_map/ppermute | solution.py:70
  15.9 3.4 %collective-permute-start.4 = (f32[192,128]{1,0:T(8,128)S(1)}, f32[192,128]{1,0:T(8,128)S(1)}, u32[]{:S(2)}, u32[]{:S(2)}) collective-permute-start(f32[192,128]{1,0:T(8,128)S(1)} %get-tuple-element.107), channel_id=1, source_target_pairs={{0,28},{4,8},{8,4},{12,16},{16,12},{20,24},{24,20},{28,0},{1,29},{... | collective-permute-start | bytes 294920 | tf_op jit(solution)/shard_map/ppermute | solution.py:70
  19.3 1.6 %collective-permute-start.5 = (f32[192,128]{1,0:T(8,128)S(1)}, f32[192,128]{1,0:T(8,128)S(1)}, u32[]{:S(2)}, u32[]{:S(2)}) collective-permute-start(f32[192,128]{1,0:T(8,128)S(1)} %get-tuple-element.108), channel_id=1, source_target_pairs={{0,24},{4,28},{8,16},{12,20},{16,8},{20,12},{24,0},{28,4},{1,25},{... | collective-permute-start | bytes 294920 | tf_op jit(solution)/shard_map/ppermute | solution.py:70
  21.2 1.2 %shard_map.83 = (bf16[512,512]{1,0:T(8,128)(2,1)S(1)}, bf16[512,512]{1,0:T(8,128)(2,1)S(1)}) custom-call(bf16[1536,1024]{1,0:T(8,128)(2,1)S(1)} %get-tuple-element.103.refs_3_.refs_1_.refs_0_, bf16[1536,1024]{1,0:T(8,128)(2,1)S(1)} %get-tuple-element.104.refs_4_.refs_2_.refs_1_, bf16[1024,512]{1,0:T(8,128)(2,1)S(1)} %get-tuple-element.96.refs_2_.refs_5_.refs_7_.refs_6_), custom_call_target="tpu_custom_call" | custom-call | bytes 1048576 | tf_op jit(solution)/shard_map/pallas_call | solution.py:49
  22.5 3.2 %shard_map.80 = (f32[128,1024]{1,0:T(8,128)S(1)}, f32[128,512]{1,0:T(8,128)S(1)}, f32[64,512]{1,0:T(8,128)S(1)}, f32[64,1024]{1,0:T(8,128)S(1)}) custom-call(bf16[256,1024]{1,0:T(8,128)(2,1)S(1)} %get-tuple-element.101.refs_0_, bf16[64,256]{1,0:T(8,128)(2,1)S(1)} %get-tuple-element.196.refs_1_, bf16[256,1024]{1,0:T(8,128)(2,1)S(1)} %get-tuple-element.102.refs_2_, ...), custom_call_target="tpu_custom_call" | custom-call | flops 805306368 | bytes 1048576 | tf_op jit(solution)/shard_map/pallas_call | solution.py:49
  27.0 3.3 %collective-permute-start.8 = (f32[192,128]{1,0:T(8,128)S(1)}, f32[192,128]{1,0:T(8,128)S(1)}, u32[]{:S(2)}, u32[]{:S(2)}) collective-permute-start(f32[192,128]{1,0:T(8,128)S(1)} %get-tuple-element.120), channel_id=1, source_target_pairs={{0,28},{4,8},{8,4},{12,16},{16,12},{20,24},{24,20},{28,0},{1,29},{... | collective-permute-start | bytes 294920 | tf_op jit(solution)/shard_map/ppermute | solution.py:70
  30.4 1.5 %collective-permute-start.9 = (f32[192,128]{1,0:T(8,128)S(1)}, f32[192,128]{1,0:T(8,128)S(1)}, u32[]{:S(2)}, u32[]{:S(2)}) collective-permute-start(f32[192,128]{1,0:T(8,128)S(1)} %get-tuple-element.121), channel_id=1, source_target_pairs={{0,24},{4,28},{8,16},{12,20},{16,8},{20,12},{24,0},{28,4},{1,25},{... | collective-permute-start | bytes 294920 | tf_op jit(solution)/shard_map/ppermute | solution.py:70
  32.4 0.9 shard_map.81
  33.3 2.7 %shard_map.82 = (f32[128,1024]{1,0:T(8,128)S(1)}, f32[128,512]{1,0:T(8,128)S(1)}, f32[64,1024]{1,0:T(8,128)S(1)}) custom-call(bf16[256,1024]{1,0:T(8,128)(2,1)S(1)} %get-tuple-element.111.refs_0_.refs_4_, bf16[64,256]{1,0:T(8,128)(2,1)S(1)} %get-tuple-element.195.refs_1_, bf16[256,1024]{1,0:T(8,128)(2,1)S(1)} %get-tuple-element.102.refs_2_, ...), custom_call_target="tpu_custom_call" | custom-call | flops 805306368 | bytes 1048576 | tf_op jit(solution)/shard_map/pallas_call | solution.py:49
  36.9 1.1 %shard_map.85 = (f32[128,1024]{1,0:T(8,128)S(1)}, bf16[256,1024]{1,0:T(8,128)(2,1)S(1)}, bf16[128,1024]{1,0:T(8,128)(2,1)S(1)}) custom-call(f32[128,1024]{1,0:T(8,128)S(1)} %get-tuple-element.114.refs_0_, bf16[1536,1024]{1,0:T(8,128)(2,1)S(1)} %get-tuple-element.103.refs_3_.refs_1_.refs_0_, ...), custom_call_target="tpu_custom_call" | custom-call | bytes 1048576 | tf_op jit(solution)/shard_map/pallas_call | solution.py:49
  39.3 1.0 collective-permute-start.11
  40.2 1.6 %collective-permute-start.12 = (f32[128,128]{1,0:T(8,128)S(1)}, f32[128,128]{1,0:T(8,128)S(1)}, u32[]{:S(2)}, u32[]{:S(2)}) collective-permute-start(f32[128,128]{1,0:T(8,128)S(1)} %get-tuple-element.128), channel_id=1, source_target_pairs={{0,28},{4,8},{8,4},{12,16},{16,12},{20,24},{24,20},{28,0},{1,29},{... | collective-permute-start | bytes 196616 | tf_op jit(solution)/shard_map/ppermute | solution.py:70
  41.9 1.9 %collective-permute-start.13 = (f32[128,128]{1,0:T(8,128)S(1)}, f32[128,128]{1,0:T(8,128)S(1)}, u32[]{:S(2)}, u32[]{:S(2)}) collective-permute-start(f32[128,128]{1,0:T(8,128)S(1)} %get-tuple-element.129), channel_id=1, source_target_pairs={{0,24},{4,28},{8,16},{12,20},{16,8},{20,12},{24,0},{28,4},{1,25},{... | collective-permute-start | bytes 196616 | tf_op jit(solution)/shard_map/ppermute | solution.py:70
  43.8 1.7 %collective-permute-start.14 = (f32[128,128]{1,0:T(8,128)S(1)}, f32[128,128]{1,0:T(8,128)S(1)}, u32[]{:S(2)}, u32[]{:S(2)}) collective-permute-start(f32[128,128]{1,0:T(8,128)S(1)} %get-tuple-element.130), channel_id=1, source_target_pairs={{0,4},{4,0},{8,12},{12,8},{16,20},{20,16},{24,28},{28,24},{1,5},{5... | collective-permute-start | bytes 196616 | tf_op jit(solution)/shard_map/ppermute | solution.py:70
  45.5 1.2 %shard_map.88 = (bf16[256,1024]{1,0:T(8,128)(2,1)}, bf16[1024,256]{1,0:T(8,128)(2,1)S(1)}, f32[128,128]{1,0:T(8,128)S(1)}, f32[128,128]{1,0:T(8,128)S(1)}, f32[128,128]{1,0:T(8,128)S(1)}) custom-call(bf16[128,1024]{1,0:T(8,128)(2,1)S(1)} %shard_map.77.refs_3_.refs_0_.refs_6_.refs_7_, bf16[128,1024]{1,0:T(8,128)(2,1)S(1)} %collective-permute-done.refs_5_.refs_1_, ...), custom_call_target="tpu_custom_call" | custom-call | bytes 1048576 | tf_op jit(solution)/shard_map/pallas_call | solution.py:49
  46.8 1.1 shard_map.86.refs_0_
  48.1 1.0 shard_map.89
  49.6 1.7 %collective-permute-start.18 = (f32[384,128]{1,0:T(8,128)S(1)}, f32[384,128]{1,0:T(8,128)S(1)}, u32[]{:S(2)}, u32[]{:S(2)}) collective-permute-start(f32[384,128]{1,0:T(8,128)S(1)} %get-tuple-element.140), channel_id=1, source_target_pairs={{0,4},{4,0},{8,12},{12,8},{16,20},{20,16},{24,28},{28,24},{1,5},{5... | collective-permute-start | bytes 589832 | tf_op jit(solution)/shard_map/ppermute | solution.py:70
  51.4 1.9 %collective-permute-start.16 = (f32[128,128]{1,0:T(8,128)S(1)}, f32[128,128]{1,0:T(8,128)S(1)}, u32[]{:S(2)}, u32[]{:S(2)}) collective-permute-start(f32[128,128]{1,0:T(8,128)S(1)} %get-tuple-element.138), channel_id=1, source_target_pairs={{0,28},{4,8},{8,4},{12,16},{16,12},{20,24},{24,20},{28,0},{1,29},{... | collective-permute-start | bytes 196616 | tf_op jit(solution)/shard_map/ppermute | solution.py:70
  53.3 1.7 %collective-permute-start.17 = (f32[128,128]{1,0:T(8,128)S(1)}, f32[128,128]{1,0:T(8,128)S(1)}, u32[]{:S(2)}, u32[]{:S(2)}) collective-permute-start(f32[128,128]{1,0:T(8,128)S(1)} %get-tuple-element.139), channel_id=1, source_target_pairs={{0,24},{4,28},{8,16},{12,20},{16,8},{20,12},{24,0},{28,4},{1,25},{... | collective-permute-start | bytes 196616 | tf_op jit(solution)/shard_map/ppermute | solution.py:70
  55.0 1.1 shard_map.90.refs_0_
  56.1 1.2 %shard_map.91 = (bf16[1024,256]{1,0:T(8,128)(2,1)S(1)}, bf16[1024,256]{1,0:T(8,128)(2,1)S(1)}, bf16[256,1024]{1,0:T(8,128)(2,1)}, f32[128,128]{1,0:T(8,128)S(1)}) custom-call(bf16[128,1024]{1,0:T(8,128)(2,1)S(1)} %get-tuple-element.142.refs_0_, bf16[128,1024]{1,0:T(8,128)(2,1)S(1)} %collective-permute-done.19.refs_1_, ...), custom_call_target="tpu_custom_call" | custom-call | bytes 1048576 | tf_op jit(solution)/shard_map/pallas_call | solution.py:49
  57.3 1.5 %collective-permute-done.16.refs_4_ = f32[128,128]{1,0:T(8,128)S(1)} collective-permute-done((f32[128,128]{1,0:T(8,128)S(1)}, f32[128,128]{1,0:T(8,128)S(1)}, u32[]{:S(2)}, u32[]{:S(2)}) %collective-permute-start.16) | collective-permute-done | bytes 65568 | tf_op jit(solution)/shard_map/ppermute | solution.py:70
  59.4 1.1 %shard_map.92 = (f32[128,1024]{1,0:T(8,128)S(1)}, bf16[256,1024]{1,0:T(8,128)(2,1)S(1)}, f32[256,128]{1,0:T(8,128)S(1)}, f32[192,128]{1,0:T(8,128)S(1)}, f32[128...) custom-call(f32[128,1024]{1,0:T(8,128)S(1)} %shard_map.90.refs_0_, ...), custom_call_target="tpu_custom_call" | custom-call | bytes 1048576 | tf_op jit(solution)/shard_map/pallas_call | solution.py:49
  60.5 1.7 %collective-permute-start.25 = (f32[320,128]{1,0:T(8,128)S(1)}, f32[320,128]{1,0:T(8,128)S(1)}, u32[]{:S(2)}, u32[]{:S(2)}) collective-permute-start(f32[320,128]{1,0:T(8,128)S(1)} %get-tuple-element.153), channel_id=1, source_target_pairs={{0,4},{4,0},{8,12},{12,8},{16,20},{20,16},{24,28},{28,24},{1,5},{5... | collective-permute-start | bytes 491528 | tf_op jit(solution)/shard_map/ppermute | solution.py:70
  63.9 2.4 %collective-permute-start.23 = (f32[128,128]{1,0:T(8,128)S(1)}, f32[128,128]{1,0:T(8,128)S(1)}, u32[]{:S(2)}, u32[]{:S(2)}) collective-permute-start(f32[128,128]{1,0:T(8,128)S(1)} %get-tuple-element.151), channel_id=1, source_target_pairs={{0,28},{4,8},{8,4},{12,16},{16,12},{20,24},{24,20},{28,0},{1,29},{... | collective-permute-start | bytes 196616 | tf_op jit(solution)/shard_map/ppermute | solution.py:70
  66.3 1.1 shard_map.93.refs_0_
  67.4 3.8 %collective-permute-done.23.refs_4_ = f32[128,128]{1,0:T(8,128)S(1)} collective-permute-done((f32[128,128]{1,0:T(8,128)S(1)}, f32[128,128]{1,0:T(8,128)S(1)}, u32[]{:S(2)}, u32[]{:S(2)}) %collective-permute-start.23) | collective-permute-done | bytes 65568 | tf_op jit(solution)/shard_map/ppermute | solution.py:70
  71.2 1.2 %shard_map.94 = (f32[128,1024]{1,0:T(8,128)S(1)}, bf16[256,1024]{1,0:T(8,128)(2,1)S(1)}, f32[256,128]{1,0:T(8,128)S(1)}, f32[192,128]{1,0:T(8,128)S(1)}, f32[128...) custom-call(f32[128,1024]{1,0:T(8,128)S(1)} %shard_map.93.refs_0_, ...), custom_call_target="tpu_custom_call" | custom-call | bytes 1048576 | tf_op jit(solution)/shard_map/pallas_call | solution.py:49
  72.5 2.7 %collective-permute-start.28 = (f32[352,128]{1,0:T(8,128)S(1)}, f32[352,128]{1,0:T(8,128)S(1)}, u32[]{:S(2)}, u32[]{:S(2)}) collective-permute-start(f32[352,128]{1,0:T(8,128)S(1)} %get-tuple-element.161), channel_id=1, source_target_pairs={{0,24},{4,28},{8,16},{12,20},{16,8},{20,12},{24,0},{28,4},{1,25},{... | collective-permute-start | bytes 540680 | tf_op jit(solution)/shard_map/ppermute | solution.py:70
  75.9 2.1 %collective-permute-start.27 = (f32[128,128]{1,0:T(8,128)S(1)}, f32[128,128]{1,0:T(8,128)S(1)}, u32[]{:S(2)}, u32[]{:S(2)}) collective-permute-start(f32[128,128]{1,0:T(8,128)S(1)} %get-tuple-element.160), channel_id=1, source_target_pairs={{0,28},{4,8},{8,4},{12,16},{16,12},{20,24},{24,20},{28,0},{1,29},{... | collective-permute-start | bytes 196616 | tf_op jit(solution)/shard_map/ppermute | solution.py:70
  77.9 1.1 shard_map.95.refs_0_
  79.0 4.3 %collective-permute-done.27.refs_4_ = f32[128,128]{1,0:T(8,128)S(1)} collective-permute-done((f32[128,128]{1,0:T(8,128)S(1)}, f32[128,128]{1,0:T(8,128)S(1)}, u32[]{:S(2)}, u32[]{:S(2)}) %collective-permute-start.27) | collective-permute-done | bytes 65568 | tf_op jit(solution)/shard_map/ppermute | solution.py:70
  83.3 1.1 %shard_map.96 = (f32[128,1024]{1,0:T(8,128)S(1)}, bf16[256,1024]{1,0:T(8,128)(2,1)S(1)}, f32[256,128]{1,0:T(8,128)S(1)}, f32[192,128]{1,0:T(8,128)S(1)}, f32[128...) custom-call(f32[128,1024]{1,0:T(8,128)S(1)} %shard_map.95.refs_0_, ...), custom_call_target="tpu_custom_call" | custom-call | bytes 1048576 | tf_op jit(solution)/shard_map/pallas_call | solution.py:49
  84.6 2.7 %collective-permute-start.32 = (f32[352,128]{1,0:T(8,128)S(1)}, f32[352,128]{1,0:T(8,128)S(1)}, u32[]{:S(2)}, u32[]{:S(2)}) collective-permute-start(f32[352,128]{1,0:T(8,128)S(1)} %get-tuple-element.172), channel_id=1, source_target_pairs={{0,24},{4,28},{8,16},{12,20},{16,8},{20,12},{24,0},{28,4},{1,25},{... | collective-permute-start | bytes 540680 | tf_op jit(solution)/shard_map/ppermute | solution.py:70
  87.2 2.3 %collective-permute-start.31 = (f32[192,128]{1,0:T(8,128)S(1)}, f32[192,128]{1,0:T(8,128)S(1)}, u32[]{:S(2)}, u32[]{:S(2)}) collective-permute-start(f32[192,128]{1,0:T(8,128)S(1)} %get-tuple-element.171), channel_id=1, source_target_pairs={{0,28},{4,8},{8,4},{12,16},{16,12},{20,24},{24,20},{28,0},{1,29},{... | collective-permute-start | bytes 294920 | tf_op jit(solution)/shard_map/ppermute | solution.py:70
  89.5 1.0 shard_map.97
  90.5 5.4 %collective-permute-done.31.refs_4_ = f32[192,128]{1,0:T(8,128)S(1)} collective-permute-done((f32[192,128]{1,0:T(8,128)S(1)}, f32[192,128]{1,0:T(8,128)S(1)}, u32[]{:S(2)}, u32[]{:S(2)}) %collective-permute-start.31) | collective-permute-done | bytes 98336 | tf_op jit(solution)/shard_map/ppermute | solution.py:70
  96.3 1.5 %collective-permute-start.34 = (f32[256,128]{1,0:T(8,128)S(1)}, f32[256,128]{1,0:T(8,128)S(1)}, u32[]{:S(2)}, u32[]{:S(2)}) collective-permute-start(f32[256,128]{1,0:T(8,128)S(1)} %get-tuple-element.181), channel_id=1, source_target_pairs={{0,8},{4,12},{8,0},{12,4},{16,24},{20,28},{24,16},{28,20},{1,9},{5... | collective-permute-start | bytes 393224 | tf_op jit(solution)/shard_map/ppermute | solution.py:70
  97.8 1.0 collective-permute-start.36
  98.8 3.1 %collective-permute-start.35 = (f32[64,128]{1,0:T(8,128)S(1)}, f32[64,128]{1,0:T(8,128)S(1)}, u32[]{:S(2)}, u32[]{:S(2)}) collective-permute-start(f32[64,128]{1,0:T(8,128)S(1)} %get-tuple-element.182), channel_id=1, source_target_pairs={{0,28},{4,8},{8,4},{12,16},{16,12},{20,24},{24,20},{28,0},{1,29},{... | collective-permute-start | bytes 98312 | tf_op jit(solution)/shard_map/ppermute | solution.py:70
  101.9 1.2 %shard_map.98 = (f32[64,1024]{1,0:T(8,128)}, bf16[128,1024]{1,0:T(8,128)(2,1)S(1)}) custom-call(f32[64,1024]{1,0:T(8,128)S(1)} %get-tuple-element.169.refs_0_, bf16[1536,1024]{1,0:T(8,128)(2,1)S(1)} %get-tuple-element.103.refs_3_.refs_1_.refs_0_, bf16[1536,1024]{1,0:T(8,128)(2,1)S(1)} %get-tuple-element.104.refs_4_.refs_2_.refs_1_, ...), custom_call_target="tpu_custom_call" | custom-call | bytes 1048576 | tf_op jit(solution)/shard_map/pallas_call | solution.py:49
  104.0 1.5 %collective-permute-done.35.refs_4_ = f32[64,128]{1,0:T(8,128)S(1)} collective-permute-done((f32[64,128]{1,0:T(8,128)S(1)}, f32[64,128]{1,0:T(8,128)S(1)}, u32[]{:S(2)}, u32[]{:S(2)}) %collective-permute-start.35) | collective-permute-done | bytes 32800 | tf_op jit(solution)/shard_map/ppermute | solution.py:70
  105.5 1.4 %shard_map.101 = (f32[64,1024]{1,0:T(8,128)}, f32[9,64,256]{2,1,0:T(8,128)}) custom-call(f32[64,1024]{1,0:T(8,128)S(1)} %shard_map.99.refs_0_, bf16[1536,1024]{1,0:T(8,128)(2,1)S(1)} %get-tuple-element.103.refs_3_.refs_1_.refs_0_, bf16[1536,1024]{1,0:T(8,128)(2,1)S(1)} %get-tuple-element.104.refs_4_.refs_2_.refs_1_, ...), custom_call_target="tpu_custom_call" | custom-call | bytes 1048576 | tf_op jit(solution)/shard_map/pallas_call | solution.py:49
  (56 shorter events, 11.1 us)
Async XLA Ops:
  1.6 10.7 %copy-start = (bf16[9,64,256]{2,1,0:T(8,128)(2,1)S(1)}, bf16[9,64,256]{2,1,0:T(8,128)(2,1)}, u32[]{:S(2)}) copy-start(bf16[9,64,256]{2,1,0:T(8,128)(2,1)} %param.8) | copy-start | bytes 884740
  1.6 10.2 %collective-permute-start = (bf16[128,1024]{1,0:T(8,128)(2,1)S(1)}, bf16[128,1024]{1,0:T(8,128)(2,1)S(1)}, u32[]{:S(2)}, u32[]{:S(2)}) collective-permute-start(bf16[128,1024]{1,0:T(8,128)(2,1)S(1)} %shard_map.77.refs_3_.refs_0_.refs_6_.refs_7_), channel_id=1, source_target_pairs={{0,2},{1,3},{2,0},{3,1},{4,6},{5,7},{6,4},{7,5},{8,10},{9,11},{10,... | collective-permute-start | bytes 786440 | tf_op jit(solution)/shard_map/ppermute | solution.py:124
  11.8 1.6 %collective-permute-start.1 = (bf16[128,1024]{1,0:T(8,128)(2,1)S(1)}, bf16[128,1024]{1,0:T(8,128)(2,1)S(1)}, u32[]{:S(2)}, u32[]{:S(2)}) collective-permute-start(bf16[128,1024]{1,0:T(8,128)(2,1)S(1)} %shard_map.77.refs_3_.refs_0_.refs_6_.refs_7_), channel_id=1, source_target_pairs={{0,1},{1,0},{2,3},{3,2},{4,5},{5,4},{6,7},{7,6},{8,9},{9,8},{10,11... | collective-permute-start | bytes 786440 | tf_op jit(solution)/shard_map/ppermute | solution.py:124
  11.9 1.9 %collective-permute-start.2 = (bf16[128,1024]{1,0:T(8,128)(2,1)S(1)}, bf16[128,1024]{1,0:T(8,128)(2,1)S(1)}, u32[]{:S(2)}, u32[]{:S(2)}) collective-permute-start(bf16[128,1024]{1,0:T(8,128)(2,1)S(1)} %collective-permute-done.refs_5_.refs_1_), channel_id=1, source_target_pairs={{0,1},{1,0},{2,3},{3,2},{4,5},{5,4},{6,7},{7,6},{8,9},{9,8},{10,11... | collective-permute-start | bytes 786440 | tf_op jit(solution)/shard_map/ppermute | solution.py:124
  14.3 11.4 %collective-permute-start.3 = (f32[192,128]{1,0:T(8,128)S(1)}, f32[192,128]{1,0:T(8,128)S(1)}, u32[]{:S(2)}, u32[]{:S(2)}) collective-permute-start(f32[192,128]{1,0:T(8,128)S(1)} %get-tuple-element.106), channel_id=1, source_target_pairs={{0,8},{4,12},{8,0},{12,4},{16,24},{20,28},{24,16},{28,20},{1,9},{5... | collective-permute-start | bytes 294920 | tf_op jit(solution)/shard_map/ppermute | solution.py:70
  15.9 9.7 %collective-permute-start.4 = (f32[192,128]{1,0:T(8,128)S(1)}, f32[192,128]{1,0:T(8,128)S(1)}, u32[]{:S(2)}, u32[]{:S(2)}) collective-permute-start(f32[192,128]{1,0:T(8,128)S(1)} %get-tuple-element.107), channel_id=1, source_target_pairs={{0,28},{4,8},{8,4},{12,16},{16,12},{20,24},{24,20},{28,0},{1,29},{... | collective-permute-start | bytes 294920 | tf_op jit(solution)/shard_map/ppermute | solution.py:70
  19.3 6.4 %collective-permute-start.5 = (f32[192,128]{1,0:T(8,128)S(1)}, f32[192,128]{1,0:T(8,128)S(1)}, u32[]{:S(2)}, u32[]{:S(2)}) collective-permute-start(f32[192,128]{1,0:T(8,128)S(1)} %get-tuple-element.108), channel_id=1, source_target_pairs={{0,24},{4,28},{8,16},{12,20},{16,8},{20,12},{24,0},{28,4},{1,25},{... | collective-permute-start | bytes 294920 | tf_op jit(solution)/shard_map/ppermute | solution.py:70
  20.9 5.4 %collective-permute-start.6 = (f32[192,128]{1,0:T(8,128)S(1)}, f32[192,128]{1,0:T(8,128)S(1)}, u32[]{:S(2)}, u32[]{:S(2)}) collective-permute-start(f32[192,128]{1,0:T(8,128)S(1)} %get-tuple-element.109), channel_id=1, source_target_pairs={{0,4},{4,0},{8,12},{12,8},{16,20},{20,16},{24,28},{28,24},{1,5},{5... | collective-permute-start | bytes 294920 | tf_op jit(solution)/shard_map/ppermute | solution.py:70
  27.0 9.0 %collective-permute-start.7 = (f32[192,128]{1,0:T(8,128)S(1)}, f32[192,128]{1,0:T(8,128)S(1)}, u32[]{:S(2)}, u32[]{:S(2)}) collective-permute-start(f32[192,128]{1,0:T(8,128)S(1)} %get-tuple-element.119), channel_id=1, source_target_pairs={{0,8},{4,12},{8,0},{12,4},{16,24},{20,28},{24,16},{28,20},{1,9},{5... | collective-permute-start | bytes 294920 | tf_op jit(solution)/shard_map/ppermute | solution.py:70
  27.0 9.1 %collective-permute-start.8 = (f32[192,128]{1,0:T(8,128)S(1)}, f32[192,128]{1,0:T(8,128)S(1)}, u32[]{:S(2)}, u32[]{:S(2)}) collective-permute-start(f32[192,128]{1,0:T(8,128)S(1)} %get-tuple-element.120), channel_id=1, source_target_pairs={{0,28},{4,8},{8,4},{12,16},{16,12},{20,24},{24,20},{28,0},{1,29},{... | collective-permute-start | bytes 294920 | tf_op jit(solution)/shard_map/ppermute | solution.py:70
  30.4 6.5 %collective-permute-start.9 = (f32[192,128]{1,0:T(8,128)S(1)}, f32[192,128]{1,0:T(8,128)S(1)}, u32[]{:S(2)}, u32[]{:S(2)}) collective-permute-start(f32[192,128]{1,0:T(8,128)S(1)} %get-tuple-element.121), channel_id=1, source_target_pairs={{0,24},{4,28},{8,16},{12,20},{16,8},{20,12},{24,0},{28,4},{1,25},{... | collective-permute-start | bytes 294920 | tf_op jit(solution)/shard_map/ppermute | solution.py:70
  31.9 5.0 %collective-permute-start.10 = (f32[192,128]{1,0:T(8,128)S(1)}, f32[192,128]{1,0:T(8,128)S(1)}, u32[]{:S(2)}, u32[]{:S(2)}) collective-permute-start(f32[192,128]{1,0:T(8,128)S(1)} %get-tuple-element.122), channel_id=1, source_target_pairs={{0,4},{4,0},{8,12},{12,8},{16,20},{20,16},{24,28},{28,24},{1,5},{5... | collective-permute-start | bytes 294920 | tf_op jit(solution)/shard_map/ppermute | solution.py:70
  38.0 11.0 %collective-permute-start.19 = (bf16[128,1024]{1,0:T(8,128)(2,1)S(1)}, bf16[128,1024]{1,0:T(8,128)(2,1)S(1)}, u32[]{:S(2)}, u32[]{:S(2)}) collective-permute-start(bf16[128,1024]{1,0:T(8,128)(2,1)S(1)} %get-tuple-element.142.refs_0_), channel_id=1, source_target_pairs={{0,2},{1,3},{2,0},{3,1},{4,6},{5,7},{6,4},{7,5},{8,10},{9,11},{10,... | collective-permute-start | bytes 786440 | tf_op jit(solution)/shard_map/ppermute | solution.py:124
  39.3 8.6 %collective-permute-start.11 = (f32[128,128]{1,0:T(8,128)S(1)}, f32[128,128]{1,0:T(8,128)S(1)}, u32[]{:S(2)}, u32[]{:S(2)}) collective-permute-start(f32[128,128]{1,0:T(8,128)S(1)} %get-tuple-element.127), channel_id=1, source_target_pairs={{0,8},{4,12},{8,0},{12,4},{16,24},{20,28},{24,16},{28,20},{1,9},{5... | collective-permute-start | bytes 196616 | tf_op jit(solution)/shard_map/ppermute | solution.py:70
  40.2 7.6 %collective-permute-start.12 = (f32[128,128]{1,0:T(8,128)S(1)}, f32[128,128]{1,0:T(8,128)S(1)}, u32[]{:S(2)}, u32[]{:S(2)}) collective-permute-start(f32[128,128]{1,0:T(8,128)S(1)} %get-tuple-element.128), channel_id=1, source_target_pairs={{0,28},{4,8},{8,4},{12,16},{16,12},{20,24},{24,20},{28,0},{1,29},{... | collective-permute-start | bytes 196616 | tf_op jit(solution)/shard_map/ppermute | solution.py:70
  41.9 6.1 %collective-permute-start.13 = (f32[128,128]{1,0:T(8,128)S(1)}, f32[128,128]{1,0:T(8,128)S(1)}, u32[]{:S(2)}, u32[]{:S(2)}) collective-permute-start(f32[128,128]{1,0:T(8,128)S(1)} %get-tuple-element.129), channel_id=1, source_target_pairs={{0,24},{4,28},{8,16},{12,20},{16,8},{20,12},{24,0},{28,4},{1,25},{... | collective-permute-start | bytes 196616 | tf_op jit(solution)/shard_map/ppermute | solution.py:70
  43.8 4.3 %collective-permute-start.14 = (f32[128,128]{1,0:T(8,128)S(1)}, f32[128,128]{1,0:T(8,128)S(1)}, u32[]{:S(2)}, u32[]{:S(2)}) collective-permute-start(f32[128,128]{1,0:T(8,128)S(1)} %get-tuple-element.130), channel_id=1, source_target_pairs={{0,4},{4,0},{8,12},{12,8},{16,20},{20,16},{24,28},{28,24},{1,5},{5... | collective-permute-start | bytes 196616 | tf_op jit(solution)/shard_map/ppermute | solution.py:70
  49.0 4.3 %collective-permute-start.20 = (bf16[128,1024]{1,0:T(8,128)(2,1)S(1)}, bf16[128,1024]{1,0:T(8,128)(2,1)S(1)}, u32[]{:S(2)}, u32[]{:S(2)}) collective-permute-start(bf16[128,1024]{1,0:T(8,128)(2,1)S(1)} %get-tuple-element.142.refs_0_), channel_id=1, source_target_pairs={{0,1},{1,0},{2,3},{3,2},{4,5},{5,4},{6,7},{7,6},{8,9},{9,8},{10,11... | collective-permute-start | bytes 786440 | tf_op jit(solution)/shard_map/ppermute | solution.py:124
  49.1 6.9 %collective-permute-start.21 = (bf16[128,1024]{1,0:T(8,128)(2,1)S(1)}, bf16[128,1024]{1,0:T(8,128)(2,1)S(1)}, u32[]{:S(2)}, u32[]{:S(2)}) collective-permute-start(bf16[128,1024]{1,0:T(8,128)(2,1)S(1)} %collective-permute-done.19.refs_1_), channel_id=1, source_target_pairs={{0,1},{1,0},{2,3},{3,2},{4,5},{5,4},{6,7},{7,6},{8,9},{9,8},{10,11... | collective-permute-start | bytes 786440 | tf_op jit(solution)/shard_map/ppermute | solution.py:124
  49.6 9.7 %collective-permute-start.18 = (f32[384,128]{1,0:T(8,128)S(1)}, f32[384,128]{1,0:T(8,128)S(1)}, u32[]{:S(2)}, u32[]{:S(2)}) collective-permute-start(f32[384,128]{1,0:T(8,128)S(1)} %get-tuple-element.140), channel_id=1, source_target_pairs={{0,4},{4,0},{8,12},{12,8},{16,20},{20,16},{24,28},{28,24},{1,5},{5... | collective-permute-start | bytes 589832 | tf_op jit(solution)/shard_map/ppermute | solution.py:70
  51.3 8.0 %collective-permute-start.15 = (f32[128,128]{1,0:T(8,128)S(1)}, f32[128,128]{1,0:T(8,128)S(1)}, u32[]{:S(2)}, u32[]{:S(2)}) collective-permute-start(f32[128,128]{1,0:T(8,128)S(1)} %get-tuple-element.137), channel_id=1, source_target_pairs={{0,8},{4,12},{8,0},{12,4},{16,24},{20,28},{24,16},{28,20},{1,9},{5... | collective-permute-start | bytes 196616 | tf_op jit(solution)/shard_map/ppermute | solution.py:70
  51.4 7.4 %collective-permute-start.16 = (f32[128,128]{1,0:T(8,128)S(1)}, f32[128,128]{1,0:T(8,128)S(1)}, u32[]{:S(2)}, u32[]{:S(2)}) collective-permute-start(f32[128,128]{1,0:T(8,128)S(1)} %get-tuple-element.138), channel_id=1, source_target_pairs={{0,28},{4,8},{8,4},{12,16},{16,12},{20,24},{24,20},{28,0},{1,29},{... | collective-permute-start | bytes 196616 | tf_op jit(solution)/shard_map/ppermute | solution.py:70
  53.3 6.1 %collective-permute-start.17 = (f32[128,128]{1,0:T(8,128)S(1)}, f32[128,128]{1,0:T(8,128)S(1)}, u32[]{:S(2)}, u32[]{:S(2)}) collective-permute-start(f32[128,128]{1,0:T(8,128)S(1)} %get-tuple-element.139), channel_id=1, source_target_pairs={{0,24},{4,28},{8,16},{12,20},{16,8},{20,12},{24,0},{28,4},{1,25},{... | collective-permute-start | bytes 196616 | tf_op jit(solution)/shard_map/ppermute | solution.py:70
  60.5 10.7 %collective-permute-start.25 = (f32[320,128]{1,0:T(8,128)S(1)}, f32[320,128]{1,0:T(8,128)S(1)}, u32[]{:S(2)}, u32[]{:S(2)}) collective-permute-start(f32[320,128]{1,0:T(8,128)S(1)} %get-tuple-element.153), channel_id=1, source_target_pairs={{0,4},{4,0},{8,12},{12,8},{16,20},{20,16},{24,28},{28,24},{1,5},{5... | collective-permute-start | bytes 491528 | tf_op jit(solution)/shard_map/ppermute | solution.py:70
  62.2 8.9 %collective-permute-start.22 = (f32[256,128]{1,0:T(8,128)S(1)}, f32[256,128]{1,0:T(8,128)S(1)}, u32[]{:S(2)}, u32[]{:S(2)}) collective-permute-start(f32[256,128]{1,0:T(8,128)S(1)} %get-tuple-element.150), channel_id=1, source_target_pairs={{0,8},{4,12},{8,0},{12,4},{16,24},{20,28},{24,16},{28,20},{1,9},{5... | collective-permute-start | bytes 393224 | tf_op jit(solution)/shard_map/ppermute | solution.py:70
  63.0 8.2 %collective-permute-start.24 = (f32[256,128]{1,0:T(8,128)S(1)}, f32[256,128]{1,0:T(8,128)S(1)}, u32[]{:S(2)}, u32[]{:S(2)}) collective-permute-start(f32[256,128]{1,0:T(8,128)S(1)} %get-tuple-element.152), channel_id=1, source_target_pairs={{0,24},{4,28},{8,16},{12,20},{16,8},{20,12},{24,0},{28,4},{1,25},{... | collective-permute-start | bytes 393224 | tf_op jit(solution)/shard_map/ppermute | solution.py:70
  63.9 7.2 %collective-permute-start.23 = (f32[128,128]{1,0:T(8,128)S(1)}, f32[128,128]{1,0:T(8,128)S(1)}, u32[]{:S(2)}, u32[]{:S(2)}) collective-permute-start(f32[128,128]{1,0:T(8,128)S(1)} %get-tuple-element.151), channel_id=1, source_target_pairs={{0,28},{4,8},{8,4},{12,16},{16,12},{20,24},{24,20},{28,0},{1,29},{... | collective-permute-start | bytes 196616 | tf_op jit(solution)/shard_map/ppermute | solution.py:70
  72.4 11.0 %collective-permute-start.26 = (f32[352,128]{1,0:T(8,128)S(1)}, f32[352,128]{1,0:T(8,128)S(1)}, u32[]{:S(2)}, u32[]{:S(2)}) collective-permute-start(f32[352,128]{1,0:T(8,128)S(1)} %get-tuple-element.159), channel_id=1, source_target_pairs={{0,8},{4,12},{8,0},{12,4},{16,24},{20,28},{24,16},{28,20},{1,9},{5... | collective-permute-start | bytes 540680 | tf_op jit(solution)/shard_map/ppermute | solution.py:70
  72.5 10.9 %collective-permute-start.28 = (f32[352,128]{1,0:T(8,128)S(1)}, f32[352,128]{1,0:T(8,128)S(1)}, u32[]{:S(2)}, u32[]{:S(2)}) collective-permute-start(f32[352,128]{1,0:T(8,128)S(1)} %get-tuple-element.161), channel_id=1, source_target_pairs={{0,24},{4,28},{8,16},{12,20},{16,8},{20,12},{24,0},{28,4},{1,25},{... | collective-permute-start | bytes 540680 | tf_op jit(solution)/shard_map/ppermute | solution.py:70
  75.1 8.2 %collective-permute-start.29 = (f32[256,128]{1,0:T(8,128)S(1)}, f32[256,128]{1,0:T(8,128)S(1)}, u32[]{:S(2)}, u32[]{:S(2)}) collective-permute-start(f32[256,128]{1,0:T(8,128)S(1)} %get-tuple-element.162), channel_id=1, source_target_pairs={{0,4},{4,0},{8,12},{12,8},{16,20},{20,16},{24,28},{28,24},{1,5},{5... | collective-permute-start | bytes 393224 | tf_op jit(solution)/shard_map/ppermute | solution.py:70
  75.9 7.5 %collective-permute-start.27 = (f32[128,128]{1,0:T(8,128)S(1)}, f32[128,128]{1,0:T(8,128)S(1)}, u32[]{:S(2)}, u32[]{:S(2)}) collective-permute-start(f32[128,128]{1,0:T(8,128)S(1)} %get-tuple-element.160), channel_id=1, source_target_pairs={{0,28},{4,8},{8,4},{12,16},{16,12},{20,24},{24,20},{28,0},{1,29},{... | collective-permute-start | bytes 196616 | tf_op jit(solution)/shard_map/ppermute | solution.py:70
  84.5 11.4 %collective-permute-start.30 = (f32[352,128]{1,0:T(8,128)S(1)}, f32[352,128]{1,0:T(8,128)S(1)}, u32[]{:S(2)}, u32[]{:S(2)}) collective-permute-start(f32[352,128]{1,0:T(8,128)S(1)} %get-tuple-element.170), channel_id=1, source_target_pairs={{0,8},{4,12},{8,0},{12,4},{16,24},{20,28},{24,16},{28,20},{1,9},{5... | collective-permute-start | bytes 540680 | tf_op jit(solution)/shard_map/ppermute | solution.py:70
  84.6 11.3 %collective-permute-start.32 = (f32[352,128]{1,0:T(8,128)S(1)}, f32[352,128]{1,0:T(8,128)S(1)}, u32[]{:S(2)}, u32[]{:S(2)}) collective-permute-start(f32[352,128]{1,0:T(8,128)S(1)} %get-tuple-element.172), channel_id=1, source_target_pairs={{0,24},{4,28},{8,16},{12,20},{16,8},{20,12},{24,0},{28,4},{1,25},{... | collective-permute-start | bytes 540680 | tf_op jit(solution)/shard_map/ppermute | solution.py:70
  87.2 8.7 %collective-permute-start.31 = (f32[192,128]{1,0:T(8,128)S(1)}, f32[192,128]{1,0:T(8,128)S(1)}, u32[]{:S(2)}, u32[]{:S(2)}) collective-permute-start(f32[192,128]{1,0:T(8,128)S(1)} %get-tuple-element.171), channel_id=1, source_target_pairs={{0,28},{4,8},{8,4},{12,16},{16,12},{20,24},{24,20},{28,0},{1,29},{... | collective-permute-start | bytes 294920 | tf_op jit(solution)/shard_map/ppermute | solution.py:70
  89.5 6.4 %collective-permute-start.33 = (f32[192,128]{1,0:T(8,128)S(1)}, f32[192,128]{1,0:T(8,128)S(1)}, u32[]{:S(2)}, u32[]{:S(2)}) collective-permute-start(f32[192,128]{1,0:T(8,128)S(1)} %get-tuple-element.173), channel_id=1, source_target_pairs={{0,4},{4,0},{8,12},{12,8},{16,20},{20,16},{24,28},{28,24},{1,5},{5... | collective-permute-start | bytes 294920 | tf_op jit(solution)/shard_map/ppermute | solution.py:70
  96.2 9.2 %collective-permute-start.37 = (f32[512,128]{1,0:T(8,128)S(1)}, f32[512,128]{1,0:T(8,128)S(1)}, u32[]{:S(2)}, u32[]{:S(2)}) collective-permute-start(f32[512,128]{1,0:T(8,128)S(1)} %get-tuple-element.184), channel_id=1, source_target_pairs={{0,4},{4,0},{8,12},{12,8},{16,20},{20,16},{24,28},{28,24},{1,5},{5... | collective-permute-start | bytes 786440 | tf_op jit(solution)/shard_map/ppermute | solution.py:70
  96.3 9.1 %collective-permute-start.34 = (f32[256,128]{1,0:T(8,128)S(1)}, f32[256,128]{1,0:T(8,128)S(1)}, u32[]{:S(2)}, u32[]{:S(2)}) collective-permute-start(f32[256,128]{1,0:T(8,128)S(1)} %get-tuple-element.181), channel_id=1, source_target_pairs={{0,8},{4,12},{8,0},{12,4},{16,24},{20,28},{24,16},{28,20},{1,9},{5... | collective-permute-start | bytes 393224 | tf_op jit(solution)/shard_map/ppermute | solution.py:70
  97.8 7.7 %collective-permute-start.36 = (f32[256,128]{1,0:T(8,128)S(1)}, f32[256,128]{1,0:T(8,128)S(1)}, u32[]{:S(2)}, u32[]{:S(2)}) collective-permute-start(f32[256,128]{1,0:T(8,128)S(1)} %get-tuple-element.183), channel_id=1, source_target_pairs={{0,24},{4,28},{8,16},{12,20},{16,8},{20,12},{24,0},{28,4},{1,25},{... | collective-permute-start | bytes 393224 | tf_op jit(solution)/shard_map/ppermute | solution.py:70
  98.8 6.7 %collective-permute-start.35 = (f32[64,128]{1,0:T(8,128)S(1)}, f32[64,128]{1,0:T(8,128)S(1)}, u32[]{:S(2)}, u32[]{:S(2)}) collective-permute-start(f32[64,128]{1,0:T(8,128)S(1)} %get-tuple-element.182), channel_id=1, source_target_pairs={{0,28},{4,8},{8,4},{12,16},{16,12},{20,24},{24,20},{28,0},{1,29},{... | collective-permute-start | bytes 98312 | tf_op jit(solution)/shard_map/ppermute | solution.py:70

commit v4 on v3

--- a/solution.py
+++ b/solution.py
@@ -12,7 +12,8 @@
 WIDE = 256
 MIB = 1 << 20
 RING = 8
-QUICK = (1, 2, 7)
+QUICK = (1, 2, 4, 5, 6, 7)
+BESIDE = ("base4", "base6", "fifth", "f_through_high", "f_through_low")
 KINDS = (2, 0, 3, 1)
 
 
@@ -286,33 +287,69 @@
             o.picked[...] = summed(dot(jnp.concatenate(halves(o.part[...]), axis=0), i.pick[...]))
         if step == 1:
             o.back[...] = back_halo(jnp.concatenate(halves(o.fpart[...]), axis=0), i, nodes)
+        if step in (5, 6):
+            o.base[...] = correlate(*halves(o.part[local:, :]), i.g_high[...], i.g_low[...])
 
     return inner
 
 
-def make_quick(step, ring):
+def make_quick(step, chains, following, ring):
     def quick(i, o):
         rows = i.picked.shape[0]
+        local = rows // chains
         both = split_halos(i, rows)
         total = summed(dot(both, i.through_high[...])) + dot(both[:rows], i.through_low[...])
         if step == 1:
-            half = rows // 2
-            total = jnp.concatenate([2.0 * total[:half], total[half:]], axis=0)
+            total = jnp.concatenate([2.0 * total[:local], total[local:]], axis=0)
         else:
             total = 2.0 * total
-        parts = [i.picked[...] + total]
+        parts = [(i.picked[...] + total)[: following * local]]
         if step == 1:
-            local = i.back.shape[0]
             got = [getattr(i, f"halo{k}")[rows : rows + local, :] for k in range(SLOTS)]
-            both = jnp.concatenate(halves(jnp.concatenate(got, axis=1)), axis=0)
-            total = summed(dot(both, i.through_high[...], (1, 1)))
-            parts.append(i.back[...] + total + dot(both[:local], i.through_low[...], (1, 1)))
-        extra = None
-        if step == 7 and ring:
-
-            def got(kind, index):
-                return carried(i, step, rows, kind, index)
-
+            back = jnp.concatenate(halves(jnp.concatenate(got, axis=1)), axis=0)
+            total = summed(dot(back, i.through_high[...], (1, 1)))
+            parts.append(i.back[...] + total + dot(back[:local], i.through_low[...], (1, 1)))
+        if not ring or step <= 2:
+            write_sends(o, parts)
+            return
+        if chains > 1:
+            arrived = both[local : 2 * local], both[rows + local :]
+
+        def got(kind, index):
+            return carried(i, step, rows, kind, index)
+
+        def newest(base, old):
+            return 2.0 * (base + 2.0 * correlate(*arrived, i.g_through_high[...], i.g_through_low[...])) - old
+
+        if step == 4:
+            one = i.one[...] + got(1, 0)
+            half = one.shape[0] // 2
+            o.one[...] = one
+            o.fourth[...] = i.base4[...] + 2.0 * correlate(*arrived, i.f_through_high[...], i.f_through_low[...])
+            group = [o.fourth[...], i.fifth[...], newest(i.base6[...], i.grad2[...])]
+            o.two[...], away = parted(jnp.concatenate(group, axis=0))
+            extra = {1: [away], 2: [one[:half]], 3: [one[half:]]}
+        if step == 5:
+            one = added(i.one[...], got(2, 0), got(3, 0))
+            two = i.two[...] + got(1, 0)
+            half, quarter = one.shape[0] // 2, two.shape[0] // 2
+            o.one[...], o.two[...] = one, two
+            o.seven[...] = newest(i.base[...], i.third[...])
+            extra = {1: [o.seven[...]], 2: [one[half:], two[:quarter]], 3: [one[:half], two[quarter:]]}
+        if step == 6:
+            one = added(i.one[...], got(3, 0), got(2, 0))
+            two = added(i.two[...], got(2, 1), got(3, 1))
+            seven = i.seven[...] + got(1, 0)
+            eight = newest(i.base[...], i.fourth[...])
+            half, quarter = seven.shape[0] // 2, two.shape[0] // 2
+            o.one[...], o.two[...], o.seven[...], o.eight[...] = one, two, seven, eight
+            extra = {
+                0: [eight],
+                1: [eight],
+                2: [two[quarter:], seven[:half], eight],
+                3: [two[:quarter], seven[half:], eight],
+            }
+        if step == 7:
             two = added(i.two[...], got(3, 0), got(2, 0))
             seven = added(i.seven[...], got(2, 1), got(3, 1))
             m1, p1, m2, p2 = from_pairs({0: got(0, 0), 1: got(1, 0), 2: got(2, 2), 3: got(3, 2)})
@@ -385,34 +422,6 @@
                 group = jnp.concatenate([i.grad0[...], i.grad1[...], i.grad2[...], o.third[...]], axis=0)
                 o.one[...], away = parted(group)
                 extra = {1: [away]}
-            if step == 4:
-                one = i.one[...] + got(1, 0)
-                half = one.shape[0] // 2
-                o.one[...] = one
-                o.fourth[...] = correlate(*state, i.feat_t[...])
-                group = jnp.concatenate([o.fourth[...], i.fifth[...], newest(i.grad2[...])], axis=0)
-                o.two[...], away = parted(group)
-                extra = {1: [away], 2: [one[:half]], 3: [one[half:]]}
-            if step == 5:
-                one = added(i.one[...], got(2, 0), got(3, 0))
-                two = i.two[...] + got(1, 0)
-                half, quarter = one.shape[0] // 2, two.shape[0] // 2
-                o.one[...], o.two[...] = one, two
-                o.seven[...] = newest(i.third[...])
-                extra = {1: [o.seven[...]], 2: [one[half:], two[:quarter]], 3: [one[:half], two[quarter:]]}
-            if step == 6:
-                one = added(i.one[...], got(3, 0), got(2, 0))
-                two = added(i.two[...], got(2, 1), got(3, 1))
-                seven = i.seven[...] + got(1, 0)
-                eight = newest(i.fourth[...])
-                half, quarter = seven.shape[0] // 2, two.shape[0] // 2
-                o.one[...], o.two[...], o.seven[...], o.eight[...] = one, two, seven, eight
-                extra = {
-                    0: [eight],
-                    1: [eight],
-                    2: [two[quarter:], seven[:half], eight],
-                    3: [two[:quarter], seven[half:], eight],
-                }
         write_sends(o, parts, extra)
 
     return outer
@@ -428,6 +437,15 @@
     o.fifth[...] = 2.0 * correlate(
         i.both[local : 2 * local], i.both[3 * local :], o.g_high[...], o.g_low[...]
     ) - i.grad1[...]
+    nodes = i.part.shape[1]
+    part = halves(i.part[local:, :])
+    o.base4[...] = correlate(*part, i.feat_t[...])
+    o.base6[...] = correlate(*part, o.g_high[...], o.g_low[...])
+    high, low = i.high[nodes:, :], i.low[nodes:, :]
+    product = dot(high, i.feat_t[...]) + dot(low, i.feat_t[...])
+    o.f_through_high[...], o.f_through_low[...] = halves(product)
+    product = dot(high, o.g_high[...]) + dot(high, o.g_low[...]) + dot(low, o.g_high[...])
+    o.g_through_high[...], o.g_through_low[...] = halves(product)
 
 
 def make_last(step, scale, ring):
@@ -473,6 +491,7 @@
     whole = ((every, nodes), BF16, True)
     turned = ((nodes, every), BF16, True)
     chunk = ((2 * channels, every // 2), F32, True)
+    along = ((SLOTS * tile, every), BF16, True)
 
     stacked = call(
         stack,
@@ -558,6 +577,9 @@
         if step in QUICK:
             ins.update(pick)
             outs["picked"] = ((chains * channels, SLOTS * tile), F32, True)
+        if step in (5, 6):
+            ins.update(g_high=back["g_high"], g_low=back["g_low"])
+            outs["base"] = chunk
         if step == 1:
             outs["back"] = sent_shape
         if step <= 2:
@@ -582,9 +604,16 @@
             back = call(
                 settle,
                 dict(
-                    **{f"block{k}": (x, "") for k, x in enumerate(gather(back_blocks, got["send0"]))}, both=boths[3], grad1=grads[1]
+                    **{f"block{k}": (x, "") for k, x in enumerate(gather(back_blocks, got["send0"]))}, both=boths[3],
+                    grad1=grads[1],
+                    part=part,
+                    feat_t=feat_t,
+                    **matrix,
                 ),
-                dict(g_high=turned, g_low=turned, whole=whole, fifth=chunk),
+                dict(
+                    g_high=turned, g_low=turned, whole=whole, fifth=chunk, base4=chunk, base6=chunk,
+                    **{f"{name}_through_{half}": along for name in "fg" for half in ("high", "low")},
+                ),
             )
         ins = dict(part=part, **matrix, **halos)
         if step == top:
@@ -599,27 +628,9 @@
         if step <= 2:
             ins["fpart"] = inside["fpart"]
             outs["fboth"] = ((2 * channels, nodes), BF16, True)
-        if ring and step >= 3:
-            one = ((4 * channels, every // 2), F32, True)
-            two = ((3 * channels, every // 2), F32, True)
-            if step in (3, 4):
-                ins["feat_t"] = feat_t
-            if step in (4, 5, 6):
-                ins.update(g_high=back["g_high"], g_low=back["g_low"])
-            if step == 3:
-                ins.update({f"grad{k}": grads[k] for k in range(3)})
-                outs.update(one=one, third=chunk)
-            if step == 4:
-                grads[3] = got["third"]
-                ins.update(one=got["one"], grad2=grads[2], fifth=back["fifth"])
-                outs.update(one=one, two=two, fourth=chunk)
-            if step == 5:
-                grads[4] = got["fourth"]
-                ins.update(one=got["one"], two=got["two"], third=grads[3])
-                outs.update(one=one, two=two, seven=chunk)
-            if step == 6:
-                ins.update({k: got[k] for k in ("one", "two", "seven")}, fourth=grads[4])
-                outs.update(one=one, two=two, seven=chunk, eight=chunk)
+        if ring and step == 3:
+            ins.update(feat_t=feat_t, **{f"grad{k}": grads[k] for k in range(3)})
+            outs.update(one=((4 * channels, every // 2), F32, True), third=chunk)
         sent = following + (1 if step == 1 else 0)
         sends = messages(sent * channels, step + 1)
         ready = {}
@@ -627,16 +638,41 @@
             told = dict(picked=inside["picked"], **through, **halos)
             if step == 1:
                 told["back"] = inside["back"]
-            if step == 7 and ring:
-                told.update({k: got[k] for k in ("one", "two", "seven", "eight")})
-                sends.update(two=two, seven=chunk, eight=chunk)
-                ready["one"] = got["one"]
-            ready.update(call(make_quick(step, ring), told, sends))
+            if ring and step >= 4:
+                told["one"] = got["one"]
+                if step < 7:
+                    sends["one"] = ((4 * channels, every // 2), F32, True)
+                else:
+                    ready["one"] = got["one"]
+                sends["two"] = ((3 * channels, every // 2), F32, True)
+                if step >= 5:
+                    told["two"] = got["two"]
+                    sends["seven"] = chunk
+                if step >= 6:
+                    told["seven"] = got["seven"]
+                    sends["eight"] = chunk
+                if step in (4, 5, 6):
+                    told.update({k: back[k] for k in ("g_through_high", "g_through_low")})
+                if step == 4:
+                    told.update(grad2=grads[2], **{k: x for k, x in back.items() if k in BESIDE})
+                    sends["fourth"] = chunk
+                if step == 5:
+                    told.update(base=inside["base"], third=third)
+                if step == 6:
+                    told.update(base=inside["base"], fourth=fourth)
+                if step == 7:
+                    told["eight"] = got["eight"]
+            ready.update(call(make_quick(step, chains, following, ring), told, sends))
         else:
             outs.update(sends)
         before = got["state"]
-        got = call(make_outer(step, chains, following, ring and step >= 3), ins, outs)
+        weight = 2 * chains * channels * nodes * nodes * 3 if step in QUICK else 0
+        got = call(make_outer(step, chains, following, ring and step == 3), ins, outs, flops=weight)
         got.update(ready)
+        if ring and step == 3:
+            third = got["third"]
+        if ring and step == 4:
+            fourth = got["fourth"]
         boths[step] = got["both"]
     if ring:
         return got["result"], jnp.swapaxes(got["grads"], 1, 2)

time: 107 us -> 107 us (level)
  waiting for transfers between devices: 20.1 us -> 17.2 us
  Pallas kernels: 34.7 us -> 36.8 us
    ppermute x32, waiting for transfers between devices: 18.7 us -> 15.8 us  [exchange(): lax.ppermute(block, 'dom', pairs[kind])]
    pallas_call x25 -> x28, Pallas kernels: 34.7 us -> 36.8 us  [call(): pl.pallas_call(kernel, out_shape=shapes, in_specs=specs, out_specs=[pl.Bl...]
  transfers between devices with their start and end apart: 38 -> 38, of which waited for: 14 -> 15; matrix products, arithmetic and copies ran while one was open for 0% -> 0% of each run, Pallas kernels for 25% -> 29%
where the time goes in v4:
time: 107 us; the launch traced here: 106 us
  starting transfers between devices  51.5 us (48%)
  Pallas kernels  36.8 us (34%)
  waiting for transfers between devices  17.2 us (16%)
    ppermute x32, starting transfers between devices, exchange(): lax.ppermute(block, 'dom', pairs[kind])  46.5 us
    pallas_call x28, Pallas kernels, call(): pl.pallas_call(kernel, out_shape=shapes, in_specs=specs, out_specs=[pl.Bl...  36.8 us
    ppermute x32, waiting for transfers between devices, exchange(): lax.ppermute(block, 'dom', pairs[kind])  15.8 us
    ppermute x6, starting transfers between devices, hop(): lax.ppermute(block, 'chan', [(c, c ^ bit) for c in range(lax.axis_size('c...  5.05 us
  transfers between devices with their start and end apart: 38, of which 15 were waited for; matrix products, arithmetic and copies ran while one was open for 0% of the time, Pallas kernels for 29%

profile of v4, /device:TPU:0, one launch (start us, length us, event | category | flops | bytes accessed | tf_op | source)
XLA Modules:
  0.0 106.5 jit_solution(17438000752880925005)
XLA Ops:
  0.6 1.0 shard_map.77.refs_3_.refs_0_.refs_6_.refs_7_
  1.6 3.0 %collective-permute-start = (bf16[128,1024]{1,0:T(8,128)(2,1)S(1)}, bf16[128,1024]{1,0:T(8,128)(2,1)S(1)}, u32[]{:S(2)}, u32[]{:S(2)}) collective-permute-start(bf16[128,1024]{1,0:T(8,128)(2,1)S(1)} %shard_map.77.refs_3_.refs_0_.refs_6_.refs_7_), channel_id=1, source_target_pairs={{0,2},{1,3},{2,0},{3,1},{4,6},{5,7},{6,4},{7,5},{8,10},{9,11},{10,... | collective-permute-start | bytes 786440 | tf_op jit(solution)/shard_map/ppermute | solution.py:125
  4.6 7.1 %shard_map.78 = (bf16[1536,1024]{1,0:T(8,128)(2,1)S(1)}, bf16[1536,1024]{1,0:T(8,128)(2,1)S(1)}, bf16[1024,512]{1,0:T(8,128)(2,1)S(1)}, f32[64,512]{1,0:T(8,128)S(1)}, f32[64,512]{1,0:T(8,128)S(1)}) custom-call(s32[1,8,8]{2,1,0:T(8,128)} %refs_0_.3, s32[1,4,128]{2,1,0:T(4,128)} %refs_1_.3, f32[64,128,128]{2,1,0:T(8,128)} %refs_2_.1, ...), custom_call_target="tpu_custom_call" | custom-call | flops 10000000000 | bytes 1048576 | tf_op jit(solution)/shard_map/pallas_call | solution.py:50
  12.4 1.0 collective-permute-done.1.refs_6_.refs_2_
  14.3 1.6 %collective-permute-start.3 = (f32[192,128]{1,0:T(8,128)S(1)}, f32[192,128]{1,0:T(8,128)S(1)}, u32[]{:S(2)}, u32[]{:S(2)}) collective-permute-start(f32[192,128]{1,0:T(8,128)S(1)} %get-tuple-element.120), channel_id=1, source_target_pairs={{0,8},{4,12},{8,0},{12,4},{16,24},{20,28},{24,16},{28,20},{1,9},{5... | collective-permute-start | bytes 294920 | tf_op jit(solution)/shard_map/ppermute | solution.py:71
  15.9 3.4 %collective-permute-start.4 = (f32[192,128]{1,0:T(8,128)S(1)}, f32[192,128]{1,0:T(8,128)S(1)}, u32[]{:S(2)}, u32[]{:S(2)}) collective-permute-start(f32[192,128]{1,0:T(8,128)S(1)} %get-tuple-element.121), channel_id=1, source_target_pairs={{0,28},{4,8},{8,4},{12,16},{16,12},{20,24},{24,20},{28,0},{1,29},{... | collective-permute-start | bytes 294920 | tf_op jit(solution)/shard_map/ppermute | solution.py:71
  19.3 1.6 %collective-permute-start.5 = (f32[192,128]{1,0:T(8,128)S(1)}, f32[192,128]{1,0:T(8,128)S(1)}, u32[]{:S(2)}, u32[]{:S(2)}) collective-permute-start(f32[192,128]{1,0:T(8,128)S(1)} %get-tuple-element.122), channel_id=1, source_target_pairs={{0,24},{4,28},{8,16},{12,20},{16,8},{20,12},{24,0},{28,4},{1,25},{... | collective-permute-start | bytes 294920 | tf_op jit(solution)/shard_map/ppermute | solution.py:71
  21.2 1.2 %shard_map.83 = (bf16[512,512]{1,0:T(8,128)(2,1)S(1)}, bf16[512,512]{1,0:T(8,128)(2,1)S(1)}) custom-call(bf16[1536,1024]{1,0:T(8,128)(2,1)S(1)} %get-tuple-element.117.refs_3_.refs_1_.refs_0_.refs_8_, bf16[1536,1024]{1,0:T(8,128)(2,1)S(1)} %get-tuple-element.118.refs_4_.refs_2_.refs_1_.refs_9_, ...), custom_call_target="tpu_custom_call" | custom-call | bytes 1048576 | tf_op jit(solution)/shard_map/pallas_call | solution.py:50
  22.5 3.2 %shard_map.80 = (f32[128,1024]{1,0:T(8,128)S(1)}, f32[128,512]{1,0:T(8,128)S(1)}, f32[64,512]{1,0:T(8,128)S(1)}, f32[64,1024]{1,0:T(8,128)S(1)}) custom-call(bf16[256,1024]{1,0:T(8,128)(2,1)S(1)} %get-tuple-element.115.refs_0_, bf16[64,256]{1,0:T(8,128)(2,1)S(1)} %get-tuple-element.224.refs_1_, bf16[256,1024]{1,0:T(8,128)(2,1)S(1)} %get-tuple-element.116.refs_2_, ...), custom_call_target="tpu_custom_call" | custom-call | flops 805306368 | bytes 1048576 | tf_op jit(solution)/shard_map/pallas_call | solution.py:50
  27.0 3.3 %collective-permute-start.8 = (f32[192,128]{1,0:T(8,128)S(1)}, f32[192,128]{1,0:T(8,128)S(1)}, u32[]{:S(2)}, u32[]{:S(2)}) collective-permute-start(f32[192,128]{1,0:T(8,128)S(1)} %get-tuple-element.134), channel_id=1, source_target_pairs={{0,28},{4,8},{8,4},{12,16},{16,12},{20,24},{24,20},{28,0},{1,29},{... | collective-permute-start | bytes 294920 | tf_op jit(solution)/shard_map/ppermute | solution.py:71
  30.4 1.5 %collective-permute-start.9 = (f32[192,128]{1,0:T(8,128)S(1)}, f32[192,128]{1,0:T(8,128)S(1)}, u32[]{:S(2)}, u32[]{:S(2)}) collective-permute-start(f32[192,128]{1,0:T(8,128)S(1)} %get-tuple-element.135), channel_id=1, source_target_pairs={{0,24},{4,28},{8,16},{12,20},{16,8},{20,12},{24,0},{28,4},{1,25},{... | collective-permute-start | bytes 294920 | tf_op jit(solution)/shard_map/ppermute | solution.py:71
  32.4 0.9 shard_map.81
  33.3 2.7 %shard_map.82 = (f32[128,1024]{1,0:T(8,128)S(1)}, f32[128,512]{1,0:T(8,128)S(1)}, f32[64,1024]{1,0:T(8,128)S(1)}) custom-call(bf16[256,1024]{1,0:T(8,128)(2,1)S(1)} %get-tuple-element.125.refs_0_.refs_4_, bf16[64,256]{1,0:T(8,128)(2,1)S(1)} %get-tuple-element.223.refs_1_, bf16[256,1024]{1,0:T(8,128)(2,1)S(1)} %get-tuple-element.116.refs_2_, ...), custom_call_target="tpu_custom_call" | custom-call | flops 805306368 | bytes 1048576 | tf_op jit(solution)/shard_map/pallas_call | solution.py:50
  36.9 1.1 %shard_map.85 = (f32[128,1024]{1,0:T(8,128)S(1)}, bf16[256,1024]{1,0:T(8,128)(2,1)S(1)}, bf16[128,1024]{1,0:T(8,128)(2,1)S(1)}) custom-call(f32[128,1024]{1,0:T(8,128)S(1)} %get-tuple-element.128.refs_0_, bf16[1536,1024]{1,0:T(8,128)(2,1)S(1)} %get-tuple-element.117.refs_3_.refs_1_.refs_0_.refs_8_, ...), custom_call_target="tpu_custom_call" | custom-call | flops 805306368 | bytes 1048576 | tf_op jit(solution)/shard_map/pallas_call | solution.py:50
  38.0 0.9 collective-permute-start.19
  39.3 1.0 collective-permute-start.11
  40.2 1.6 %collective-permute-start.12 = (f32[128,128]{1,0:T(8,128)S(1)}, f32[128,128]{1,0:T(8,128)S(1)}, u32[]{:S(2)}, u32[]{:S(2)}) collective-permute-start(f32[128,128]{1,0:T(8,128)S(1)} %get-tuple-element.142), channel_id=1, source_target_pairs={{0,28},{4,8},{8,4},{12,16},{16,12},{20,24},{24,20},{28,0},{1,29},{... | collective-permute-start | bytes 196616 | tf_op jit(solution)/shard_map/ppermute | solution.py:71
  41.9 1.9 %collective-permute-start.13 = (f32[128,128]{1,0:T(8,128)S(1)}, f32[128,128]{1,0:T(8,128)S(1)}, u32[]{:S(2)}, u32[]{:S(2)}) collective-permute-start(f32[128,128]{1,0:T(8,128)S(1)} %get-tuple-element.143), channel_id=1, source_target_pairs={{0,24},{4,28},{8,16},{12,20},{16,8},{20,12},{24,0},{28,4},{1,25},{... | collective-permute-start | bytes 196616 | tf_op jit(solution)/shard_map/ppermute | solution.py:71
  43.8 1.7 %collective-permute-start.14 = (f32[128,128]{1,0:T(8,128)S(1)}, f32[128,128]{1,0:T(8,128)S(1)}, u32[]{:S(2)}, u32[]{:S(2)}) collective-permute-start(f32[128,128]{1,0:T(8,128)S(1)} %get-tuple-element.144), channel_id=1, source_target_pairs={{0,4},{4,0},{8,12},{12,8},{16,20},{20,16},{24,28},{28,24},{1,5},{5... | collective-permute-start | bytes 196616 | tf_op jit(solution)/shard_map/ppermute | solution.py:71
  45.5 1.2 %shard_map.88 = (bf16[256,1024]{1,0:T(8,128)(2,1)}, bf16[1024,256]{1,0:T(8,128)(2,1)S(1)}, f32[128,128]{1,0:T(8,128)S(1)}, f32[128,128]{1,0:T(8,128)S(1)}, f32[128,128]{1,0:T(8,128)S(1)}) custom-call(bf16[128,1024]{1,0:T(8,128)(2,1)S(1)} %shard_map.77.refs_3_.refs_0_.refs_6_.refs_7_, bf16[128,1024]{1,0:T(8,128)(2,1)S(1)} %collective-permute-done.refs_5_.refs_1_, ...), custom_call_target="tpu_custom_call" | custom-call | bytes 1048576 | tf_op jit(solution)/shard_map/pallas_call | solution.py:50
  46.8 1.1 shard_map.86.refs_0_
  48.1 1.0 shard_map.89
  49.6 1.7 %collective-permute-start.18 = (f32[384,128]{1,0:T(8,128)S(1)}, f32[384,128]{1,0:T(8,128)S(1)}, u32[]{:S(2)}, u32[]{:S(2)}) collective-permute-start(f32[384,128]{1,0:T(8,128)S(1)} %get-tuple-element.155), channel_id=1, source_target_pairs={{0,4},{4,0},{8,12},{12,8},{16,20},{20,16},{24,28},{28,24},{1,5},{5... | collective-permute-start | bytes 589832 | tf_op jit(solution)/shard_map/ppermute | solution.py:71
  51.4 1.9 %collective-permute-start.16 = (f32[128,128]{1,0:T(8,128)S(1)}, f32[128,128]{1,0:T(8,128)S(1)}, u32[]{:S(2)}, u32[]{:S(2)}) collective-permute-start(f32[128,128]{1,0:T(8,128)S(1)} %get-tuple-element.153), channel_id=1, source_target_pairs={{0,28},{4,8},{8,4},{12,16},{16,12},{20,24},{24,20},{28,0},{1,29},{... | collective-permute-start | bytes 196616 | tf_op jit(solution)/shard_map/ppermute | solution.py:71
  53.3 1.7 %collective-permute-start.17 = (f32[128,128]{1,0:T(8,128)S(1)}, f32[128,128]{1,0:T(8,128)S(1)}, u32[]{:S(2)}, u32[]{:S(2)}) collective-permute-start(f32[128,128]{1,0:T(8,128)S(1)} %get-tuple-element.154), channel_id=1, source_target_pairs={{0,24},{4,28},{8,16},{12,20},{16,8},{20,12},{24,0},{28,4},{1,25},{... | collective-permute-start | bytes 196616 | tf_op jit(solution)/shard_map/ppermute | solution.py:71
  55.0 1.3 %shard_map.90 = (f32[128,1024]{1,0:T(8,128)S(1)}, f32[128,512]{1,0:T(8,128)S(1)}) custom-call(bf16[256,1024]{1,0:T(8,128)(2,1)S(1)} %get-tuple-element.149.refs_0_.refs_4_, bf16[64,256]{1,0:T(8,128)(2,1)S(1)} %get-tuple-element.221.refs_1_, bf16[256,1024]{1,0:T(8,128)(2,1)S(1)} %get-tuple-element.116.refs_2_, ...), custom_call_target="tpu_custom_call" | custom-call | flops 805306368 | bytes 1048576 | tf_op jit(solution)/shard_map/pallas_call | solution.py:50
  56.3 2.2 %shard_map.92 = (bf16[1024,256]{1,0:T(8,128)(2,1)S(1)}, bf16[1024,256]{1,0:T(8,128)(2,1)S(1)}, bf16[256,1024]{1,0:T(8,128)(2,1)}, f32[128,128]{1,0:T(8,128)S(1)}...) custom-call(bf16[128,1024]{1,0:T(8,128)(2,1)S(1)} %get-tuple-element, ...), custom_call_target="tpu_custom_call" | custom-call | bytes 1048576 | tf_op jit(solution)/shard_map/pallas_call | solution.py:50
  59.9 1.7 %collective-permute-start.25 = (f32[320,128]{1,0:T(8,128)S(1)}, f32[320,128]{1,0:T(8,128)S(1)}, u32[]{:S(2)}, u32[]{:S(2)}) collective-permute-start(f32[320,128]{1,0:T(8,128)S(1)} %get-tuple-element.176), channel_id=1, source_target_pairs={{0,4},{4,0},{8,12},{12,8},{16,20},{20,16},{24,28},{28,24},{1,5},{5... | collective-permute-start | bytes 491528 | tf_op jit(solution)/shard_map/ppermute | solution.py:71
  61.6 0.8 collective-permute-start.22
  62.4 0.9 collective-permute-start.24
  63.9 2.5 %collective-permute-start.23 = (f32[128,128]{1,0:T(8,128)S(1)}, f32[128,128]{1,0:T(8,128)S(1)}, u32[]{:S(2)}, u32[]{:S(2)}) collective-permute-start(f32[128,128]{1,0:T(8,128)S(1)} %get-tuple-element.174), channel_id=1, source_target_pairs={{0,28},{4,8},{8,4},{12,16},{16,12},{20,24},{24,20},{28,0},{1,29},{... | collective-permute-start | bytes 196616 | tf_op jit(solution)/shard_map/ppermute | solution.py:71
  66.4 1.6 %shard_map.93 = (f32[128,1024]{1,0:T(8,128)S(1)}, f32[128,512]{1,0:T(8,128)S(1)}, f32[128,128]{1,0:T(8,128)S(1)}) custom-call(bf16[256,1024]{1,0:T(8,128)(2,1)S(1)} %get-tuple-element.156.refs_0_, bf16[64,256]{1,0:T(8,128)(2,1)S(1)} %get-tuple-element.220.refs_1_, bf16[256,1024]{1,0:T(8,128)(2,1)S(1)} %get-tuple-element.116.refs_2_, ...), custom_call_target="tpu_custom_call" | custom-call | flops 805306368 | bytes 1048576 | tf_op jit(solution)/shard_map/pallas_call | solution.py:50
  68.0 3.0 %collective-permute-done.23.refs_4_ = f32[128,128]{1,0:T(8,128)S(1)} collective-permute-done((f32[128,128]{1,0:T(8,128)S(1)}, f32[128,128]{1,0:T(8,128)S(1)}, u32[]{:S(2)}, u32[]{:S(2)}) %collective-permute-start.23) | collective-permute-done | bytes 65568 | tf_op jit(solution)/shard_map/ppermute | solution.py:71
  71.5 2.3 %collective-permute-start.28 = (f32[352,128]{1,0:T(8,128)S(1)}, f32[352,128]{1,0:T(8,128)S(1)}, u32[]{:S(2)}, u32[]{:S(2)}) collective-permute-start(f32[352,128]{1,0:T(8,128)S(1)} %get-tuple-element.187), channel_id=1, source_target_pairs={{0,24},{4,28},{8,16},{12,20},{16,8},{20,12},{24,0},{28,4},{1,25},{... | collective-permute-start | bytes 540680 | tf_op jit(solution)/shard_map/ppermute | solution.py:71
  73.8 2.8 %collective-permute-start.27 = (f32[128,128]{1,0:T(8,128)S(1)}, f32[128,128]{1,0:T(8,128)S(1)}, u32[]{:S(2)}, u32[]{:S(2)}) collective-permute-start(f32[128,128]{1,0:T(8,128)S(1)} %get-tuple-element.186), channel_id=1, source_target_pairs={{0,28},{4,8},{8,4},{12,16},{16,12},{20,24},{24,20},{28,0},{1,29},{... | collective-permute-start | bytes 196616 | tf_op jit(solution)/shard_map/ppermute | solution.py:71
  77.2 1.6 %shard_map.96 = (f32[128,1024]{1,0:T(8,128)S(1)}, f32[128,512]{1,0:T(8,128)S(1)}, f32[128,128]{1,0:T(8,128)S(1)}) custom-call(bf16[256,1024]{1,0:T(8,128)(2,1)S(1)} %get-tuple-element.177.refs_0_, bf16[64,256]{1,0:T(8,128)(2,1)S(1)} %get-tuple-element.219.refs_1_, bf16[256,1024]{1,0:T(8,128)(2,1)S(1)} %get-tuple-element.116.refs_2_, ...), custom_call_target="tpu_custom_call" | custom-call | flops 805306368 | bytes 1048576 | tf_op jit(solution)/shard_map/pallas_call | solution.py:50
  78.8 3.3 %collective-permute-done.27.refs_4_ = f32[128,128]{1,0:T(8,128)S(1)} collective-permute-done((f32[128,128]{1,0:T(8,128)S(1)}, f32[128,128]{1,0:T(8,128)S(1)}, u32[]{:S(2)}, u32[]{:S(2)}) %collective-permute-start.27) | collective-permute-done | bytes 65568 | tf_op jit(solution)/shard_map/ppermute | solution.py:71
  82.8 3.0 %collective-permute-start.32 = (f32[352,128]{1,0:T(8,128)S(1)}, f32[352,128]{1,0:T(8,128)S(1)}, u32[]{:S(2)}, u32[]{:S(2)}) collective-permute-start(f32[352,128]{1,0:T(8,128)S(1)} %get-tuple-element.200), channel_id=1, source_target_pairs={{0,24},{4,28},{8,16},{12,20},{16,8},{20,12},{24,0},{28,4},{1,25},{... | collective-permute-start | bytes 540680 | tf_op jit(solution)/shard_map/ppermute | solution.py:71
  85.8 2.4 %collective-permute-start.31 = (f32[192,128]{1,0:T(8,128)S(1)}, f32[192,128]{1,0:T(8,128)S(1)}, u32[]{:S(2)}, u32[]{:S(2)}) collective-permute-start(f32[192,128]{1,0:T(8,128)S(1)} %get-tuple-element.199), channel_id=1, source_target_pairs={{0,28},{4,8},{8,4},{12,16},{16,12},{20,24},{24,20},{28,0},{1,29},{... | collective-permute-start | bytes 294920 | tf_op jit(solution)/shard_map/ppermute | solution.py:71
  88.8 1.0 shard_map.99
  89.9 4.8 %collective-permute-done.31.refs_4_ = f32[192,128]{1,0:T(8,128)S(1)} collective-permute-done((f32[192,128]{1,0:T(8,128)S(1)}, f32[192,128]{1,0:T(8,128)S(1)}, u32[]{:S(2)}, u32[]{:S(2)}) %collective-permute-start.31) | collective-permute-done | bytes 98336 | tf_op jit(solution)/shard_map/ppermute | solution.py:71
  95.1 1.7 %collective-permute-start.34 = (f32[256,128]{1,0:T(8,128)S(1)}, f32[256,128]{1,0:T(8,128)S(1)}, u32[]{:S(2)}, u32[]{:S(2)}) collective-permute-start(f32[256,128]{1,0:T(8,128)S(1)} %get-tuple-element.209), channel_id=1, source_target_pairs={{0,8},{4,12},{8,0},{12,4},{16,24},{20,28},{24,16},{28,20},{1,9},{5... | collective-permute-start | bytes 393224 | tf_op jit(solution)/shard_map/ppermute | solution.py:71
  96.8 1.7 %collective-permute-start.36 = (f32[256,128]{1,0:T(8,128)S(1)}, f32[256,128]{1,0:T(8,128)S(1)}, u32[]{:S(2)}, u32[]{:S(2)}) collective-permute-start(f32[256,128]{1,0:T(8,128)S(1)} %get-tuple-element.211), channel_id=1, source_target_pairs={{0,24},{4,28},{8,16},{12,20},{16,8},{20,12},{24,0},{28,4},{1,25},{... | collective-permute-start | bytes 393224 | tf_op jit(solution)/shard_map/ppermute | solution.py:71
  98.5 2.5 %collective-permute-start.35 = (f32[64,128]{1,0:T(8,128)S(1)}, f32[64,128]{1,0:T(8,128)S(1)}, u32[]{:S(2)}, u32[]{:S(2)}) collective-permute-start(f32[64,128]{1,0:T(8,128)S(1)} %get-tuple-element.210), channel_id=1, source_target_pairs={{0,28},{4,8},{8,4},{12,16},{16,12},{20,24},{24,20},{28,0},{1,29},{... | collective-permute-start | bytes 98312 | tf_op jit(solution)/shard_map/ppermute | solution.py:71
  101.0 1.2 %shard_map.101 = (f32[64,1024]{1,0:T(8,128)}, bf16[128,1024]{1,0:T(8,128)(2,1)S(1)}) custom-call(f32[64,1024]{1,0:T(8,128)S(1)} %get-tuple-element.191.refs_0_, bf16[1536,1024]{1,0:T(8,128)(2,1)S(1)} %get-tuple-element.117.refs_3_.refs_1_.refs_0_.refs_8_, bf16[1536,1024]{1,0:T(8,128)(2,1)S(1)} %get-tuple-element.118.refs_4_.refs_2_.refs_1_.refs_9_, ...), custom_call_target="tpu_custom_call" | custom-call | flops 402653184 | bytes 1048576 | tf_op jit(solution)/shard_map/pallas_call | solution.py:50
  102.2 0.9 shard_map.102.refs_0_
  103.0 2.1 %collective-permute-done.35.refs_4_ = f32[64,128]{1,0:T(8,128)S(1)} collective-permute-done((f32[64,128]{1,0:T(8,128)S(1)}, f32[64,128]{1,0:T(8,128)S(1)}, u32[]{:S(2)}, u32[]{:S(2)}) %collective-permute-start.35) | collective-permute-done | bytes 32800 | tf_op jit(solution)/shard_map/ppermute | solution.py:71
  105.1 1.4 %shard_map.104 = (f32[64,1024]{1,0:T(8,128)}, f32[9,64,256]{2,1,0:T(8,128)}) custom-call(f32[64,1024]{1,0:T(8,128)S(1)} %shard_map.102.refs_0_, bf16[1536,1024]{1,0:T(8,128)(2,1)S(1)} %get-tuple-element.117.refs_3_.refs_1_.refs_0_.refs_8_, bf16[1536,1024]{1,0:T(8,128)(2,1)S(1)} %get-tuple-element.118.refs_4_.refs_2_.refs_1_.refs_9_, ...), custom_call_target="tpu_custom_call" | custom-call | bytes 1048576 | tf_op jit(solution)/shard_map/pallas_call | solution.py:50
  (59 shorter events, 10.5 us)
Async XLA Ops:
  1.6 10.7 %copy-start = (bf16[9,64,256]{2,1,0:T(8,128)(2,1)S(1)}, bf16[9,64,256]{2,1,0:T(8,128)(2,1)}, u32[]{:S(2)}) copy-start(bf16[9,64,256]{2,1,0:T(8,128)(2,1)} %param.8) | copy-start | bytes 884740
  1.6 10.2 %collective-permute-start = (bf16[128,1024]{1,0:T(8,128)(2,1)S(1)}, bf16[128,1024]{1,0:T(8,128)(2,1)S(1)}, u32[]{:S(2)}, u32[]{:S(2)}) collective-permute-start(bf16[128,1024]{1,0:T(8,128)(2,1)S(1)} %shard_map.77.refs_3_.refs_0_.refs_6_.refs_7_), channel_id=1, source_target_pairs={{0,2},{1,3},{2,0},{3,1},{4,6},{5,7},{6,4},{7,5},{8,10},{9,11},{10,... | collective-permute-start | bytes 786440 | tf_op jit(solution)/shard_map/ppermute | solution.py:125
  11.8 1.6 %collective-permute-start.1 = (bf16[128,1024]{1,0:T(8,128)(2,1)S(1)}, bf16[128,1024]{1,0:T(8,128)(2,1)S(1)}, u32[]{:S(2)}, u32[]{:S(2)}) collective-permute-start(bf16[128,1024]{1,0:T(8,128)(2,1)S(1)} %shard_map.77.refs_3_.refs_0_.refs_6_.refs_7_), channel_id=1, source_target_pairs={{0,1},{1,0},{2,3},{3,2},{4,5},{5,4},{6,7},{7,6},{8,9},{9,8},{10,11... | collective-permute-start | bytes 786440 | tf_op jit(solution)/shard_map/ppermute | solution.py:125
  11.9 1.9 %collective-permute-start.2 = (bf16[128,1024]{1,0:T(8,128)(2,1)S(1)}, bf16[128,1024]{1,0:T(8,128)(2,1)S(1)}, u32[]{:S(2)}, u32[]{:S(2)}) collective-permute-start(bf16[128,1024]{1,0:T(8,128)(2,1)S(1)} %collective-permute-done.refs_5_.refs_1_), channel_id=1, source_target_pairs={{0,1},{1,0},{2,3},{3,2},{4,5},{5,4},{6,7},{7,6},{8,9},{9,8},{10,11... | collective-permute-start | bytes 786440 | tf_op jit(solution)/shard_map/ppermute | solution.py:125
  14.3 11.4 %collective-permute-start.3 = (f32[192,128]{1,0:T(8,128)S(1)}, f32[192,128]{1,0:T(8,128)S(1)}, u32[]{:S(2)}, u32[]{:S(2)}) collective-permute-start(f32[192,128]{1,0:T(8,128)S(1)} %get-tuple-element.120), channel_id=1, source_target_pairs={{0,8},{4,12},{8,0},{12,4},{16,24},{20,28},{24,16},{28,20},{1,9},{5... | collective-permute-start | bytes 294920 | tf_op jit(solution)/shard_map/ppermute | solution.py:71
  15.9 9.7 %collective-permute-start.4 = (f32[192,128]{1,0:T(8,128)S(1)}, f32[192,128]{1,0:T(8,128)S(1)}, u32[]{:S(2)}, u32[]{:S(2)}) collective-permute-start(f32[192,128]{1,0:T(8,128)S(1)} %get-tuple-element.121), channel_id=1, source_target_pairs={{0,28},{4,8},{8,4},{12,16},{16,12},{20,24},{24,20},{28,0},{1,29},{... | collective-permute-start | bytes 294920 | tf_op jit(solution)/shard_map/ppermute | solution.py:71
  19.3 6.4 %collective-permute-start.5 = (f32[192,128]{1,0:T(8,128)S(1)}, f32[192,128]{1,0:T(8,128)S(1)}, u32[]{:S(2)}, u32[]{:S(2)}) collective-permute-start(f32[192,128]{1,0:T(8,128)S(1)} %get-tuple-element.122), channel_id=1, source_target_pairs={{0,24},{4,28},{8,16},{12,20},{16,8},{20,12},{24,0},{28,4},{1,25},{... | collective-permute-start | bytes 294920 | tf_op jit(solution)/shard_map/ppermute | solution.py:71
  20.9 5.4 %collective-permute-start.6 = (f32[192,128]{1,0:T(8,128)S(1)}, f32[192,128]{1,0:T(8,128)S(1)}, u32[]{:S(2)}, u32[]{:S(2)}) collective-permute-start(f32[192,128]{1,0:T(8,128)S(1)} %get-tuple-element.123), channel_id=1, source_target_pairs={{0,4},{4,0},{8,12},{12,8},{16,20},{20,16},{24,28},{28,24},{1,5},{5... | collective-permute-start | bytes 294920 | tf_op jit(solution)/shard_map/ppermute | solution.py:71
  27.0 9.0 %collective-permute-start.7 = (f32[192,128]{1,0:T(8,128)S(1)}, f32[192,128]{1,0:T(8,128)S(1)}, u32[]{:S(2)}, u32[]{:S(2)}) collective-permute-start(f32[192,128]{1,0:T(8,128)S(1)} %get-tuple-element.133), channel_id=1, source_target_pairs={{0,8},{4,12},{8,0},{12,4},{16,24},{20,28},{24,16},{28,20},{1,9},{5... | collective-permute-start | bytes 294920 | tf_op jit(solution)/shard_map/ppermute | solution.py:71
  27.0 9.1 %collective-permute-start.8 = (f32[192,128]{1,0:T(8,128)S(1)}, f32[192,128]{1,0:T(8,128)S(1)}, u32[]{:S(2)}, u32[]{:S(2)}) collective-permute-start(f32[192,128]{1,0:T(8,128)S(1)} %get-tuple-element.134), channel_id=1, source_target_pairs={{0,28},{4,8},{8,4},{12,16},{16,12},{20,24},{24,20},{28,0},{1,29},{... | collective-permute-start | bytes 294920 | tf_op jit(solution)/shard_map/ppermute | solution.py:71
  30.4 6.5 %collective-permute-start.9 = (f32[192,128]{1,0:T(8,128)S(1)}, f32[192,128]{1,0:T(8,128)S(1)}, u32[]{:S(2)}, u32[]{:S(2)}) collective-permute-start(f32[192,128]{1,0:T(8,128)S(1)} %get-tuple-element.135), channel_id=1, source_target_pairs={{0,24},{4,28},{8,16},{12,20},{16,8},{20,12},{24,0},{28,4},{1,25},{... | collective-permute-start | bytes 294920 | tf_op jit(solution)/shard_map/ppermute | solution.py:71
  31.9 5.0 %collective-permute-start.10 = (f32[192,128]{1,0:T(8,128)S(1)}, f32[192,128]{1,0:T(8,128)S(1)}, u32[]{:S(2)}, u32[]{:S(2)}) collective-permute-start(f32[192,128]{1,0:T(8,128)S(1)} %get-tuple-element.136), channel_id=1, source_target_pairs={{0,4},{4,0},{8,12},{12,8},{16,20},{20,16},{24,28},{28,24},{1,5},{5... | collective-permute-start | bytes 294920 | tf_op jit(solution)/shard_map/ppermute | solution.py:71
  38.0 11.0 %collective-permute-start.19 = (bf16[128,1024]{1,0:T(8,128)(2,1)S(1)}, bf16[128,1024]{1,0:T(8,128)(2,1)S(1)}, u32[]{:S(2)}, u32[]{:S(2)}) collective-permute-start(bf16[128,1024]{1,0:T(8,128)(2,1)S(1)} %get-tuple-element.159.refs_0_), channel_id=1, source_target_pairs={{0,2},{1,3},{2,0},{3,1},{4,6},{5,7},{6,4},{7,5},{8,10},{9,11},{10,... | collective-permute-start | bytes 786440 | tf_op jit(solution)/shard_map/ppermute | solution.py:125
  39.3 8.6 %collective-permute-start.11 = (f32[128,128]{1,0:T(8,128)S(1)}, f32[128,128]{1,0:T(8,128)S(1)}, u32[]{:S(2)}, u32[]{:S(2)}) collective-permute-start(f32[128,128]{1,0:T(8,128)S(1)} %get-tuple-element.141), channel_id=1, source_target_pairs={{0,8},{4,12},{8,0},{12,4},{16,24},{20,28},{24,16},{28,20},{1,9},{5... | collective-permute-start | bytes 196616 | tf_op jit(solution)/shard_map/ppermute | solution.py:71
  40.2 7.6 %collective-permute-start.12 = (f32[128,128]{1,0:T(8,128)S(1)}, f32[128,128]{1,0:T(8,128)S(1)}, u32[]{:S(2)}, u32[]{:S(2)}) collective-permute-start(f32[128,128]{1,0:T(8,128)S(1)} %get-tuple-element.142), channel_id=1, source_target_pairs={{0,28},{4,8},{8,4},{12,16},{16,12},{20,24},{24,20},{28,0},{1,29},{... | collective-permute-start | bytes 196616 | tf_op jit(solution)/shard_map/ppermute | solution.py:71
  41.9 6.1 %collective-permute-start.13 = (f32[128,128]{1,0:T(8,128)S(1)}, f32[128,128]{1,0:T(8,128)S(1)}, u32[]{:S(2)}, u32[]{:S(2)}) collective-permute-start(f32[128,128]{1,0:T(8,128)S(1)} %get-tuple-element.143), channel_id=1, source_target_pairs={{0,24},{4,28},{8,16},{12,20},{16,8},{20,12},{24,0},{28,4},{1,25},{... | collective-permute-start | bytes 196616 | tf_op jit(solution)/shard_map/ppermute | solution.py:71
  43.8 4.3 %collective-permute-start.14 = (f32[128,128]{1,0:T(8,128)S(1)}, f32[128,128]{1,0:T(8,128)S(1)}, u32[]{:S(2)}, u32[]{:S(2)}) collective-permute-start(f32[128,128]{1,0:T(8,128)S(1)} %get-tuple-element.144), channel_id=1, source_target_pairs={{0,4},{4,0},{8,12},{12,8},{16,20},{20,16},{24,28},{28,24},{1,5},{5... | collective-permute-start | bytes 196616 | tf_op jit(solution)/shard_map/ppermute | solution.py:71
  49.0 4.3 %collective-permute-start.20 = (bf16[128,1024]{1,0:T(8,128)(2,1)S(1)}, bf16[128,1024]{1,0:T(8,128)(2,1)S(1)}, u32[]{:S(2)}, u32[]{:S(2)}) collective-permute-start(bf16[128,1024]{1,0:T(8,128)(2,1)S(1)} %get-tuple-element.159.refs_0_), channel_id=1, source_target_pairs={{0,1},{1,0},{2,3},{3,2},{4,5},{5,4},{6,7},{7,6},{8,9},{9,8},{10,11... | collective-permute-start | bytes 786440 | tf_op jit(solution)/shard_map/ppermute | solution.py:125
  49.1 7.2 %collective-permute-start.21 = (bf16[128,1024]{1,0:T(8,128)(2,1)S(1)}, bf16[128,1024]{1,0:T(8,128)(2,1)S(1)}, u32[]{:S(2)}, u32[]{:S(2)}) collective-permute-start(bf16[128,1024]{1,0:T(8,128)(2,1)S(1)} %collective-permute-done.19.refs_1_), channel_id=1, source_target_pairs={{0,1},{1,0},{2,3},{3,2},{4,5},{5,4},{6,7},{7,6},{8,9},{9,8},{10,11... | collective-permute-start | bytes 786440 | tf_op jit(solution)/shard_map/ppermute | solution.py:125
  49.6 9.7 %collective-permute-start.18 = (f32[384,128]{1,0:T(8,128)S(1)}, f32[384,128]{1,0:T(8,128)S(1)}, u32[]{:S(2)}, u32[]{:S(2)}) collective-permute-start(f32[384,128]{1,0:T(8,128)S(1)} %get-tuple-element.155), channel_id=1, source_target_pairs={{0,4},{4,0},{8,12},{12,8},{16,20},{20,16},{24,28},{28,24},{1,5},{5... | collective-permute-start | bytes 589832 | tf_op jit(solution)/shard_map/ppermute | solution.py:71
  51.3 8.0 %collective-permute-start.15 = (f32[128,128]{1,0:T(8,128)S(1)}, f32[128,128]{1,0:T(8,128)S(1)}, u32[]{:S(2)}, u32[]{:S(2)}) collective-permute-start(f32[128,128]{1,0:T(8,128)S(1)} %get-tuple-element.152), channel_id=1, source_target_pairs={{0,8},{4,12},{8,0},{12,4},{16,24},{20,28},{24,16},{28,20},{1,9},{5... | collective-permute-start | bytes 196616 | tf_op jit(solution)/shard_map/ppermute | solution.py:71
  51.4 7.4 %collective-permute-start.16 = (f32[128,128]{1,0:T(8,128)S(1)}, f32[128,128]{1,0:T(8,128)S(1)}, u32[]{:S(2)}, u32[]{:S(2)}) collective-permute-start(f32[128,128]{1,0:T(8,128)S(1)} %get-tuple-element.153), channel_id=1, source_target_pairs={{0,28},{4,8},{8,4},{12,16},{16,12},{20,24},{24,20},{28,0},{1,29},{... | collective-permute-start | bytes 196616 | tf_op jit(solution)/shard_map/ppermute | solution.py:71
  53.3 6.1 %collective-permute-start.17 = (f32[128,128]{1,0:T(8,128)S(1)}, f32[128,128]{1,0:T(8,128)S(1)}, u32[]{:S(2)}, u32[]{:S(2)}) collective-permute-start(f32[128,128]{1,0:T(8,128)S(1)} %get-tuple-element.154), channel_id=1, source_target_pairs={{0,24},{4,28},{8,16},{12,20},{16,8},{20,12},{24,0},{28,4},{1,25},{... | collective-permute-start | bytes 196616 | tf_op jit(solution)/shard_map/ppermute | solution.py:71
  59.9 11.1 %collective-permute-start.25 = (f32[320,128]{1,0:T(8,128)S(1)}, f32[320,128]{1,0:T(8,128)S(1)}, u32[]{:S(2)}, u32[]{:S(2)}) collective-permute-start(f32[320,128]{1,0:T(8,128)S(1)} %get-tuple-element.176), channel_id=1, source_target_pairs={{0,4},{4,0},{8,12},{12,8},{16,20},{20,16},{24,28},{28,24},{1,5},{5... | collective-permute-start | bytes 491528 | tf_op jit(solution)/shard_map/ppermute | solution.py:71
  61.6 9.4 %collective-permute-start.22 = (f32[256,128]{1,0:T(8,128)S(1)}, f32[256,128]{1,0:T(8,128)S(1)}, u32[]{:S(2)}, u32[]{:S(2)}) collective-permute-start(f32[256,128]{1,0:T(8,128)S(1)} %get-tuple-element.173), channel_id=1, source_target_pairs={{0,8},{4,12},{8,0},{12,4},{16,24},{20,28},{24,16},{28,20},{1,9},{5... | collective-permute-start | bytes 393224 | tf_op jit(solution)/shard_map/ppermute | solution.py:71
  62.4 8.6 %collective-permute-start.24 = (f32[256,128]{1,0:T(8,128)S(1)}, f32[256,128]{1,0:T(8,128)S(1)}, u32[]{:S(2)}, u32[]{:S(2)}) collective-permute-start(f32[256,128]{1,0:T(8,128)S(1)} %get-tuple-element.175), channel_id=1, source_target_pairs={{0,24},{4,28},{8,16},{12,20},{16,8},{20,12},{24,0},{28,4},{1,25},{... | collective-permute-start | bytes 393224 | tf_op jit(solution)/shard_map/ppermute | solution.py:71
  63.9 7.1 %collective-permute-start.23 = (f32[128,128]{1,0:T(8,128)S(1)}, f32[128,128]{1,0:T(8,128)S(1)}, u32[]{:S(2)}, u32[]{:S(2)}) collective-permute-start(f32[128,128]{1,0:T(8,128)S(1)} %get-tuple-element.174), channel_id=1, source_target_pairs={{0,28},{4,8},{8,4},{12,16},{16,12},{20,24},{24,20},{28,0},{1,29},{... | collective-permute-start | bytes 196616 | tf_op jit(solution)/shard_map/ppermute | solution.py:71
  71.4 10.8 %collective-permute-start.26 = (f32[352,128]{1,0:T(8,128)S(1)}, f32[352,128]{1,0:T(8,128)S(1)}, u32[]{:S(2)}, u32[]{:S(2)}) collective-permute-start(f32[352,128]{1,0:T(8,128)S(1)} %get-tuple-element.185), channel_id=1, source_target_pairs={{0,8},{4,12},{8,0},{12,4},{16,24},{20,28},{24,16},{28,20},{1,9},{5... | collective-permute-start | bytes 540680 | tf_op jit(solution)/shard_map/ppermute | solution.py:71
  71.5 10.7 %collective-permute-start.28 = (f32[352,128]{1,0:T(8,128)S(1)}, f32[352,128]{1,0:T(8,128)S(1)}, u32[]{:S(2)}, u32[]{:S(2)}) collective-permute-start(f32[352,128]{1,0:T(8,128)S(1)} %get-tuple-element.187), channel_id=1, source_target_pairs={{0,24},{4,28},{8,16},{12,20},{16,8},{20,12},{24,0},{28,4},{1,25},{... | collective-permute-start | bytes 540680 | tf_op jit(solution)/shard_map/ppermute | solution.py:71
  73.8 8.3 %collective-permute-start.27 = (f32[128,128]{1,0:T(8,128)S(1)}, f32[128,128]{1,0:T(8,128)S(1)}, u32[]{:S(2)}, u32[]{:S(2)}) collective-permute-start(f32[128,128]{1,0:T(8,128)S(1)} %get-tuple-element.186), channel_id=1, source_target_pairs={{0,28},{4,8},{8,4},{12,16},{16,12},{20,24},{24,20},{28,0},{1,29},{... | collective-permute-start | bytes 196616 | tf_op jit(solution)/shard_map/ppermute | solution.py:71
  76.6 5.7 %collective-permute-start.29 = (f32[256,128]{1,0:T(8,128)S(1)}, f32[256,128]{1,0:T(8,128)S(1)}, u32[]{:S(2)}, u32[]{:S(2)}) collective-permute-start(f32[256,128]{1,0:T(8,128)S(1)} %get-tuple-element.188), channel_id=1, source_target_pairs={{0,4},{4,0},{8,12},{12,8},{16,20},{20,16},{24,28},{28,24},{1,5},{5... | collective-permute-start | bytes 393224 | tf_op jit(solution)/shard_map/ppermute | solution.py:71
  82.7 12.0 %collective-permute-start.30 = (f32[352,128]{1,0:T(8,128)S(1)}, f32[352,128]{1,0:T(8,128)S(1)}, u32[]{:S(2)}, u32[]{:S(2)}) collective-permute-start(f32[352,128]{1,0:T(8,128)S(1)} %get-tuple-element.198), channel_id=1, source_target_pairs={{0,8},{4,12},{8,0},{12,4},{16,24},{20,28},{24,16},{28,20},{1,9},{5... | collective-permute-start | bytes 540680 | tf_op jit(solution)/shard_map/ppermute | solution.py:71
  82.8 11.9 %collective-permute-start.32 = (f32[352,128]{1,0:T(8,128)S(1)}, f32[352,128]{1,0:T(8,128)S(1)}, u32[]{:S(2)}, u32[]{:S(2)}) collective-permute-start(f32[352,128]{1,0:T(8,128)S(1)} %get-tuple-element.200), channel_id=1, source_target_pairs={{0,24},{4,28},{8,16},{12,20},{16,8},{20,12},{24,0},{28,4},{1,25},{... | collective-permute-start | bytes 540680 | tf_op jit(solution)/shard_map/ppermute | solution.py:71
  85.8 8.8 %collective-permute-start.31 = (f32[192,128]{1,0:T(8,128)S(1)}, f32[192,128]{1,0:T(8,128)S(1)}, u32[]{:S(2)}, u32[]{:S(2)}) collective-permute-start(f32[192,128]{1,0:T(8,128)S(1)} %get-tuple-element.199), channel_id=1, source_target_pairs={{0,28},{4,8},{8,4},{12,16},{16,12},{20,24},{24,20},{28,0},{1,29},{... | collective-permute-start | bytes 294920 | tf_op jit(solution)/shard_map/ppermute | solution.py:71
  88.2 6.4 %collective-permute-start.33 = (f32[192,128]{1,0:T(8,128)S(1)}, f32[192,128]{1,0:T(8,128)S(1)}, u32[]{:S(2)}, u32[]{:S(2)}) collective-permute-start(f32[192,128]{1,0:T(8,128)S(1)} %get-tuple-element.201), channel_id=1, source_target_pairs={{0,4},{4,0},{8,12},{12,8},{16,20},{20,16},{24,28},{28,24},{1,5},{5... | collective-permute-start | bytes 294920 | tf_op jit(solution)/shard_map/ppermute | solution.py:71
  95.0 10.1 %collective-permute-start.37 = (f32[512,128]{1,0:T(8,128)S(1)}, f32[512,128]{1,0:T(8,128)S(1)}, u32[]{:S(2)}, u32[]{:S(2)}) collective-permute-start(f32[512,128]{1,0:T(8,128)S(1)} %get-tuple-element.212), channel_id=1, source_target_pairs={{0,4},{4,0},{8,12},{12,8},{16,20},{20,16},{24,28},{28,24},{1,5},{5... | collective-permute-start | bytes 786440 | tf_op jit(solution)/shard_map/ppermute | solution.py:71
  95.1 10.0 %collective-permute-start.34 = (f32[256,128]{1,0:T(8,128)S(1)}, f32[256,128]{1,0:T(8,128)S(1)}, u32[]{:S(2)}, u32[]{:S(2)}) collective-permute-start(f32[256,128]{1,0:T(8,128)S(1)} %get-tuple-element.209), channel_id=1, source_target_pairs={{0,8},{4,12},{8,0},{12,4},{16,24},{20,28},{24,16},{28,20},{1,9},{5... | collective-permute-start | bytes 393224 | tf_op jit(solution)/shard_map/ppermute | solution.py:71
  96.8 8.4 %collective-permute-start.36 = (f32[256,128]{1,0:T(8,128)S(1)}, f32[256,128]{1,0:T(8,128)S(1)}, u32[]{:S(2)}, u32[]{:S(2)}) collective-permute-start(f32[256,128]{1,0:T(8,128)S(1)} %get-tuple-element.211), channel_id=1, source_target_pairs={{0,24},{4,28},{8,16},{12,20},{16,8},{20,12},{24,0},{28,4},{1,25},{... | collective-permute-start | bytes 393224 | tf_op jit(solution)/shard_map/ppermute | solution.py:71
  98.5 6.6 %collective-permute-start.35 = (f32[64,128]{1,0:T(8,128)S(1)}, f32[64,128]{1,0:T(8,128)S(1)}, u32[]{:S(2)}, u32[]{:S(2)}) collective-permute-start(f32[64,128]{1,0:T(8,128)S(1)} %get-tuple-element.210), channel_id=1, source_target_pairs={{0,28},{4,8},{8,4},{12,16},{16,12},{20,24},{24,20},{28,0},{1,29},{... | collective-permute-start | bytes 98312 | tf_op jit(solution)/shard_map/ppermute | solution.py:71

commit v5 on v4

--- a/solution.py
+++ b/solution.py
@@ -82,20 +82,16 @@
 
 
 def from_pairs(got):
-    odd, far = sides()
-    odd, far = odd == 1, far == 1
-    near = (None, None)
-    if 0 in got:
-        near = (jnp.where(odd, got[1], got[0]), jnp.where(odd, got[0], got[1]))
-    return *near, jnp.where(far, got[2], got[3]), jnp.where(far, got[3], got[2])
+    far = sides()[1] == 1
+    return jnp.where(far, got[2], got[3]), jnp.where(far, got[3], got[2])
 
 
 LAYOUT = {
     4: {1: (256,)},
     5: {1: (192,), 2: (128,), 3: (128,)},
     6: {1: (128,), 2: (128, 96), 3: (128, 96)},
-    7: {0: (128,), 1: (128,), 2: (96, 64, 128), 3: (96, 64, 128)},
-    8: {1: (192, 256), 2: (64, 128), 3: (64, 128)},
+    7: {1: (128,), 2: (96, 64, 128), 3: (96, 64, 128)},
+    8: {0: (128,), 1: (192, 256), 2: (64, 128), 3: (64, 128)},
 }
 
 
@@ -344,7 +340,6 @@
             half, quarter = seven.shape[0] // 2, two.shape[0] // 2
             o.one[...], o.two[...], o.seven[...], o.eight[...] = one, two, seven, eight
             extra = {
-                0: [eight],
                 1: [eight],
                 2: [two[quarter:], seven[:half], eight],
                 3: [two[:quarter], seven[half:], eight],
@@ -352,12 +347,13 @@
         if step == 7:
             two = added(i.two[...], got(3, 0), got(2, 0))
             seven = added(i.seven[...], got(2, 1), got(3, 1))
-            m1, p1, m2, p2 = from_pairs({0: got(0, 0), 1: got(1, 0), 2: got(2, 2), 3: got(3, 2)})
+            near, (m2, p2) = got(1, 0), from_pairs({2: got(2, 2), 3: got(3, 2)})
             half = seven.shape[0] // 2
             o.two[...], o.seven[...] = two, seven
-            o.eight[...] = i.eight[...] + m1 + p1 + m2 + p2
-            on = pairs_of_two(m1, p1 + p2)
-            extra = {1: [two, i.one[...]], 2: [seven[half:], on[2]], 3: [seven[:half], on[3]]}
+            o.eight[...] = i.eight[...] + near + m2 + p2
+            on = pairs_of_two(near, near + p2)
+            across = jnp.where(sides()[0] == 1, m2, p2)
+            extra = {0: [across], 1: [two, i.one[...]], 2: [seven[half:], on[2]], 3: [seven[:half], on[3]]}
         write_sends(o, parts, extra)
 
     return quick
@@ -472,8 +468,8 @@
         for k in range(3):
             put(4 + k, two[k * size : (k + 1) * size])
         put(7, added(i.seven[...], got(3, 0), got(2, 0)))
-        _, _, m2, p2 = from_pairs({2: got(2, 1), 3: got(3, 1)})
-        put(8, i.eight[...] + m2 + p2)
+        m2, p2 = from_pairs({2: got(2, 1), 3: got(3, 1)})
+        put(8, i.eight[...] + m2 + p2 + got(0, 0))
 
     return last
 

time: 107 us -> 106 us (level)
  no operation moved by 1% of the time
where the time goes in v5:
time: 106 us
  starting transfers between devices  51.6 us (49%)
  Pallas kernels  36.7 us (35%)
  waiting for transfers between devices  16.6 us (16%)
    ppermute x32, starting transfers between devices, exchange(): lax.ppermute(block, 'dom', pairs[kind])  46.5 us
    pallas_call x28, Pallas kernels, call(): pl.pallas_call(kernel, out_shape=shapes, in_specs=specs, out_specs=[pl.Bl...  36.7 us
    ppermute x32, waiting for transfers between devices, exchange(): lax.ppermute(block, 'dom', pairs[kind])  15.2 us
    ppermute x6, starting transfers between devices, hop(): lax.ppermute(block, 'chan', [(c, c ^ bit) for c in range(lax.axis_size('c...  5.05 us
  transfers between devices with their start and end apart: 38, of which 15 were waited for; matrix products, arithmetic and copies ran while one was open for 0% of the time, Pallas kernels for 29%

profile of v5, /device:TPU:0, one launch (start us, length us, event | category | flops | bytes accessed | tf_op | source)
XLA Modules:
  0.0 105.8 jit_solution(9067973118860971653)
XLA Ops:
  0.6 1.0 shard_map.77.refs_3_.refs_0_.refs_6_.refs_7_
  1.6 3.0 %collective-permute-start = (bf16[128,1024]{1,0:T(8,128)(2,1)S(1)}, bf16[128,1024]{1,0:T(8,128)(2,1)S(1)}, u32[]{:S(2)}, u32[]{:S(2)}) collective-permute-start(bf16[128,1024]{1,0:T(8,128)(2,1)S(1)} %shard_map.77.refs_3_.refs_0_.refs_6_.refs_7_), channel_id=1, source_target_pairs={{0,2},{1,3},{2,0},{3,1},{4,6},{5,7},{6,4},{7,5},{8,10},{9,11},{10,... | collective-permute-start | bytes 786440 | tf_op jit(solution)/shard_map/ppermute | solution.py:121
  4.6 7.1 %shard_map.78 = (bf16[1536,1024]{1,0:T(8,128)(2,1)S(1)}, bf16[1536,1024]{1,0:T(8,128)(2,1)S(1)}, bf16[1024,512]{1,0:T(8,128)(2,1)S(1)}, f32[64,512]{1,0:T(8,128)S(1)}, f32[64,512]{1,0:T(8,128)S(1)}) custom-call(s32[1,8,8]{2,1,0:T(8,128)} %refs_0_.3, s32[1,4,128]{2,1,0:T(4,128)} %refs_1_.3, f32[64,128,128]{2,1,0:T(8,128)} %refs_2_.1, ...), custom_call_target="tpu_custom_call" | custom-call | flops 10000000000 | bytes 1048576 | tf_op jit(solution)/shard_map/pallas_call | solution.py:50
  12.4 1.0 collective-permute-done.1.refs_6_.refs_2_
  14.3 1.6 %collective-permute-start.3 = (f32[192,128]{1,0:T(8,128)S(1)}, f32[192,128]{1,0:T(8,128)S(1)}, u32[]{:S(2)}, u32[]{:S(2)}) collective-permute-start(f32[192,128]{1,0:T(8,128)S(1)} %get-tuple-element.120), channel_id=1, source_target_pairs={{0,8},{4,12},{8,0},{12,4},{16,24},{20,28},{24,16},{28,20},{1,9},{5... | collective-permute-start | bytes 294920 | tf_op jit(solution)/shard_map/ppermute | solution.py:71
  15.9 3.4 %collective-permute-start.4 = (f32[192,128]{1,0:T(8,128)S(1)}, f32[192,128]{1,0:T(8,128)S(1)}, u32[]{:S(2)}, u32[]{:S(2)}) collective-permute-start(f32[192,128]{1,0:T(8,128)S(1)} %get-tuple-element.121), channel_id=1, source_target_pairs={{0,28},{4,8},{8,4},{12,16},{16,12},{20,24},{24,20},{28,0},{1,29},{... | collective-permute-start | bytes 294920 | tf_op jit(solution)/shard_map/ppermute | solution.py:71
  19.3 1.6 %collective-permute-start.5 = (f32[192,128]{1,0:T(8,128)S(1)}, f32[192,128]{1,0:T(8,128)S(1)}, u32[]{:S(2)}, u32[]{:S(2)}) collective-permute-start(f32[192,128]{1,0:T(8,128)S(1)} %get-tuple-element.122), channel_id=1, source_target_pairs={{0,24},{4,28},{8,16},{12,20},{16,8},{20,12},{24,0},{28,4},{1,25},{... | collective-permute-start | bytes 294920 | tf_op jit(solution)/shard_map/ppermute | solution.py:71
  21.2 1.2 %shard_map.83 = (bf16[512,512]{1,0:T(8,128)(2,1)S(1)}, bf16[512,512]{1,0:T(8,128)(2,1)S(1)}) custom-call(bf16[1536,1024]{1,0:T(8,128)(2,1)S(1)} %get-tuple-element.117.refs_3_.refs_1_.refs_0_.refs_8_, bf16[1536,1024]{1,0:T(8,128)(2,1)S(1)} %get-tuple-element.118.refs_4_.refs_2_.refs_1_.refs_9_, ...), custom_call_target="tpu_custom_call" | custom-call | bytes 1048576 | tf_op jit(solution)/shard_map/pallas_call | solution.py:50
  22.5 3.2 %shard_map.80 = (f32[128,1024]{1,0:T(8,128)S(1)}, f32[128,512]{1,0:T(8,128)S(1)}, f32[64,512]{1,0:T(8,128)S(1)}, f32[64,1024]{1,0:T(8,128)S(1)}) custom-call(bf16[256,1024]{1,0:T(8,128)(2,1)S(1)} %get-tuple-element.115.refs_0_, bf16[64,256]{1,0:T(8,128)(2,1)S(1)} %get-tuple-element.224.refs_1_, bf16[256,1024]{1,0:T(8,128)(2,1)S(1)} %get-tuple-element.116.refs_2_, ...), custom_call_target="tpu_custom_call" | custom-call | flops 805306368 | bytes 1048576 | tf_op jit(solution)/shard_map/pallas_call | solution.py:50
  27.0 3.3 %collective-permute-start.8 = (f32[192,128]{1,0:T(8,128)S(1)}, f32[192,128]{1,0:T(8,128)S(1)}, u32[]{:S(2)}, u32[]{:S(2)}) collective-permute-start(f32[192,128]{1,0:T(8,128)S(1)} %get-tuple-element.134), channel_id=1, source_target_pairs={{0,28},{4,8},{8,4},{12,16},{16,12},{20,24},{24,20},{28,0},{1,29},{... | collective-permute-start | bytes 294920 | tf_op jit(solution)/shard_map/ppermute | solution.py:71
  30.4 1.5 %collective-permute-start.9 = (f32[192,128]{1,0:T(8,128)S(1)}, f32[192,128]{1,0:T(8,128)S(1)}, u32[]{:S(2)}, u32[]{:S(2)}) collective-permute-start(f32[192,128]{1,0:T(8,128)S(1)} %get-tuple-element.135), channel_id=1, source_target_pairs={{0,24},{4,28},{8,16},{12,20},{16,8},{20,12},{24,0},{28,4},{1,25},{... | collective-permute-start | bytes 294920 | tf_op jit(solution)/shard_map/ppermute | solution.py:71
  32.4 0.9 shard_map.81
  33.3 2.7 %shard_map.82 = (f32[128,1024]{1,0:T(8,128)S(1)}, f32[128,512]{1,0:T(8,128)S(1)}, f32[64,1024]{1,0:T(8,128)S(1)}) custom-call(bf16[256,1024]{1,0:T(8,128)(2,1)S(1)} %get-tuple-element.125.refs_0_.refs_4_, bf16[64,256]{1,0:T(8,128)(2,1)S(1)} %get-tuple-element.223.refs_1_, bf16[256,1024]{1,0:T(8,128)(2,1)S(1)} %get-tuple-element.116.refs_2_, ...), custom_call_target="tpu_custom_call" | custom-call | flops 805306368 | bytes 1048576 | tf_op jit(solution)/shard_map/pallas_call | solution.py:50
  36.9 1.1 %shard_map.85 = (f32[128,1024]{1,0:T(8,128)S(1)}, bf16[256,1024]{1,0:T(8,128)(2,1)S(1)}, bf16[128,1024]{1,0:T(8,128)(2,1)S(1)}) custom-call(f32[128,1024]{1,0:T(8,128)S(1)} %get-tuple-element.128.refs_0_, bf16[1536,1024]{1,0:T(8,128)(2,1)S(1)} %get-tuple-element.117.refs_3_.refs_1_.refs_0_.refs_8_, ...), custom_call_target="tpu_custom_call" | custom-call | flops 805306368 | bytes 1048576 | tf_op jit(solution)/shard_map/pallas_call | solution.py:50
  38.0 0.9 collective-permute-start.19
  39.3 1.0 collective-permute-start.11
  40.2 1.6 %collective-permute-start.12 = (f32[128,128]{1,0:T(8,128)S(1)}, f32[128,128]{1,0:T(8,128)S(1)}, u32[]{:S(2)}, u32[]{:S(2)}) collective-permute-start(f32[128,128]{1,0:T(8,128)S(1)} %get-tuple-element.142), channel_id=1, source_target_pairs={{0,28},{4,8},{8,4},{12,16},{16,12},{20,24},{24,20},{28,0},{1,29},{... | collective-permute-start | bytes 196616 | tf_op jit(solution)/shard_map/ppermute | solution.py:71
  41.9 1.9 %collective-permute-start.13 = (f32[128,128]{1,0:T(8,128)S(1)}, f32[128,128]{1,0:T(8,128)S(1)}, u32[]{:S(2)}, u32[]{:S(2)}) collective-permute-start(f32[128,128]{1,0:T(8,128)S(1)} %get-tuple-element.143), channel_id=1, source_target_pairs={{0,24},{4,28},{8,16},{12,20},{16,8},{20,12},{24,0},{28,4},{1,25},{... | collective-permute-start | bytes 196616 | tf_op jit(solution)/shard_map/ppermute | solution.py:71
  43.8 1.7 %collective-permute-start.14 = (f32[128,128]{1,0:T(8,128)S(1)}, f32[128,128]{1,0:T(8,128)S(1)}, u32[]{:S(2)}, u32[]{:S(2)}) collective-permute-start(f32[128,128]{1,0:T(8,128)S(1)} %get-tuple-element.144), channel_id=1, source_target_pairs={{0,4},{4,0},{8,12},{12,8},{16,20},{20,16},{24,28},{28,24},{1,5},{5... | collective-permute-start | bytes 196616 | tf_op jit(solution)/shard_map/ppermute | solution.py:71
  45.5 1.2 %shard_map.88 = (bf16[256,1024]{1,0:T(8,128)(2,1)}, bf16[1024,256]{1,0:T(8,128)(2,1)S(1)}, f32[128,128]{1,0:T(8,128)S(1)}, f32[128,128]{1,0:T(8,128)S(1)}, f32[128,128]{1,0:T(8,128)S(1)}) custom-call(bf16[128,1024]{1,0:T(8,128)(2,1)S(1)} %shard_map.77.refs_3_.refs_0_.refs_6_.refs_7_, bf16[128,1024]{1,0:T(8,128)(2,1)S(1)} %collective-permute-done.refs_5_.refs_1_, ...), custom_call_target="tpu_custom_call" | custom-call | bytes 1048576 | tf_op jit(solution)/shard_map/pallas_call | solution.py:50
  46.8 1.1 shard_map.86.refs_0_
  48.1 1.0 shard_map.89
  49.6 1.7 %collective-permute-start.18 = (f32[384,128]{1,0:T(8,128)S(1)}, f32[384,128]{1,0:T(8,128)S(1)}, u32[]{:S(2)}, u32[]{:S(2)}) collective-permute-start(f32[384,128]{1,0:T(8,128)S(1)} %get-tuple-element.155), channel_id=1, source_target_pairs={{0,4},{4,0},{8,12},{12,8},{16,20},{20,16},{24,28},{28,24},{1,5},{5... | collective-permute-start | bytes 589832 | tf_op jit(solution)/shard_map/ppermute | solution.py:71
  51.4 1.9 %collective-permute-start.16 = (f32[128,128]{1,0:T(8,128)S(1)}, f32[128,128]{1,0:T(8,128)S(1)}, u32[]{:S(2)}, u32[]{:S(2)}) collective-permute-start(f32[128,128]{1,0:T(8,128)S(1)} %get-tuple-element.153), channel_id=1, source_target_pairs={{0,28},{4,8},{8,4},{12,16},{16,12},{20,24},{24,20},{28,0},{1,29},{... | collective-permute-start | bytes 196616 | tf_op jit(solution)/shard_map/ppermute | solution.py:71
  53.3 1.7 %collective-permute-start.17 = (f32[128,128]{1,0:T(8,128)S(1)}, f32[128,128]{1,0:T(8,128)S(1)}, u32[]{:S(2)}, u32[]{:S(2)}) collective-permute-start(f32[128,128]{1,0:T(8,128)S(1)} %get-tuple-element.154), channel_id=1, source_target_pairs={{0,24},{4,28},{8,16},{12,20},{16,8},{20,12},{24,0},{28,4},{1,25},{... | collective-permute-start | bytes 196616 | tf_op jit(solution)/shard_map/ppermute | solution.py:71
  55.0 1.3 %shard_map.90 = (f32[128,1024]{1,0:T(8,128)S(1)}, f32[128,512]{1,0:T(8,128)S(1)}) custom-call(bf16[256,1024]{1,0:T(8,128)(2,1)S(1)} %get-tuple-element.149.refs_0_.refs_4_, bf16[64,256]{1,0:T(8,128)(2,1)S(1)} %get-tuple-element.221.refs_1_, bf16[256,1024]{1,0:T(8,128)(2,1)S(1)} %get-tuple-element.116.refs_2_, ...), custom_call_target="tpu_custom_call" | custom-call | flops 805306368 | bytes 1048576 | tf_op jit(solution)/shard_map/pallas_call | solution.py:50
  56.3 2.2 %shard_map.92 = (bf16[1024,256]{1,0:T(8,128)(2,1)S(1)}, bf16[1024,256]{1,0:T(8,128)(2,1)S(1)}, bf16[256,1024]{1,0:T(8,128)(2,1)}, f32[128,128]{1,0:T(8,128)S(1)}...) custom-call(bf16[128,1024]{1,0:T(8,128)(2,1)S(1)} %get-tuple-element, ...), custom_call_target="tpu_custom_call" | custom-call | bytes 1048576 | tf_op jit(solution)/shard_map/pallas_call | solution.py:50
  59.9 1.7 %collective-permute-start.25 = (f32[320,128]{1,0:T(8,128)S(1)}, f32[320,128]{1,0:T(8,128)S(1)}, u32[]{:S(2)}, u32[]{:S(2)}) collective-permute-start(f32[320,128]{1,0:T(8,128)S(1)} %get-tuple-element.176), channel_id=1, source_target_pairs={{0,4},{4,0},{8,12},{12,8},{16,20},{20,16},{24,28},{28,24},{1,5},{5... | collective-permute-start | bytes 491528 | tf_op jit(solution)/shard_map/ppermute | solution.py:71
  61.6 0.8 collective-permute-start.22
  62.4 0.9 collective-permute-start.24
  63.9 2.5 %collective-permute-start.23 = (f32[128,128]{1,0:T(8,128)S(1)}, f32[128,128]{1,0:T(8,128)S(1)}, u32[]{:S(2)}, u32[]{:S(2)}) collective-permute-start(f32[128,128]{1,0:T(8,128)S(1)} %get-tuple-element.174), channel_id=1, source_target_pairs={{0,28},{4,8},{8,4},{12,16},{16,12},{20,24},{24,20},{28,0},{1,29},{... | collective-permute-start | bytes 196616 | tf_op jit(solution)/shard_map/ppermute | solution.py:71
  66.4 1.6 %shard_map.93 = (f32[128,1024]{1,0:T(8,128)S(1)}, f32[128,512]{1,0:T(8,128)S(1)}, f32[128,128]{1,0:T(8,128)S(1)}) custom-call(bf16[256,1024]{1,0:T(8,128)(2,1)S(1)} %get-tuple-element.156.refs_0_, bf16[64,256]{1,0:T(8,128)(2,1)S(1)} %get-tuple-element.220.refs_1_, bf16[256,1024]{1,0:T(8,128)(2,1)S(1)} %get-tuple-element.116.refs_2_, ...), custom_call_target="tpu_custom_call" | custom-call | flops 805306368 | bytes 1048576 | tf_op jit(solution)/shard_map/pallas_call | solution.py:50
  68.0 3.0 %collective-permute-done.23.refs_4_ = f32[128,128]{1,0:T(8,128)S(1)} collective-permute-done((f32[128,128]{1,0:T(8,128)S(1)}, f32[128,128]{1,0:T(8,128)S(1)}, u32[]{:S(2)}, u32[]{:S(2)}) %collective-permute-start.23) | collective-permute-done | bytes 65568 | tf_op jit(solution)/shard_map/ppermute | solution.py:71
  71.5 2.3 %collective-permute-start.28 = (f32[352,128]{1,0:T(8,128)S(1)}, f32[352,128]{1,0:T(8,128)S(1)}, u32[]{:S(2)}, u32[]{:S(2)}) collective-permute-start(f32[352,128]{1,0:T(8,128)S(1)} %get-tuple-element.187), channel_id=1, source_target_pairs={{0,24},{4,28},{8,16},{12,20},{16,8},{20,12},{24,0},{28,4},{1,25},{... | collective-permute-start | bytes 540680 | tf_op jit(solution)/shard_map/ppermute | solution.py:71
  73.8 2.8 %collective-permute-start.27 = (f32[128,128]{1,0:T(8,128)S(1)}, f32[128,128]{1,0:T(8,128)S(1)}, u32[]{:S(2)}, u32[]{:S(2)}) collective-permute-start(f32[128,128]{1,0:T(8,128)S(1)} %get-tuple-element.186), channel_id=1, source_target_pairs={{0,28},{4,8},{8,4},{12,16},{16,12},{20,24},{24,20},{28,0},{1,29},{... | collective-permute-start | bytes 196616 | tf_op jit(solution)/shard_map/ppermute | solution.py:71
  77.2 1.6 %shard_map.96 = (f32[128,1024]{1,0:T(8,128)S(1)}, f32[128,512]{1,0:T(8,128)S(1)}, f32[128,128]{1,0:T(8,128)S(1)}) custom-call(bf16[256,1024]{1,0:T(8,128)(2,1)S(1)} %get-tuple-element.177.refs_0_, bf16[64,256]{1,0:T(8,128)(2,1)S(1)} %get-tuple-element.219.refs_1_, bf16[256,1024]{1,0:T(8,128)(2,1)S(1)} %get-tuple-element.116.refs_2_, ...), custom_call_target="tpu_custom_call" | custom-call | flops 805306368 | bytes 1048576 | tf_op jit(solution)/shard_map/pallas_call | solution.py:50
  78.8 3.3 %collective-permute-done.27.refs_4_ = f32[128,128]{1,0:T(8,128)S(1)} collective-permute-done((f32[128,128]{1,0:T(8,128)S(1)}, f32[128,128]{1,0:T(8,128)S(1)}, u32[]{:S(2)}, u32[]{:S(2)}) %collective-permute-start.27) | collective-permute-done | bytes 65568 | tf_op jit(solution)/shard_map/ppermute | solution.py:71
  82.8 3.0 %collective-permute-start.32 = (f32[352,128]{1,0:T(8,128)S(1)}, f32[352,128]{1,0:T(8,128)S(1)}, u32[]{:S(2)}, u32[]{:S(2)}) collective-permute-start(f32[352,128]{1,0:T(8,128)S(1)} %get-tuple-element.200), channel_id=1, source_target_pairs={{0,24},{4,28},{8,16},{12,20},{16,8},{20,12},{24,0},{28,4},{1,25},{... | collective-permute-start | bytes 540680 | tf_op jit(solution)/shard_map/ppermute | solution.py:71
  85.8 2.4 %collective-permute-start.31 = (f32[64,128]{1,0:T(8,128)S(1)}, f32[64,128]{1,0:T(8,128)S(1)}, u32[]{:S(2)}, u32[]{:S(2)}) collective-permute-start(f32[64,128]{1,0:T(8,128)S(1)} %get-tuple-element.199), channel_id=1, source_target_pairs={{0,28},{4,8},{8,4},{12,16},{16,12},{20,24},{24,20},{28,0},{1,29},{... | collective-permute-start | bytes 98312 | tf_op jit(solution)/shard_map/ppermute | solution.py:71
  88.8 1.0 shard_map.99
  89.9 3.4 %collective-permute-done.31.refs_4_ = f32[64,128]{1,0:T(8,128)S(1)} collective-permute-done((f32[64,128]{1,0:T(8,128)S(1)}, f32[64,128]{1,0:T(8,128)S(1)}, u32[]{:S(2)}, u32[]{:S(2)}) %collective-permute-start.31) | collective-permute-done | bytes 32800 | tf_op jit(solution)/shard_map/ppermute | solution.py:71
  93.8 1.7 %collective-permute-start.34 = (f32[256,128]{1,0:T(8,128)S(1)}, f32[256,128]{1,0:T(8,128)S(1)}, u32[]{:S(2)}, u32[]{:S(2)}) collective-permute-start(f32[256,128]{1,0:T(8,128)S(1)} %get-tuple-element.209), channel_id=1, source_target_pairs={{0,8},{4,12},{8,0},{12,4},{16,24},{20,28},{24,16},{28,20},{1,9},{5... | collective-permute-start | bytes 393224 | tf_op jit(solution)/shard_map/ppermute | solution.py:71
  95.5 1.6 %collective-permute-start.36 = (f32[256,128]{1,0:T(8,128)S(1)}, f32[256,128]{1,0:T(8,128)S(1)}, u32[]{:S(2)}, u32[]{:S(2)}) collective-permute-start(f32[256,128]{1,0:T(8,128)S(1)} %get-tuple-element.211), channel_id=1, source_target_pairs={{0,24},{4,28},{8,16},{12,20},{16,8},{20,12},{24,0},{28,4},{1,25},{... | collective-permute-start | bytes 393224 | tf_op jit(solution)/shard_map/ppermute | solution.py:71
  97.1 2.5 %collective-permute-start.35 = (f32[192,128]{1,0:T(8,128)S(1)}, f32[192,128]{1,0:T(8,128)S(1)}, u32[]{:S(2)}, u32[]{:S(2)}) collective-permute-start(f32[192,128]{1,0:T(8,128)S(1)} %get-tuple-element.210), channel_id=1, source_target_pairs={{0,28},{4,8},{8,4},{12,16},{16,12},{20,24},{24,20},{28,0},{1,29},{... | collective-permute-start | bytes 294920 | tf_op jit(solution)/shard_map/ppermute | solution.py:71
  99.5 1.2 %shard_map.101 = (f32[64,1024]{1,0:T(8,128)}, bf16[128,1024]{1,0:T(8,128)(2,1)S(1)}) custom-call(f32[64,1024]{1,0:T(8,128)S(1)} %get-tuple-element.191.refs_0_, bf16[1536,1024]{1,0:T(8,128)(2,1)S(1)} %get-tuple-element.117.refs_3_.refs_1_.refs_0_.refs_8_, bf16[1536,1024]{1,0:T(8,128)(2,1)S(1)} %get-tuple-element.118.refs_4_.refs_2_.refs_1_.refs_9_, ...), custom_call_target="tpu_custom_call" | custom-call | flops 402653184 | bytes 1048576 | tf_op jit(solution)/shard_map/pallas_call | solution.py:50
  100.7 0.9 shard_map.102.refs_0_
  101.6 2.8 %collective-permute-done.35.refs_4_ = f32[192,128]{1,0:T(8,128)S(1)} collective-permute-done((f32[192,128]{1,0:T(8,128)S(1)}, f32[192,128]{1,0:T(8,128)S(1)}, u32[]{:S(2)}, u32[]{:S(2)}) %collective-permute-start.35) | collective-permute-done | bytes 98336 | tf_op jit(solution)/shard_map/ppermute | solution.py:71
  104.4 1.4 %shard_map.104 = (f32[64,1024]{1,0:T(8,128)}, f32[9,64,256]{2,1,0:T(8,128)}) custom-call(f32[64,1024]{1,0:T(8,128)S(1)} %shard_map.102.refs_0_, bf16[1536,1024]{1,0:T(8,128)(2,1)S(1)} %get-tuple-element.117.refs_3_.refs_1_.refs_0_.refs_8_, bf16[1536,1024]{1,0:T(8,128)(2,1)S(1)} %get-tuple-element.118.refs_4_.refs_2_.refs_1_.refs_9_, ...), custom_call_target="tpu_custom_call" | custom-call | bytes 1048576 | tf_op jit(solution)/shard_map/pallas_call | solution.py:50
  (59 shorter events, 10.6 us)
Async XLA Ops:
  1.6 10.7 %copy-start = (bf16[9,64,256]{2,1,0:T(8,128)(2,1)S(1)}, bf16[9,64,256]{2,1,0:T(8,128)(2,1)}, u32[]{:S(2)}) copy-start(bf16[9,64,256]{2,1,0:T(8,128)(2,1)} %param.8) | copy-start | bytes 884740
  1.6 10.2 %collective-permute-start = (bf16[128,1024]{1,0:T(8,128)(2,1)S(1)}, bf16[128,1024]{1,0:T(8,128)(2,1)S(1)}, u32[]{:S(2)}, u32[]{:S(2)}) collective-permute-start(bf16[128,1024]{1,0:T(8,128)(2,1)S(1)} %shard_map.77.refs_3_.refs_0_.refs_6_.refs_7_), channel_id=1, source_target_pairs={{0,2},{1,3},{2,0},{3,1},{4,6},{5,7},{6,4},{7,5},{8,10},{9,11},{10,... | collective-permute-start | bytes 786440 | tf_op jit(solution)/shard_map/ppermute | solution.py:121
  11.8 1.6 %collective-permute-start.1 = (bf16[128,1024]{1,0:T(8,128)(2,1)S(1)}, bf16[128,1024]{1,0:T(8,128)(2,1)S(1)}, u32[]{:S(2)}, u32[]{:S(2)}) collective-permute-start(bf16[128,1024]{1,0:T(8,128)(2,1)S(1)} %shard_map.77.refs_3_.refs_0_.refs_6_.refs_7_), channel_id=1, source_target_pairs={{0,1},{1,0},{2,3},{3,2},{4,5},{5,4},{6,7},{7,6},{8,9},{9,8},{10,11... | collective-permute-start | bytes 786440 | tf_op jit(solution)/shard_map/ppermute | solution.py:121
  11.9 1.9 %collective-permute-start.2 = (bf16[128,1024]{1,0:T(8,128)(2,1)S(1)}, bf16[128,1024]{1,0:T(8,128)(2,1)S(1)}, u32[]{:S(2)}, u32[]{:S(2)}) collective-permute-start(bf16[128,1024]{1,0:T(8,128)(2,1)S(1)} %collective-permute-done.refs_5_.refs_1_), channel_id=1, source_target_pairs={{0,1},{1,0},{2,3},{3,2},{4,5},{5,4},{6,7},{7,6},{8,9},{9,8},{10,11... | collective-permute-start | bytes 786440 | tf_op jit(solution)/shard_map/ppermute | solution.py:121
  14.3 11.4 %collective-permute-start.3 = (f32[192,128]{1,0:T(8,128)S(1)}, f32[192,128]{1,0:T(8,128)S(1)}, u32[]{:S(2)}, u32[]{:S(2)}) collective-permute-start(f32[192,128]{1,0:T(8,128)S(1)} %get-tuple-element.120), channel_id=1, source_target_pairs={{0,8},{4,12},{8,0},{12,4},{16,24},{20,28},{24,16},{28,20},{1,9},{5... | collective-permute-start | bytes 294920 | tf_op jit(solution)/shard_map/ppermute | solution.py:71
  15.9 9.7 %collective-permute-start.4 = (f32[192,128]{1,0:T(8,128)S(1)}, f32[192,128]{1,0:T(8,128)S(1)}, u32[]{:S(2)}, u32[]{:S(2)}) collective-permute-start(f32[192,128]{1,0:T(8,128)S(1)} %get-tuple-element.121), channel_id=1, source_target_pairs={{0,28},{4,8},{8,4},{12,16},{16,12},{20,24},{24,20},{28,0},{1,29},{... | collective-permute-start | bytes 294920 | tf_op jit(solution)/shard_map/ppermute | solution.py:71
  19.3 6.4 %collective-permute-start.5 = (f32[192,128]{1,0:T(8,128)S(1)}, f32[192,128]{1,0:T(8,128)S(1)}, u32[]{:S(2)}, u32[]{:S(2)}) collective-permute-start(f32[192,128]{1,0:T(8,128)S(1)} %get-tuple-element.122), channel_id=1, source_target_pairs={{0,24},{4,28},{8,16},{12,20},{16,8},{20,12},{24,0},{28,4},{1,25},{... | collective-permute-start | bytes 294920 | tf_op jit(solution)/shard_map/ppermute | solution.py:71
  20.9 5.4 %collective-permute-start.6 = (f32[192,128]{1,0:T(8,128)S(1)}, f32[192,128]{1,0:T(8,128)S(1)}, u32[]{:S(2)}, u32[]{:S(2)}) collective-permute-start(f32[192,128]{1,0:T(8,128)S(1)} %get-tuple-element.123), channel_id=1, source_target_pairs={{0,4},{4,0},{8,12},{12,8},{16,20},{20,16},{24,28},{28,24},{1,5},{5... | collective-permute-start | bytes 294920 | tf_op jit(solution)/shard_map/ppermute | solution.py:71
  27.0 9.0 %collective-permute-start.7 = (f32[192,128]{1,0:T(8,128)S(1)}, f32[192,128]{1,0:T(8,128)S(1)}, u32[]{:S(2)}, u32[]{:S(2)}) collective-permute-start(f32[192,128]{1,0:T(8,128)S(1)} %get-tuple-element.133), channel_id=1, source_target_pairs={{0,8},{4,12},{8,0},{12,4},{16,24},{20,28},{24,16},{28,20},{1,9},{5... | collective-permute-start | bytes 294920 | tf_op jit(solution)/shard_map/ppermute | solution.py:71
  27.0 9.1 %collective-permute-start.8 = (f32[192,128]{1,0:T(8,128)S(1)}, f32[192,128]{1,0:T(8,128)S(1)}, u32[]{:S(2)}, u32[]{:S(2)}) collective-permute-start(f32[192,128]{1,0:T(8,128)S(1)} %get-tuple-element.134), channel_id=1, source_target_pairs={{0,28},{4,8},{8,4},{12,16},{16,12},{20,24},{24,20},{28,0},{1,29},{... | collective-permute-start | bytes 294920 | tf_op jit(solution)/shard_map/ppermute | solution.py:71
  30.4 6.5 %collective-permute-start.9 = (f32[192,128]{1,0:T(8,128)S(1)}, f32[192,128]{1,0:T(8,128)S(1)}, u32[]{:S(2)}, u32[]{:S(2)}) collective-permute-start(f32[192,128]{1,0:T(8,128)S(1)} %get-tuple-element.135), channel_id=1, source_target_pairs={{0,24},{4,28},{8,16},{12,20},{16,8},{20,12},{24,0},{28,4},{1,25},{... | collective-permute-start | bytes 294920 | tf_op jit(solution)/shard_map/ppermute | solution.py:71
  31.9 5.0 %collective-permute-start.10 = (f32[192,128]{1,0:T(8,128)S(1)}, f32[192,128]{1,0:T(8,128)S(1)}, u32[]{:S(2)}, u32[]{:S(2)}) collective-permute-start(f32[192,128]{1,0:T(8,128)S(1)} %get-tuple-element.136), channel_id=1, source_target_pairs={{0,4},{4,0},{8,12},{12,8},{16,20},{20,16},{24,28},{28,24},{1,5},{5... | collective-permute-start | bytes 294920 | tf_op jit(solution)/shard_map/ppermute | solution.py:71
  38.0 11.0 %collective-permute-start.19 = (bf16[128,1024]{1,0:T(8,128)(2,1)S(1)}, bf16[128,1024]{1,0:T(8,128)(2,1)S(1)}, u32[]{:S(2)}, u32[]{:S(2)}) collective-permute-start(bf16[128,1024]{1,0:T(8,128)(2,1)S(1)} %get-tuple-element.159.refs_0_), channel_id=1, source_target_pairs={{0,2},{1,3},{2,0},{3,1},{4,6},{5,7},{6,4},{7,5},{8,10},{9,11},{10,... | collective-permute-start | bytes 786440 | tf_op jit(solution)/shard_map/ppermute | solution.py:121
  39.3 8.6 %collective-permute-start.11 = (f32[128,128]{1,0:T(8,128)S(1)}, f32[128,128]{1,0:T(8,128)S(1)}, u32[]{:S(2)}, u32[]{:S(2)}) collective-permute-start(f32[128,128]{1,0:T(8,128)S(1)} %get-tuple-element.141), channel_id=1, source_target_pairs={{0,8},{4,12},{8,0},{12,4},{16,24},{20,28},{24,16},{28,20},{1,9},{5... | collective-permute-start | bytes 196616 | tf_op jit(solution)/shard_map/ppermute | solution.py:71
  40.2 7.6 %collective-permute-start.12 = (f32[128,128]{1,0:T(8,128)S(1)}, f32[128,128]{1,0:T(8,128)S(1)}, u32[]{:S(2)}, u32[]{:S(2)}) collective-permute-start(f32[128,128]{1,0:T(8,128)S(1)} %get-tuple-element.142), channel_id=1, source_target_pairs={{0,28},{4,8},{8,4},{12,16},{16,12},{20,24},{24,20},{28,0},{1,29},{... | collective-permute-start | bytes 196616 | tf_op jit(solution)/shard_map/ppermute | solution.py:71
  41.9 6.1 %collective-permute-start.13 = (f32[128,128]{1,0:T(8,128)S(1)}, f32[128,128]{1,0:T(8,128)S(1)}, u32[]{:S(2)}, u32[]{:S(2)}) collective-permute-start(f32[128,128]{1,0:T(8,128)S(1)} %get-tuple-element.143), channel_id=1, source_target_pairs={{0,24},{4,28},{8,16},{12,20},{16,8},{20,12},{24,0},{28,4},{1,25},{... | collective-permute-start | bytes 196616 | tf_op jit(solution)/shard_map/ppermute | solution.py:71
  43.8 4.3 %collective-permute-start.14 = (f32[128,128]{1,0:T(8,128)S(1)}, f32[128,128]{1,0:T(8,128)S(1)}, u32[]{:S(2)}, u32[]{:S(2)}) collective-permute-start(f32[128,128]{1,0:T(8,128)S(1)} %get-tuple-element.144), channel_id=1, source_target_pairs={{0,4},{4,0},{8,12},{12,8},{16,20},{20,16},{24,28},{28,24},{1,5},{5... | collective-permute-start | bytes 196616 | tf_op jit(solution)/shard_map/ppermute | solution.py:71
  49.0 4.3 %collective-permute-start.20 = (bf16[128,1024]{1,0:T(8,128)(2,1)S(1)}, bf16[128,1024]{1,0:T(8,128)(2,1)S(1)}, u32[]{:S(2)}, u32[]{:S(2)}) collective-permute-start(bf16[128,1024]{1,0:T(8,128)(2,1)S(1)} %get-tuple-element.159.refs_0_), channel_id=1, source_target_pairs={{0,1},{1,0},{2,3},{3,2},{4,5},{5,4},{6,7},{7,6},{8,9},{9,8},{10,11... | collective-permute-start | bytes 786440 | tf_op jit(solution)/shard_map/ppermute | solution.py:121
  49.1 7.2 %collective-permute-start.21 = (bf16[128,1024]{1,0:T(8,128)(2,1)S(1)}, bf16[128,1024]{1,0:T(8,128)(2,1)S(1)}, u32[]{:S(2)}, u32[]{:S(2)}) collective-permute-start(bf16[128,1024]{1,0:T(8,128)(2,1)S(1)} %collective-permute-done.19.refs_1_), channel_id=1, source_target_pairs={{0,1},{1,0},{2,3},{3,2},{4,5},{5,4},{6,7},{7,6},{8,9},{9,8},{10,11... | collective-permute-start | bytes 786440 | tf_op jit(solution)/shard_map/ppermute | solution.py:121
  49.6 9.7 %collective-permute-start.18 = (f32[384,128]{1,0:T(8,128)S(1)}, f32[384,128]{1,0:T(8,128)S(1)}, u32[]{:S(2)}, u32[]{:S(2)}) collective-permute-start(f32[384,128]{1,0:T(8,128)S(1)} %get-tuple-element.155), channel_id=1, source_target_pairs={{0,4},{4,0},{8,12},{12,8},{16,20},{20,16},{24,28},{28,24},{1,5},{5... | collective-permute-start | bytes 589832 | tf_op jit(solution)/shard_map/ppermute | solution.py:71
  51.3 8.0 %collective-permute-start.15 = (f32[128,128]{1,0:T(8,128)S(1)}, f32[128,128]{1,0:T(8,128)S(1)}, u32[]{:S(2)}, u32[]{:S(2)}) collective-permute-start(f32[128,128]{1,0:T(8,128)S(1)} %get-tuple-element.152), channel_id=1, source_target_pairs={{0,8},{4,12},{8,0},{12,4},{16,24},{20,28},{24,16},{28,20},{1,9},{5... | collective-permute-start | bytes 196616 | tf_op jit(solution)/shard_map/ppermute | solution.py:71
  51.4 7.4 %collective-permute-start.16 = (f32[128,128]{1,0:T(8,128)S(1)}, f32[128,128]{1,0:T(8,128)S(1)}, u32[]{:S(2)}, u32[]{:S(2)}) collective-permute-start(f32[128,128]{1,0:T(8,128)S(1)} %get-tuple-element.153), channel_id=1, source_target_pairs={{0,28},{4,8},{8,4},{12,16},{16,12},{20,24},{24,20},{28,0},{1,29},{... | collective-permute-start | bytes 196616 | tf_op jit(solution)/shard_map/ppermute | solution.py:71
  53.3 6.1 %collective-permute-start.17 = (f32[128,128]{1,0:T(8,128)S(1)}, f32[128,128]{1,0:T(8,128)S(1)}, u32[]{:S(2)}, u32[]{:S(2)}) collective-permute-start(f32[128,128]{1,0:T(8,128)S(1)} %get-tuple-element.154), channel_id=1, source_target_pairs={{0,24},{4,28},{8,16},{12,20},{16,8},{20,12},{24,0},{28,4},{1,25},{... | collective-permute-start | bytes 196616 | tf_op jit(solution)/shard_map/ppermute | solution.py:71
  59.9 11.1 %collective-permute-start.25 = (f32[320,128]{1,0:T(8,128)S(1)}, f32[320,128]{1,0:T(8,128)S(1)}, u32[]{:S(2)}, u32[]{:S(2)}) collective-permute-start(f32[320,128]{1,0:T(8,128)S(1)} %get-tuple-element.176), channel_id=1, source_target_pairs={{0,4},{4,0},{8,12},{12,8},{16,20},{20,16},{24,28},{28,24},{1,5},{5... | collective-permute-start | bytes 491528 | tf_op jit(solution)/shard_map/ppermute | solution.py:71
  61.6 9.4 %collective-permute-start.22 = (f32[256,128]{1,0:T(8,128)S(1)}, f32[256,128]{1,0:T(8,128)S(1)}, u32[]{:S(2)}, u32[]{:S(2)}) collective-permute-start(f32[256,128]{1,0:T(8,128)S(1)} %get-tuple-element.173), channel_id=1, source_target_pairs={{0,8},{4,12},{8,0},{12,4},{16,24},{20,28},{24,16},{28,20},{1,9},{5... | collective-permute-start | bytes 393224 | tf_op jit(solution)/shard_map/ppermute | solution.py:71
  62.4 8.6 %collective-permute-start.24 = (f32[256,128]{1,0:T(8,128)S(1)}, f32[256,128]{1,0:T(8,128)S(1)}, u32[]{:S(2)}, u32[]{:S(2)}) collective-permute-start(f32[256,128]{1,0:T(8,128)S(1)} %get-tuple-element.175), channel_id=1, source_target_pairs={{0,24},{4,28},{8,16},{12,20},{16,8},{20,12},{24,0},{28,4},{1,25},{... | collective-permute-start | bytes 393224 | tf_op jit(solution)/shard_map/ppermute | solution.py:71
  63.9 7.1 %collective-permute-start.23 = (f32[128,128]{1,0:T(8,128)S(1)}, f32[128,128]{1,0:T(8,128)S(1)}, u32[]{:S(2)}, u32[]{:S(2)}) collective-permute-start(f32[128,128]{1,0:T(8,128)S(1)} %get-tuple-element.174), channel_id=1, source_target_pairs={{0,28},{4,8},{8,4},{12,16},{16,12},{20,24},{24,20},{28,0},{1,29},{... | collective-permute-start | bytes 196616 | tf_op jit(solution)/shard_map/ppermute | solution.py:71
  71.4 10.8 %collective-permute-start.26 = (f32[352,128]{1,0:T(8,128)S(1)}, f32[352,128]{1,0:T(8,128)S(1)}, u32[]{:S(2)}, u32[]{:S(2)}) collective-permute-start(f32[352,128]{1,0:T(8,128)S(1)} %get-tuple-element.185), channel_id=1, source_target_pairs={{0,8},{4,12},{8,0},{12,4},{16,24},{20,28},{24,16},{28,20},{1,9},{5... | collective-permute-start | bytes 540680 | tf_op jit(solution)/shard_map/ppermute | solution.py:71
  71.5 10.7 %collective-permute-start.28 = (f32[352,128]{1,0:T(8,128)S(1)}, f32[352,128]{1,0:T(8,128)S(1)}, u32[]{:S(2)}, u32[]{:S(2)}) collective-permute-start(f32[352,128]{1,0:T(8,128)S(1)} %get-tuple-element.187), channel_id=1, source_target_pairs={{0,24},{4,28},{8,16},{12,20},{16,8},{20,12},{24,0},{28,4},{1,25},{... | collective-permute-start | bytes 540680 | tf_op jit(solution)/shard_map/ppermute | solution.py:71
  73.8 8.3 %collective-permute-start.27 = (f32[128,128]{1,0:T(8,128)S(1)}, f32[128,128]{1,0:T(8,128)S(1)}, u32[]{:S(2)}, u32[]{:S(2)}) collective-permute-start(f32[128,128]{1,0:T(8,128)S(1)} %get-tuple-element.186), channel_id=1, source_target_pairs={{0,28},{4,8},{8,4},{12,16},{16,12},{20,24},{24,20},{28,0},{1,29},{... | collective-permute-start | bytes 196616 | tf_op jit(solution)/shard_map/ppermute | solution.py:71
  76.6 5.7 %collective-permute-start.29 = (f32[256,128]{1,0:T(8,128)S(1)}, f32[256,128]{1,0:T(8,128)S(1)}, u32[]{:S(2)}, u32[]{:S(2)}) collective-permute-start(f32[256,128]{1,0:T(8,128)S(1)} %get-tuple-element.188), channel_id=1, source_target_pairs={{0,4},{4,0},{8,12},{12,8},{16,20},{20,16},{24,28},{28,24},{1,5},{5... | collective-permute-start | bytes 393224 | tf_op jit(solution)/shard_map/ppermute | solution.py:71
  82.7 10.6 %collective-permute-start.30 = (f32[352,128]{1,0:T(8,128)S(1)}, f32[352,128]{1,0:T(8,128)S(1)}, u32[]{:S(2)}, u32[]{:S(2)}) collective-permute-start(f32[352,128]{1,0:T(8,128)S(1)} %get-tuple-element.198), channel_id=1, source_target_pairs={{0,8},{4,12},{8,0},{12,4},{16,24},{20,28},{24,16},{28,20},{1,9},{5... | collective-permute-start | bytes 540680 | tf_op jit(solution)/shard_map/ppermute | solution.py:71
  82.8 10.5 %collective-permute-start.32 = (f32[352,128]{1,0:T(8,128)S(1)}, f32[352,128]{1,0:T(8,128)S(1)}, u32[]{:S(2)}, u32[]{:S(2)}) collective-permute-start(f32[352,128]{1,0:T(8,128)S(1)} %get-tuple-element.200), channel_id=1, source_target_pairs={{0,24},{4,28},{8,16},{12,20},{16,8},{20,12},{24,0},{28,4},{1,25},{... | collective-permute-start | bytes 540680 | tf_op jit(solution)/shard_map/ppermute | solution.py:71
  85.8 7.4 %collective-permute-start.31 = (f32[64,128]{1,0:T(8,128)S(1)}, f32[64,128]{1,0:T(8,128)S(1)}, u32[]{:S(2)}, u32[]{:S(2)}) collective-permute-start(f32[64,128]{1,0:T(8,128)S(1)} %get-tuple-element.199), channel_id=1, source_target_pairs={{0,28},{4,8},{8,4},{12,16},{16,12},{20,24},{24,20},{28,0},{1,29},{... | collective-permute-start | bytes 98312 | tf_op jit(solution)/shard_map/ppermute | solution.py:71
  88.2 5.0 %collective-permute-start.33 = (f32[192,128]{1,0:T(8,128)S(1)}, f32[192,128]{1,0:T(8,128)S(1)}, u32[]{:S(2)}, u32[]{:S(2)}) collective-permute-start(f32[192,128]{1,0:T(8,128)S(1)} %get-tuple-element.201), channel_id=1, source_target_pairs={{0,4},{4,0},{8,12},{12,8},{16,20},{20,16},{24,28},{28,24},{1,5},{5... | collective-permute-start | bytes 294920 | tf_op jit(solution)/shard_map/ppermute | solution.py:71
  93.5 10.9 %collective-permute-start.37 = (f32[512,128]{1,0:T(8,128)S(1)}, f32[512,128]{1,0:T(8,128)S(1)}, u32[]{:S(2)}, u32[]{:S(2)}) collective-permute-start(f32[512,128]{1,0:T(8,128)S(1)} %get-tuple-element.212), channel_id=1, source_target_pairs={{0,4},{4,0},{8,12},{12,8},{16,20},{20,16},{24,28},{28,24},{1,5},{5... | collective-permute-start | bytes 786440 | tf_op jit(solution)/shard_map/ppermute | solution.py:71
  93.8 10.6 %collective-permute-start.34 = (f32[256,128]{1,0:T(8,128)S(1)}, f32[256,128]{1,0:T(8,128)S(1)}, u32[]{:S(2)}, u32[]{:S(2)}) collective-permute-start(f32[256,128]{1,0:T(8,128)S(1)} %get-tuple-element.209), channel_id=1, source_target_pairs={{0,8},{4,12},{8,0},{12,4},{16,24},{20,28},{24,16},{28,20},{1,9},{5... | collective-permute-start | bytes 393224 | tf_op jit(solution)/shard_map/ppermute | solution.py:71
  95.5 9.0 %collective-permute-start.36 = (f32[256,128]{1,0:T(8,128)S(1)}, f32[256,128]{1,0:T(8,128)S(1)}, u32[]{:S(2)}, u32[]{:S(2)}) collective-permute-start(f32[256,128]{1,0:T(8,128)S(1)} %get-tuple-element.211), channel_id=1, source_target_pairs={{0,24},{4,28},{8,16},{12,20},{16,8},{20,12},{24,0},{28,4},{1,25},{... | collective-permute-start | bytes 393224 | tf_op jit(solution)/shard_map/ppermute | solution.py:71
  97.1 7.4 %collective-permute-start.35 = (f32[192,128]{1,0:T(8,128)S(1)}, f32[192,128]{1,0:T(8,128)S(1)}, u32[]{:S(2)}, u32[]{:S(2)}) collective-permute-start(f32[192,128]{1,0:T(8,128)S(1)} %get-tuple-element.210), channel_id=1, source_target_pairs={{0,28},{4,8},{8,4},{12,16},{16,12},{20,24},{24,20},{28,0},{1,29},{... | collective-permute-start | bytes 294920 | tf_op jit(solution)/shard_map/ppermute | solution.py:71

commit v6 on v5

--- a/solution.py
+++ b/solution.py
@@ -531,6 +531,14 @@
         rows = chains * channels
         return dict(state=((rows, nodes), F32, True), both=((2 * rows, nodes), BF16, True))
 
+    def pass_through(i, o):
+        for matrix, out in ((i.high, o.through_high), (i.low, o.through_low)):
+            out[...] = dot(matrix[nodes:, :], i.pick[...]).astype(BF16)
+
+    through = ((SLOTS * tile, SLOTS * tile), BF16, True)
+    through = call(pass_through, dict(**matrix, **pick), dict(through_high=through, through_low=through))
+
+    sent_first = lax.optimization_barrier((ready["sent"], through["through_high"]))[0]
     named = {f"block{k}": (block, "") for k, block in enumerate(blocks[1:])}
     got = call(
         begin,
@@ -538,20 +546,13 @@
             stacked=stacked,
             weight=(weights[top], ""),
             **pick,
-            sent=ready["sent"],
+            sent=sent_first,
             back=ready["back"],
             **named,
         ),
         dict(gathered=whole, **state_outs(2), **messages(3 * channels, 1)),
     )
     gathered = got["gathered"]
-
-    def pass_through(i, o):
-        for matrix, out in ((i.high, o.through_high), (i.low, o.through_low)):
-            out[...] = dot(matrix[nodes:, :], i.pick[...]).astype(BF16)
-
-    through = ((SLOTS * tile, SLOTS * tile), BF16, True)
-    through = call(pass_through, dict(**matrix, **pick), dict(through_high=through, through_low=through))
 
     def opening(i, o):
         rows = [ref[channels:, :] for name, ref in vars(i).items() if name.startswith("block")]

time: 106 us -> 106 us (level)
    ppermute x6, waiting for transfers between devices: 1.38 us -> 0.11 us  [hop(): lax.ppermute(block, 'chan', [(c, c ^ bit) for c in range(lax.axis_size('c...]
    ppermute x32, waiting for transfers between devices: 15.2 us -> 16.4 us  [exchange(): lax.ppermute(block, 'dom', pairs[kind])]
where the time goes in v6:
time: 106 us
  starting transfers between devices  51.6 us (49%)
  Pallas kernels  36.7 us (35%)
  waiting for transfers between devices  16.5 us (16%)
    ppermute x32, starting transfers between devices, exchange(): lax.ppermute(block, 'dom', pairs[kind])  46.6 us
    pallas_call x28, Pallas kernels, call(): pl.pallas_call(kernel, out_shape=shapes, in_specs=specs, out_specs=[pl.Bl...  36.7 us
    ppermute x32, waiting for transfers between devices, exchange(): lax.ppermute(block, 'dom', pairs[kind])  16.4 us
    ppermute x6, starting transfers between devices, hop(): lax.ppermute(block, 'chan', [(c, c ^ bit) for c in range(lax.axis_size('c...  5.03 us
  transfers between devices with their start and end apart: 38, of which 15 were waited for; matrix products, arithmetic and copies ran while one was open for 0% of the time, Pallas kernels for 29%

profile of v6, /device:TPU:0, one launch (start us, length us, event | category | flops | bytes accessed | tf_op | source)
XLA Modules:
  0.0 105.8 jit_solution(2711535847909301275)
XLA Ops:
  0.6 1.0 shard_map.77.refs_3_.refs_0_.refs_6_.refs_7_
  1.6 3.0 %collective-permute-start = (bf16[128,1024]{1,0:T(8,128)(2,1)S(1)}, bf16[128,1024]{1,0:T(8,128)(2,1)S(1)}, u32[]{:S(2)}, u32[]{:S(2)}) collective-permute-start(bf16[128,1024]{1,0:T(8,128)(2,1)S(1)} %shard_map.77.refs_3_.refs_0_.refs_6_.refs_7_), channel_id=1, source_target_pairs={{0,2},{1,3},{2,0},{3,1},{4,6},{5,7},{6,4},{7,5},{8,10},{9,11},{10,... | collective-permute-start | bytes 786440 | tf_op jit(solution)/shard_map/ppermute | solution.py:121
  4.6 7.1 %shard_map.78 = (bf16[1536,1024]{1,0:T(8,128)(2,1)S(1)}, bf16[1536,1024]{1,0:T(8,128)(2,1)S(1)}, bf16[1024,512]{1,0:T(8,128)(2,1)S(1)}, f32[64,512]{1,0:T(8,128)S(1)}, f32[64,512]{1,0:T(8,128)S(1)}) custom-call(s32[1,8,8]{2,1,0:T(8,128)} %refs_0_.3, s32[1,4,128]{2,1,0:T(4,128)} %refs_1_.3, f32[64,128,128]{2,1,0:T(8,128)} %refs_2_.1, ...), custom_call_target="tpu_custom_call" | custom-call | flops 10000000000 | bytes 1048576 | tf_op jit(solution)/shard_map/pallas_call | solution.py:50
  12.4 1.2 %shard_map.79 = (bf16[512,512]{1,0:T(8,128)(2,1)S(1)}, bf16[512,512]{1,0:T(8,128)(2,1)S(1)}) custom-call(bf16[1536,1024]{1,0:T(8,128)(2,1)S(1)} %get-tuple-element.113.refs_0_.refs_3_.refs_1_.refs_8_, bf16[1536,1024]{1,0:T(8,128)(2,1)S(1)} %get-tuple-element.114.refs_1_.refs_4_.refs_2_.refs_9_, ...), custom_call_target="tpu_custom_call" | custom-call | bytes 1048576 | tf_op jit(solution)/shard_map/pallas_call | solution.py:50
  14.3 1.6 %collective-permute-start.3 = (f32[192,128]{1,0:T(8,128)S(1)}, f32[192,128]{1,0:T(8,128)S(1)}, u32[]{:S(2)}, u32[]{:S(2)}) collective-permute-start(f32[192,128]{1,0:T(8,128)S(1)} %get-tuple-element.123), channel_id=1, source_target_pairs={{0,8},{4,12},{8,0},{12,4},{16,24},{20,28},{24,16},{28,20},{1,9},{5... | collective-permute-start | bytes 294920 | tf_op jit(solution)/shard_map/ppermute | solution.py:71
  15.9 3.4 %collective-permute-start.4 = (f32[192,128]{1,0:T(8,128)S(1)}, f32[192,128]{1,0:T(8,128)S(1)}, u32[]{:S(2)}, u32[]{:S(2)}) collective-permute-start(f32[192,128]{1,0:T(8,128)S(1)} %get-tuple-element.124), channel_id=1, source_target_pairs={{0,28},{4,8},{8,4},{12,16},{16,12},{20,24},{24,20},{28,0},{1,29},{... | collective-permute-start | bytes 294920 | tf_op jit(solution)/shard_map/ppermute | solution.py:71
  19.3 1.6 %collective-permute-start.5 = (f32[192,128]{1,0:T(8,128)S(1)}, f32[192,128]{1,0:T(8,128)S(1)}, u32[]{:S(2)}, u32[]{:S(2)}) collective-permute-start(f32[192,128]{1,0:T(8,128)S(1)} %get-tuple-element.125), channel_id=1, source_target_pairs={{0,24},{4,28},{8,16},{12,20},{16,8},{20,12},{24,0},{28,4},{1,25},{... | collective-permute-start | bytes 294920 | tf_op jit(solution)/shard_map/ppermute | solution.py:71
  21.2 3.2 %shard_map.81 = (f32[128,1024]{1,0:T(8,128)S(1)}, f32[128,512]{1,0:T(8,128)S(1)}, f32[64,512]{1,0:T(8,128)S(1)}, f32[64,1024]{1,0:T(8,128)S(1)}) custom-call(bf16[256,1024]{1,0:T(8,128)(2,1)S(1)} %get-tuple-element.120.refs_0_, bf16[64,256]{1,0:T(8,128)(2,1)S(1)} %get-tuple-element.226.refs_1_, bf16[256,1024]{1,0:T(8,128)(2,1)S(1)} %get-tuple-element.121.refs_2_, ...), custom_call_target="tpu_custom_call" | custom-call | flops 805306368 | bytes 1048576 | tf_op jit(solution)/shard_map/pallas_call | solution.py:50
  24.4 0.8 collective-permute-done.4.refs_4_
  27.0 3.3 %collective-permute-start.8 = (f32[192,128]{1,0:T(8,128)S(1)}, f32[192,128]{1,0:T(8,128)S(1)}, u32[]{:S(2)}, u32[]{:S(2)}) collective-permute-start(f32[192,128]{1,0:T(8,128)S(1)} %get-tuple-element.136), channel_id=1, source_target_pairs={{0,28},{4,8},{8,4},{12,16},{16,12},{20,24},{24,20},{28,0},{1,29},{... | collective-permute-start | bytes 294920 | tf_op jit(solution)/shard_map/ppermute | solution.py:71
  30.4 1.2 %collective-permute-start.9 = (f32[192,128]{1,0:T(8,128)S(1)}, f32[192,128]{1,0:T(8,128)S(1)}, u32[]{:S(2)}, u32[]{:S(2)}) collective-permute-start(f32[192,128]{1,0:T(8,128)S(1)} %get-tuple-element.137), channel_id=1, source_target_pairs={{0,24},{4,28},{8,16},{12,20},{16,8},{20,12},{24,0},{28,4},{1,25},{... | collective-permute-start | bytes 294920 | tf_op jit(solution)/shard_map/ppermute | solution.py:71
  31.6 0.8 collective-permute-start.10
  32.4 0.9 shard_map.82
  33.3 2.7 %shard_map.83 = (f32[128,1024]{1,0:T(8,128)S(1)}, f32[128,512]{1,0:T(8,128)S(1)}, f32[64,1024]{1,0:T(8,128)S(1)}) custom-call(bf16[256,1024]{1,0:T(8,128)(2,1)S(1)} %get-tuple-element.128.refs_0_.refs_4_, bf16[64,256]{1,0:T(8,128)(2,1)S(1)} %get-tuple-element.225.refs_1_, bf16[256,1024]{1,0:T(8,128)(2,1)S(1)} %get-tuple-element.121.refs_2_, ...), custom_call_target="tpu_custom_call" | custom-call | flops 805306368 | bytes 1048576 | tf_op jit(solution)/shard_map/pallas_call | solution.py:50
  36.8 1.1 %shard_map.85 = (f32[128,1024]{1,0:T(8,128)S(1)}, bf16[256,1024]{1,0:T(8,128)(2,1)S(1)}, bf16[128,1024]{1,0:T(8,128)(2,1)S(1)}) custom-call(f32[128,1024]{1,0:T(8,128)S(1)} %get-tuple-element.131.refs_0_, bf16[1536,1024]{1,0:T(8,128)(2,1)S(1)} %get-tuple-element.113.refs_0_.refs_3_.refs_1_.refs_8_, ...), custom_call_target="tpu_custom_call" | custom-call | flops 805306368 | bytes 1048576 | tf_op jit(solution)/shard_map/pallas_call | solution.py:50
  38.0 0.9 collective-permute-start.19
  39.2 1.0 collective-permute-start.11
  40.2 1.6 %collective-permute-start.12 = (f32[128,128]{1,0:T(8,128)S(1)}, f32[128,128]{1,0:T(8,128)S(1)}, u32[]{:S(2)}, u32[]{:S(2)}) collective-permute-start(f32[128,128]{1,0:T(8,128)S(1)} %get-tuple-element.144), channel_id=1, source_target_pairs={{0,28},{4,8},{8,4},{12,16},{16,12},{20,24},{24,20},{28,0},{1,29},{... | collective-permute-start | bytes 196616 | tf_op jit(solution)/shard_map/ppermute | solution.py:71
  41.8 1.9 %collective-permute-start.13 = (f32[128,128]{1,0:T(8,128)S(1)}, f32[128,128]{1,0:T(8,128)S(1)}, u32[]{:S(2)}, u32[]{:S(2)}) collective-permute-start(f32[128,128]{1,0:T(8,128)S(1)} %get-tuple-element.145), channel_id=1, source_target_pairs={{0,24},{4,28},{8,16},{12,20},{16,8},{20,12},{24,0},{28,4},{1,25},{... | collective-permute-start | bytes 196616 | tf_op jit(solution)/shard_map/ppermute | solution.py:71
  43.8 1.7 %collective-permute-start.14 = (f32[128,128]{1,0:T(8,128)S(1)}, f32[128,128]{1,0:T(8,128)S(1)}, u32[]{:S(2)}, u32[]{:S(2)}) collective-permute-start(f32[128,128]{1,0:T(8,128)S(1)} %get-tuple-element.146), channel_id=1, source_target_pairs={{0,4},{4,0},{8,12},{12,8},{16,20},{20,16},{24,28},{28,24},{1,5},{5... | collective-permute-start | bytes 196616 | tf_op jit(solution)/shard_map/ppermute | solution.py:71
  45.5 1.2 %shard_map.88 = (bf16[256,1024]{1,0:T(8,128)(2,1)}, bf16[1024,256]{1,0:T(8,128)(2,1)S(1)}, f32[128,128]{1,0:T(8,128)S(1)}, f32[128,128]{1,0:T(8,128)S(1)}, f32[128,128]{1,0:T(8,128)S(1)}) custom-call(bf16[128,1024]{1,0:T(8,128)(2,1)S(1)} %shard_map.77.refs_3_.refs_0_.refs_6_.refs_7_, bf16[128,1024]{1,0:T(8,128)(2,1)S(1)} %collective-permute-done.refs_5_.refs_1_, ...), custom_call_target="tpu_custom_call" | custom-call | bytes 1048576 | tf_op jit(solution)/shard_map/pallas_call | solution.py:50
  46.8 1.1 shard_map.86.refs_0_
  48.0 1.0 shard_map.89
  49.6 1.7 %collective-permute-start.18 = (f32[384,128]{1,0:T(8,128)S(1)}, f32[384,128]{1,0:T(8,128)S(1)}, u32[]{:S(2)}, u32[]{:S(2)}) collective-permute-start(f32[384,128]{1,0:T(8,128)S(1)} %get-tuple-element.157), channel_id=1, source_target_pairs={{0,4},{4,0},{8,12},{12,8},{16,20},{20,16},{24,28},{28,24},{1,5},{5... | collective-permute-start | bytes 589832 | tf_op jit(solution)/shard_map/ppermute | solution.py:71
  51.3 1.9 %collective-permute-start.16 = (f32[128,128]{1,0:T(8,128)S(1)}, f32[128,128]{1,0:T(8,128)S(1)}, u32[]{:S(2)}, u32[]{:S(2)}) collective-permute-start(f32[128,128]{1,0:T(8,128)S(1)} %get-tuple-element.155), channel_id=1, source_target_pairs={{0,28},{4,8},{8,4},{12,16},{16,12},{20,24},{24,20},{28,0},{1,29},{... | collective-permute-start | bytes 196616 | tf_op jit(solution)/shard_map/ppermute | solution.py:71
  53.3 1.7 %collective-permute-start.17 = (f32[128,128]{1,0:T(8,128)S(1)}, f32[128,128]{1,0:T(8,128)S(1)}, u32[]{:S(2)}, u32[]{:S(2)}) collective-permute-start(f32[128,128]{1,0:T(8,128)S(1)} %get-tuple-element.156), channel_id=1, source_target_pairs={{0,24},{4,28},{8,16},{12,20},{16,8},{20,12},{24,0},{28,4},{1,25},{... | collective-permute-start | bytes 196616 | tf_op jit(solution)/shard_map/ppermute | solution.py:71
  55.0 1.3 %shard_map.90 = (f32[128,1024]{1,0:T(8,128)S(1)}, f32[128,512]{1,0:T(8,128)S(1)}) custom-call(bf16[256,1024]{1,0:T(8,128)(2,1)S(1)} %get-tuple-element.151.refs_0_.refs_4_, bf16[64,256]{1,0:T(8,128)(2,1)S(1)} %get-tuple-element.223.refs_1_, bf16[256,1024]{1,0:T(8,128)(2,1)S(1)} %get-tuple-element.121.refs_2_, ...), custom_call_target="tpu_custom_call" | custom-call | flops 805306368 | bytes 1048576 | tf_op jit(solution)/shard_map/pallas_call | solution.py:50
  56.3 2.2 %shard_map.92 = (bf16[1024,256]{1,0:T(8,128)(2,1)S(1)}, bf16[1024,256]{1,0:T(8,128)(2,1)S(1)}, bf16[256,1024]{1,0:T(8,128)(2,1)}, f32[128,128]{1,0:T(8,128)S(1)}...) custom-call(bf16[128,1024]{1,0:T(8,128)(2,1)S(1)} %get-tuple-element, ...), custom_call_target="tpu_custom_call" | custom-call | bytes 1048576 | tf_op jit(solution)/shard_map/pallas_call | solution.py:50
  59.9 1.7 %collective-permute-start.25 = (f32[320,128]{1,0:T(8,128)S(1)}, f32[320,128]{1,0:T(8,128)S(1)}, u32[]{:S(2)}, u32[]{:S(2)}) collective-permute-start(f32[320,128]{1,0:T(8,128)S(1)} %get-tuple-element.178), channel_id=1, source_target_pairs={{0,4},{4,0},{8,12},{12,8},{16,20},{20,16},{24,28},{28,24},{1,5},{5... | collective-permute-start | bytes 491528 | tf_op jit(solution)/shard_map/ppermute | solution.py:71
  62.4 0.9 collective-permute-start.24
  63.9 2.5 %collective-permute-start.23 = (f32[128,128]{1,0:T(8,128)S(1)}, f32[128,128]{1,0:T(8,128)S(1)}, u32[]{:S(2)}, u32[]{:S(2)}) collective-permute-start(f32[128,128]{1,0:T(8,128)S(1)} %get-tuple-element.176), channel_id=1, source_target_pairs={{0,28},{4,8},{8,4},{12,16},{16,12},{20,24},{24,20},{28,0},{1,29},{... | collective-permute-start | bytes 196616 | tf_op jit(solution)/shard_map/ppermute | solution.py:71
  66.4 1.6 %shard_map.93 = (f32[128,1024]{1,0:T(8,128)S(1)}, f32[128,512]{1,0:T(8,128)S(1)}, f32[128,128]{1,0:T(8,128)S(1)}) custom-call(bf16[256,1024]{1,0:T(8,128)(2,1)S(1)} %get-tuple-element.158.refs_0_, bf16[64,256]{1,0:T(8,128)(2,1)S(1)} %get-tuple-element.222.refs_1_, bf16[256,1024]{1,0:T(8,128)(2,1)S(1)} %get-tuple-element.121.refs_2_, ...), custom_call_target="tpu_custom_call" | custom-call | flops 805306368 | bytes 1048576 | tf_op jit(solution)/shard_map/pallas_call | solution.py:50
  68.0 2.9 %collective-permute-done.23.refs_4_ = f32[128,128]{1,0:T(8,128)S(1)} collective-permute-done((f32[128,128]{1,0:T(8,128)S(1)}, f32[128,128]{1,0:T(8,128)S(1)}, u32[]{:S(2)}, u32[]{:S(2)}) %collective-permute-start.23) | collective-permute-done | bytes 65568 | tf_op jit(solution)/shard_map/ppermute | solution.py:71
  71.5 2.3 %collective-permute-start.28 = (f32[352,128]{1,0:T(8,128)S(1)}, f32[352,128]{1,0:T(8,128)S(1)}, u32[]{:S(2)}, u32[]{:S(2)}) collective-permute-start(f32[352,128]{1,0:T(8,128)S(1)} %get-tuple-element.189), channel_id=1, source_target_pairs={{0,24},{4,28},{8,16},{12,20},{16,8},{20,12},{24,0},{28,4},{1,25},{... | collective-permute-start | bytes 540680 | tf_op jit(solution)/shard_map/ppermute | solution.py:71
  73.8 2.8 %collective-permute-start.27 = (f32[128,128]{1,0:T(8,128)S(1)}, f32[128,128]{1,0:T(8,128)S(1)}, u32[]{:S(2)}, u32[]{:S(2)}) collective-permute-start(f32[128,128]{1,0:T(8,128)S(1)} %get-tuple-element.188), channel_id=1, source_target_pairs={{0,28},{4,8},{8,4},{12,16},{16,12},{20,24},{24,20},{28,0},{1,29},{... | collective-permute-start | bytes 196616 | tf_op jit(solution)/shard_map/ppermute | solution.py:71
  77.2 1.6 %shard_map.96 = (f32[128,1024]{1,0:T(8,128)S(1)}, f32[128,512]{1,0:T(8,128)S(1)}, f32[128,128]{1,0:T(8,128)S(1)}) custom-call(bf16[256,1024]{1,0:T(8,128)(2,1)S(1)} %get-tuple-element.179.refs_0_, bf16[64,256]{1,0:T(8,128)(2,1)S(1)} %get-tuple-element.221.refs_1_, bf16[256,1024]{1,0:T(8,128)(2,1)S(1)} %get-tuple-element.121.refs_2_, ...), custom_call_target="tpu_custom_call" | custom-call | flops 805306368 | bytes 1048576 | tf_op jit(solution)/shard_map/pallas_call | solution.py:50
  78.8 3.3 %collective-permute-done.27.refs_4_ = f32[128,128]{1,0:T(8,128)S(1)} collective-permute-done((f32[128,128]{1,0:T(8,128)S(1)}, f32[128,128]{1,0:T(8,128)S(1)}, u32[]{:S(2)}, u32[]{:S(2)}) %collective-permute-start.27) | collective-permute-done | bytes 65568 | tf_op jit(solution)/shard_map/ppermute | solution.py:71
  82.8 3.1 %collective-permute-start.32 = (f32[352,128]{1,0:T(8,128)S(1)}, f32[352,128]{1,0:T(8,128)S(1)}, u32[]{:S(2)}, u32[]{:S(2)}) collective-permute-start(f32[352,128]{1,0:T(8,128)S(1)} %get-tuple-element.202), channel_id=1, source_target_pairs={{0,24},{4,28},{8,16},{12,20},{16,8},{20,12},{24,0},{28,4},{1,25},{... | collective-permute-start | bytes 540680 | tf_op jit(solution)/shard_map/ppermute | solution.py:71
  85.8 2.4 %collective-permute-start.31 = (f32[64,128]{1,0:T(8,128)S(1)}, f32[64,128]{1,0:T(8,128)S(1)}, u32[]{:S(2)}, u32[]{:S(2)}) collective-permute-start(f32[64,128]{1,0:T(8,128)S(1)} %get-tuple-element.201), channel_id=1, source_target_pairs={{0,28},{4,8},{8,4},{12,16},{16,12},{20,24},{24,20},{28,0},{1,29},{... | collective-permute-start | bytes 98312 | tf_op jit(solution)/shard_map/ppermute | solution.py:71
  88.8 1.0 shard_map.99
  89.9 3.4 %collective-permute-done.31.refs_4_ = f32[64,128]{1,0:T(8,128)S(1)} collective-permute-done((f32[64,128]{1,0:T(8,128)S(1)}, f32[64,128]{1,0:T(8,128)S(1)}, u32[]{:S(2)}, u32[]{:S(2)}) %collective-permute-start.31) | collective-permute-done | bytes 32800 | tf_op jit(solution)/shard_map/ppermute | solution.py:71
  93.8 1.7 %collective-permute-start.34 = (f32[256,128]{1,0:T(8,128)S(1)}, f32[256,128]{1,0:T(8,128)S(1)}, u32[]{:S(2)}, u32[]{:S(2)}) collective-permute-start(f32[256,128]{1,0:T(8,128)S(1)} %get-tuple-element.211), channel_id=1, source_target_pairs={{0,8},{4,12},{8,0},{12,4},{16,24},{20,28},{24,16},{28,20},{1,9},{5... | collective-permute-start | bytes 393224 | tf_op jit(solution)/shard_map/ppermute | solution.py:71
  95.5 1.6 %collective-permute-start.36 = (f32[256,128]{1,0:T(8,128)S(1)}, f32[256,128]{1,0:T(8,128)S(1)}, u32[]{:S(2)}, u32[]{:S(2)}) collective-permute-start(f32[256,128]{1,0:T(8,128)S(1)} %get-tuple-element.213), channel_id=1, source_target_pairs={{0,24},{4,28},{8,16},{12,20},{16,8},{20,12},{24,0},{28,4},{1,25},{... | collective-permute-start | bytes 393224 | tf_op jit(solution)/shard_map/ppermute | solution.py:71
  97.0 2.5 %collective-permute-start.35 = (f32[192,128]{1,0:T(8,128)S(1)}, f32[192,128]{1,0:T(8,128)S(1)}, u32[]{:S(2)}, u32[]{:S(2)}) collective-permute-start(f32[192,128]{1,0:T(8,128)S(1)} %get-tuple-element.212), channel_id=1, source_target_pairs={{0,28},{4,8},{8,4},{12,16},{16,12},{20,24},{24,20},{28,0},{1,29},{... | collective-permute-start | bytes 294920 | tf_op jit(solution)/shard_map/ppermute | solution.py:71
  99.5 1.2 %shard_map.101 = (f32[64,1024]{1,0:T(8,128)}, bf16[128,1024]{1,0:T(8,128)(2,1)S(1)}) custom-call(f32[64,1024]{1,0:T(8,128)S(1)} %get-tuple-element.193.refs_0_, bf16[1536,1024]{1,0:T(8,128)(2,1)S(1)} %get-tuple-element.113.refs_0_.refs_3_.refs_1_.refs_8_, bf16[1536,1024]{1,0:T(8,128)(2,1)S(1)} %get-tuple-element.114.refs_1_.refs_4_.refs_2_.refs_9_, ...), custom_call_target="tpu_custom_call" | custom-call | flops 402653184 | bytes 1048576 | tf_op jit(solution)/shard_map/pallas_call | solution.py:50
  100.7 0.9 shard_map.102.refs_0_
  101.6 2.8 %collective-permute-done.35.refs_4_ = f32[192,128]{1,0:T(8,128)S(1)} collective-permute-done((f32[192,128]{1,0:T(8,128)S(1)}, f32[192,128]{1,0:T(8,128)S(1)}, u32[]{:S(2)}, u32[]{:S(2)}) %collective-permute-start.35) | collective-permute-done | bytes 98336 | tf_op jit(solution)/shard_map/ppermute | solution.py:71
  104.4 1.4 %shard_map.104 = (f32[64,1024]{1,0:T(8,128)}, f32[9,64,256]{2,1,0:T(8,128)}) custom-call(f32[64,1024]{1,0:T(8,128)S(1)} %shard_map.102.refs_0_, bf16[1536,1024]{1,0:T(8,128)(2,1)S(1)} %get-tuple-element.113.refs_0_.refs_3_.refs_1_.refs_8_, bf16[1536,1024]{1,0:T(8,128)(2,1)S(1)} %get-tuple-element.114.refs_1_.refs_4_.refs_2_.refs_9_, ...), custom_call_target="tpu_custom_call" | custom-call | bytes 1048576 | tf_op jit(solution)/shard_map/pallas_call | solution.py:50
  (59 shorter events, 11.1 us)
Async XLA Ops:
  1.6 10.1 %collective-permute-start = (bf16[128,1024]{1,0:T(8,128)(2,1)S(1)}, bf16[128,1024]{1,0:T(8,128)(2,1)S(1)}, u32[]{:S(2)}, u32[]{:S(2)}) collective-permute-start(bf16[128,1024]{1,0:T(8,128)(2,1)S(1)} %shard_map.77.refs_3_.refs_0_.refs_6_.refs_7_), channel_id=1, source_target_pairs={{0,2},{1,3},{2,0},{3,1},{4,6},{5,7},{6,4},{7,5},{8,10},{9,11},{10,... | collective-permute-start | bytes 786440 | tf_op jit(solution)/shard_map/ppermute | solution.py:121
  11.8 1.9 %collective-permute-start.1 = (bf16[128,1024]{1,0:T(8,128)(2,1)S(1)}, bf16[128,1024]{1,0:T(8,128)(2,1)S(1)}, u32[]{:S(2)}, u32[]{:S(2)}) collective-permute-start(bf16[128,1024]{1,0:T(8,128)(2,1)S(1)} %shard_map.77.refs_3_.refs_0_.refs_6_.refs_7_), channel_id=1, source_target_pairs={{0,1},{1,0},{2,3},{3,2},{4,5},{5,4},{6,7},{7,6},{8,9},{9,8},{10,11... | collective-permute-start | bytes 786440 | tf_op jit(solution)/shard_map/ppermute | solution.py:121
  11.9 1.9 %collective-permute-start.2 = (bf16[128,1024]{1,0:T(8,128)(2,1)S(1)}, bf16[128,1024]{1,0:T(8,128)(2,1)S(1)}, u32[]{:S(2)}, u32[]{:S(2)}) collective-permute-start(bf16[128,1024]{1,0:T(8,128)(2,1)S(1)} %collective-permute-done.refs_5_.refs_1_), channel_id=1, source_target_pairs={{0,1},{1,0},{2,3},{3,2},{4,5},{5,4},{6,7},{7,6},{8,9},{9,8},{10,11... | collective-permute-start | bytes 786440 | tf_op jit(solution)/shard_map/ppermute | solution.py:121
  12.4 1.3 %copy-start = (bf16[9,64,256]{2,1,0:T(8,128)(2,1)S(1)}, bf16[9,64,256]{2,1,0:T(8,128)(2,1)}, u32[]{:S(2)}) copy-start(bf16[9,64,256]{2,1,0:T(8,128)(2,1)} %param.8) | copy-start | bytes 884740
  14.3 10.1 %collective-permute-start.3 = (f32[192,128]{1,0:T(8,128)S(1)}, f32[192,128]{1,0:T(8,128)S(1)}, u32[]{:S(2)}, u32[]{:S(2)}) collective-permute-start(f32[192,128]{1,0:T(8,128)S(1)} %get-tuple-element.123), channel_id=1, source_target_pairs={{0,8},{4,12},{8,0},{12,4},{16,24},{20,28},{24,16},{28,20},{1,9},{5... | collective-permute-start | bytes 294920 | tf_op jit(solution)/shard_map/ppermute | solution.py:71
  15.9 9.3 %collective-permute-start.4 = (f32[192,128]{1,0:T(8,128)S(1)}, f32[192,128]{1,0:T(8,128)S(1)}, u32[]{:S(2)}, u32[]{:S(2)}) collective-permute-start(f32[192,128]{1,0:T(8,128)S(1)} %get-tuple-element.124), channel_id=1, source_target_pairs={{0,28},{4,8},{8,4},{12,16},{16,12},{20,24},{24,20},{28,0},{1,29},{... | collective-permute-start | bytes 294920 | tf_op jit(solution)/shard_map/ppermute | solution.py:71
  19.3 6.4 %collective-permute-start.5 = (f32[192,128]{1,0:T(8,128)S(1)}, f32[192,128]{1,0:T(8,128)S(1)}, u32[]{:S(2)}, u32[]{:S(2)}) collective-permute-start(f32[192,128]{1,0:T(8,128)S(1)} %get-tuple-element.125), channel_id=1, source_target_pairs={{0,24},{4,28},{8,16},{12,20},{16,8},{20,12},{24,0},{28,4},{1,25},{... | collective-permute-start | bytes 294920 | tf_op jit(solution)/shard_map/ppermute | solution.py:71
  20.9 5.4 %collective-permute-start.6 = (f32[192,128]{1,0:T(8,128)S(1)}, f32[192,128]{1,0:T(8,128)S(1)}, u32[]{:S(2)}, u32[]{:S(2)}) collective-permute-start(f32[192,128]{1,0:T(8,128)S(1)} %get-tuple-element.126), channel_id=1, source_target_pairs={{0,4},{4,0},{8,12},{12,8},{16,20},{20,16},{24,28},{28,24},{1,5},{5... | collective-permute-start | bytes 294920 | tf_op jit(solution)/shard_map/ppermute | solution.py:71
  26.9 9.0 %collective-permute-start.7 = (f32[192,128]{1,0:T(8,128)S(1)}, f32[192,128]{1,0:T(8,128)S(1)}, u32[]{:S(2)}, u32[]{:S(2)}) collective-permute-start(f32[192,128]{1,0:T(8,128)S(1)} %get-tuple-element.135), channel_id=1, source_target_pairs={{0,8},{4,12},{8,0},{12,4},{16,24},{20,28},{24,16},{28,20},{1,9},{5... | collective-permute-start | bytes 294920 | tf_op jit(solution)/shard_map/ppermute | solution.py:71
  27.0 9.1 %collective-permute-start.8 = (f32[192,128]{1,0:T(8,128)S(1)}, f32[192,128]{1,0:T(8,128)S(1)}, u32[]{:S(2)}, u32[]{:S(2)}) collective-permute-start(f32[192,128]{1,0:T(8,128)S(1)} %get-tuple-element.136), channel_id=1, source_target_pairs={{0,28},{4,8},{8,4},{12,16},{16,12},{20,24},{24,20},{28,0},{1,29},{... | collective-permute-start | bytes 294920 | tf_op jit(solution)/shard_map/ppermute | solution.py:71
  30.4 6.5 %collective-permute-start.9 = (f32[192,128]{1,0:T(8,128)S(1)}, f32[192,128]{1,0:T(8,128)S(1)}, u32[]{:S(2)}, u32[]{:S(2)}) collective-permute-start(f32[192,128]{1,0:T(8,128)S(1)} %get-tuple-element.137), channel_id=1, source_target_pairs={{0,24},{4,28},{8,16},{12,20},{16,8},{20,12},{24,0},{28,4},{1,25},{... | collective-permute-start | bytes 294920 | tf_op jit(solution)/shard_map/ppermute | solution.py:71
  31.6 5.3 %collective-permute-start.10 = (f32[192,128]{1,0:T(8,128)S(1)}, f32[192,128]{1,0:T(8,128)S(1)}, u32[]{:S(2)}, u32[]{:S(2)}) collective-permute-start(f32[192,128]{1,0:T(8,128)S(1)} %get-tuple-element.138), channel_id=1, source_target_pairs={{0,4},{4,0},{8,12},{12,8},{16,20},{20,16},{24,28},{28,24},{1,5},{5... | collective-permute-start | bytes 294920 | tf_op jit(solution)/shard_map/ppermute | solution.py:71
  38.0 11.1 %collective-permute-start.19 = (bf16[128,1024]{1,0:T(8,128)(2,1)S(1)}, bf16[128,1024]{1,0:T(8,128)(2,1)S(1)}, u32[]{:S(2)}, u32[]{:S(2)}) collective-permute-start(bf16[128,1024]{1,0:T(8,128)(2,1)S(1)} %get-tuple-element.161.refs_0_), channel_id=1, source_target_pairs={{0,2},{1,3},{2,0},{3,1},{4,6},{5,7},{6,4},{7,5},{8,10},{9,11},{10,... | collective-permute-start | bytes 786440 | tf_op jit(solution)/shard_map/ppermute | solution.py:121
  39.2 8.6 %collective-permute-start.11 = (f32[128,128]{1,0:T(8,128)S(1)}, f32[128,128]{1,0:T(8,128)S(1)}, u32[]{:S(2)}, u32[]{:S(2)}) collective-permute-start(f32[128,128]{1,0:T(8,128)S(1)} %get-tuple-element.143), channel_id=1, source_target_pairs={{0,8},{4,12},{8,0},{12,4},{16,24},{20,28},{24,16},{28,20},{1,9},{5... | collective-permute-start | bytes 196616 | tf_op jit(solution)/shard_map/ppermute | solution.py:71
  40.2 7.6 %collective-permute-start.12 = (f32[128,128]{1,0:T(8,128)S(1)}, f32[128,128]{1,0:T(8,128)S(1)}, u32[]{:S(2)}, u32[]{:S(2)}) collective-permute-start(f32[128,128]{1,0:T(8,128)S(1)} %get-tuple-element.144), channel_id=1, source_target_pairs={{0,28},{4,8},{8,4},{12,16},{16,12},{20,24},{24,20},{28,0},{1,29},{... | collective-permute-start | bytes 196616 | tf_op jit(solution)/shard_map/ppermute | solution.py:71
  41.8 6.1 %collective-permute-start.13 = (f32[128,128]{1,0:T(8,128)S(1)}, f32[128,128]{1,0:T(8,128)S(1)}, u32[]{:S(2)}, u32[]{:S(2)}) collective-permute-start(f32[128,128]{1,0:T(8,128)S(1)} %get-tuple-element.145), channel_id=1, source_target_pairs={{0,24},{4,28},{8,16},{12,20},{16,8},{20,12},{24,0},{28,4},{1,25},{... | collective-permute-start | bytes 196616 | tf_op jit(solution)/shard_map/ppermute | solution.py:71
  43.8 4.3 %collective-permute-start.14 = (f32[128,128]{1,0:T(8,128)S(1)}, f32[128,128]{1,0:T(8,128)S(1)}, u32[]{:S(2)}, u32[]{:S(2)}) collective-permute-start(f32[128,128]{1,0:T(8,128)S(1)} %get-tuple-element.146), channel_id=1, source_target_pairs={{0,4},{4,0},{8,12},{12,8},{16,20},{20,16},{24,28},{28,24},{1,5},{5... | collective-permute-start | bytes 196616 | tf_op jit(solution)/shard_map/ppermute | solution.py:71
  49.0 4.3 %collective-permute-start.20 = (bf16[128,1024]{1,0:T(8,128)(2,1)S(1)}, bf16[128,1024]{1,0:T(8,128)(2,1)S(1)}, u32[]{:S(2)}, u32[]{:S(2)}) collective-permute-start(bf16[128,1024]{1,0:T(8,128)(2,1)S(1)} %get-tuple-element.161.refs_0_), channel_id=1, source_target_pairs={{0,1},{1,0},{2,3},{3,2},{4,5},{5,4},{6,7},{7,6},{8,9},{9,8},{10,11... | collective-permute-start | bytes 786440 | tf_op jit(solution)/shard_map/ppermute | solution.py:121
  49.1 7.2 %collective-permute-start.21 = (bf16[128,1024]{1,0:T(8,128)(2,1)S(1)}, bf16[128,1024]{1,0:T(8,128)(2,1)S(1)}, u32[]{:S(2)}, u32[]{:S(2)}) collective-permute-start(bf16[128,1024]{1,0:T(8,128)(2,1)S(1)} %collective-permute-done.19.refs_1_), channel_id=1, source_target_pairs={{0,1},{1,0},{2,3},{3,2},{4,5},{5,4},{6,7},{7,6},{8,9},{9,8},{10,11... | collective-permute-start | bytes 786440 | tf_op jit(solution)/shard_map/ppermute | solution.py:121
  49.6 9.8 %collective-permute-start.18 = (f32[384,128]{1,0:T(8,128)S(1)}, f32[384,128]{1,0:T(8,128)S(1)}, u32[]{:S(2)}, u32[]{:S(2)}) collective-permute-start(f32[384,128]{1,0:T(8,128)S(1)} %get-tuple-element.157), channel_id=1, source_target_pairs={{0,4},{4,0},{8,12},{12,8},{16,20},{20,16},{24,28},{28,24},{1,5},{5... | collective-permute-start | bytes 589832 | tf_op jit(solution)/shard_map/ppermute | solution.py:71
  51.3 8.0 %collective-permute-start.15 = (f32[128,128]{1,0:T(8,128)S(1)}, f32[128,128]{1,0:T(8,128)S(1)}, u32[]{:S(2)}, u32[]{:S(2)}) collective-permute-start(f32[128,128]{1,0:T(8,128)S(1)} %get-tuple-element.154), channel_id=1, source_target_pairs={{0,8},{4,12},{8,0},{12,4},{16,24},{20,28},{24,16},{28,20},{1,9},{5... | collective-permute-start | bytes 196616 | tf_op jit(solution)/shard_map/ppermute | solution.py:71
  51.3 7.4 %collective-permute-start.16 = (f32[128,128]{1,0:T(8,128)S(1)}, f32[128,128]{1,0:T(8,128)S(1)}, u32[]{:S(2)}, u32[]{:S(2)}) collective-permute-start(f32[128,128]{1,0:T(8,128)S(1)} %get-tuple-element.155), channel_id=1, source_target_pairs={{0,28},{4,8},{8,4},{12,16},{16,12},{20,24},{24,20},{28,0},{1,29},{... | collective-permute-start | bytes 196616 | tf_op jit(solution)/shard_map/ppermute | solution.py:71
  53.3 6.1 %collective-permute-start.17 = (f32[128,128]{1,0:T(8,128)S(1)}, f32[128,128]{1,0:T(8,128)S(1)}, u32[]{:S(2)}, u32[]{:S(2)}) collective-permute-start(f32[128,128]{1,0:T(8,128)S(1)} %get-tuple-element.156), channel_id=1, source_target_pairs={{0,24},{4,28},{8,16},{12,20},{16,8},{20,12},{24,0},{28,4},{1,25},{... | collective-permute-start | bytes 196616 | tf_op jit(solution)/shard_map/ppermute | solution.py:71
  59.9 11.1 %collective-permute-start.25 = (f32[320,128]{1,0:T(8,128)S(1)}, f32[320,128]{1,0:T(8,128)S(1)}, u32[]{:S(2)}, u32[]{:S(2)}) collective-permute-start(f32[320,128]{1,0:T(8,128)S(1)} %get-tuple-element.178), channel_id=1, source_target_pairs={{0,4},{4,0},{8,12},{12,8},{16,20},{20,16},{24,28},{28,24},{1,5},{5... | collective-permute-start | bytes 491528 | tf_op jit(solution)/shard_map/ppermute | solution.py:71
  61.6 9.3 %collective-permute-start.22 = (f32[256,128]{1,0:T(8,128)S(1)}, f32[256,128]{1,0:T(8,128)S(1)}, u32[]{:S(2)}, u32[]{:S(2)}) collective-permute-start(f32[256,128]{1,0:T(8,128)S(1)} %get-tuple-element.175), channel_id=1, source_target_pairs={{0,8},{4,12},{8,0},{12,4},{16,24},{20,28},{24,16},{28,20},{1,9},{5... | collective-permute-start | bytes 393224 | tf_op jit(solution)/shard_map/ppermute | solution.py:71
  62.4 8.6 %collective-permute-start.24 = (f32[256,128]{1,0:T(8,128)S(1)}, f32[256,128]{1,0:T(8,128)S(1)}, u32[]{:S(2)}, u32[]{:S(2)}) collective-permute-start(f32[256,128]{1,0:T(8,128)S(1)} %get-tuple-element.177), channel_id=1, source_target_pairs={{0,24},{4,28},{8,16},{12,20},{16,8},{20,12},{24,0},{28,4},{1,25},{... | collective-permute-start | bytes 393224 | tf_op jit(solution)/shard_map/ppermute | solution.py:71
  63.9 7.0 %collective-permute-start.23 = (f32[128,128]{1,0:T(8,128)S(1)}, f32[128,128]{1,0:T(8,128)S(1)}, u32[]{:S(2)}, u32[]{:S(2)}) collective-permute-start(f32[128,128]{1,0:T(8,128)S(1)} %get-tuple-element.176), channel_id=1, source_target_pairs={{0,28},{4,8},{8,4},{12,16},{16,12},{20,24},{24,20},{28,0},{1,29},{... | collective-permute-start | bytes 196616 | tf_op jit(solution)/shard_map/ppermute | solution.py:71
  71.4 10.8 %collective-permute-start.26 = (f32[352,128]{1,0:T(8,128)S(1)}, f32[352,128]{1,0:T(8,128)S(1)}, u32[]{:S(2)}, u32[]{:S(2)}) collective-permute-start(f32[352,128]{1,0:T(8,128)S(1)} %get-tuple-element.187), channel_id=1, source_target_pairs={{0,8},{4,12},{8,0},{12,4},{16,24},{20,28},{24,16},{28,20},{1,9},{5... | collective-permute-start | bytes 540680 | tf_op jit(solution)/shard_map/ppermute | solution.py:71
  71.5 10.8 %collective-permute-start.28 = (f32[352,128]{1,0:T(8,128)S(1)}, f32[352,128]{1,0:T(8,128)S(1)}, u32[]{:S(2)}, u32[]{:S(2)}) collective-permute-start(f32[352,128]{1,0:T(8,128)S(1)} %get-tuple-element.189), channel_id=1, source_target_pairs={{0,24},{4,28},{8,16},{12,20},{16,8},{20,12},{24,0},{28,4},{1,25},{... | collective-permute-start | bytes 540680 | tf_op jit(solution)/shard_map/ppermute | solution.py:71
  73.8 8.3 %collective-permute-start.27 = (f32[128,128]{1,0:T(8,128)S(1)}, f32[128,128]{1,0:T(8,128)S(1)}, u32[]{:S(2)}, u32[]{:S(2)}) collective-permute-start(f32[128,128]{1,0:T(8,128)S(1)} %get-tuple-element.188), channel_id=1, source_target_pairs={{0,28},{4,8},{8,4},{12,16},{16,12},{20,24},{24,20},{28,0},{1,29},{... | collective-permute-start | bytes 196616 | tf_op jit(solution)/shard_map/ppermute | solution.py:71
  76.5 5.7 %collective-permute-start.29 = (f32[256,128]{1,0:T(8,128)S(1)}, f32[256,128]{1,0:T(8,128)S(1)}, u32[]{:S(2)}, u32[]{:S(2)}) collective-permute-start(f32[256,128]{1,0:T(8,128)S(1)} %get-tuple-element.190), channel_id=1, source_target_pairs={{0,4},{4,0},{8,12},{12,8},{16,20},{20,16},{24,28},{28,24},{1,5},{5... | collective-permute-start | bytes 393224 | tf_op jit(solution)/shard_map/ppermute | solution.py:71
  82.7 10.6 %collective-permute-start.30 = (f32[352,128]{1,0:T(8,128)S(1)}, f32[352,128]{1,0:T(8,128)S(1)}, u32[]{:S(2)}, u32[]{:S(2)}) collective-permute-start(f32[352,128]{1,0:T(8,128)S(1)} %get-tuple-element.200), channel_id=1, source_target_pairs={{0,8},{4,12},{8,0},{12,4},{16,24},{20,28},{24,16},{28,20},{1,9},{5... | collective-permute-start | bytes 540680 | tf_op jit(solution)/shard_map/ppermute | solution.py:71
  82.8 10.5 %collective-permute-start.32 = (f32[352,128]{1,0:T(8,128)S(1)}, f32[352,128]{1,0:T(8,128)S(1)}, u32[]{:S(2)}, u32[]{:S(2)}) collective-permute-start(f32[352,128]{1,0:T(8,128)S(1)} %get-tuple-element.202), channel_id=1, source_target_pairs={{0,24},{4,28},{8,16},{12,20},{16,8},{20,12},{24,0},{28,4},{1,25},{... | collective-permute-start | bytes 540680 | tf_op jit(solution)/shard_map/ppermute | solution.py:71
  85.8 7.4 %collective-permute-start.31 = (f32[64,128]{1,0:T(8,128)S(1)}, f32[64,128]{1,0:T(8,128)S(1)}, u32[]{:S(2)}, u32[]{:S(2)}) collective-permute-start(f32[64,128]{1,0:T(8,128)S(1)} %get-tuple-element.201), channel_id=1, source_target_pairs={{0,28},{4,8},{8,4},{12,16},{16,12},{20,24},{24,20},{28,0},{1,29},{... | collective-permute-start | bytes 98312 | tf_op jit(solution)/shard_map/ppermute | solution.py:71
  88.2 5.0 %collective-permute-start.33 = (f32[192,128]{1,0:T(8,128)S(1)}, f32[192,128]{1,0:T(8,128)S(1)}, u32[]{:S(2)}, u32[]{:S(2)}) collective-permute-start(f32[192,128]{1,0:T(8,128)S(1)} %get-tuple-element.203), channel_id=1, source_target_pairs={{0,4},{4,0},{8,12},{12,8},{16,20},{20,16},{24,28},{28,24},{1,5},{5... | collective-permute-start | bytes 294920 | tf_op jit(solution)/shard_map/ppermute | solution.py:71
  93.5 10.9 %collective-permute-start.37 = (f32[512,128]{1,0:T(8,128)S(1)}, f32[512,128]{1,0:T(8,128)S(1)}, u32[]{:S(2)}, u32[]{:S(2)}) collective-permute-start(f32[512,128]{1,0:T(8,128)S(1)} %get-tuple-element.214), channel_id=1, source_target_pairs={{0,4},{4,0},{8,12},{12,8},{16,20},{20,16},{24,28},{28,24},{1,5},{5... | collective-permute-start | bytes 786440 | tf_op jit(solution)/shard_map/ppermute | solution.py:71
  93.8 10.6 %collective-permute-start.34 = (f32[256,128]{1,0:T(8,128)S(1)}, f32[256,128]{1,0:T(8,128)S(1)}, u32[]{:S(2)}, u32[]{:S(2)}) collective-permute-start(f32[256,128]{1,0:T(8,128)S(1)} %get-tuple-element.211), channel_id=1, source_target_pairs={{0,8},{4,12},{8,0},{12,4},{16,24},{20,28},{24,16},{28,20},{1,9},{5... | collective-permute-start | bytes 393224 | tf_op jit(solution)/shard_map/ppermute | solution.py:71
  95.5 8.9 %collective-permute-start.36 = (f32[256,128]{1,0:T(8,128)S(1)}, f32[256,128]{1,0:T(8,128)S(1)}, u32[]{:S(2)}, u32[]{:S(2)}) collective-permute-start(f32[256,128]{1,0:T(8,128)S(1)} %get-tuple-element.213), channel_id=1, source_target_pairs={{0,24},{4,28},{8,16},{12,20},{16,8},{20,12},{24,0},{28,4},{1,25},{... | collective-permute-start | bytes 393224 | tf_op jit(solution)/shard_map/ppermute | solution.py:71
  97.0 7.4 %collective-permute-start.35 = (f32[192,128]{1,0:T(8,128)S(1)}, f32[192,128]{1,0:T(8,128)S(1)}, u32[]{:S(2)}, u32[]{:S(2)}) collective-permute-start(f32[192,128]{1,0:T(8,128)S(1)} %get-tuple-element.212), channel_id=1, source_target_pairs={{0,28},{4,8},{8,4},{12,16},{16,12},{20,24},{24,20},{28,0},{1,29},{... | collective-permute-start | bytes 294920 | tf_op jit(solution)/shard_map/ppermute | solution.py:71
